TPU v7x, 32 devices: a whole 2x2x4 slice. The times are simulated.
32 devices in a mesh: dp: 16 (over z, y, x), tensor: 2 (over core).
Axes of the slice: x: 2, y: 2, z: 4, core: 2. Of those that a mesh axis runs over, the one named last changes fastest.
Arguments:
- hidden_in: bfloat16 [4096, 2048], P(('dp', 'tensor')), may hold values from -6 to 6
- segments: int32 [16, 256], P('dp'), may hold values from 0 to 3, never falling along the last dimension, each value on 1 to 128 neighbouring positions
- mix_weights: bfloat16 [2048, 4, 2048], P('dp', None, 'tensor'), may hold values from -0.125 to 0.125
- ffn_weights: bfloat16 [2048, 3, 5632], P('dp', None, 'tensor'), may hold values from -0.125 to 0.125
- norm1_gain: float32 [2048], replicated, may hold values from 0.25 to 1.75
- norm2_gain: float32 [2048], replicated, may hold values from 0.25 to 1.75
- head_gain: float32 [128], replicated, may hold values from 0.25 to 1.75
- lower_bound: float32 [2048], P('tensor'), may hold values from 0.05 to 0.97
- out_grad: bfloat16 [4096, 2048], P(('dp', 'tensor')), may hold values from -6 to 6
Outputs:
- block_out: bfloat16 [4096, 2048], P(('dp', 'tensor'))
- input_grad: float32 [4096, 2048], P(('dp', 'tensor'))
- mix_weights_grad: float32 [2048, 4, 2048], P('dp', None, 'tensor')
- ffn_weights_grad: float32 [2048, 3, 5632], P('dp', None, 'tensor')
- norm1_gain_grad: float32 [2048], replicated
- norm2_gain_grad: float32 [2048], replicated
- head_gain_grad: float32 [128], replicated
- lower_bound_grad: float32 [2048], replicated
Inputs may be any that keep to these rules, and one draw needn't show every extreme that they name: `segments`: along each sequence the numbers never fall; each of the 4 documents of a sequence is a run of 1 to 128 tokens, and one run is exactly 128 long.
All inputs are finite; a program needn't handle non-finite values.
Results may differ from a plain program's by a relative error of at most 0.0085.
Values may be sent and summed in bfloat16 or wider, within the bound.
No kernel may reach another device: no remote copies, remote signals or barrier semaphores. Data moves between devices by JAX's collectives and lax.ppermute only.
A program may use at most 320 MiB of HBM per device.

v0:
```python
import jax
import jax.numpy as jnp
from jax import lax
from jax.sharding import PartitionSpec as P

SPAN = 64


epsilon = 1e-06
peak_value = lax.Precision.HIGHEST


def rms_norm(values, scales):
    return values * lax.rsqrt(jnp.mean(values * values, axis=-1, keepdims=True) + epsilon) * scales


def block_step(carried, inputs):
    running_state, last_seen = carried
    query_rows, incoming_keys, incoming_values, log_decay, labels = inputs
    float_kind = query_rows.dtype
    block_len = labels.shape[0]
    grand_totals = jnp.cumsum(log_decay, axis=1)
    position = jnp.arange(block_len, dtype=jnp.int32)
    allowed = (labels[:, None] == labels[None, :]) & (position[:, None] >= position[None, :])
    allowed_full = allowed[None, :, :, None]
    spread_log = grand_totals[:, :, None, :] - grand_totals[:, None, :, :]
    weights_in = jnp.exp(jnp.where(allowed_full, spread_log, 0.0)) * allowed_full.astype(float_kind)
    scores = jnp.sum(query_rows[:, :, None, :] * incoming_keys[:, None, :, :] * weights_in, axis=-1)
    inside = jnp.einsum("hts,hsv->htv", scores, incoming_values, precision=peak_value)
    joined_rows = (labels == last_seen).astype(float_kind)
    external_part = (
        jnp.einsum(
            "ewy,eyi->ewi", query_rows * jnp.exp(grand_totals), running_state, precision=peak_value
        )
        * joined_rows[None, :, None]
    )
    final_log = grand_totals[:, -1:, :]
    same_last = (labels == labels[-1])[None, :, None]
    toward_final = jnp.exp(jnp.where(same_last, final_log - grand_totals, 0.0)) * same_last.astype(
        float_kind
    )
    renewed_sum = jnp.einsum(
        "rfj,rfe->rje", incoming_keys * toward_final, incoming_values, precision=peak_value
    )
    survive = (labels[-1] == last_seen).astype(float_kind)
    running_state = running_state * jnp.exp(final_log[:, 0, :])[:, :, None] * survive + renewed_sum
    return ((running_state, labels[-1]), inside + external_part)


def mixer_core(projected, floor_gate, head_scale, labels):
    length = projected.shape[0]
    size_head = head_scale.shape[0]
    count_heads = projected.shape[2] // size_head
    query_rows = jax.nn.silu(projected[:, 0])
    forget = floor_gate + (1.0 - floor_gate) * jax.nn.sigmoid(projected[:, 1])
    incoming_keys = 1.0 - forget
    log_decay = jnp.log(forget)
    incoming_values = projected[:, 2]
    blocks_count = length // SPAN

    def arrange(source):
        return source.reshape(blocks_count, SPAN, count_heads, size_head).transpose(0, 2, 1, 3)

    inputs = (
        arrange(query_rows),
        arrange(incoming_keys),
        arrange(incoming_values),
        arrange(log_decay),
        labels.reshape(blocks_count, SPAN),
    )
    initial = (
        jnp.zeros((count_heads, size_head, size_head), projected.dtype),
        jnp.asarray(-1, jnp.int32),
    )
    _, produced = lax.scan(jax.checkpoint(block_step), initial, inputs)
    recurrent = produced.transpose(0, 2, 1, 3).reshape(length, count_heads, size_head)
    return rms_norm(recurrent, head_scale).reshape(length, count_heads * size_head)


def swiglu(gate_up):
    return jax.nn.silu(gate_up[:, 0]) * gate_up[:, 1]


def spread_rows(local_rows):
    return lax.all_gather(local_rows, "tensor", axis=0, tiled=True)


def spread_grads(local_rows):
    return lax.all_gather(local_rows, "tensor", axis=0, tiled=True)


def project_out(source, weight):
    share_rows = source.shape[0] // lax.axis_size("tensor")

    def row_term(offset, amount):
        return jnp.einsum("tx,dx->td", source, weight, preferred_element_type=jnp.float32)

    return lax.psum_scatter(
        row_term(jnp.int32(0), share_rows * lax.axis_size("tensor")),
        "tensor",
        scatter_dimension=0,
        tiled=True,
    )


def project_back(source, weight):
    share_rows = source.shape[0] // lax.axis_size("tensor")

    def row_term(offset, amount):
        return jnp.einsum("tkx,dkx->td", source, weight, preferred_element_type=jnp.float32)

    return lax.psum_scatter(
        row_term(jnp.int32(0), share_rows * lax.axis_size("tensor")),
        "tensor",
        scatter_dimension=0,
        tiled=True,
    )


def body(
    hidden_in,
    segments,
    mix_weights,
    ffn_weights,
    norm1_gain,
    norm2_gain,
    head_gain,
    lower_bound,
    out_grad,
):
    mix_full = lax.all_gather(mix_weights, "dp", axis=0, tiled=True)
    hidden = hidden_in.astype(jnp.float32)
    normed, norm_one_back = jax.vjp(rms_norm, hidden, norm1_gain)
    normed_full = spread_rows(normed.astype(jnp.bfloat16))
    projected = jnp.einsum(
        "td,dkx->tkx", normed_full, mix_full[:, :3], preferred_element_type=jnp.float32
    )
    labels = segments[0]

    def local_mixer(source, floor_gate, gain_head):
        return mixer_core(source, floor_gate, gain_head, labels)

    mixed_out, mixer_back = jax.vjp(local_mixer, projected, lower_bound, head_gain)
    mixed_low = mixed_out.astype(jnp.bfloat16)
    middle = hidden + project_out(mixed_low, mix_full[:, 3])
    ffn_full = lax.all_gather(ffn_weights, "dp", axis=0, tiled=True)
    normed_two, norm_two_back = jax.vjp(rms_norm, middle, norm2_gain)
    normed_two_full = spread_rows(normed_two.astype(jnp.bfloat16))
    gate_up = jnp.einsum(
        "td,dkx->tkx", normed_two_full, ffn_full[:, :2], preferred_element_type=jnp.float32
    )
    active, active_back = jax.vjp(swiglu, gate_up)
    active_low = active.astype(jnp.bfloat16)
    block_out = (middle + project_out(active_low, ffn_full[:, 2])).astype(jnp.bfloat16)
    ffn_back = lax.all_gather(ffn_weights, "dp", axis=0, tiled=True)
    out_grad_full = spread_grads(out_grad)
    active_grad = jnp.einsum(
        "td,dx->tx", out_grad_full, ffn_back[:, 2], preferred_element_type=jnp.float32
    )
    gate_up_grad = active_back(active_grad)[0].astype(jnp.bfloat16)
    left_cols = normed_two_full
    right_cols = out_grad_full
    inputs_part = jnp.einsum(
        "tr,tkx->rkx", left_cols, gate_up_grad, preferred_element_type=jnp.float32
    )
    output_part = jnp.einsum(
        "tr,tx->rx", right_cols, active_low, preferred_element_type=jnp.float32
    )
    ffn_grad = lax.psum_scatter(
        jnp.concatenate([inputs_part, output_part[:, None, :]], axis=1),
        "dp",
        scatter_dimension=0,
        tiled=True,
    )
    normed_two_grad = project_back(gate_up_grad, ffn_back[:, :2])
    middle_extra, gain_two_grad = norm_two_back(normed_two_grad)
    middle_grad = out_grad.astype(jnp.float32) + middle_extra
    middle_grad_full = spread_grads(middle_grad.astype(jnp.bfloat16))
    mix_back = lax.all_gather(mix_weights, "dp", axis=0, tiled=True)
    mixed_grad = jnp.einsum(
        "td,dx->tx", middle_grad_full, mix_back[:, 3], preferred_element_type=jnp.float32
    )
    projected_grad, lower_grad, head_grad = mixer_back(mixed_grad)
    projected_low = projected_grad.astype(jnp.bfloat16)
    left_cols = normed_full
    right_cols = middle_grad_full
    inputs_part = jnp.einsum(
        "tr,tkx->rkx", left_cols, projected_low, preferred_element_type=jnp.float32
    )
    output_part = jnp.einsum("tr,tx->rx", right_cols, mixed_low, preferred_element_type=jnp.float32)
    mix_grad = lax.psum_scatter(
        jnp.concatenate([inputs_part, output_part[:, None, :]], axis=1),
        "dp",
        scatter_dimension=0,
        tiled=True,
    )
    normed_grad = project_back(projected_low, mix_back[:, :3])
    hidden_extra, gain_one_grad = norm_one_back(normed_grad)
    input_grad = middle_grad + hidden_extra
    channels = lower_bound.shape[0]
    lower_full = jnp.zeros((channels * lax.axis_size("tensor"),), jnp.float32)
    lower_full = lax.dynamic_update_slice_in_dim(
        lower_full, lower_grad, lax.axis_index("tensor") * channels, 0
    )
    summed = lax.psum((gain_one_grad, gain_two_grad, head_grad, lower_full), ("dp", "tensor"))
    return (block_out, input_grad, mix_grad, ffn_grad, summed[0], summed[1], summed[2], summed[3])


def solution(mesh):
    return jax.shard_map(
        body,
        mesh=mesh,
        in_specs=(
            P(("dp", "tensor"), None),
            P("dp", None),
            P("dp", None, "tensor"),
            P("dp", None, "tensor"),
            P(),
            P(),
            P(),
            P("tensor"),
            P(("dp", "tensor"), None),
        ),
        out_specs=(
            P(("dp", "tensor"), None),
            P(("dp", "tensor"), None),
            P("dp", None, "tensor"),
            P("dp", None, "tensor"),
            P(),
            P(),
            P(),
            P(),
        ),
        check_vma=False,
    )
```

profile of v0, /device:TPU:0, one launch (start us, length us, event | category | flops | bytes accessed | tf_op | source)
XLA Modules:
  0.0 3109.8 jit_solution(17172381875248232534)
XLA Ops:
  16.1 7.4 all-gather.7.cloned.1.call-done
  23.5 196.0 %all-gather.9.cloned.1.call-done = bf16[2048,4,1024]{2,0,1:T(8,128)(2,1)} async-done(((bf16[128,4,1024]{2,0,1:T(8,128)(2,1)}), bf16[2048,4,1024]{2,0,1:T(8,128)(2,1)}) %all-gather.9.cloned.1.call-update) | async-done | bytes 16777232 | tf_op jit(solution)/shard_map/all_gather | solution.py:131
  219.4 6.7 fusion.62
  231.5 71.4 %while.43 = (s32[]{:T(128)}, f32[8,128,128]{2,1,0:T(8,128)S(1)}, s32[]{:T(128)}, f32[4,8,64,128]{3,2,1,0:T(8,128)S(1)}, f32[4,8,128,128]{3,2,1,0:T(8,128)}, /*in...) while((s32[]{:T(128)}, f32[8,128,128]{2,1,0:T(8,128)S(1)}, ...), condition=%wide.region_4.5_spmd.clone, body=%wide.region_1.4_spmd.clone.sunk | while | flops 282181888 | bytes 13831543 | solution.py:75
  236.7 9.4 multiply_reduce_fusion.10
  254.6 9.4 multiply_reduce_fusion.10
  272.4 9.4 multiply_reduce_fusion.10
  290.2 9.4 multiply_reduce_fusion.10
  308.9 7.9 reduce-scatter.7.cloned.1.call-done
  320.9 8.9 all-gather.11.cloned.1.call-done
  329.8 365.0 %all-gather.13.cloned.1.call-done = bf16[2048,3,2816]{2,0,1:T(8,128)(2,1)} async-done(((bf16[128,3,2816]{2,0,1:T(8,128)(2,1)}), bf16[2048,3,2816]{2,0,1:T(8,128)(2,1)}) %all-gather.13.cloned.1.call-update) | async-done | bytes 34603024 | tf_op jit(solution)/shard_map/all_gather | solution.py:146
  694.8 13.1 fusion.58
  707.9 9.9 multiply_bitcast_fusion
  717.8 13.3 fusion.76
  731.2 7.6 reduce-scatter.11.cloned.1.call-done
  748.6 6.6 copy.114
  765.9 178.9 %while.44 = (s32[]{:T(128)}, f32[8,128,128]{2,1,0:T(8,128)}, f32[4,8,64,128]{3,2,1,0:T(8,128)}, f32[4,8,64,128]{3,1,2,0:T(8,128)}, f32[4,8,64,128]{3,2,1,0:T(8,1...) while((s32[]{:T(128)}, f32[8,128,128]{2,1,0:T(8,128)}, ...), condition=%wide.region_22.23_spmd.clone, body=%wide.region_12.22_spmd.clone.sunk | while | flops 585744640 | bytes 21863696 | solution.py:75
  785.0 19.4 fusion.212
  817.7 6.3 fusion.208
  830.0 19.4 fusion.212
  862.6 6.3 fusion.208
  874.9 19.4 fusion.212
  919.8 19.4 fusion.212
  961.2 9.4 fusion.79
  970.7 10.5 fusion.65
  993.8 14.4 pad_maximum_fusion.1
  1008.4 14.6 convolution_bitcast_fusion
  1023.0 19.6 fusion.111
  1042.7 45.6 %pad_maximum_fusion = f32[2048,3,2816]{2,0,1:T(8,128)} fusion(f32[2048,1,2816]{2,0,1:T(8,128)} %convolution_bitcast_fusion, f32[2048,2,2816]{2,0,1:T(8,128)} %fusion.111), kind=kLoop, calls=%fused_computation.98 | loop fusion | flops 17301504 | bytes 138412032 | tf_op jit(solution)/shard_map/concatenate | solution.py:170
  1093.1 47.2 %all-reduce.6 = (f32[2048]{0:T(1024)}, f32[2048]{0:T(1024)}, f32[128]{0:T(128)}, f32[2048]{0:T(1024)}) all-reduce(f32[2048]{0:T(1024)S(1)} %get-tuple-element.579, f32[2048]{0:T(1024)S(1)} %copy-done.22, f32[128]{0:T(128)S(1)} %copy-done.34, ...), channel_id=1, replica_groups=mesh['dp'=16,'tensor'=2] {'dp','tensor'}, use_global_device_ids=true, to_apply=%region_28.29 | all-reduce | flops 6272 | bytes 50176 | tf_op jit(solution)/shard_map/psum | solution.py:205
  1143.8 550.6 %reduce-scatter.15.cloned.1.call-done = f32[128,4,1024]{2,0,1:T(8,128)} async-done(((f32[2048,4,1024]{2,0,1:T(8,128)}), f32[128,4,1024]{2,0,1:T(8,128)}) %reduce-scatter.15.cloned.1.call-update) | async-done | bytes 2097168 | tf_op jit(solution)/shard_map/reduce_scatter | solution.py:191
  1698.6 1403.9 %reduce-scatter.17.cloned.1.call-done = f32[128,3,2816]{2,0,1:T(8,128)} async-done(((f32[2048,3,2816]{2,0,1:T(8,128)}), f32[128,3,2816]{2,0,1:T(8,128)}) %reduce-scatter.17.cloned.1.call-update) | async-done | bytes 4325392 | tf_op jit(solution)/shard_map/reduce_scatter | solution.py:169
  (338 shorter events, 197.2 us)
Async XLA Ops:
  7.2 16.3 all-gather.7.cloned.1.call-start
  11.6 207.9 %all-gather.9.cloned.1.call-start = ((), (), s32[]{:S(2)}) async-start(), calls=%async_computation.7 | async-start | bytes 17825792 | tf_op jit(solution)/shard_map/all_gather | solution.py:131
  14.2 302.6 %reduce-scatter.7.cloned.1.call-start = ((), (), s32[]{:S(2)}) async-start(), calls=%async_computation.8 | async-start | bytes 3145728 | tf_op jit(solution)/shard_map/reduce_scatter | solution.py:98
  16.1 213.4 %copy-start.20 = (f32[8,128]{1,0:T(8,128)}, f32[8,128]{1,0:T(8,128)S(1)}, u32[]{:S(2)}) copy-start(f32[8,128]{1,0:T(8,128)S(1)} %get-tuple-element.678) | copy-start | bytes 12292
  231.5 71.7 %copy-start.28 = (f32[128]{0:T(128)S(1)}, f32[128]{0:T(128)}, u32[]{:S(2)}) copy-start(f32[128]{0:T(128)} %param.19) | copy-start | bytes 1540
  236.7 9.5 copy-start.2
  254.5 9.5 copy-start.2
  272.3 9.5 copy-start.2
  290.2 9.5 copy-start.2
  303.9 12.8 copy-start.3
  308.8 9.5 copy-start.16
  308.8 21.0 all-gather.11.cloned.1.call-start
  318.2 422.6 %copy-start = (f32[128,2048]{1,0:T(8,128)}, f32[128,2048]{1,0:T(8,128)S(1)}, u32[]{:S(2)}) copy-start(f32[128,2048]{1,0:T(8,128)S(1)} %get-tuple-element.646) | copy-start | bytes 3145732
  318.2 422.6 %copy-start.24 = (f32[128]{0:T(128)}, f32[128]{0:T(128)S(1)}, u32[]{:S(2)}) copy-start(f32[128]{0:T(128)S(1)} %fusion.123) | copy-start | bytes 1540
  319.4 375.3 %all-gather.13.cloned.1.call-start = ((), (), s32[]{:S(2)}) async-start(), calls=%async_computation.10 | async-start | bytes 36765696 | tf_op jit(solution)/shard_map/all_gather | solution.py:146
  320.0 387.8 %all-gather.15.cloned.1.call-start = ((), (), s32[]{:S(2)}) async-start(), calls=%async_computation.12 | async-start | bytes 1572864 | tf_op jit(solution)/shard_map/all_gather | solution.py:89
  320.6 418.2 %reduce-scatter.11.cloned.1.call-start = ((), (), s32[]{:S(2)}) async-start(), calls=%async_computation.13 | async-start | bytes 3145728 | tf_op jit(solution)/shard_map/reduce_scatter | solution.py:112
  731.1 9.7 copy-start.10
  731.1 24.1 all-gather.17.cloned.1.call-start
  743.3 348.1 %reduce-scatter.13.cloned.1.call-start = ((), (), s32[]{:S(2)}) async-start(), calls=%async_computation.15 | async-start | bytes 3145728 | tf_op jit(solution)/shard_map/reduce_scatter | solution.py:112
  944.8 10.6 copy-start.7
  947.7 8.8 copy-start.8
  970.6 169.6 %reduce-scatter.9.cloned.1.call-start = ((), (), s32[]{:S(2)}) async-start(), calls=%async_computation.11 | async-start | bytes 3145728 | tf_op jit(solution)/shard_map/reduce_scatter | solution.py:98
  981.2 713.2 %reduce-scatter.15.cloned.1.call-start = ((), (), s32[]{:S(2)}) async-start(), calls=%async_computation.16 | async-start | bytes 35651584 | tf_op jit(solution)/shard_map/reduce_scatter | solution.py:191
  1008.2 14.9 copy-start.15
  1008.2 2094.4 %reduce-scatter.17.cloned.1.call-start = ((), (), s32[]{:S(2)}) async-start(), calls=%async_computation.17 | async-start | bytes 73531392 | tf_op jit(solution)/shard_map/reduce_scatter | solution.py:169
  1088.3 51.9 %copy-start.33 = (f32[128]{0:T(128)S(1)}, f32[128]{0:T(128)}, u32[]{:S(2)}) copy-start(f32[128]{0:T(128)} %copy-done.32) | copy-start | bytes 1540
  1088.3 52.0 %copy-start.1 = (f32[128,2048]{1,0:T(8,128)S(1)}, f32[128,2048]{1,0:T(8,128)}, u32[]{:S(2)}) copy-start(f32[128,2048]{1,0:T(8,128)} %copy-done) | copy-start | bytes 3145732
  1088.3 52.0 %copy-start.11 = (bf16[128,2048]{1,0:T(8,128)(2,1)S(1)}, bf16[128,2048]{1,0:T(8,128)(2,1)}, u32[]{:S(2)}) copy-start(bf16[128,2048]{1,0:T(8,128)(2,1)} %param.21) | copy-start | bytes 1572868
  1088.4 52.0 %copy-start.17 = (f32[2048]{0:T(1024)S(1)}, f32[2048]{0:T(1024)}, u32[]{:S(2)}) copy-start(f32[2048]{0:T(1024)} %param.18) | copy-start | bytes 24580
  1088.4 51.9 %copy-start.25 = (f32[128]{0:T(128)S(1)}, f32[128]{0:T(128)}, u32[]{:S(2)}) copy-start(f32[128]{0:T(128)} %copy-done.24) | copy-start | bytes 1540
  1088.4 51.9 %copy-start.30 = (f32[128]{0:T(128)S(1)}, f32[128]{0:T(128)}, u32[]{:S(2)}) copy-start(f32[128]{0:T(128)} %copy-done.29) | copy-start | bytes 1540
  (18 other events, 56.7 us)
Sparse Core Ops, SparseCore 0:
  11.7 11.7 all-gather.6
  26.8 192.6 all-gather.8
  308.9 7.7 reduce-scatter.6
  319.6 10.2 all-gather.10
  332.8 361.9 all-gather.12
  696.2 7.2 all-gather.14
  731.3 7.4 reduce-scatter.10
  743.4 10.2 all-gather.16
  970.8 10.7 reduce-scatter.12
  983.8 10.7 reduce-scatter.8
  1008.3 686.0 reduce-scatter.14
  1697.2 1405.3 reduce-scatter.16
where the time goes:
time: 3120 us; the launch traced here: 3110 us
  waiting for transfers between devices  2550 us (82%)
  other arithmetic  256 us (8%)
  matrix products  157 us (5%)
  local copies, waits for them, and re-layouts  73.1 us (2%)
  blocking collectives  47.2 us (2%)
    reduce_scatter x2, waiting for transfers between devices, body(): lax.psum_scatter(jnp.concatenate([inputs_part, output_part[:, None, :]],...  1950 us
    all_gather x1, waiting for transfers between devices, body(): ffn_full = lax.all_gather(ffn_weights, 'dp', axis=0, tiled=True)  365 us
    all_gather x1, waiting for transfers between devices, body(): mix_full = lax.all_gather(mix_weights, 'dp', axis=0, tiled=True)  196 us
    reduce_sum x4, other arithmetic, block_step(): spread_log = grand_totals[:, :, None, :] - grand_totals[:, None, :, :]  77.5 us
  transfers between devices with their start and end apart: 12, of which 8 were waited for; matrix products, arithmetic and copies ran while one was open for 5% of the time, Pallas kernels for 0%

commit v1 on v0

v1 whole, which is shorter than its diff:
```python
import jax
import jax.numpy as jnp
from jax import lax
from jax.experimental import pallas as pl
from jax.experimental.pallas import tpu as pltpu
from jax.sharding import PartitionSpec as P

HEAD = 128
STRIP = 32
CAP = 50.0
epsilon = 1e-06


def dot(a, b, dims):
    return lax.dot_general(a, b, (dims, ((), ())), preferred_element_type=jnp.float32)


def exact_dot(ones, values):
    high = values.astype(jnp.bfloat16)
    rest = values - high.astype(jnp.float32)
    mid = rest.astype(jnp.bfloat16)
    tail = (rest - mid.astype(jnp.float32)).astype(jnp.bfloat16)
    dims = ((1,), (0,))
    return dot(ones, high, dims) + dot(ones, mid, dims) + dot(ones, tail, dims)


def gates(p0, p1, floor):
    swish = jax.nn.sigmoid(p0)
    gate = jax.nn.sigmoid(p1)
    forget = floor + (1.0 - floor) * gate
    return swish, gate, forget


def masks(seg_col, seg_row, length):
    row = lax.broadcasted_iota(jnp.int32, (length, length), 0)
    col = lax.broadcasted_iota(jnp.int32, (length, length), 1)
    same = seg_col == seg_row
    return same, row, col


def strips(length):
    out = []
    for start in range(0, length, STRIP):
        out.append((start, -(-(start + STRIP) // 128) * 128))
    return out


def fill_scores(length, query, key, totals, allowed, scores, keep=None):
    for start, wide in strips(length):
        rows = slice(start, start + STRIP)
        ref = totals[start + STRIP // 2 - 1 : start + STRIP // 2]
        lead = (query[rows] * jnp.exp(totals[rows] - ref)).astype(jnp.bfloat16)
        trail = (key[:wide] * jnp.exp(jnp.minimum(ref - totals[:wide], CAP))).astype(jnp.bfloat16)
        part = dot(lead, trail, ((1,), (1,)))
        part = jnp.where(allowed[rows, :wide], part, 0.0)
        scores[rows, :wide] = part.astype(jnp.bfloat16)
        if wide < length:
            scores[rows, wide:] = jnp.zeros((STRIP, length - wide), jnp.bfloat16)


def forward_kernel(p0_ref, p1_ref, p2_ref, col_ref, row_ref, floor_ref, gain_ref, out_ref, scores):
    length = p0_ref.shape[0]
    p0 = p0_ref[...]
    swish, gate, forget = gates(p0, p1_ref[...], floor_ref[...])
    same, row, col = masks(col_ref[0], row_ref[0], length)
    tri = (col <= row).astype(jnp.bfloat16)
    totals = exact_dot(tri, jnp.log(forget))
    fill_scores(length, p0 * swish, 1.0 - forget, totals, same & (col <= row), scores)
    rec = dot(scores[...], p2_ref[...].astype(jnp.bfloat16), ((1,), (0,)))
    rms = lax.rsqrt(jnp.mean(rec * rec, axis=-1, keepdims=True) + epsilon)
    out_ref[...] = (rec * rms * gain_ref[...]).astype(jnp.bfloat16)


def backward_kernel(
    p0_ref, p1_ref, p2_ref, grad_ref, col_ref, row_ref, floor_ref, gain_ref,
    g0_ref, g1_ref, g2_ref, floor_grad_ref, gain_grad_ref,
    scores, key_grad, decay_grad, query_grad,
):
    length = p0_ref.shape[0]
    bf = jnp.bfloat16
    p0 = p0_ref[...]
    floor = floor_ref[...]
    swish, gate, forget = gates(p0, p1_ref[...], floor)
    query = p0 * swish
    key = 1.0 - forget
    same, row, col = masks(col_ref[0], row_ref[0], length)
    allowed = same & (col <= row)
    tri = (col <= row).astype(bf)
    totals = exact_dot(tri, jnp.log(forget))
    fill_scores(length, query, key, totals, allowed, scores)
    value = p2_ref[...].astype(bf)
    rec = dot(scores[...], value, ((1,), (0,)))
    rms = lax.rsqrt(jnp.mean(rec * rec, axis=-1, keepdims=True) + epsilon)
    mixed_grad = grad_ref[...]
    unit = rec * rms
    scaled = mixed_grad * gain_ref[...]
    rec_grad = rms * (scaled - unit * jnp.mean(scaled * unit, axis=-1, keepdims=True))
    rec_low = rec_grad.astype(bf)
    g2_ref[...] = dot(scores[...], rec_low, ((0,), (0,))).astype(bf)
    score_grad = jnp.where(allowed, dot(rec_low, value, ((1,), (1,))), 0.0).astype(bf)
    key_grad[...] = jnp.zeros_like(key_grad)
    decay_grad[...] = jnp.zeros_like(decay_grad)
    for start, wide in strips(length):
        rows = slice(start, start + STRIP)
        ref = totals[start + STRIP // 2 - 1 : start + STRIP // 2]
        lead_scale = jnp.exp(totals[rows] - ref)
        trail_scale = jnp.exp(jnp.minimum(ref - totals[:wide], CAP))
        lead = (query[rows] * lead_scale).astype(bf)
        trail = (key[:wide] * trail_scale).astype(bf)
        part = score_grad[rows, :wide]
        lead_grad = dot(part, trail, ((1,), (0,)))
        trail_grad = dot(part, lead, ((0,), (0,)))
        query_grad[rows, :] = lead_grad * lead_scale
        key_grad[:wide, :] += trail_grad * trail_scale
        decay_grad[:wide, :] -= trail_grad * trail.astype(jnp.float32)
        decay_grad[rows, :] += lead_grad * lead.astype(jnp.float32)
    joined = (row > 0) & same & (col >= row)
    seg_col = col_ref[0]
    before = jnp.concatenate([seg_col[:1] - 1, seg_col[:-1]], axis=0)
    carry = (seg_col == before).astype(jnp.float32)
    later = (same & (col >= row)).astype(bf)
    forget_grad = exact_dot(later, decay_grad[...]) * carry / forget
    joint = forget_grad - key_grad[...]
    floor_grad_ref[0] = jnp.broadcast_to(jnp.sum(joint * (1.0 - gate), axis=0, keepdims=True), (8, HEAD)) * 0.125
    gain_grad_ref[0] = jnp.broadcast_to(jnp.sum(mixed_grad * unit, axis=0, keepdims=True), (8, HEAD)) * 0.125
    g0_ref[...] = (query_grad[...] * swish * (1.0 + p0 * (1.0 - swish))).astype(bf)
    g1_ref[...] = (joint * (1.0 - floor) * gate * (1.0 - gate)).astype(bf)


def specs(length):
    tile = pl.BlockSpec((length, HEAD), lambda s, h: (s, h))
    col = pl.BlockSpec((1, length, 1), lambda s, h: (s, 0, 0))
    row = pl.BlockSpec((1, 1, length), lambda s, h: (s, 0, 0))
    floor = pl.BlockSpec((1, HEAD), lambda s, h: (0, h))
    gain = pl.BlockSpec((1, HEAD), lambda s, h: (0, 0))
    return tile, col, row, floor, gain


PARAMS = dict(vmem_limit_bytes=32 * 1024 * 1024)


def mixer_forward(p0, p1, p2, segments, floor, gain):
    count, length = segments.shape
    tile, col, row, floor_spec, gain_spec = specs(length)
    heads = p0.shape[1] // HEAD
    return pl.pallas_call(
        forward_kernel,
        grid=(count, heads),
        in_specs=[tile, tile, tile, col, row, floor_spec, gain_spec],
        out_specs=tile,
        out_shape=jax.ShapeDtypeStruct(p0.shape, jnp.bfloat16),
        scratch_shapes=[pltpu.VMEM((length, length), jnp.bfloat16)],
        compiler_params=pltpu.CompilerParams(**PARAMS),
        name="mixer_forward",
    )(p0, p1, p2, segments[:, :, None], segments[:, None, :], floor[None], gain[None])


def mixer_backward(p0, p1, p2, grad, segments, floor, gain):
    count, length = segments.shape
    tile, col, row, floor_spec, gain_spec = specs(length)
    heads = p0.shape[1] // HEAD
    small = pl.BlockSpec((1, 8, HEAD), lambda s, h: (s, 0, h))
    low = jax.ShapeDtypeStruct(p0.shape, jnp.bfloat16)
    sums = jax.ShapeDtypeStruct((count, 8, p0.shape[1]), jnp.float32)
    return pl.pallas_call(
        backward_kernel,
        grid=(count, heads),
        in_specs=[tile, tile, tile, tile, col, row, floor_spec, gain_spec],
        out_specs=[tile, tile, tile, small, small],
        out_shape=[low, low, low, sums, sums],
        scratch_shapes=[
            pltpu.VMEM((length, length), jnp.bfloat16),
            pltpu.VMEM((length, HEAD), jnp.float32),
            pltpu.VMEM((length, HEAD), jnp.float32),
            pltpu.VMEM((length, HEAD), jnp.float32),
        ],
        compiler_params=pltpu.CompilerParams(**PARAMS),
        name="mixer_backward",
    )(p0, p1, p2, grad, segments[:, :, None], segments[:, None, :], floor[None], gain[None])


MEMBERS = ((1, 1), (4, 2), (5, 3))
BF = jnp.bfloat16


def swap(values, bits):
    total = lax.axis_size("dp")
    return lax.ppermute(values, "dp", [(s, s ^ bits) for s in range(total)])


def shift(values, steps):
    total = lax.axis_size("dp")
    return lax.ppermute(values, "dp", [(s, (s + 8 * steps) % total) for s in range(total)])


def other_core(values):
    return lax.ppermute(values, "tensor", [(0, 1), (1, 0)])


def pick(values, index, axis=0):
    return lax.dynamic_index_in_dim(values, index, axis, keepdims=False)


def put(values, part, index, axis=0):
    return lax.dynamic_update_index_in_dim(values, part, index, axis)


def place():
    me = lax.axis_index("dp")
    x, y, z, high = me & 1, (me >> 1) & 1, (me >> 2) & 1, me >> 3
    return x, y, z, high, z * 2 + x


def gather_weight(local):
    _, y, _, high, member = place()
    highs = lax.axis_size("dp") // 8
    rows = local.shape[0]
    slices = local.reshape(rows, 4, -1).transpose(1, 0, 2)
    width = slices.shape[2]
    block = slices
    for bits, flip in MEMBERS:
        block = put(block, swap(pick(slices, member ^ flip), bits), member ^ flip)
    full = jnp.zeros((highs, 2, 2, 2, rows, width), local.dtype)

    def store(full, part, h, yy):
        return lax.dynamic_update_slice(
            full, part.reshape(1, 2, 1, 2, rows, width), (h, 0, yy, 0, 0, 0)
        )

    full = store(full, block, high, y)
    full = store(full, swap(block, 2), high, 1 - y)
    for k in range(1, highs):
        far = shift(block, k)
        full = store(full, far, (high - k) % highs, y)
        full = store(full, swap(far, 2), (high - k) % highs, 1 - y)
    return full.reshape(highs * 8 * rows, width)


def scatter_grad(tokens, grads):
    _, y, _, high, member = place()
    highs = lax.axis_size("dp") // 8
    rows = tokens.shape[1] // (8 * highs)
    width = grads.shape[1]
    split = tokens.reshape(tokens.shape[0], highs * 2, 2, 2 * rows)

    def half(yy):
        return jnp.einsum(
            "tad,tx->adx", pick(split, yy, 2), grads, preferred_element_type=jnp.float32
        ).reshape(highs, 4, rows, width)

    came = swap(half(1 - y).astype(BF), 2)
    total = half(y) + came.astype(jnp.float32)
    mine = pick(total, high)
    for k in range(1, highs):
        sent = pick(total, (high + k) % highs).astype(BF)
        mine = mine + shift(sent, k).astype(jnp.float32)
    out = mine
    for bits, flip in MEMBERS:
        got = swap(pick(mine, member ^ flip).astype(BF), bits)
        out = put(out, got.astype(jnp.float32), member ^ flip)
    return out.transpose(1, 0, 2).reshape(rows, 4 * width)


def gather_rows(rows):
    core = lax.axis_index("tensor")
    member = place()[4]
    column = jnp.zeros((4,) + rows.shape, rows.dtype)
    column = put(column, rows, member)
    for bits, flip in MEMBERS:
        column = put(column, swap(rows, bits), member ^ flip)
    full = jnp.zeros((4, 2) + rows.shape, rows.dtype)
    full = put(full, column, core, 1)
    return put(full, other_core(column), 1 - core, 1)


def scatter_rows(count, product, *sources):
    core = lax.axis_index("tensor")
    member = place()[4]
    split = [s.reshape(4, 2, count, s.shape[-1]) for s in sources]

    def half(which):
        return product(*[pick(s, which, 1).reshape(4 * count, -1) for s in split])

    came = other_core(half(1 - core).astype(BF))
    total = (half(core) + came.astype(jnp.float32)).reshape(4, count, -1)
    mine = pick(total, member)
    for bits, flip in MEMBERS:
        got = swap(pick(total, member ^ flip).astype(BF), bits)
        mine = mine + got.astype(jnp.float32)
    return mine


def sum_all(values):
    bits = 1
    while bits < lax.axis_size("dp"):
        values = values + swap(values, bits)
        bits *= 2
    return values + other_core(values)


def rms_of(values):
    return lax.rsqrt(jnp.mean(values * values, axis=-1, keepdims=True) + epsilon)


def norm_back(values, scale, gain, grad):
    unit = values * scale
    wide = grad * gain
    out = scale * (wide - unit * jnp.mean(wide * unit, axis=-1, keepdims=True))
    return out, jnp.sum(grad * unit, axis=0)


def mul(left, right):
    return lax.dot_general(left, right, (((1,), (0,)), ((), ())), preferred_element_type=jnp.float32)


def mul_back(left, right):
    return lax.dot_general(left, right, (((1,), (1,)), ((), ())), preferred_element_type=jnp.float32)


def body(
    hidden_in,
    segments,
    mix_weights,
    ffn_weights,
    norm1_gain,
    norm2_gain,
    head_gain,
    lower_bound,
    out_grad,
):
    core = lax.axis_index("tensor")
    member = place()[4]
    count, model = hidden_in.shape
    hidden = hidden_in.astype(jnp.float32)
    scale_one = rms_of(hidden)
    normed = (hidden * scale_one * norm1_gain).astype(BF)
    normed_full = gather_rows(normed).reshape(-1, model)
    labels = segments
    group_labels = jnp.zeros((4,) + labels.shape, labels.dtype)
    group_labels = put(group_labels, labels, member)
    for bits, flip in MEMBERS:
        group_labels = put(group_labels, swap(labels, bits), member ^ flip)
    group_labels = group_labels.reshape(-1, labels.shape[-1])
    quarter = lower_bound.shape[0] // 4
    floor = lax.dynamic_slice_in_dim(lower_bound, member * quarter, quarter)

    mix = [gather_weight(mix_weights[:, j]) for j in range(4)]
    projected = [mul(normed_full, mix[j]) for j in range(3)]
    mixed = mixer_forward(*projected, group_labels, floor, head_gain)
    middle = hidden + scatter_rows(count, lambda m: mul_back(m, mix[3]), mixed)

    ffn = [gather_weight(ffn_weights[:, j]) for j in range(3)]
    scale_two = rms_of(middle)
    normed_two = (middle * scale_two * norm2_gain).astype(BF)
    normed_two_full = gather_rows(normed_two).reshape(-1, model)
    out_grad_full = gather_rows(out_grad).reshape(-1, model)
    gate = mul(normed_two_full, ffn[0])
    up = mul(normed_two_full, ffn[1])
    active_grad = mul(out_grad_full, ffn[2])
    squash = jax.nn.sigmoid(gate)
    swish = gate * squash
    active = (swish * up).astype(BF)
    gate_grad = (active_grad * up * squash * (1.0 + gate * (1.0 - squash))).astype(BF)
    up_grad = (active_grad * swish).astype(BF)
    normed_two_grad = scatter_rows(
        count, lambda g, u: mul_back(g, ffn[0]) + mul_back(u, ffn[1]), gate_grad, up_grad
    )
    extra_two, gain_two_grad = norm_back(middle, scale_two, norm2_gain, normed_two_grad)
    middle_grad = out_grad.astype(jnp.float32) + extra_two
    middle_grad_full = gather_rows(middle_grad.astype(BF)).reshape(-1, model)
    ffn_grad = [
        scatter_grad(normed_two_full, gate_grad),
        scatter_grad(normed_two_full, up_grad),
        scatter_grad(out_grad_full, active),
    ]
    block_out = (middle + scatter_rows(count, lambda a: mul_back(a, ffn[2]), active)).astype(BF)

    mixed_grad = mul(middle_grad_full, mix[3])
    *projected_grad, floor_sums, gain_sums = mixer_backward(
        *projected, mixed_grad, group_labels, floor, head_gain
    )
    normed_grad = scatter_rows(
        count,
        lambda a, b, c: mul_back(a, mix[0]) + mul_back(b, mix[1]) + mul_back(c, mix[2]),
        *projected_grad,
    )
    extra_one, gain_one_grad = norm_back(hidden, scale_one, norm1_gain, normed_grad)
    input_grad = middle_grad + extra_one
    mix_grad = [scatter_grad(normed_full, g) for g in projected_grad]
    mix_grad.append(scatter_grad(middle_grad_full, mixed))

    head_grad = jnp.sum(gain_sums.reshape(-1, HEAD), axis=0)
    lower_grad = jnp.zeros((2, 4, quarter), jnp.float32)
    lower_grad = lax.dynamic_update_slice(
        lower_grad, jnp.sum(floor_sums, axis=(0, 1)).reshape(1, 1, quarter), (core, member, 0)
    )
    sums = jnp.concatenate([gain_one_grad, gain_two_grad, head_grad, lower_grad.reshape(-1)])
    sums = sum_all(sums.reshape(-1, HEAD)).reshape(-1)
    edges = [model, 2 * model, 2 * model + HEAD]
    one, two, head, lower = jnp.split(sums, edges)
    return (
        block_out,
        input_grad,
        jnp.stack(mix_grad, axis=1),
        jnp.stack(ffn_grad, axis=1),
        one,
        two,
        head,
        lower,
    )


def solution(mesh):
    rows = P(("dp", "tensor"), None)
    weights = P("dp", None, "tensor")
    return jax.shard_map(
        body,
        mesh=mesh,
        in_specs=(rows, P("dp", None), weights, weights, P(), P(), P(), P("tensor"), rows),
        out_specs=(rows, rows, weights, weights, P(), P(), P(), P()),
        check_vma=False,
    )
```

time: 3120 us -> 1040 us (0.33)
  waiting for transfers between devices: 2550 us -> 325 us
  local copies, waits for them, and re-layouts: 73.1 us -> 407 us
  other arithmetic: 256 us -> 30.2 us
  starting transfers between devices: 1.32 us -> 124 us
  blocking collectives: 47.2 us -> 0 us
  matrix products: 157 us -> 118 us
    reduce_scatter x6 -> x0, waiting for transfers between devices: 1970 us -> none  [the longest x2 1950 us: body(): lax.psum_scatter(jnp.concatenate([inputs_part, output_part[:, None, :]],...]
    all_gather x6 -> x0, waiting for transfers between devices: 577 us -> none  [the longest x1 365 us: body(): ffn_full = lax.all_gather(ffn_weights, 'dp', axis=0, tiled=True)]
    ppermute x0 -> x117, waiting for transfers between devices: none -> 325 us  [the longest x94 237 us: swap(): return lax.ppermute(values, 'dp', [(s, s ^ bits) for s in range(total)])]
    ppermute x0 -> x117, starting transfers between devices: none -> 124 us  [the longest x94 106 us: swap(): return lax.ppermute(values, 'dp', [(s, s ^ bits) for s in range(total)])]
    reduce_sum x18 -> x6, other arithmetic: 125 us -> 2.68 us  [the longest x2 1.95 us: norm_back(): return (out, jnp.sum(grad * unit, axis=0))]
    dynamic_update_slice x8 -> x78, local copies, waits for them, and re-layouts: 3.89 us -> 87.5 us  [the longest x49 49.9 us: put(): return lax.dynamic_update_index_in_dim(values, part, index, axis)]
    dot_general x2 -> x8, local copies, waits for them, and re-layouts: 11.2 us -> 83.6 us  [half(): jnp.einsum('tad,tx->adx', pick(split, yy, 2), grads, preferred_element_ty...]
    dynamic_slice x16 -> x10, local copies, waits for them, and re-layouts: 7.12 us -> 73 us  [the longest x9 72.2 us: pick(): return lax.dynamic_index_in_dim(values, index, axis, keepdims=False)]
  transfers between devices with their start and end apart: 12 -> 117, of which waited for: 8 -> 43; matrix products, arithmetic and copies ran while one was open for 5% -> 43% of each run, Pallas kernels for 0% -> 2%
where the time goes in v1:
time: 1040 us; the launch traced here: 1030 us
  local copies, waits for them, and re-layouts  407 us (39%)
  waiting for transfers between devices  325 us (31%)
  starting transfers between devices  124 us (12%)
  matrix products  118 us (11%)
  other arithmetic  30.2 us (3%)
  Pallas kernels  20.4 us (2%)
    ppermute x94, waiting for transfers between devices, swap(): return lax.ppermute(values, 'dp', [(s, s ^ bits) for s in range(total)])  237 us
    ppermute x94, starting transfers between devices, swap(): return lax.ppermute(values, 'dp', [(s, s ^ bits) for s in range(total)])  106 us
    ppermute x14, waiting for transfers between devices, shift(): lax.ppermute(values, 'dp', [(s, (s + 8 * steps) % total) for s in range(t...  88.3 us
    dot_general x8, local copies, waits for them, and re-layouts, half(): jnp.einsum('tad,tx->adx', pick(split, yy, 2), grads, preferred_element_ty...  83.6 us
    dynamic_slice x9, local copies, waits for them, and re-layouts, pick(): return lax.dynamic_index_in_dim(values, index, axis, keepdims=False)  72.2 us
    dynamic_update_slice x49, local copies, waits for them, and re-layouts, put(): return lax.dynamic_update_index_in_dim(values, part, index, axis)  49.9 us
    dot_general x14, matrix products, mul_back(): lax.dot_general(left, right, (((1,), (1,)), ((), ())), preferred_element_...  43.7 us
    dot_general x14, matrix products, half(): jnp.einsum('tad,tx->adx', pick(split, yy, 2), grads, preferred_element_ty...  37.8 us
  transfers between devices with their start and end apart: 117, of which 43 were waited for; matrix products, arithmetic and copies ran while one was open for 43% of the time, Pallas kernels for 2%

profile of v1, /device:TPU:0, one launch (start us, length us, event | category | flops | bytes accessed | tf_op | source)
XLA Modules:
  0.0 1028.7 jit_solution(3248933858354015906)
XLA Ops:
  71.0 15.3 %collective-permute-done.51 = bf16[128,704]{0,1:T(8,128)(2,1)} collective-permute-done((bf16[128,704]{0,1:T(8,128)(2,1)}, bf16[128,704]{0,1:T(8,128)(2,1)}, u32[]{:S(2)}, u32[]{:S(2)}) %collective-permute-start.51) | collective-permute-done | bytes 180256 | tf_op jit(solution)/shard_map/ppermute | solution.py:188
  261.2 9.5 collective-permute-done.49
  275.4 12.2 %collective-permute-done.34 = bf16[128,2048]{1,0:T(8,128)(2,1)S(1)} collective-permute-done((bf16[128,2048]{1,0:T(8,128)(2,1)S(1)}, bf16[128,2048]{1,0:T(8,128)(2,1)S(1)}, u32[]{:S(2)}, u32[]{:S(2)}) %collective-permute-start.34) | collective-permute-done | bytes 524320 | tf_op jit(solution)/shard_map/ppermute | solution.py:188
  288.6 19.9 %collective-permute-done.33 = bf16[128,2048]{1,0:T(8,128)(2,1)S(1)} collective-permute-done((bf16[128,2048]{1,0:T(8,128)(2,1)S(1)}, bf16[128,2048]{1,0:T(8,128)(2,1)S(1)}, u32[]{:S(2)}, u32[]{:S(2)}) %collective-permute-start.33) | collective-permute-done | bytes 524320 | tf_op jit(solution)/shard_map/ppermute | solution.py:188
  340.0 8.2 collective-permute-done.37
  358.1 7.8 reshape_reshape.15
  369.1 7.8 reshape_reshape.18
  376.9 7.9 fusion.120
  405.8 8.1 multiply_convert_fusion.1
  423.7 21.1 %constant_dynamic-slice_fusion.1 = (bf16[1024,4,1,256]{3,2,1,0:T(2,128)(2,1)}, bf16[1024,4,1,256]{3,2,1,0:T(2,128)(2,1)}, bf16[1024,4,1,256]{3,2,1,0:T(2,128)(2,1)}, bf16[1024,4,1,256]{3,2,1,0:T(2,128)(2,1)}) fusion(bf16[1024,4,2,256]{3,2,1,0:T(2,128)(2,1)} %reshape_reshape.18, s32[]{:T(128)S(6)} %select_n.326, s32[]{:T(128)S(6)} %select_n.327, ...), kind=kLoop, calls=%fused_computation.265 | loop fusion | bytes 16777224 | tf_op jit(solution)/shard_map/jit(dynamic_index_in_dim)/dynamic_slice | solution.py:201
  444.8 10.5 %copy.214 = bf16[1024,4,1,256]{0,3,1,2:T(8,128)(2,1)} copy(bf16[1024,4,1,256]{3,2,1,0:T(2,128)(2,1)} %get-tuple-element.139) | data formatting | bytes 4194304 | tf_op jit(solution)/shard_map/tad,tx->adx/dot_general | solution.py:247
  463.2 9.9 dynamic-slice_reduce_fusion.3
  473.2 10.1 dynamic-slice_reduce_fusion.2
  488.4 11.6 %dynamic-slice_reduce_fusion.5 = (bf16[4,128,704]{1,0,2:T(4,128)(2,1)}, bf16[4,128,704]{1,0,2:T(4,128)(2,1)S(1)}) fusion(bf16[4,2,128,704]{2,1,0,3:T(2,128)(2,1)} %reshape.411, s32[]{:T(128)S(6)} %select_n.323, s32[]{:T(128)S(6)} %select_n.324), kind=kLoop, calls=%fused_computation.56 | loop fusion | bytes 2883592 | tf_op jit(solution)/shard_map/jit(dynamic_index_in_dim)/dynamic_slice | solution.py:201
  503.8 10.6 %copy.216 = bf16[1024,4,1,256]{0,3,1,2:T(8,128)(2,1)} copy(bf16[1024,4,1,256]{3,2,1,0:T(2,128)(2,1)} %get-tuple-element.60) | data formatting | bytes 4194304 | tf_op jit(solution)/shard_map/tad,tx->adx/dot_general | solution.py:247
  531.4 10.6 %copy.215 = bf16[1024,4,1,256]{0,3,1,2:T(8,128)(2,1)} copy(bf16[1024,4,1,256]{3,2,1,0:T(2,128)(2,1)} %get-tuple-element.59) | data formatting | bytes 4194304 | tf_op jit(solution)/shard_map/tad,tx->adx/dot_general | solution.py:247
  542.0 10.8 %copy.213 = bf16[1024,4,1,256]{0,3,1,2:T(8,128)(2,1)} copy(bf16[1024,4,1,256]{3,2,1,0:T(2,128)(2,1)} %get-tuple-element.140) | data formatting | bytes 4194304 | tf_op jit(solution)/shard_map/tad,tx->adx/dot_general | solution.py:247
  560.7 54.3 %collective-permute-done.102 = bf16[2,4,128,704]{2,3,1,0:T(8,128)(2,1)} collective-permute-done((bf16[2,4,128,704]{2,3,1,0:T(8,128)(2,1)}, bf16[2,4,128,704]{2,3,1,0:T(8,128)(2,1)}, u32[]{:S(2)}, u32[]{:S(2)}) %collective-permute-start.102) | collective-permute-done | bytes 1441824 | tf_op jit(solution)/shard_map/ppermute | solution.py:188
  641.9 26.8 %collective-permute-done.103 = bf16[4,128,704]{1,2,0:T(8,128)(2,1)S(1)} collective-permute-done((bf16[4,128,704]{1,2,0:T(8,128)(2,1)S(1)}, bf16[4,128,704]{1,2,0:T(8,128)(2,1)S(1)}, u32[]{:S(2)}, u32[]{:S(2)}) %collective-permute-start.103) | collective-permute-done | bytes 720928 | tf_op jit(solution)/shard_map/ppermute | solution.py:193
  670.0 13.0 %collective-permute-done.98 = bf16[4,128,704]{1,2,0:T(8,128)(2,1)S(1)} collective-permute-done((bf16[4,128,704]{1,2,0:T(8,128)(2,1)S(1)}, bf16[4,128,704]{1,2,0:T(8,128)(2,1)S(1)}, u32[]{:S(2)}, u32[]{:S(2)}) %collective-permute-start.98) | collective-permute-done | bytes 720928 | tf_op jit(solution)/shard_map/ppermute | solution.py:193
  764.6 7.8 reshape_reshape.16
  776.2 13.5 %mixer_backward.1 = (bf16[1024,256]{1,0:T(8,128)(2,1)S(1)}, bf16[1024,256]{1,0:T(8,128)(2,1)S(1)}, bf16[1024,256]{1,0:T(8,128)(2,1)S(1)}, f32[4,8,256]{2,1,0:T(8,128)S(1)}, f32[4,8,256]{2,1,0:T(8,128)S(1)}) custom-call(f32[1024,256]{1,0:T(8,128)S(1)} %copy-done.3, f32[1024,256]{1,0:T(8,128)S(1)} %fusion.117.p1_ref, f32[1024,256]{1,0:T(8,128)S(1)} %fusion.118.p2_ref, ...), custom_call_target="tpu_custom_call" | custom-call | tf_op jit(solution)/shard_map/mixer_backward/pallas_call | solution.py:165
  802.5 18.5 %constant_dynamic-slice_fusion.4 = (bf16[1024,4,1,256]{3,2,1,0:T(2,128)(2,1)}, bf16[1024,4,1,256]{3,2,1,0:T(2,128)(2,1)}, bf16[1024,4,1,256]{3,2,1,0:T(2,128)(2,1)}, bf16[1024,4,1,256]{3,2,1,0:T(2,128)(2,1)}) fusion(bf16[1024,4,2,256]{3,2,1,0:T(2,128)(2,1)S(1)} %copy-done.10, s32[]{:T(128)S(6)} %select_n.327, s32[]{:T(128)S(6)} %select_n.326, ...), kind=kLoop, calls=%fused_computation.268 | loop fusion | bytes 16777224 | tf_op jit(solution)/shard_map/jit(dynamic_index_in_dim)/dynamic_slice | solution.py:201
  821.0 9.1 copy.212
  832.3 10.8 %copy.210 = bf16[1024,4,1,256]{0,3,1,2:T(8,128)(2,1)} copy(bf16[1024,4,1,256]{3,2,1,0:T(2,128)(2,1)} %get-tuple-element.141) | data formatting | bytes 4194304 | tf_op jit(solution)/shard_map/tad,tx->adx/dot_general | solution.py:247
  856.9 10.6 %copy.211 = bf16[1024,4,1,256]{0,3,1,2:T(8,128)(2,1)} copy(bf16[1024,4,1,256]{3,2,1,0:T(2,128)(2,1)} %get-tuple-element.64) | data formatting | bytes 4194304 | tf_op jit(solution)/shard_map/tad,tx->adx/dot_general | solution.py:247
  868.2 10.6 %copy.209 = bf16[1024,4,1,256]{0,3,1,2:T(8,128)(2,1)} copy(bf16[1024,4,1,256]{3,2,1,0:T(2,128)(2,1)} %get-tuple-element.142) | data formatting | bytes 4194304 | tf_op jit(solution)/shard_map/tad,tx->adx/dot_general | solution.py:247
  885.2 8.0 collective-permute-done.82
  898.8 9.2 collective-permute-done.93
  908.2 11.1 %collective-permute-done.88 = bf16[4,128,256]{2,1,0:T(8,128)(2,1)S(1)} collective-permute-done((bf16[4,128,256]{2,1,0:T(8,128)(2,1)S(1)}, bf16[4,128,256]{2,1,0:T(8,128)(2,1)S(1)}, u32[]{:S(2)}, u32[]{:S(2)}) %collective-permute-start.88) | collective-permute-done | bytes 262176 | tf_op jit(solution)/shard_map/ppermute | solution.py:193
  962.9 20.1 %collective-permute-done.86 = bf16[128,256]{1,0:T(8,128)(2,1)S(1)} collective-permute-done((bf16[128,256]{1,0:T(8,128)(2,1)S(1)}, bf16[128,256]{1,0:T(8,128)(2,1)S(1)}, u32[]{:S(2)}, u32[]{:S(2)}) %collective-permute-start.86) | collective-permute-done | bytes 65568 | tf_op jit(solution)/shard_map/ppermute | solution.py:188
  989.5 15.3 %collective-permute-done.80 = bf16[128,256]{1,0:T(8,128)(2,1)S(1)} collective-permute-done((bf16[128,256]{1,0:T(8,128)(2,1)S(1)}, bf16[128,256]{1,0:T(8,128)(2,1)S(1)}, u32[]{:S(2)}, u32[]{:S(2)}) %collective-permute-start.80) | collective-permute-done | bytes 65568 | tf_op jit(solution)/shard_map/ppermute | solution.py:188
  (688 shorter events, 595.2 us)
Async XLA Ops:
  0.6 39.7 %collective-permute-start.22 = (s32[1,256]{1,0:T(1,128)}, s32[1,256]{1,0:T(1,128)S(1)}, u32[]{:S(2)}, u32[]{:S(2)}) collective-permute-start(s32[1,256]{1,0:T(1,128)} %param.10), channel_id=1, source_target_pairs={{0,2},{2,0},{4,6},{6,4},{8,10},{10,8},{12,14},{14,12},{16,18},{18,... | collective-permute-start | bytes 3080 | tf_op jit(solution)/shard_map/ppermute | solution.py:188
  3.6 36.7 %collective-permute-start.24 = (s32[1,256]{1,0:T(1,128)}, s32[1,256]{1,0:T(1,128)S(1)}, u32[]{:S(2)}, u32[]{:S(2)}) collective-permute-start(s32[1,256]{1,0:T(1,128)} %param.10), channel_id=1, source_target_pairs={{0,10},{2,8},{4,14},{6,12},{8,2},{10,0},{12,6},{14,4},{16,26},{18,... | collective-permute-start | bytes 3080 | tf_op jit(solution)/shard_map/ppermute | solution.py:188
  5.2 37.2 %collective-permute-start.23 = (s32[1,256]{1,0:T(1,128)}, s32[1,256]{1,0:T(1,128)S(1)}, u32[]{:S(2)}, u32[]{:S(2)}) collective-permute-start(s32[1,256]{1,0:T(1,128)} %param.10), channel_id=1, source_target_pairs={{0,8},{2,10},{4,12},{6,14},{8,0},{10,2},{12,4},{14,6},{16,24},{18,... | collective-permute-start | bytes 3080 | tf_op jit(solution)/shard_map/ppermute | solution.py:188
  53.2 86.5 %collective-permute-start.1 = (bf16[128,2048]{1,0:T(8,128)(2,1)}, bf16[128,2048]{1,0:T(8,128)(2,1)}, u32[]{:S(2)}, u32[]{:S(2)}) collective-permute-start(bf16[128,2048]{1,0:T(8,128)(2,1)} %get-tuple-element.53), channel_id=1, source_target_pairs={{0,8},{2,10},{4,12},{6,14},{8,0},{10,2},{12,4},{14,6},{16,24},{18,... | collective-permute-start | bytes 1572872 | tf_op jit(solution)/shard_map/ppermute | solution.py:188
  54.4 83.2 %collective-permute-start = (bf16[128,2048]{1,0:T(8,128)(2,1)}, bf16[128,2048]{1,0:T(8,128)(2,1)}, u32[]{:S(2)}, u32[]{:S(2)}) collective-permute-start(bf16[128,2048]{1,0:T(8,128)(2,1)} %get-tuple-element.53), channel_id=1, source_target_pairs={{0,2},{2,0},{4,6},{6,4},{8,10},{10,8},{12,14},{14,12},{16,18},{18,... | collective-permute-start | bytes 1572872 | tf_op jit(solution)/shard_map/ppermute | solution.py:188
  55.9 96.7 %collective-permute-start.2 = (bf16[128,2048]{1,0:T(8,128)(2,1)}, bf16[128,2048]{1,0:T(8,128)(2,1)}, u32[]{:S(2)}, u32[]{:S(2)}) collective-permute-start(bf16[128,2048]{1,0:T(8,128)(2,1)} %get-tuple-element.53), channel_id=1, source_target_pairs={{0,10},{2,8},{4,14},{6,12},{8,2},{10,0},{12,6},{14,4},{16,26},{18,... | collective-permute-start | bytes 1572872 | tf_op jit(solution)/shard_map/ppermute | solution.py:188
  57.3 77.7 %collective-permute-start.41 = (bf16[128,704]{0,1:T(8,128)(2,1)}, bf16[128,704]{0,1:T(8,128)(2,1)}, u32[]{:S(2)}, u32[]{:S(2)}) collective-permute-start(bf16[128,704]{0,1:T(8,128)(2,1)} %get-tuple-element.95), channel_id=1, source_target_pairs={{0,10},{2,8},{4,14},{6,12},{8,2},{10,0},{12,6},{14,4},{16,26},{18,... | collective-permute-start | bytes 540680 | tf_op jit(solution)/shard_map/ppermute | solution.py:188
  155.0 54.8 %collective-permute-start.3 = (bf16[4,128,2048]{2,1,0:T(8,128)(2,1)}, bf16[4,128,2048]{2,1,0:T(8,128)(2,1)}, u32[]{:S(2)}, u32[]{:S(2)}) collective-permute-start(bf16[4,128,2048]{2,1,0:T(8,128)(2,1)} %bitcast_dynamic-update-slice_fusion.20), channel_id=1, source_target_pairs={{0,1},{1,0},{2,3},{3,2},{4,5},{5,4},{6,7},{7,6},{8,9},{9,8},{10,11... | collective-permute-start | bytes 6291464 | tf_op jit(solution)/shard_map/ppermute | solution.py:197
  192.4 41.3 %collective-permute-start.61 = (bf16[128,2048]{1,0:T(8,128)(2,1)}, bf16[128,2048]{1,0:T(8,128)(2,1)}, u32[]{:S(2)}, u32[]{:S(2)}) collective-permute-start(bf16[128,2048]{1,0:T(8,128)(2,1)} %param.17), channel_id=1, source_target_pairs={{0,2},{2,0},{4,6},{6,4},{8,10},{10,8},{12,14},{14,12},{16,18},{18,... | collective-permute-start | bytes 1572872 | tf_op jit(solution)/shard_map/ppermute | solution.py:188
  194.0 45.0 %collective-permute-start.63 = (bf16[128,2048]{1,0:T(8,128)(2,1)}, bf16[128,2048]{1,0:T(8,128)(2,1)}, u32[]{:S(2)}, u32[]{:S(2)}) collective-permute-start(bf16[128,2048]{1,0:T(8,128)(2,1)} %param.17), channel_id=1, source_target_pairs={{0,10},{2,8},{4,14},{6,12},{8,2},{10,0},{12,6},{14,4},{16,26},{18,... | collective-permute-start | bytes 1572872 | tf_op jit(solution)/shard_map/ppermute | solution.py:188
  201.2 45.8 %collective-permute-start.55 = (bf16[4,128,704]{1,2,0:T(8,128)(2,1)}, bf16[4,128,704]{1,2,0:T(8,128)(2,1)}, u32[]{:S(2)}, u32[]{:S(2)}) collective-permute-start(bf16[4,128,704]{1,2,0:T(8,128)(2,1)} %copy-done.51), channel_id=1, source_target_pairs={{0,16},{2,18},{4,20},{6,22},{8,24},{10,26},{12,28},{14,30},{16,0},... | collective-permute-start | bytes 2162696 | tf_op jit(solution)/shard_map/ppermute | solution.py:193
  257.9 50.6 %collective-permute-start.33 = (bf16[128,2048]{1,0:T(8,128)(2,1)S(1)}, bf16[128,2048]{1,0:T(8,128)(2,1)S(1)}, u32[]{:S(2)}, u32[]{:S(2)}) collective-permute-start(bf16[128,2048]{1,0:T(8,128)(2,1)S(1)} %get-tuple-element.76), channel_id=1, source_target_pairs={{0,8},{2,10},{4,12},{6,14},{8,0},{10,2},{12,4},{14,6},{16,24},{18,... | collective-permute-start | bytes 1572872 | tf_op jit(solution)/shard_map/ppermute | solution.py:188
  270.7 40.4 %collective-permute-start.43 = (bf16[4,128,704]{1,2,0:T(8,128)(2,1)S(1)}, bf16[4,128,704]{1,2,0:T(8,128)(2,1)}, u32[]{:S(2)}, u32[]{:S(2)}) collective-permute-start(bf16[4,128,704]{1,2,0:T(8,128)(2,1)S(1)} %copy-done.45), channel_id=1, source_target_pairs={{0,16},{2,18},{4,20},{6,22},{8,24},{10,26},{12,28},{14,30},{16,0},... | collective-permute-start | bytes 2162696 | tf_op jit(solution)/shard_map/ppermute | solution.py:193
  272.6 93.3 %collective-permute-start.64 = (bf16[4,128,2048]{2,1,0:T(8,128)(2,1)}, bf16[4,128,2048]{2,1,0:T(8,128)(2,1)}, u32[]{:S(2)}, u32[]{:S(2)}) collective-permute-start(bf16[4,128,2048]{2,1,0:T(8,128)(2,1)} %bitcast_dynamic-update-slice_fusion.12), channel_id=1, source_target_pairs={{0,1},{1,0},{2,3},{3,2},{4,5},{5,4},{6,7},{7,6},{8,9},{9,8},{10,11... | collective-permute-start | bytes 6291464 | tf_op jit(solution)/shard_map/ppermute | solution.py:197
  274.3 40.7 %collective-permute-start.56 = (bf16[4,128,704]{1,2,0:T(8,128)(2,1)}, bf16[4,128,704]{1,2,0:T(8,128)(2,1)S(1)}, u32[]{:S(2)}, u32[]{:S(2)}) collective-permute-start(bf16[4,128,704]{1,2,0:T(8,128)(2,1)} %collective-permute-done.55), channel_id=1, source_target_pairs={{0,4},{2,6},{4,0},{6,2},{8,12},{10,14},{12,8},{14,10},{16,20},{18,... | collective-permute-start | bytes 2162696 | tf_op jit(solution)/shard_map/ppermute | solution.py:188
  349.0 39.8 %collective-permute-start.38 = (bf16[4,128,2048]{2,1,0:T(8,128)(2,1)}, bf16[4,128,2048]{2,1,0:T(8,128)(2,1)}, u32[]{:S(2)}, u32[]{:S(2)}) collective-permute-start(bf16[4,128,2048]{2,1,0:T(8,128)(2,1)} %bitcast_dynamic-update-slice_fusion.16), channel_id=1, source_target_pairs={{0,1},{1,0},{2,3},{3,2},{4,5},{5,4},{6,7},{7,6},{8,9},{9,8},{10,11... | collective-permute-start | bytes 6291464 | tf_op jit(solution)/shard_map/ppermute | solution.py:197
  503.3 121.5 %collective-permute-start.57 = (bf16[512,2048]{1,0:T(8,128)(2,1)}, bf16[512,2048]{1,0:T(8,128)(2,1)}, u32[]{:S(2)}, u32[]{:S(2)}) collective-permute-start(bf16[512,2048]{1,0:T(8,128)(2,1)} %convolution_convert_fusion.1), channel_id=1, source_target_pairs={{0,1},{1,0},{2,3},{3,2},{4,5},{5,4},{6,7},{7,6},{8,9},{9,8},{10,11... | collective-permute-start | bytes 6291464 | tf_op jit(solution)/shard_map/ppermute | solution.py:197
  520.2 100.3 %collective-permute-start.97 = (bf16[2,4,128,704]{2,3,1,0:T(8,128)(2,1)}, bf16[2,4,128,704]{2,3,1,0:T(8,128)(2,1)}, u32[]{:S(2)}, u32[]{:S(2)}) collective-permute-start(bf16[2,4,128,704]{2,3,1,0:T(8,128)(2,1)} %convolution_convert_fusion.4), channel_id=1, source_target_pairs={{0,4},{2,6},{4,0},{6,2},{8,12},{10,14},{12,8},{14,10},{16,20},{18,... | collective-permute-start | bytes 4325384 | tf_op jit(solution)/shard_map/ppermute | solution.py:188
  521.5 93.6 %collective-permute-start.102 = (bf16[2,4,128,704]{2,3,1,0:T(8,128)(2,1)}, bf16[2,4,128,704]{2,3,1,0:T(8,128)(2,1)}, u32[]{:S(2)}, u32[]{:S(2)}) collective-permute-start(bf16[2,4,128,704]{2,3,1,0:T(8,128)(2,1)} %convolution_convert_fusion.3), channel_id=1, source_target_pairs={{0,4},{2,6},{4,0},{6,2},{8,12},{10,14},{12,8},{14,10},{16,20},{18,... | collective-permute-start | bytes 4325384 | tf_op jit(solution)/shard_map/ppermute | solution.py:188
  531.4 99.3 %collective-permute-start.65 = (bf16[512,2048]{1,0:T(8,128)(2,1)}, bf16[512,2048]{1,0:T(8,128)(2,1)}, u32[]{:S(2)}, u32[]{:S(2)}) collective-permute-start(bf16[512,2048]{1,0:T(8,128)(2,1)} %add_convert_fusion.1), channel_id=1, source_target_pairs={{0,1},{1,0},{2,3},{3,2},{4,5},{5,4},{6,7},{7,6},{8,9},{9,8},{10,11... | collective-permute-start | bytes 6291464 | tf_op jit(solution)/shard_map/ppermute | solution.py:197
  558.6 78.7 %collective-permute-start.108 = (bf16[4,128,704]{1,2,0:T(8,128)(2,1)S(1)}, bf16[4,128,704]{1,2,0:T(8,128)(2,1)S(1)}, u32[]{:S(2)}, u32[]{:S(2)}) collective-permute-start(bf16[4,128,704]{1,2,0:T(8,128)(2,1)S(1)} %fusion.39), channel_id=1, source_target_pairs={{0,16},{2,18},{4,20},{6,22},{8,24},{10,26},{12,28},{14,30},{16,0},... | collective-permute-start | bytes 2162696 | tf_op jit(solution)/shard_map/ppermute | solution.py:193
  618.3 50.4 %collective-permute-start.103 = (bf16[4,128,704]{1,2,0:T(8,128)(2,1)S(1)}, bf16[4,128,704]{1,2,0:T(8,128)(2,1)S(1)}, u32[]{:S(2)}, u32[]{:S(2)}) collective-permute-start(bf16[4,128,704]{1,2,0:T(8,128)(2,1)S(1)} %fusion.38), channel_id=1, source_target_pairs={{0,16},{2,18},{4,20},{6,22},{8,24},{10,26},{12,28},{14,30},{16,0},... | collective-permute-start | bytes 2162696 | tf_op jit(solution)/shard_map/ppermute | solution.py:193
  623.8 59.1 %collective-permute-start.98 = (bf16[4,128,704]{1,2,0:T(8,128)(2,1)S(1)}, bf16[4,128,704]{1,2,0:T(8,128)(2,1)S(1)}, u32[]{:S(2)}, u32[]{:S(2)}) collective-permute-start(bf16[4,128,704]{1,2,0:T(8,128)(2,1)S(1)} %fusion.37), channel_id=1, source_target_pairs={{0,16},{2,18},{4,20},{6,22},{8,24},{10,26},{12,28},{14,30},{16,0},... | collective-permute-start | bytes 2162696 | tf_op jit(solution)/shard_map/ppermute | solution.py:193
  629.7 393.3 %collective-permute-start.58 = (bf16[128,2048]{1,0:T(8,128)(2,1)}, bf16[128,2048]{1,0:T(8,128)(2,1)}, u32[]{:S(2)}, u32[]{:S(2)}) collective-permute-start(bf16[128,2048]{1,0:T(8,128)(2,1)} %get-tuple-element.71), channel_id=1, source_target_pairs={{0,2},{2,0},{4,6},{6,4},{8,10},{10,8},{12,14},{14,12},{16,18},{18,... | collective-permute-start | bytes 1572872 | tf_op jit(solution)/shard_map/ppermute | solution.py:188
  636.2 53.1 %collective-permute-start.66 = (bf16[128,2048]{1,0:T(8,128)(2,1)S(1)}, bf16[128,2048]{1,0:T(8,128)(2,1)S(1)}, u32[]{:S(2)}, u32[]{:S(2)}) collective-permute-start(bf16[128,2048]{1,0:T(8,128)(2,1)S(1)} %get-tuple-element.68), channel_id=1, source_target_pairs={{0,2},{2,0},{4,6},{6,4},{8,10},{10,8},{12,14},{14,12},{16,18},{18,... | collective-permute-start | bytes 1572872 | tf_op jit(solution)/shard_map/ppermute | solution.py:188
  637.3 54.5 %collective-permute-start.68 = (bf16[128,2048]{1,0:T(8,128)(2,1)S(1)}, bf16[128,2048]{1,0:T(8,128)(2,1)S(1)}, u32[]{:S(2)}, u32[]{:S(2)}) collective-permute-start(bf16[128,2048]{1,0:T(8,128)(2,1)S(1)} %get-tuple-element.69), channel_id=1, source_target_pairs={{0,10},{2,8},{4,14},{6,12},{8,2},{10,0},{12,6},{14,4},{16,26},{18,... | collective-permute-start | bytes 1572872 | tf_op jit(solution)/shard_map/ppermute | solution.py:188
  691.7 47.6 %collective-permute-start.106 = (bf16[128,704]{0,1:T(8,128)(2,1)}, bf16[128,704]{0,1:T(8,128)(2,1)}, u32[]{:S(2)}, u32[]{:S(2)}) collective-permute-start(bf16[128,704]{0,1:T(8,128)(2,1)} %get-tuple-element.83), channel_id=1, source_target_pairs={{0,10},{2,8},{4,14},{6,12},{8,2},{10,0},{12,6},{14,4},{16,26},{18,... | collective-permute-start | bytes 540680 | tf_op jit(solution)/shard_map/ppermute | solution.py:188
  831.6 47.3 %collective-permute-start.92 = (bf16[2,4,128,256]{3,2,1,0:T(8,128)(2,1)}, bf16[2,4,128,256]{3,2,1,0:T(8,128)(2,1)}, u32[]{:S(2)}, u32[]{:S(2)}) collective-permute-start(bf16[2,4,128,256]{3,2,1,0:T(8,128)(2,1)} %convolution_convert_fusion.5), channel_id=1, source_target_pairs={{0,4},{2,6},{4,0},{6,2},{8,12},{10,14},{12,8},{14,10},{16,20},{18,... | collective-permute-start | bytes 1572872 | tf_op jit(solution)/shard_map/ppermute | solution.py:188
  846.3 36.3 %collective-permute-start.87 = (bf16[2,4,128,256]{3,2,1,0:T(8,128)(2,1)}, bf16[2,4,128,256]{3,2,1,0:T(8,128)(2,1)S(1)}, u32[]{:S(2)}, u32[]{:S(2)}) collective-permute-start(bf16[2,4,128,256]{3,2,1,0:T(8,128)(2,1)} %convolution_convert_fusion.6), channel_id=1, source_target_pairs={{0,4},{2,6},{4,0},{6,2},{8,12},{10,14},{12,8},{14,10},{16,20},{18,... | collective-permute-start | bytes 1572872 | tf_op jit(solution)/shard_map/ppermute | solution.py:188
  856.8 97.3 %collective-permute-start.73 = (bf16[512,2048]{1,0:T(8,128)(2,1)}, bf16[512,2048]{1,0:T(8,128)(2,1)}, u32[]{:S(2)}, u32[]{:S(2)}) collective-permute-start(bf16[512,2048]{1,0:T(8,128)(2,1)} %add_convert_fusion), channel_id=1, source_target_pairs={{0,1},{1,0},{2,3},{3,2},{4,5},{5,4},{6,7},{7,6},{8,9},{9,8},{10,11... | collective-permute-start | bytes 6291464 | tf_op jit(solution)/shard_map/ppermute | solution.py:197
  983.0 40.0 %collective-permute-start.60 = (bf16[128,2048]{1,0:T(8,128)(2,1)}, bf16[128,2048]{1,0:T(8,128)(2,1)}, u32[]{:S(2)}, u32[]{:S(2)}) collective-permute-start(bf16[128,2048]{1,0:T(8,128)(2,1)} %get-tuple-element.72), channel_id=1, source_target_pairs={{0,10},{2,8},{4,14},{6,12},{8,2},{10,0},{12,6},{14,4},{16,26},{18,... | collective-permute-start | bytes 1572872 | tf_op jit(solution)/shard_map/ppermute | solution.py:188
  984.9 38.1 %collective-permute-start.59 = (bf16[128,2048]{1,0:T(8,128)(2,1)}, bf16[128,2048]{1,0:T(8,128)(2,1)}, u32[]{:S(2)}, u32[]{:S(2)}) collective-permute-start(bf16[128,2048]{1,0:T(8,128)(2,1)} %get-tuple-element.73), channel_id=1, source_target_pairs={{0,8},{2,10},{4,12},{6,14},{8,0},{10,2},{12,4},{14,6},{16,24},{18,... | collective-permute-start | bytes 1572872 | tf_op jit(solution)/shard_map/ppermute | solution.py:188
  (181 other events, 2651.8 us)

commit v2 on v0

v2 whole, which is shorter than its diff:
```python
import functools

import jax
import jax.numpy as jnp
from jax import lax
from jax.experimental import pallas as pl
from jax.experimental.pallas import tpu as pltpu
from jax.sharding import Mesh, PartitionSpec as P

HEAD = 128
STRIP = 32
CAP = 50.0
BF = jnp.bfloat16
epsilon = 1e-06
PARAMS = pltpu.CompilerParams(vmem_limit_bytes=56 * 1024 * 1024)


def cost(us):
    return pl.CostEstimate(flops=int(us * 1e9), bytes_accessed=1, transcendentals=0)


NN, NT, TN = ((1,), (0,)), ((1,), (1,)), ((0,), (0,))


def dot(a, b, dims=NN):
    return lax.dot_general(a, b, (dims, ((), ())), preferred_element_type=jnp.float32)


def exact_dot(ones, values):
    high = values.astype(BF)
    rest = values - high.astype(jnp.float32)
    mid = rest.astype(BF)
    tail = (rest - mid.astype(jnp.float32)).astype(BF)
    return dot(ones, high) + dot(ones, mid) + dot(ones, tail)


def gates(p0, p1, floor):
    swish = jax.nn.sigmoid(p0)
    gate = jax.nn.sigmoid(p1)
    return swish, gate, floor + (1.0 - floor) * gate


def masks(seg_col, seg_row):
    length = seg_col.shape[0]
    row = lax.broadcasted_iota(jnp.int32, (length, length), 0)
    col = lax.broadcasted_iota(jnp.int32, (length, length), 1)
    return seg_col == seg_row, row, col


def strips(length):
    return [(s, -(-(s + STRIP) // 128) * 128) for s in range(0, length, STRIP)]


def fill_scores(query, key, totals, allowed, scores):
    length = query.shape[0]
    for start, wide in strips(length):
        rows = slice(start, start + STRIP)
        ref = totals[start + STRIP // 2 - 1 : start + STRIP // 2]
        lead = (query[rows] * jnp.exp(totals[rows] - ref)).astype(BF)
        trail = (key[:wide] * jnp.exp(jnp.minimum(ref - totals[:wide], CAP))).astype(BF)
        part = jnp.where(allowed[rows, :wide], dot(lead, trail, NT), 0.0)
        scores[rows, :wide] = part.astype(BF)
        if wide < length:
            scores[rows, wide:] = jnp.zeros((STRIP, length - wide), BF)


def head_forward(p0, p1, p2, seg_col, seg_row, floor, gain, scores):
    swish, gate, forget = gates(p0, p1, floor)
    same, row, col = masks(seg_col, seg_row)
    totals = exact_dot((col <= row).astype(BF), jnp.log(forget))
    fill_scores(p0 * swish, 1.0 - forget, totals, same & (col <= row), scores)
    rec = dot(scores[...], p2.astype(BF))
    rms = lax.rsqrt(jnp.mean(rec * rec, axis=-1, keepdims=True) + epsilon)
    return (rec * rms * gain).astype(BF)


def head_backward(
    p0, p1, p2, mixed_grad, seg_col, seg_row, floor, gain, scores, key_grad, decay_grad, query_grad
):
    length = p0.shape[0]
    swish, gate, forget = gates(p0, p1, floor)
    query = p0 * swish
    key = 1.0 - forget
    same, row, col = masks(seg_col, seg_row)
    allowed = same & (col <= row)
    totals = exact_dot((col <= row).astype(BF), jnp.log(forget))
    fill_scores(query, key, totals, allowed, scores)
    value = p2.astype(BF)
    rec = dot(scores[...], value)
    rms = lax.rsqrt(jnp.mean(rec * rec, axis=-1, keepdims=True) + epsilon)
    unit = rec * rms
    scaled = mixed_grad * gain
    rec_grad = rms * (scaled - unit * jnp.mean(scaled * unit, axis=-1, keepdims=True))
    rec_low = rec_grad.astype(BF)
    value_grad = dot(scores[...], rec_low, TN).astype(BF)
    score_grad = jnp.where(allowed, dot(rec_low, value, NT), 0.0).astype(BF)
    key_grad[...] = jnp.zeros_like(key_grad)
    decay_grad[...] = jnp.zeros_like(decay_grad)
    for start, wide in strips(length):
        rows = slice(start, start + STRIP)
        ref = totals[start + STRIP // 2 - 1 : start + STRIP // 2]
        lead_scale = jnp.exp(totals[rows] - ref)
        trail_scale = jnp.exp(jnp.minimum(ref - totals[:wide], CAP))
        lead = (query[rows] * lead_scale).astype(BF)
        trail = (key[:wide] * trail_scale).astype(BF)
        part = score_grad[rows, :wide]
        lead_grad = dot(part, trail)
        trail_grad = dot(part, lead, TN)
        query_grad[rows, :] = lead_grad * lead_scale
        key_grad[:wide, :] += trail_grad * trail_scale
        decay_grad[:wide, :] -= trail_grad * trail.astype(jnp.float32)
        decay_grad[rows, :] += lead_grad * lead.astype(jnp.float32)
    before = jnp.concatenate([seg_col[:1] - 1, seg_col[:-1]], axis=0)
    carry = (seg_col == before).astype(jnp.float32)
    later = (same & (col >= row)).astype(BF)
    forget_grad = exact_dot(later, decay_grad[...]) * carry / forget
    joint = forget_grad - key_grad[...]
    floor_sum = jnp.sum(joint * (1.0 - gate), axis=0, keepdims=True)
    gain_sum = jnp.sum(mixed_grad * unit, axis=0, keepdims=True)
    g0 = (query_grad[...] * swish * (1.0 + p0 * (1.0 - swish))).astype(BF)
    g1 = (joint * (1.0 - floor) * gate * (1.0 - gate)).astype(BF)
    return g0, g1, value_grad, floor_sum, gain_sum


def load_weight(offsets_ref, sources, refs, whole, sems, begin=0):
    end = begin + whole.shape[1]
    copies = []
    for (piece, low), ref in zip(sources, refs):
        rows, lanes = ref.shape[1:]
        first, last = max(low, begin), min(low + lanes, end)
        if first >= last:
            continue
        for m in range(4):
            at = pl.multiple_of(offsets_ref[4 * piece + m], rows)
            copies.append(
                pltpu.make_async_copy(
                    ref.at[m, :, pl.ds(first - low, last - first)],
                    whole.at[pl.ds(at, rows), pl.ds(first - begin, last - first)],
                    sems.at[len(copies)],
                )
            )
    for copy in copies:
        copy.start()
    for copy in copies:
        copy.wait()


def mixer_forward_kernel(core_ref, offsets_ref, rows_ref, *refs, sources):
    (col_ref, row_ref, floor_ref, gain_ref, p_ref, mixed_ref, send_ref, keep_ref, scores, whole,
     weight, sems) = refs[len(sources) :]

    @pl.when(pl.program_id(0) == 0)
    def _():
        load_weight(offsets_ref, sources, refs, weight, sems)

    count = rows_ref.shape[1] // 2
    width = whole.shape[1]
    mine = pl.multiple_of(core_ref[0] * count, count)
    theirs = pl.multiple_of((1 - core_ref[0]) * count, count)
    p_ref[0] = dot(rows_ref[0], weight[:, : 3 * width])
    for h in range(width // HEAD):
        p0, p1, p2 = [p_ref[0, :, pl.ds(j * width + h * HEAD, HEAD)] for j in range(3)]
        lanes = slice(h * HEAD, (h + 1) * HEAD)
        whole[:, lanes] = head_forward(
            p0, p1, p2, col_ref[0], row_ref[0], floor_ref[:, lanes], gain_ref[...], scores.at[h]
        )
    mixed_ref[0] = whole[...]
    send_ref[0] = dot(whole[pl.ds(theirs, count), :], weight[:, 3 * width :], NT).astype(BF)
    keep_ref[0] = dot(whole[pl.ds(mine, count), :], weight[:, 3 * width :], NT)


def mixer_backward_kernel(core_ref, offsets_ref, rows_ref, *refs, sources):
    (p_ref, col_ref, row_ref, floor_ref, gain_ref, g_one_ref, g_two_ref, send_ref, keep_ref,
     floor_sum_ref, gain_sum_ref, scores, key_grad, decay_grad, query_grad, mixed_grad, parts,
     weight, sems) = refs[len(sources) :]

    @pl.when(pl.program_id(0) == 0)
    def _():
        load_weight(offsets_ref, sources, refs, weight, sems)

    count = rows_ref.shape[1] // 2
    width = mixed_grad.shape[1]
    mine = pl.multiple_of(core_ref[0] * count, count)
    theirs = pl.multiple_of((1 - core_ref[0]) * count, count)
    mixed_grad[...] = dot(rows_ref[0], weight[:, 3 * width :])
    for h in range(width // HEAD):
        p0, p1, p2 = [p_ref[0, :, pl.ds(j * width + h * HEAD, HEAD)] for j in range(3)]
        lanes = slice(h * HEAD, (h + 1) * HEAD)
        g0, g1, g2, floor_sum, gain_sum = head_backward(
            p0, p1, p2, mixed_grad[:, lanes], col_ref[0], row_ref[0], floor_ref[:, lanes],
            gain_ref[...], scores.at[h], key_grad.at[h], decay_grad.at[h], query_grad.at[h],
        )
        for j, g in enumerate((g0, g1, g2)):
            parts[:, pl.ds(j * width + h * HEAD, HEAD)] = g
        floor_sum_ref[0, :, lanes] = jnp.broadcast_to(floor_sum, (8, HEAD)) * 0.125
        gain_sum_ref[0, :, lanes] = jnp.broadcast_to(gain_sum, (8, HEAD)) * 0.125

    def back(at):
        return dot(parts[pl.ds(at, count), :], weight[:, : 3 * width], NT)

    g_one_ref[0] = parts[:, : 2 * width]
    g_two_ref[0] = parts[:, 2 * width :]
    send_ref[0] = back(theirs).astype(BF)
    keep_ref[0] = back(mine)


def mixer_specs(count, model, width, length):
    def at(shape, index):
        return pl.BlockSpec(shape, lambda s, c, o: index(s))

    rows = at((1, length, model), lambda s: (s, 0, 0))
    side = at((1, count, model), lambda s: (s, 0, 0))
    col = at((1, length, 1), lambda s: (s, 0, 0))
    row = at((1, 1, length), lambda s: (s, 0, 0))
    floor = at((1, width), lambda s: (0, 0))
    gain = at((1, HEAD), lambda s: (0, 0))
    wide = at((1, length, 3 * width), lambda s: (s, 0, 0))
    pairs = [at((1, length, k * width), lambda s: (s, 0, 0)) for k in (1, 2)]
    return at, rows, side, wide, pairs, [col, row, floor, gain]


def weight_scratch(model, lanes, sources):
    return [pltpu.VMEM((model, lanes), BF), pltpu.SemaphoreType.DMA((4 * len(sources),))]


def layout_of(sources):
    return tuple((piece, low) for piece, low, _ in sources), [part for _, _, part in sources]


def mixer_forward(core, offsets, tokens, sources, segments, floor, gain):
    groups, length, model = tokens.shape
    width, count = floor.shape[0], length // 2
    half = (groups, count, model)
    at, rows, side, wide, pairs, small = mixer_specs(count, model, width, length)
    layout, parts = layout_of(sources)
    shape = jax.ShapeDtypeStruct
    return pl.pallas_call(
        functools.partial(mixer_forward_kernel, sources=layout),
        grid_spec=pltpu.PrefetchScalarGridSpec(
            num_scalar_prefetch=2,
            grid=(groups,),
            in_specs=[rows] + [pl.BlockSpec(memory_space=pl.ANY)] * len(parts) + small,
            out_specs=[wide, pairs[0], side, side],
            scratch_shapes=[
                pltpu.VMEM((width // HEAD, length, length), BF),
                pltpu.VMEM((length, width), BF),
            ]
            + weight_scratch(model, 4 * width, parts),
        ),
        out_shape=[
            shape((groups, length, 3 * width), jnp.float32),
            shape((groups, length, width), BF),
            shape(half, BF),
            shape(half, jnp.float32),
        ],
        compiler_params=PARAMS,
        cost_estimate=cost(17),
        name="mixer_forward",
    )(
        core, offsets, tokens, *parts, segments[:, :, None],
        segments[:, None, :], floor[None], gain[None],
    )


def mixer_backward(core, offsets, tokens, sources, projected, segments, floor, gain):
    groups, length, model = tokens.shape
    width, count = floor.shape[0], length // 2
    half = (groups, count, model)
    at, rows, side, wide, pairs, small = mixer_specs(count, model, width, length)
    layout, parts = layout_of(sources)
    heads = width // HEAD
    sums = at((1, 8, width), lambda s: (s, 0, 0))
    shape = jax.ShapeDtypeStruct
    return pl.pallas_call(
        functools.partial(mixer_backward_kernel, sources=layout),
        grid_spec=pltpu.PrefetchScalarGridSpec(
            num_scalar_prefetch=2,
            grid=(groups,),
            in_specs=[rows]
            + [pl.BlockSpec(memory_space=pl.ANY)] * len(parts)
            + [wide]
            + small,
            out_specs=[pairs[1], pairs[0], side, side, sums, sums],
            scratch_shapes=[pltpu.VMEM((heads, length, length), BF)]
            + [pltpu.VMEM((heads, length, HEAD), jnp.float32)] * 3
            + [pltpu.VMEM((length, width), jnp.float32), pltpu.VMEM((length, 3 * width), BF)]
            + weight_scratch(model, 4 * width, parts),
        ),
        out_shape=[
            shape((groups, length, 2 * width), BF),
            shape((groups, length, width), BF),
            shape(half, BF),
            shape(half, jnp.float32),
        ]
        + [shape((groups, 8, width), jnp.float32)] * 2,
        compiler_params=PARAMS,
        cost_estimate=cost(27),
        name="mixer_backward",
    )(
        core, offsets, tokens, *parts, projected, segments[:, :, None],
        segments[:, None, :], floor[None], gain[None],
    )


def ffn_kernel(core_ref, offsets_ref, rows_ref, top_ref, *refs, sources):
    (active_one_ref, active_two_ref, one_ref, two_ref, send_ref, keep_ref, grads, weight,
     sems) = refs[len(sources) :]

    @pl.when(pl.program_id(0) == 0)
    def _():
        load_weight(offsets_ref, sources, refs, weight, sems)

    width, cut = grads.shape[1] // 2, one_ref.shape[2]
    count = rows_ref.shape[1] // 2
    mine = pl.multiple_of(core_ref[0] * count, count)
    theirs = pl.multiple_of((1 - core_ref[0]) * count, count)
    both = dot(rows_ref[0], weight[:, : 2 * width])
    gate, up = both[:, :width], both[:, width:]
    active_grad = dot(top_ref[0], weight[:, 2 * width : 3 * width])
    squash = jax.nn.sigmoid(gate)
    swish = gate * squash
    half = active_one_ref.shape[2]
    spare = jnp.zeros((2 * count, 2 * half - width), BF)
    active = (swish * up).astype(BF)
    active_one_ref[0] = active[:, :half]
    active_two_ref[0] = jnp.concatenate([active[:, half:], spare], axis=1)
    gate_grad = active_grad * up * squash * (1.0 + gate * (1.0 - squash))
    grads[...] = jnp.concatenate([gate_grad, active_grad * swish], axis=1).astype(BF)
    one_ref[0] = grads[:, :cut]
    two_ref[0] = grads[:, cut:]
    send_ref[0] = dot(grads[pl.ds(theirs, count), :], weight[:, : 2 * width], NT).astype(BF)
    keep_ref[0] = dot(grads[pl.ds(mine, count), :], weight[:, : 2 * width], NT)


def ffn(core, offsets, tokens, tops, sources, width, total):
    groups, length, model = tokens.shape
    cut = width // 128 * 128
    widths = [(total - 2 * width) // 2] * 2 + [cut, 2 * width - cut]
    layout, parts = layout_of(sources)

    def at(rows, lanes):
        return pl.BlockSpec((1, rows, lanes), lambda s, c, o: (s, 0, 0))

    shape = jax.ShapeDtypeStruct
    return pl.pallas_call(
        functools.partial(ffn_kernel, sources=layout),
        grid_spec=pltpu.PrefetchScalarGridSpec(
            num_scalar_prefetch=2,
            grid=(groups,),
            in_specs=[at(length, model)] * 2 + [pl.BlockSpec(memory_space=pl.ANY)] * len(parts),
            out_specs=[at(length, n) for n in widths] + [at(length // 2, model)] * 2,
            scratch_shapes=[pltpu.VMEM((length, 2 * width), BF)]
            + weight_scratch(model, total, parts),
        ),
        out_shape=[
            *[shape((groups, length, n), BF) for n in widths],
            shape((groups, length // 2, model), BF),
            shape((groups, length // 2, model), jnp.float32),
        ],
        compiler_params=PARAMS,
        cost_estimate=cost(36),
        name="ffn",
    )(core, offsets, tokens, tops, *parts)


def rows_kernel(core_ref, offsets_ref, one_ref, two_ref, *refs, sources, begin):
    send_ref, keep_ref, whole, sems = refs[len(sources) :]

    @pl.when(pl.program_id(0) == 0)
    def _():
        load_weight(offsets_ref, sources, refs, whole, sems, begin)

    count = one_ref.shape[1] // 2
    mine = pl.multiple_of(core_ref[0] * count, count)
    theirs = pl.multiple_of((1 - core_ref[0]) * count, count)

    def product(at):
        parts = [one_ref[0, pl.ds(at, count), :], two_ref[0, pl.ds(at, count), :]]
        return dot(jnp.concatenate(parts, axis=1), whole[...], NT)

    send_ref[0] = product(theirs).astype(BF)
    keep_ref[0] = product(mine)


def rows_product(core, offsets, one, two, sources, begin, model):
    groups, length, width = one.shape
    layout, parts = layout_of(sources)

    def at(rows, lanes):
        return pl.BlockSpec((1, rows, lanes), lambda s, c, o: (s, 0, 0))

    shape = jax.ShapeDtypeStruct
    return pl.pallas_call(
        functools.partial(rows_kernel, sources=layout, begin=begin),
        grid_spec=pltpu.PrefetchScalarGridSpec(
            num_scalar_prefetch=2,
            grid=(groups,),
            in_specs=[at(length, width)] * 2 + [pl.BlockSpec(memory_space=pl.ANY)] * len(parts),
            out_specs=[at(length // 2, model)] * 2,
            scratch_shapes=weight_scratch(model, 2 * width, parts),
        ),
        out_shape=[
            shape((groups, length // 2, model), BF),
            shape((groups, length // 2, model), jnp.float32),
        ],
        compiler_params=PARAMS,
        cost_estimate=cost(13),
        name="rows_product",
    )(core, offsets, one, two, *parts)


def grad_kernel(blocks_ref, rows_ref, *refs):
    half = len(refs) // 2
    for grad_ref, out_ref in zip(refs[:half], refs[half:]):
        out_ref[0] = dot(rows_ref[...], grad_ref[...], TN).astype(out_ref.dtype)


def grad_product(tokens, grads, blocks, wide, kind):
    count, model = tokens.shape
    side = pl.BlockSpec((count, wide), lambda i, b: (0, b[i]))
    number = blocks.shape[0]
    return pl.pallas_call(
        grad_kernel,
        grid_spec=pltpu.PrefetchScalarGridSpec(
            num_scalar_prefetch=1,
            grid=(number,),
            in_specs=[side] + [pl.BlockSpec(g.shape, lambda i, b: (0, 0)) for g in grads],
            out_specs=[pl.BlockSpec((1, wide, g.shape[1]), lambda i, b: (i, 0, 0)) for g in grads],
        ),
        out_shape=[jax.ShapeDtypeStruct((number, wide, g.shape[1]), kind) for g in grads],
        compiler_params=PARAMS,
        cost_estimate=cost(6),
        name="grad_product",
    )(blocks, tokens, *grads)


GROUP = ("l", "x")


def swap(values, axes):
    total = 2 ** len(axes)
    return lax.ppermute(values, axes, [(s, total - 1 - s) for s in range(total)])


def shift(values, steps):
    total = lax.axis_size("h")
    return lax.ppermute(values, "h", [(s, (s + steps) % total) for s in range(total)])


def own_member():
    return lax.axis_index("l") * 2 + lax.axis_index("x")


def source_rows(rows):
    y, high = lax.axis_index("y"), lax.axis_index("h")
    highs = lax.axis_size("h")
    starts = []
    for k in range(highs):
        for side in (y, 1 - y):
            for member in range(4):
                block = ((high - k) % highs) * 8 + (member >> 1) * 4 + side * 2 + (member & 1)
                starts.append(block * rows)
    return jnp.stack(starts).astype(jnp.int32)


def trade(slices):
    return lax.all_to_all(slices, GROUP, 0, 0, tiled=True)


def after(values, *others):
    return lax.optimization_barrier((values, others))[0]


def far(block):
    return [shift(block, k) for k in range(1, lax.axis_size("h"))]


def near(parts):
    return [swap(part, ("y",)) for part in parts]


def pieces(low, straight, crossed):
    out = []
    for k, (one, two) in enumerate(zip(straight, crossed), 1):
        out += [(2 * k, low, one), (2 * k + 1, low, two)]
    return out


def half_grads(tokens, grads, yy, kind):
    highs, high = lax.axis_size("h"), lax.axis_index("h")
    wide = tokens.shape[1] // (4 * highs)
    order = [(high + k) % highs for k in range(1, highs)] + [high]
    blocks = jnp.stack([(h * 2 + z) * 2 + yy for h in order for z in range(2)]).astype(jnp.int32)
    if wide % 128 == 0:
        return grad_product(tokens, grads, blocks, wide, kind)
    split = jnp.take(tokens.reshape(tokens.shape[0], -1, wide), blocks, axis=1)
    return [
        jnp.einsum("tad,tx->adx", split, g, preferred_element_type=jnp.float32).astype(kind)
        for g in grads
    ]


def grad_sends(tokens, grads):
    return half_grads(flat(tokens), [flat(g) for g in grads], 1 - lax.axis_index("y"), BF)


def grad_keeps(tokens, grads):
    return half_grads(flat(tokens), [flat(g) for g in grads], lax.axis_index("y"), jnp.float32)


def add_near(keep, came):
    highs = lax.axis_size("h")
    total = keep + came.astype(jnp.float32)
    cuts = [2 * k for k in range(1, highs)]
    *away, home = jnp.split(total, cuts)
    return home, [part.astype(BF) for part in away]


def send_far(away):
    return [shift(part, k) for k, part in enumerate(away, 1)]


def add_far(home, fars):
    for far in fars:
        home = home + far.astype(jnp.float32)
    return home.reshape(4, -1, home.shape[-1]).astype(BF)


def flat(values):
    return values.reshape(-1, values.shape[-1])


def gather_rows(rows):
    full = lax.all_gather(rows, GROUP + ("tensor",), axis=0, tiled=True)
    return full.reshape(4, -1, rows.shape[1])


def add_cores(keep, came):
    return (keep + came.astype(jnp.float32)).astype(BF)


def add_members(parts):
    return jnp.sum(parts.astype(jnp.float32), axis=0)


def sum_all(values):
    for axis in ("x", "y", "l", "tensor"):
        values = values + swap(values, (axis,))
    size, bits = lax.axis_size("h"), 1
    while bits < size:
        values = values + lax.ppermute(values, "h", [(s, s ^ bits) for s in range(size)])
        bits *= 2
    return values


def rms_of(values):
    return lax.rsqrt(jnp.mean(values * values, axis=-1, keepdims=True) + epsilon)


def norm_back(values, scale, gain, grad):
    unit = values * scale
    wide = grad * gain
    out = scale * (wide - unit * jnp.mean(wide * unit, axis=-1, keepdims=True))
    return out, jnp.sum(grad * unit, axis=0)


def body(
    hidden_in,
    segments,
    mix_weights,
    ffn_weights,
    norm1_gain,
    norm2_gain,
    head_gain,
    lower_bound,
    out_grad,
):
    core, member = lax.axis_index("tensor"), own_member()
    core_at = core.astype(jnp.int32).reshape(1)
    rows = mix_weights.shape[0]
    offsets = source_rows(rows)
    quarter, units = lower_bound.shape[0] // 4, ffn_weights.shape[2] // 4
    model = hidden_in.shape[1]
    channels = 4 * quarter
    lanes = -(-3 * units // 128) * 128

    def slices(weights, width):
        split = weights.reshape(rows, weights.shape[1], 4, -1).transpose(2, 0, 1, 3)
        split = split.reshape(4, rows, -1)
        return jnp.pad(split, ((0, 0), (0, 0), (0, width - split.shape[2])))

    length = segments.shape[1]
    labels = jnp.pad(segments.astype(BF), ((0, 15), (0, channels - length)))
    labels = jnp.broadcast_to(labels, (4,) + labels.shape)
    hidden = hidden_in.astype(jnp.float32)
    scale_one = rms_of(hidden)
    normed = (hidden * scale_one * norm1_gain).astype(BF)
    floor = lax.dynamic_slice_in_dim(lower_bound, member * quarter, quarter)
    feed = slices(ffn_weights, lanes)
    mix = trade(jnp.concatenate([slices(mix_weights, channels), labels], axis=1))

    gate = (mix, normed, feed)
    mix, normed, feed = lax.optimization_barrier(gate)
    labels = mix[:, rows, :length].astype(jnp.int32)
    mix = mix[:, :rows]
    cut = 640
    mix_far_a = far(mix[..., :cut])
    mix_near = swap(mix, ("y",))
    feed = trade(feed)

    gate = (mix_far_a, mix_near, feed)
    mix_far_b = far(after(mix[..., cut:], gate))
    mix_cross_a = near(after(mix_far_a, gate))
    normed = gather_rows(after(normed, gate))

    gate = (mix_far_b, mix_cross_a)
    cuts = [0, 384, 768, 1024, 1664, lanes]
    feeds = [feed[..., low:high] for low, high in zip(cuts[:-1], cuts[1:])]
    far_a = far(after(feeds[0], gate))
    mix_cross_b = near(after(mix_far_b, gate))
    mix_sources = [(0, 0, mix), (1, 0, mix_near)]
    mix_sources += pieces(0, mix_far_a, mix_cross_a) + pieces(cut, mix_far_b, mix_cross_b)

    gate = (far_a, mix_cross_b, normed)
    far_b = far(after(feeds[1], gate))
    near_a = swap(after(feed[..., :768], gate), ("y",))
    tops = gather_rows(after(out_grad, gate))
    projected, mixed, send, keep = mixer_forward(
        core_at, offsets, after(normed, gate), mix_sources, labels, floor, head_gain
    )

    gate = (send, far_b, near_a)
    came = swap(after(send, gate), ("tensor",))
    far_c = far(after(feeds[2], gate))
    near_b = swap(after(feed[..., 768:1280], gate), ("y",))
    total = add_cores(keep, came)

    gate = (total, far_c, near_b)
    parts = trade(after(total, gate))
    far_d = far(after(feeds[3], gate))
    near_c = swap(after(feed[..., 1280:], gate), ("y",))
    cross_a = near(after(far_a, near_c))

    gate = (parts, far_d, near_c, cross_a)
    far_e = far(after(feeds[4], gate))
    cross_b = near(after(far_b, gate))
    cross_c = near(after(far_c, cross_b))
    middle = hidden + add_members(after(parts, gate))
    scale_two = rms_of(middle)
    normed_two = gather_rows((middle * scale_two * norm2_gain).astype(BF))

    gate = (far_e, cross_c)
    cross_d = near(after(far_d, gate))
    cross_e = near(after(far_e, gate))
    feed_sources = [(0, 0, feed), (1, 0, near_a), (1, 768, near_b), (1, 1280, near_c)]
    crosses = [cross_a, cross_b, cross_c, cross_d, cross_e]
    for low, straight, crossed in zip(cuts, [far_a, far_b, far_c, far_d, far_e], crosses):
        feed_sources += pieces(low, straight, crossed)

    active_one, active_two, grad_one, grad_two, send, keep = ffn(
        core_at, offsets, normed_two, tops, feed_sources, units, lanes
    )
    came = swap(send, ("tensor",))
    down_send, down_send_two = grad_sends(after(tops, send), [active_one, active_two])
    down_came = swap(down_send, ("y",))
    total = add_cores(keep, after(came, down_send))

    gate = (total,)
    parts = trade(total)
    one_send, two_send = grad_sends(after(normed_two, gate), [grad_one, grad_two])
    down_keep, down_keep_two = grad_keeps(after(tops, one_send), [active_one, active_two])

    gate = (down_came, down_keep)
    down_home, down_away = add_near(down_keep, after(down_came, gate))
    down_fars = send_far(down_away)
    down_came_two = swap(after(down_send_two, gate), ("y",))

    gate = (parts, down_fars, down_came_two)
    normed_two_grad = add_members(after(parts, gate))
    extra_two, gain_two_grad = norm_back(middle, scale_two, norm2_gain, normed_two_grad)
    middle_grad = out_grad.astype(jnp.float32) + extra_two
    middle_low = middle_grad.astype(BF)
    middle_full = gather_rows(middle_low)
    one_came = swap(after(one_send, gate), ("y",))
    down_home_two, down_away_two = add_near(down_keep_two, after(down_came_two, gate))
    down_fars_two = send_far(down_away_two)
    one_keep, two_keep = grad_keeps(
        after(normed_two, middle_low, down_away_two), [grad_one, grad_two]
    )
    away_send, away_keep = rows_product(
        core_at, offsets, after(active_one, one_keep), active_two, feed_sources, 2 * units, model
    )

    gate = (down_fars_two, one_came, away_send)
    one_home, one_away = add_near(one_keep, after(one_came, gate))
    one_fars = send_far(one_away)
    two_came = swap(after(two_send, gate), ("y",))
    away_total = add_cores(away_keep, swap(after(away_send, gate), ("tensor",)))

    gate = (middle_full, away_total, one_away)
    middle_full = after(middle_full, gate)
    (last_send,) = grad_sends(middle_full, [mixed])
    block_parts = trade(after(away_total, gate))
    g_one, g_two, send, keep, floor_sums, gain_sums = mixer_backward(
        core_at, offsets, after(middle_full, last_send), mix_sources, projected, labels, floor,
        head_gain,
    )

    gate = (send, one_fars, two_came, block_parts)
    two_home, two_away = add_near(two_keep, after(two_came, gate))
    two_fars = send_far(two_away)
    last_came = swap(after(last_send, gate), ("y",))
    came = swap(after(send, gate), ("tensor",))
    (g_two_send,) = grad_sends(after(normed, gate), [g_two])
    total = add_cores(keep, after(came, g_two_send, two_away))

    gate = (total, last_came)
    parts = trade(after(total, gate))
    g_two_came = swap(after(g_two_send, gate), ("y",))
    (g_one_send,) = grad_sends(after(normed, gate), [g_one])
    (last_keep,) = grad_keeps(after(middle_full, g_one_send), [mixed])
    (g_two_keep,) = grad_keeps(after(normed, last_keep), [g_two])

    gate = (g_two_came, g_two_keep)
    g_one_came = swap(after(g_one_send, gate), ("y",))
    last_home, last_away = add_near(last_keep, after(last_came, gate))
    g_two_home, g_two_away = add_near(g_two_keep, after(g_two_came, gate))
    near_away = [jnp.concatenate(pair, axis=-1) for pair in zip(g_two_away, last_away)]
    near_home = jnp.concatenate([g_two_home, last_home], axis=-1)
    (g_one_keep,) = grad_keeps(after(normed, near_away), [g_one])

    gate = (parts, two_fars, g_one_keep)
    near_fars = send_far(after(near_away, gate))
    sums = [add_far(one_home, after(one_fars, gate)), add_far(two_home, after(two_fars, gate))]
    input_parts = trade(jnp.concatenate(sums, axis=-1))
    normed_grad = add_members(after(parts, gate))
    extra_one, gain_one_grad = norm_back(hidden, scale_one, norm1_gain, normed_grad)
    input_grad = middle_grad + extra_one
    block_out = (middle + add_members(after(block_parts, gate))).astype(BF)
    g_one_home, g_one_away = add_near(g_one_keep, after(g_one_came, normed_grad))

    gate = (near_fars, input_parts, g_one_away)
    g_one_fars = send_far(after(g_one_away, gate))
    sums = [
        add_far(near_home, after(near_fars, gate)),
        add_far(down_home, after(down_fars, gate)),
        add_far(down_home_two, after(down_fars_two, gate)),
    ]
    near_parts = trade(jnp.concatenate(sums, axis=-1))
    down_parts = near_parts[..., 2 * quarter :]
    g_one_parts = trade(add_far(g_one_home, after(g_one_fars, near_parts)))

    head_grad = jnp.sum(gain_sums.reshape(-1, HEAD), axis=0)
    lower_grad = jnp.zeros((2, 4, quarter), jnp.float32)
    lower_grad = lax.dynamic_update_slice(
        lower_grad, jnp.sum(floor_sums, axis=(0, 1)).reshape(1, 1, quarter), (core, member, 0)
    )
    sums = jnp.concatenate([gain_one_grad, gain_two_grad, head_grad, lower_grad.reshape(-1)])
    sums = sum_all(sums.reshape(-1, HEAD)).reshape(-1)
    gain_one, gain_two, head, lower = jnp.split(sums, [model, 2 * model, 2 * model + HEAD])

    def stacked(*parts):
        joined = [p.transpose(1, 0, 2).reshape(rows, -1) for p in parts]
        return jnp.stack(joined, axis=1).astype(jnp.float32)

    mix_grad = stacked(
        g_one_parts[..., :quarter],
        g_one_parts[..., quarter:],
        near_parts[..., :quarter],
        near_parts[..., quarter : 2 * quarter],
    )
    ffn_grad = stacked(input_parts[..., :units], input_parts[..., units:], down_parts[..., :units])
    return (block_out, input_grad, mix_grad, ffn_grad, gain_one, gain_two, head, lower)


def solution(mesh):
    total, cores = mesh.shape["dp"], mesh.shape["tensor"]
    fine = Mesh(mesh.devices.reshape(total // 8, 2, 2, 2, cores), ("h", "l", "y", "x", "tensor"))
    dp = ("h", "l", "y", "x")
    rows = P(dp + ("tensor",), None)
    weights = P(dp, None, "tensor")
    return jax.shard_map(
        body,
        mesh=fine,
        in_specs=(rows, P(dp, None), weights, weights, P(), P(), P(), P("tensor"), rows),
        out_specs=(rows, rows, weights, weights, P(), P(), P(), P()),
        check_vma=False,
    )
```

time: 3120 us -> 660 us (0.21)
  waiting for transfers between devices: 2550 us -> 261 us
  other arithmetic: 256 us -> 66.4 us
  matrix products: 157 us -> 0 us
  Pallas kernels: 0 us -> 155 us
  starting transfers between devices: 1.32 us -> 87.2 us
  blocking collectives: 47.2 us -> 0 us
    reduce_scatter x6 -> x0, waiting for transfers between devices: 1970 us -> none  [the longest x2 1950 us: body(): lax.psum_scatter(jnp.concatenate([inputs_part, output_part[:, None, :]],...]
    all_gather x6 -> x4, waiting for transfers between devices: 577 us -> 9.41 us  [gather_rows(): full = lax.all_gather(rows, GROUP + ('tensor',), axis=0, tiled=True)]
    ppermute x0 -> x40, waiting for transfers between devices: none -> 244 us  [the longest x13 132 us: shift(): lax.ppermute(values, 'h', [(s, (s + steps) % total) for s in range(total)])]
    dot_general x48 -> x0, matrix products: 157 us -> none  [the longest x2 22.7 us: row_term(): jnp.einsum('tkx,dkx->td', source, weight, preferred_element_type=jnp.floa...]
    pallas_call x0 -> x14, Pallas kernels: none -> 155 us  [the longest x10 61.5 us: grad_product(): pl.pallas_call(grad_kernel, grid_spec=pltpu.PrefetchScalarGridSpec(num_sc...]
    reduce_sum x18 -> x10, other arithmetic: 125 us -> 11.8 us  [the longest x4 8.37 us: add_members(): return jnp.sum(parts.astype(jnp.float32), axis=0)]
    concatenate x2 -> x4, other arithmetic: 60 us -> 6.78 us  [the longest x1 2.54 us: body(): input_parts = trade(jnp.concatenate(sums, axis=-1))]
    psum x1 -> x0, blocking collectives: 47.2 us -> none  [body(): lax.psum((gain_one_grad, gain_two_grad, head_grad, lower_full), ('dp', 't...]
  transfers between devices with their start and end apart: 12 -> 53, of which waited for: 8 -> 32; matrix products, arithmetic and copies ran while one was open for 5% -> 15% of each run, Pallas kernels for 0% -> 18%
where the time goes in v2:
time: 660 us; the launch traced here: 651 us
  waiting for transfers between devices  261 us (40%)
  Pallas kernels  155 us (23%)
  starting transfers between devices  87.2 us (13%)
  local copies, waits for them, and re-layouts  66.4 us (10%)
  other arithmetic  66.4 us (10%)
  between operations  14.9 us (2%)
    ppermute x13, waiting for transfers between devices, shift(): lax.ppermute(values, 'h', [(s, (s + steps) % total) for s in range(total)])  132 us
    ppermute x26, waiting for transfers between devices, swap(): lax.ppermute(values, axes, [(s, total - 1 - s) for s in range(total)])  100 us
    pallas_call x10, Pallas kernels, grad_product(): pl.pallas_call(grad_kernel, grid_spec=pltpu.PrefetchScalarGridSpec(num_sc...  61.5 us
    all_to_all x9, starting transfers between devices, trade(): return lax.all_to_all(slices, GROUP, 0, 0, tiled=True)  44.8 us
    pallas_call x1, Pallas kernels, ffn(): pl.pallas_call(functools.partial(ffn_kernel, sources=layout), grid_spec=p...  36.1 us
    pallas_call x1, Pallas kernels, mixer_backward(): pl.pallas_call(functools.partial(mixer_backward_kernel, sources=layout),...  26.9 us
    ppermute x26, starting transfers between devices, swap(): lax.ppermute(values, axes, [(s, total - 1 - s) for s in range(total)])  23.8 us
    unnamed x128, local copies, waits for them, and re-layouts  23.8 us
  transfers between devices with their start and end apart: 53, of which 32 were waited for; matrix products, arithmetic and copies ran while one was open for 15% of the time, Pallas kernels for 18%

profile of v2, /device:TPU:0, one launch (start us, length us, event | category | flops | bytes accessed | tf_op | source)
XLA Modules:
  0.0 650.8 jit_solution(2568916374112318569)
XLA Ops:
  10.7 5.2 all-to-all-start
  42.5 31.8 %collective-permute-done.refs_2_ = bf16[4,128,640]{2,1,0:T(8,128)(2,1)S(1)} collective-permute-done((bf16[4,128,640]{2,1,0:T(8,128)(2,1)S(1)}, bf16[4,128,640]{2,1,0:T(8,128)(2,1)S(1)}, u32[]{:S(2)}, u32[]{:S(2)}) %collective-permute-start) | collective-permute-done | bytes 655392 | tf_op jit(solution)/shard_map/ppermute | solution.py:447
  82.3 15.3 %collective-permute-done.2.refs_4_ = bf16[4,128,384]{2,1,0:T(8,128)(2,1)} collective-permute-done((bf16[4,128,384]{2,1,0:T(8,128)(2,1)S(1)}, bf16[4,128,384]{2,1,0:T(8,128)(2,1)}, u32[]{:S(2)}, u32[]{:S(2)}) %collective-permute-start.2) | collective-permute-done | bytes 393248 | tf_op jit(solution)/shard_map/ppermute | solution.py:447
  102.9 8.3 %collective-permute-done.4.refs_4_ = bf16[4,128,384]{2,1,0:T(8,128)(2,1)} collective-permute-done((bf16[4,128,384]{2,1,0:T(8,128)(2,1)}, bf16[4,128,384]{2,1,0:T(8,128)(2,1)}, u32[]{:S(2)}, u32[]{:S(2)}) %collective-permute-start.4) | collective-permute-done | bytes 393248 | tf_op jit(solution)/shard_map/ppermute | solution.py:447
  111.2 9.4 %all-gather.5.cloned.1.call-done = bf16[1024,2048]{1,0:T(8,128)(2,1)} async-done(((bf16[128,2048]{1,0:T(8,128)(2,1)}), bf16[1024,2048]{1,0:T(8,128)(2,1)}) %all-gather.5.cloned.1.call-update) | async-done | bytes 4194320 | tf_op jit(solution)/shard_map/all_gather | solution.py:534
  124.2 17.0 %mixer_forward.1 = (f32[4,256,768]{2,1,0:T(8,128)}, bf16[4,256,256]{2,1,0:T(8,128)(2,1)}, bf16[4,128,2048]{2,1,0:T(8,128)(2,1)}, f32[4,128,2048]{2,1,0:T(8,128)}) custom-call(s32[1]{0:T(128)} %bitcast.core_ref, s32[16]{0:T(128)} %stack.143.offsets_ref, bf16[4,256,2048]{2,1,0:T(8,128)(2,1)} %bitcast.129, bf16[4,128,1024]{2,1,0:T(8,128)(2,1)} %copy-done.21, ...), custom_call_target="tpu_custom_call" | custom-call | flops 16999999488 | bytes 1 | tf_op jit(solution)/shard_map/mixer_forward/pallas_call | solution.py:237
  150.9 5.9 collective-permute-done.9.refs_8_
  157.4 8.9 %all-to-all-start.2 = ((bf16[4,128,2048]{2,1,0:T(8,128)(2,1)}), bf16[4,128,2048]{2,1,0:T(8,128)(2,1)}, u32[]{:S(2)}, u32[]{:S(2)}) async-start(bf16[4,128,2048]{2,1,0:T(8,128)(2,1)} %add_convert_fusion.3), calls=%async_computation.2 | async-start | bytes 4194304 | tf_op jit(solution)/shard_map/all_to_all | solution.py:467
  167.7 21.0 %collective-permute-done.12.refs_3_ = bf16[4,128,896]{2,1,0:T(8,128)(2,1)S(1)} collective-permute-done((bf16[4,128,896]{2,1,0:T(8,128)(2,1)S(1)}, bf16[4,128,896]{2,1,0:T(8,128)(2,1)S(1)}, u32[]{:S(2)}, u32[]{:S(2)}) %collective-permute-start.12) | collective-permute-done | bytes 917536 | tf_op jit(solution)/shard_map/ppermute | solution.py:442
  189.3 13.7 %collective-permute-done.11.refs_10_ = bf16[4,128,640]{2,1,0:T(8,128)(2,1)S(1)} collective-permute-done((bf16[4,128,640]{2,1,0:T(8,128)(2,1)S(1)}, bf16[4,128,640]{2,1,0:T(8,128)(2,1)S(1)}, u32[]{:S(2)}, u32[]{:S(2)}) %collective-permute-start.11) | collective-permute-done | bytes 655392 | tf_op jit(solution)/shard_map/ppermute | solution.py:447
  212.3 7.9 %collective-permute-done.14.refs_7_ = bf16[4,128,384]{2,1,0:T(8,128)(2,1)S(1)} collective-permute-done((bf16[4,128,384]{2,1,0:T(8,128)(2,1)}, bf16[4,128,384]{2,1,0:T(8,128)(2,1)S(1)}, u32[]{:S(2)}, u32[]{:S(2)}) %collective-permute-start.14) | collective-permute-done | bytes 393248 | tf_op jit(solution)/shard_map/ppermute | solution.py:442
  220.5 14.6 %collective-permute-done.16.refs_12_ = bf16[4,128,512]{2,1,0:T(8,128)(2,1)S(1)} collective-permute-done((bf16[4,128,512]{2,1,0:T(8,128)(2,1)S(1)}, bf16[4,128,512]{2,1,0:T(8,128)(2,1)S(1)}, u32[]{:S(2)}, u32[]{:S(2)}) %collective-permute-start.16) | collective-permute-done | bytes 524320 | tf_op jit(solution)/shard_map/ppermute | solution.py:447
  237.2 25.5 %collective-permute-done.18.refs_13_ = bf16[4,128,512]{2,1,0:T(8,128)(2,1)S(1)} collective-permute-done((bf16[4,128,512]{2,1,0:T(8,128)(2,1)S(1)}, bf16[4,128,512]{2,1,0:T(8,128)(2,1)S(1)}, u32[]{:S(2)}, u32[]{:S(2)}) %collective-permute-start.18) | collective-permute-done | bytes 524320 | tf_op jit(solution)/shard_map/ppermute | solution.py:442
  263.7 36.1 %ffn.1 = (bf16[4,256,384]{2,1,0:T(8,128)(2,1)}, bf16[4,256,384]{2,1,0:T(8,128)(2,1)}, bf16[4,256,640]{2,1,0:T(8,128)(2,1)}, bf16[4,256,768]{2,1,0:T(8,128)(2,1)}...) custom-call(s32[1]{0:T(128)} %bitcast.core_ref, s32[16]{0:T(128)} %stack.143.offsets_ref, ...), custom_call_target="tpu_custom_call" | custom-call | flops 35999997952 | bytes 1 | tf_op jit(solution)/shard_map/ffn/pallas_call | solution.py:345
  300.6 6.9 %grad_product.10 = (bf16[4,256,384]{2,1,0:T(8,128)(2,1)}, bf16[4,256,384]{2,1,0:T(8,128)(2,1)}) custom-call(s32[4]{0:T(128)} %pad_add_fusion.1.blocks_ref, bf16[1024,2048]{1,0:T(8,128)(2,1)} %all-gather.9.cloned.1.call-done, bf16[1024,384]{1,0:T(8,128)(2,1)} %bitcast.141, bf16[1024,384]{1,0:T(8,128)(2,1)} %bitcast.143), custom_call_target="tpu_custom_call" | custom-call | flops 6000000000 | bytes 1 | tf_op jit(solution)/shard_map/grad_product/pallas_call | solution.py:422
  316.6 7.8 %grad_product.11 = (bf16[4,256,640]{2,1,0:T(8,128)(2,1)}, bf16[4,256,768]{2,1,0:T(8,128)(2,1)}) custom-call(s32[4]{0:T(128)} %pad_add_fusion.1.blocks_ref, bf16[1024,2048]{1,0:T(8,128)(2,1)} %all-gather.7.cloned.1.call-done, bf16[1024,640]{1,0:T(8,128)(2,1)} %bitcast.137, bf16[1024,768]{1,0:T(8,128)(2,1)} %bitcast.135), custom_call_target="tpu_custom_call" | custom-call | flops 6000000000 | bytes 1 | tf_op jit(solution)/shard_map/grad_product/pallas_call | solution.py:422
  324.4 6.7 %grad_product.12 = (f32[4,256,384]{2,1,0:T(8,128)}, f32[4,256,384]{2,1,0:T(8,128)}) custom-call(s32[4]{0:T(128)} %pad_add_fusion.blocks_ref, bf16[1024,2048]{1,0:T(8,128)(2,1)} %all-gather.9.cloned.1.call-done, bf16[1024,384]{1,0:T(8,128)(2,1)} %bitcast.142, bf16[1024,384]{1,0:T(8,128)(2,1)} %bitcast.144), custom_call_target="tpu_custom_call" | custom-call | flops 6000000000 | bytes 1 | tf_op jit(solution)/shard_map/grad_product/pallas_call | solution.py:422
  339.4 19.8 %collective-permute-done.21 = bf16[2,256,384]{2,1,0:T(8,128)(2,1)S(1)} collective-permute-done((bf16[2,256,384]{2,1,0:T(8,128)(2,1)S(1)}, bf16[2,256,384]{2,1,0:T(8,128)(2,1)S(1)}, u32[]{:S(2)}, u32[]{:S(2)}) %collective-permute-start.21) | collective-permute-done | bytes 393248 | tf_op jit(solution)/shard_map/ppermute | solution.py:447
  366.4 8.3 %grad_product.13 = (f32[4,256,640]{2,1,0:T(8,128)}, f32[4,256,768]{2,1,0:T(8,128)}) custom-call(s32[4]{0:T(128)} %pad_add_fusion.blocks_ref, bf16[1024,2048]{1,0:T(8,128)(2,1)} %all-gather.7.cloned.1.call-done, bf16[1024,640]{1,0:T(8,128)(2,1)} %bitcast.138, bf16[1024,768]{1,0:T(8,128)(2,1)} %bitcast.136), custom_call_target="tpu_custom_call" | custom-call | flops 6000000000 | bytes 1 | tf_op jit(solution)/shard_map/grad_product/pallas_call | solution.py:422
  374.6 13.8 %rows_product.1 = (bf16[4,128,2048]{2,1,0:T(8,128)(2,1)}, f32[4,128,2048]{2,1,0:T(8,128)}) custom-call(s32[1]{0:T(128)} %bitcast.core_ref, s32[16]{0:T(128)} %stack.143.offsets_ref, bf16[4,256,384]{2,1,0:T(8,128)(2,1)} %get-tuple-element.149.one_ref, bf16[4,256,384]{2,1,0:T(8,128)(2,1)} %get-tuple-element.132.two_ref, bf16[4,128,2176]{2,1,0:T(8,128)(2,1)} %copy-done, ...), custom_call_target="tpu_custom_call" | custom-call | flops 12999999488 | bytes 1 | tf_op jit(solution)/shard_map/rows_product/pallas_call | solution.py:393
  388.4 7.6 %collective-permute-done.24 = bf16[4,256,640]{2,1,0:T(8,128)(2,1)S(1)} collective-permute-done((bf16[4,256,640]{2,1,0:T(8,128)(2,1)}, bf16[4,256,640]{2,1,0:T(8,128)(2,1)S(1)}, u32[]{:S(2)}, u32[]{:S(2)}) %collective-permute-start.24) | collective-permute-done | bytes 1310752 | tf_op jit(solution)/shard_map/ppermute | solution.py:442
  416.2 26.9 %mixer_backward.1 = (bf16[4,256,512]{2,1,0:T(8,128)(2,1)}, bf16[4,256,256]{2,1,0:T(8,128)(2,1)}, bf16[4,128,2048]{2,1,0:T(8,128)(2,1)}, f32[4,128,2048]{2,1,0:T(...) custom-call(s32[1]{0:T(128)} %bitcast.core_ref, s32[16]{0:T(128)} %stack.143.offsets_ref, ...), custom_call_target="tpu_custom_call" | custom-call | flops 27000000512 | bytes 1 | tf_op jit(solution)/shard_map/mixer_backward/pallas_call | solution.py:274
  453.9 5.5 grad_product.15
  469.4 5.5 grad_product.16
  474.9 5.2 grad_product.17
  486.8 6.8 %collective-permute-done.31 = bf16[4,256,256]{2,1,0:T(8,128)(2,1)S(1)} collective-permute-done((bf16[4,256,256]{2,1,0:T(8,128)(2,1)S(1)}, bf16[4,256,256]{2,1,0:T(8,128)(2,1)S(1)}, u32[]{:S(2)}, u32[]{:S(2)}) %collective-permute-start.31) | collective-permute-done | bytes 524320 | tf_op jit(solution)/shard_map/ppermute | solution.py:442
  497.0 5.7 grad_product.19
  540.6 11.6 %collective-permute-done.32 = bf16[4,256,512]{2,1,0:T(8,128)(2,1)} collective-permute-done((bf16[4,256,512]{2,1,0:T(8,128)(2,1)}, bf16[4,256,512]{2,1,0:T(8,128)(2,1)}, u32[]{:S(2)}, u32[]{:S(2)}) %collective-permute-start.32) | collective-permute-done | bytes 1048608 | tf_op jit(solution)/shard_map/ppermute | solution.py:442
  585.8 8.4 %collective-permute-done.37 = f32[49,128]{1,0:T(8,128)S(1)} collective-permute-done((f32[49,128]{1,0:T(8,128)S(1)}, f32[49,128]{1,0:T(8,128)S(1)}, u32[]{:S(2)}, u32[]{:S(2)}) %collective-permute-start.37) | collective-permute-done | bytes 25120 | tf_op jit(solution)/shard_map/ppermute | solution.py:442
  601.0 11.6 %collective-permute-done.39 = f32[49,128]{1,0:T(8,128)S(1)} collective-permute-done((f32[49,128]{1,0:T(8,128)S(1)}, f32[49,128]{1,0:T(8,128)S(1)}, u32[]{:S(2)}, u32[]{:S(2)}) %collective-permute-start.39) | collective-permute-done | bytes 25120 | tf_op jit(solution)/shard_map/ppermute | solution.py:551
  613.8 10.2 %collective-permute-done.34 = bf16[2,256,512]{2,1,0:T(8,128)(2,1)} collective-permute-done((bf16[2,256,512]{2,1,0:T(8,128)(2,1)S(1)}, bf16[2,256,512]{2,1,0:T(8,128)(2,1)}, u32[]{:S(2)}, u32[]{:S(2)}) %collective-permute-start.34) | collective-permute-done | bytes 524320 | tf_op jit(solution)/shard_map/ppermute | solution.py:447
  635.0 5.7 copy.41
  (314 shorter events, 241.1 us)
Async XLA Ops:
  10.7 20.8 %all-to-all-start = ((bf16[4,144,1024]{2,1,0:T(8,128)(2,1)}), bf16[4,144,1024]{2,1,0:T(8,128)(2,1)S(1)}, u32[]{:S(2)}, u32[]{:S(2)}) async-start(bf16[4,144,1024]{2,1,0:T(8,128)(2,1)} %pad_maximum_fusion.2), calls=%async_computation | async-start | bytes 2359296 | tf_op jit(solution)/shard_map/all_to_all | solution.py:467
  32.6 44.0 %all-to-all-start.1 = ((bf16[4,128,2176]{2,1,0:T(8,128)(2,1)}), bf16[4,128,2176]{2,1,0:T(8,128)(2,1)S(1)}, u32[]{:S(2)}, u32[]{:S(2)}) async-start(bf16[4,128,2176]{2,1,0:T(8,128)(2,1)} %pad.9), calls=%async_computation.1 | async-start | bytes 4456448 | tf_op jit(solution)/shard_map/all_to_all | solution.py:467
  36.8 83.8 %all-gather.5.cloned.1.call-start = ((), (), s32[]{:S(2)}) async-start(), calls=%async_computation.9 | async-start | bytes 4718592 | tf_op jit(solution)/shard_map/all_gather | solution.py:534
  38.2 37.0 %collective-permute-start.1 = (bf16[4,128,1024]{2,1,0:T(8,128)(2,1)S(1)}, bf16[4,128,1024]{2,1,0:T(8,128)(2,1)}, u32[]{:S(2)}, u32[]{:S(2)}) collective-permute-start(bf16[4,128,1024]{2,1,0:T(8,128)(2,1)S(1)} %slice.66.refs_0_), channel_id=1, source_target_pairs={{0,4},{4,0},{1,5},{5,1},{2,6},{6,2},{3,7},{7,3},{8,12},{12,8},{9,1... | collective-permute-start | bytes 3145736 | tf_op jit(solution)/shard_map/ppermute | solution.py:442
  39.8 34.5 %collective-permute-start = (bf16[4,128,640]{2,1,0:T(8,128)(2,1)S(1)}, bf16[4,128,640]{2,1,0:T(8,128)(2,1)S(1)}, u32[]{:S(2)}, u32[]{:S(2)}) collective-permute-start(bf16[4,128,640]{2,1,0:T(8,128)(2,1)S(1)} %slice.65), channel_id=1, source_target_pairs={{0,16},{16,0},{1,17},{17,1},{2,18},{18,2},{3,19},{19,3},{4,20},{20... | collective-permute-start | bytes 1966088 | tf_op jit(solution)/shard_map/ppermute | solution.py:447
  76.5 186.2 %all-gather.9.cloned.1.call-start = ((), (), s32[]{:S(2)}) async-start(), calls=%async_computation.11 | async-start | bytes 4718592 | tf_op jit(solution)/shard_map/all_gather | solution.py:534
  76.6 21.1 %collective-permute-start.3 = (bf16[4,128,640]{2,1,0:T(8,128)(2,1)}, bf16[4,128,640]{2,1,0:T(8,128)(2,1)}, u32[]{:S(2)}, u32[]{:S(2)}) collective-permute-start(bf16[4,128,640]{2,1,0:T(8,128)(2,1)} %copy-done.51), channel_id=1, source_target_pairs={{0,4},{4,0},{1,5},{5,1},{2,6},{6,2},{3,7},{7,3},{8,12},{12,8},{9,1... | collective-permute-start | bytes 1966088 | tf_op jit(solution)/shard_map/ppermute | solution.py:442
  120.6 21.0 %collective-permute-start.6 = (bf16[4,128,384]{2,1,0:T(8,128)(2,1)}, bf16[4,128,384]{2,1,0:T(8,128)(2,1)}, u32[]{:S(2)}, u32[]{:S(2)}) collective-permute-start(bf16[4,128,384]{2,1,0:T(8,128)(2,1)} %get-tuple-element.112), channel_id=1, source_target_pairs={{0,16},{16,0},{1,17},{17,1},{2,18},{18,2},{3,19},{19,3},{4,20},{20... | collective-permute-start | bytes 1179656 | tf_op jit(solution)/shard_map/ppermute | solution.py:447
  157.4 48.1 %all-to-all-start.2 = ((bf16[4,128,2048]{2,1,0:T(8,128)(2,1)}), bf16[4,128,2048]{2,1,0:T(8,128)(2,1)}, u32[]{:S(2)}, u32[]{:S(2)}) async-start(bf16[4,128,2048]{2,1,0:T(8,128)(2,1)} %add_convert_fusion.3), calls=%async_computation.2 | async-start | bytes 4194304 | tf_op jit(solution)/shard_map/all_to_all | solution.py:467
  166.3 96.4 %all-gather.7.cloned.1.call-start = ((), (), s32[]{:S(2)}) async-start(), calls=%async_computation.10 | async-start | bytes 4718592 | tf_op jit(solution)/shard_map/all_gather | solution.py:534
  167.0 21.8 %collective-permute-start.12 = (bf16[4,128,896]{2,1,0:T(8,128)(2,1)S(1)}, bf16[4,128,896]{2,1,0:T(8,128)(2,1)S(1)}, u32[]{:S(2)}, u32[]{:S(2)}) collective-permute-start(bf16[4,128,896]{2,1,0:T(8,128)(2,1)S(1)} %slice.90), channel_id=1, source_target_pairs={{0,4},{4,0},{1,5},{5,1},{2,6},{6,2},{3,7},{7,3},{8,12},{12,8},{9,1... | collective-permute-start | bytes 2752520 | tf_op jit(solution)/shard_map/ppermute | solution.py:442
  167.7 35.3 %collective-permute-start.11 = (bf16[4,128,640]{2,1,0:T(8,128)(2,1)S(1)}, bf16[4,128,640]{2,1,0:T(8,128)(2,1)S(1)}, u32[]{:S(2)}, u32[]{:S(2)}) collective-permute-start(bf16[4,128,640]{2,1,0:T(8,128)(2,1)S(1)} %slice.89), channel_id=1, source_target_pairs={{0,16},{16,0},{1,17},{17,1},{2,18},{18,2},{3,19},{19,3},{4,20},{20... | collective-permute-start | bytes 1966088 | tf_op jit(solution)/shard_map/ppermute | solution.py:447
  210.5 24.6 %collective-permute-start.16 = (bf16[4,128,512]{2,1,0:T(8,128)(2,1)S(1)}, bf16[4,128,512]{2,1,0:T(8,128)(2,1)S(1)}, u32[]{:S(2)}, u32[]{:S(2)}) collective-permute-start(bf16[4,128,512]{2,1,0:T(8,128)(2,1)S(1)} %copy-done.24), channel_id=1, source_target_pairs={{0,16},{16,0},{1,17},{17,1},{2,18},{18,2},{3,19},{19,3},{4,20},{20... | collective-permute-start | bytes 1572872 | tf_op jit(solution)/shard_map/ppermute | solution.py:447
  235.1 27.6 %collective-permute-start.17 = (bf16[4,128,640]{2,1,0:T(8,128)(2,1)S(1)}, bf16[4,128,640]{2,1,0:T(8,128)(2,1)S(1)}, u32[]{:S(2)}, u32[]{:S(2)}) collective-permute-start(bf16[4,128,640]{2,1,0:T(8,128)(2,1)S(1)} %collective-permute-done.11.refs_10_), channel_id=1, source_target_pairs={{0,4},{4,0},{1,5},{5,1},{2,6},{6,2},{3,7},{7,3},{8,12},{12,8},{9,1... | collective-permute-start | bytes 1966088 | tf_op jit(solution)/shard_map/ppermute | solution.py:442
  236.8 25.9 %collective-permute-start.18 = (bf16[4,128,512]{2,1,0:T(8,128)(2,1)S(1)}, bf16[4,128,512]{2,1,0:T(8,128)(2,1)S(1)}, u32[]{:S(2)}, u32[]{:S(2)}) collective-permute-start(bf16[4,128,512]{2,1,0:T(8,128)(2,1)S(1)} %collective-permute-done.16.refs_12_), channel_id=1, source_target_pairs={{0,4},{4,0},{1,5},{5,1},{2,6},{6,2},{3,7},{7,3},{8,12},{12,8},{9,1... | collective-permute-start | bytes 1572872 | tf_op jit(solution)/shard_map/ppermute | solution.py:442
  309.5 49.8 %all-to-all-start.3 = ((bf16[4,128,2048]{2,1,0:T(8,128)(2,1)}), bf16[4,128,2048]{2,1,0:T(8,128)(2,1)}, u32[]{:S(2)}, u32[]{:S(2)}) async-start(bf16[4,128,2048]{2,1,0:T(8,128)(2,1)} %add_convert_fusion.2), calls=%async_computation.3 | async-start | bytes 4194304 | tf_op jit(solution)/shard_map/all_to_all | solution.py:467
  314.1 89.5 %all-gather.11.cloned.1.call-start = ((), (), s32[]{:S(2)}) async-start(), calls=%async_computation.12 | async-start | bytes 4718592 | tf_op jit(solution)/shard_map/all_gather | solution.py:534
  334.9 24.4 %collective-permute-start.22 = (bf16[4,256,384]{2,1,0:T(8,128)(2,1)S(1)}, bf16[4,256,384]{2,1,0:T(8,128)(2,1)}, u32[]{:S(2)}, u32[]{:S(2)}) collective-permute-start(bf16[4,256,384]{2,1,0:T(8,128)(2,1)S(1)} %copy-done.49), channel_id=1, source_target_pairs={{0,4},{4,0},{1,5},{5,1},{2,6},{6,2},{3,7},{7,3},{8,12},{12,8},{9,1... | collective-permute-start | bytes 2359304 | tf_op jit(solution)/shard_map/ppermute | solution.py:442
  339.3 19.9 %collective-permute-start.21 = (bf16[2,256,384]{2,1,0:T(8,128)(2,1)S(1)}, bf16[2,256,384]{2,1,0:T(8,128)(2,1)S(1)}, u32[]{:S(2)}, u32[]{:S(2)}) collective-permute-start(bf16[2,256,384]{2,1,0:T(8,128)(2,1)S(1)} %split.139), channel_id=1, source_target_pairs={{0,16},{16,0},{1,17},{17,1},{2,18},{18,2},{3,19},{19,3},{4,20},{20... | collective-permute-start | bytes 1179656 | tf_op jit(solution)/shard_map/ppermute | solution.py:447
  365.8 22.6 %collective-permute-start.23 = (bf16[2,256,384]{2,1,0:T(8,128)(2,1)S(1)}, bf16[2,256,384]{2,1,0:T(8,128)(2,1)S(1)}, u32[]{:S(2)}, u32[]{:S(2)}) collective-permute-start(bf16[2,256,384]{2,1,0:T(8,128)(2,1)S(1)} %split.138), channel_id=1, source_target_pairs={{0,16},{16,0},{1,17},{17,1},{2,18},{18,2},{3,19},{19,3},{4,20},{20... | collective-permute-start | bytes 1179656 | tf_op jit(solution)/shard_map/ppermute | solution.py:447
  365.9 30.1 %collective-permute-start.24 = (bf16[4,256,640]{2,1,0:T(8,128)(2,1)}, bf16[4,256,640]{2,1,0:T(8,128)(2,1)S(1)}, u32[]{:S(2)}, u32[]{:S(2)}) collective-permute-start(bf16[4,256,640]{2,1,0:T(8,128)(2,1)} %get-tuple-element.152), channel_id=1, source_target_pairs={{0,4},{4,0},{1,5},{5,1},{2,6},{6,2},{3,7},{7,3},{8,12},{12,8},{9,1... | collective-permute-start | bytes 3932168 | tf_op jit(solution)/shard_map/ppermute | solution.py:442
  403.6 44.6 %all-to-all-start.4 = ((bf16[4,128,2048]{2,1,0:T(8,128)(2,1)}), bf16[4,128,2048]{2,1,0:T(8,128)(2,1)}, u32[]{:S(2)}, u32[]{:S(2)}) async-start(bf16[4,128,2048]{2,1,0:T(8,128)(2,1)} %add_convert_fusion.1), calls=%async_computation.4 | async-start | bytes 4194304 | tf_op jit(solution)/shard_map/all_to_all | solution.py:467
  408.2 37.5 %collective-permute-start.26 = (bf16[2,256,640]{2,1,0:T(8,128)(2,1)}, bf16[2,256,640]{2,1,0:T(8,128)(2,1)}, u32[]{:S(2)}, u32[]{:S(2)}) collective-permute-start(bf16[2,256,640]{2,1,0:T(8,128)(2,1)} %split.136), channel_id=1, source_target_pairs={{0,16},{16,0},{1,17},{17,1},{2,18},{18,2},{3,19},{19,3},{4,20},{20... | collective-permute-start | bytes 1966088 | tf_op jit(solution)/shard_map/ppermute | solution.py:447
  410.9 36.6 %collective-permute-start.27 = (bf16[4,256,768]{2,1,0:T(8,128)(2,1)}, bf16[4,256,768]{2,1,0:T(8,128)(2,1)}, u32[]{:S(2)}, u32[]{:S(2)}) collective-permute-start(bf16[4,256,768]{2,1,0:T(8,128)(2,1)} %get-tuple-element.163), channel_id=1, source_target_pairs={{0,4},{4,0},{1,5},{5,1},{2,6},{6,2},{3,7},{7,3},{8,12},{12,8},{9,1... | collective-permute-start | bytes 4718600 | tf_op jit(solution)/shard_map/ppermute | solution.py:442
  463.0 47.5 %all-to-all-start.5 = ((bf16[4,128,2048]{2,1,0:T(8,128)(2,1)}), bf16[4,128,2048]{2,1,0:T(8,128)(2,1)}, u32[]{:S(2)}, u32[]{:S(2)}) async-start(bf16[4,128,2048]{2,1,0:T(8,128)(2,1)} %add_convert_fusion), calls=%async_computation.5 | async-start | bytes 4194304 | tf_op jit(solution)/shard_map/all_to_all | solution.py:467
  467.6 40.2 %collective-permute-start.30 = (bf16[2,256,768]{2,1,0:T(8,128)(2,1)}, bf16[2,256,768]{2,1,0:T(8,128)(2,1)}, u32[]{:S(2)}, u32[]{:S(2)}) collective-permute-start(bf16[2,256,768]{2,1,0:T(8,128)(2,1)} %split.135), channel_id=1, source_target_pairs={{0,16},{16,0},{1,17},{17,1},{2,18},{18,2},{3,19},{19,3},{4,20},{20... | collective-permute-start | bytes 2359304 | tf_op jit(solution)/shard_map/ppermute | solution.py:447
  522.6 37.1 %all-to-all-start.6 = ((bf16[4,128,1408]{1,2,0:T(8,128)(2,1)}), bf16[4,128,1408]{1,2,0:T(8,128)(2,1)}, u32[]{:S(2)}, u32[]{:S(2)}) async-start(bf16[4,128,1408]{1,2,0:T(8,128)(2,1)} %pad_maximum_fusion), calls=%async_computation.6 | async-start | bytes 2883584 | tf_op jit(solution)/shard_map/all_to_all | solution.py:467
  527.1 25.2 %collective-permute-start.32 = (bf16[4,256,512]{2,1,0:T(8,128)(2,1)}, bf16[4,256,512]{2,1,0:T(8,128)(2,1)}, u32[]{:S(2)}, u32[]{:S(2)}) collective-permute-start(bf16[4,256,512]{2,1,0:T(8,128)(2,1)} %grad_product.16), channel_id=1, source_target_pairs={{0,4},{4,0},{1,5},{5,1},{2,6},{6,2},{3,7},{7,3},{8,12},{12,8},{9,1... | collective-permute-start | bytes 3145736 | tf_op jit(solution)/shard_map/ppermute | solution.py:442
  533.9 25.8 %collective-permute-start.33 = (bf16[2,256,512]{2,1,0:T(8,128)(2,1)}, bf16[2,256,512]{2,1,0:T(8,128)(2,1)}, u32[]{:S(2)}, u32[]{:S(2)}) collective-permute-start(bf16[2,256,512]{2,1,0:T(8,128)(2,1)} %pad_maximum_fusion.3), channel_id=1, source_target_pairs={{0,16},{16,0},{1,17},{17,1},{2,18},{18,2},{3,19},{19,3},{4,20},{20... | collective-permute-start | bytes 1572872 | tf_op jit(solution)/shard_map/ppermute | solution.py:447
  538.2 40.0 %collective-permute-start.35 = (f32[49,128]{1,0:T(8,128)}, f32[49,128]{1,0:T(8,128)}, u32[]{:S(2)}, u32[]{:S(2)}) collective-permute-start(f32[49,128]{1,0:T(8,128)} %maximum_bitcast_fusion), channel_id=1, source_target_pairs={{0,2},{2,0},{1,3},{3,1},{4,6},{6,4},{5,7},{7,5},{8,10},{10,8},{9,1... | collective-permute-start | bytes 75272 | tf_op jit(solution)/shard_map/ppermute | solution.py:442
  573.5 50.5 %all-to-all-start.7 = ((bf16[4,128,1280]{1,2,0:T(8,128)(2,1)}), bf16[4,128,1280]{1,2,0:T(8,128)(2,1)}, u32[]{:S(2)}, u32[]{:S(2)}) async-start(bf16[4,128,1280]{1,2,0:T(8,128)(2,1)} %pad_maximum_fusion.1), calls=%async_computation.7 | async-start | bytes 2621440 | tf_op jit(solution)/shard_map/all_to_all | solution.py:467
  596.4 27.5 %collective-permute-start.34 = (bf16[2,256,512]{2,1,0:T(8,128)(2,1)S(1)}, bf16[2,256,512]{2,1,0:T(8,128)(2,1)}, u32[]{:S(2)}, u32[]{:S(2)}) collective-permute-start(bf16[2,256,512]{2,1,0:T(8,128)(2,1)S(1)} %copy-done.23), channel_id=1, source_target_pairs={{0,16},{16,0},{1,17},{17,1},{2,18},{18,2},{3,19},{19,3},{4,20},{20... | collective-permute-start | bytes 1572872 | tf_op jit(solution)/shard_map/ppermute | solution.py:447
  (83 other events, 991.8 us)
Sparse Core Ops, SparseCore 0:
  76.7 43.8 all-gather.4
  124.3 40.8 all-gather.8
  210.1 38.3 all-gather.6
  363.0 35.4 all-gather.10

commit v3 on v2

v3 whole, which is shorter than its diff:
```python
import functools

import jax
import jax.numpy as jnp
from jax import lax
from jax.experimental import pallas as pl
from jax.experimental.pallas import tpu as pltpu
from jax.sharding import Mesh, PartitionSpec as P

HEAD = 128
STRIP = 32
CAP = 50.0
BF = jnp.bfloat16
epsilon = 1e-06
PARAMS = pltpu.CompilerParams(vmem_limit_bytes=56 * 1024 * 1024)


LONG, SHORT = [pl.CostEstimate(flops=f, bytes_accessed=1, transcendentals=0) for f in (5 * 10**10, 1)]


NN, NT, TN = ((1,), (0,)), ((1,), (1,)), ((0,), (0,))


def dot(a, b, dims=NN):
    return lax.dot_general(a, b, (dims, ((), ())), preferred_element_type=jnp.float32)


def exact_dot(ones, values):
    high = values.astype(BF)
    rest = values - high.astype(jnp.float32)
    mid = rest.astype(BF)
    tail = (rest - mid.astype(jnp.float32)).astype(BF)
    return dot(ones, high) + dot(ones, mid) + dot(ones, tail)


def gates(p0, p1, floor):
    swish = jax.nn.sigmoid(p0)
    gate = jax.nn.sigmoid(p1)
    return swish, gate, floor + (1.0 - floor) * gate


def masks(seg_col, seg_row):
    length = seg_col.shape[0]
    row = lax.broadcasted_iota(jnp.int32, (length, length), 0)
    col = lax.broadcasted_iota(jnp.int32, (length, length), 1)
    return seg_col == seg_row, row, col


def strips(length):
    return [(s, -(-(s + STRIP) // 128) * 128) for s in range(0, length, STRIP)]


def fill_scores(query, key, totals, allowed, scores):
    length = query.shape[0]
    for start, wide in strips(length):
        rows = slice(start, start + STRIP)
        ref = totals[start + STRIP // 2 - 1 : start + STRIP // 2]
        lead = (query[rows] * jnp.exp(totals[rows] - ref)).astype(BF)
        trail = (key[:wide] * jnp.exp(jnp.minimum(ref - totals[:wide], CAP))).astype(BF)
        part = jnp.where(allowed[rows, :wide], dot(lead, trail, NT), 0.0)
        scores[rows, :wide] = part.astype(BF)
        if wide < length:
            scores[rows, wide:] = jnp.zeros((STRIP, length - wide), BF)


def head_forward(p0, p1, p2, seg_col, seg_row, floor, gain, scores):
    swish, gate, forget = gates(p0, p1, floor)
    same, row, col = masks(seg_col, seg_row)
    totals = exact_dot((col <= row).astype(BF), jnp.log(forget))
    fill_scores(p0 * swish, 1.0 - forget, totals, same & (col <= row), scores)
    rec = dot(scores[...], p2.astype(BF))
    rms = lax.rsqrt(jnp.mean(rec * rec, axis=-1, keepdims=True) + epsilon)
    return (rec * rms * gain).astype(BF)


def head_backward(
    p0, p1, p2, mixed_grad, seg_col, seg_row, floor, gain, scores, key_grad, decay_grad, query_grad
):
    length = p0.shape[0]
    swish, gate, forget = gates(p0, p1, floor)
    query = p0 * swish
    key = 1.0 - forget
    same, row, col = masks(seg_col, seg_row)
    allowed = same & (col <= row)
    totals = exact_dot((col <= row).astype(BF), jnp.log(forget))
    fill_scores(query, key, totals, allowed, scores)
    value = p2.astype(BF)
    rec = dot(scores[...], value)
    rms = lax.rsqrt(jnp.mean(rec * rec, axis=-1, keepdims=True) + epsilon)
    unit = rec * rms
    scaled = mixed_grad * gain
    rec_grad = rms * (scaled - unit * jnp.mean(scaled * unit, axis=-1, keepdims=True))
    rec_low = rec_grad.astype(BF)
    value_grad = dot(scores[...], rec_low, TN).astype(BF)
    score_grad = jnp.where(allowed, dot(rec_low, value, NT), 0.0).astype(BF)
    key_grad[...] = jnp.zeros_like(key_grad)
    decay_grad[...] = jnp.zeros_like(decay_grad)
    for start, wide in strips(length):
        rows = slice(start, start + STRIP)
        ref = totals[start + STRIP // 2 - 1 : start + STRIP // 2]
        lead_scale = jnp.exp(totals[rows] - ref)
        trail_scale = jnp.exp(jnp.minimum(ref - totals[:wide], CAP))
        lead = (query[rows] * lead_scale).astype(BF)
        trail = (key[:wide] * trail_scale).astype(BF)
        part = score_grad[rows, :wide]
        lead_grad = dot(part, trail)
        trail_grad = dot(part, lead, TN)
        query_grad[rows, :] = lead_grad * lead_scale
        key_grad[:wide, :] += trail_grad * trail_scale
        decay_grad[:wide, :] -= trail_grad * trail.astype(jnp.float32)
        decay_grad[rows, :] += lead_grad * lead.astype(jnp.float32)
    before = jnp.concatenate([seg_col[:1] - 1, seg_col[:-1]], axis=0)
    carry = (seg_col == before).astype(jnp.float32)
    later = (same & (col >= row)).astype(BF)
    forget_grad = exact_dot(later, decay_grad[...]) * carry / forget
    joint = forget_grad - key_grad[...]
    floor_sum = jnp.sum(joint * (1.0 - gate), axis=0, keepdims=True)
    gain_sum = jnp.sum(mixed_grad * unit, axis=0, keepdims=True)
    g0 = (query_grad[...] * swish * (1.0 + p0 * (1.0 - swish))).astype(BF)
    g1 = (joint * (1.0 - floor) * gate * (1.0 - gate)).astype(BF)
    return g0, g1, value_grad, floor_sum, gain_sum


def load_weight(offsets_ref, sources, refs, whole, sems, begin=0):
    end = begin + whole.shape[1]
    copies = []
    for (piece, low), ref in zip(sources, refs):
        rows, lanes = ref.shape[1:]
        first, last = max(low, begin), min(low + lanes, end)
        if first >= last:
            continue
        for m in range(4):
            at = pl.multiple_of(offsets_ref[4 * piece + m], rows)
            copies.append(
                pltpu.make_async_copy(
                    ref.at[m, :, pl.ds(first - low, last - first)],
                    whole.at[pl.ds(at, rows), pl.ds(first - begin, last - first)],
                    sems.at[len(copies)],
                )
            )
    for copy in copies:
        copy.start()
    for copy in copies:
        copy.wait()


def row_copies(core, refs, whole, sems):
    count = refs[0].shape[0]
    for side in range(2):
        at = pl.multiple_of((core if side == 0 else 1 - core) * count, count)
        for m in range(4):
            ref = refs[m] if side == 0 else refs[4].at[m] if m < 3 else refs[5]
            yield m, pltpu.make_async_copy(
                ref, whole.at[m, pl.ds(at, count), :], sems.at[side, m]
            )


def start_rows(core, refs, whole, sems):
    for _, copy in row_copies(core, refs, whole, sems):
        copy.start()


def wait_rows(core, refs, whole, sems, sequence):
    for m, copy in row_copies(core, refs, whole, sems):

        @pl.when(sequence == m)
        def _():
            copy.wait()


def row_scratch(count, model):
    return [pltpu.VMEM((4, 2 * count, model), BF), pltpu.SemaphoreType.DMA((2, 4))]


def mixer_forward_kernel(core_ref, offsets_ref, *refs, sources):
    rows, refs = refs[:6], refs[6:]
    (col_ref, row_ref, floor_ref, gain_ref, p_ref, mixed_ref, send_ref, keep_ref, scores, whole,
     back, tokens, token_sems, weight, sems) = refs[len(sources) :]

    sequence = pl.program_id(0)

    @pl.when(sequence == 0)
    def _():
        start_rows(core_ref[0], rows, tokens, token_sems)
        load_weight(offsets_ref, sources, refs, weight, sems)

    wait_rows(core_ref[0], rows, tokens, token_sems, sequence)

    count = rows[0].shape[0]
    width = whole.shape[1]
    mine = pl.multiple_of(core_ref[0] * count, count)
    theirs = pl.multiple_of((1 - core_ref[0]) * count, count)
    p_ref[0] = dot(tokens[sequence], weight[:, : 3 * width])
    for h in range(width // HEAD):
        p0, p1, p2 = [p_ref[0, :, pl.ds(j * width + h * HEAD, HEAD)] for j in range(3)]
        lanes = slice(h * HEAD, (h + 1) * HEAD)
        whole[:, lanes] = head_forward(
            p0, p1, p2, col_ref[0], row_ref[0], floor_ref[:, lanes], gain_ref[...], scores.at[h]
        )
    mixed_ref[0] = whole[...]
    back[...] = dot(whole[...], weight[:, 3 * width :], NT)
    send_ref[0] = back[pl.ds(theirs, count), :].astype(BF)
    keep_ref[0] = back[pl.ds(mine, count), :]


def mixer_backward_kernel(core_ref, offsets_ref, *refs, sources):
    rows, refs = refs[:6], refs[6:]
    (p_ref, col_ref, row_ref, floor_ref, gain_ref, g_one_ref, g_two_ref, send_ref, keep_ref,
     floor_sum_ref, gain_sum_ref, scores, key_grad, decay_grad, query_grad, mixed_grad, parts,
     back, tokens, token_sems, weight, sems) = refs[len(sources) :]

    sequence = pl.program_id(0)

    @pl.when(sequence == 0)
    def _():
        start_rows(core_ref[0], rows, tokens, token_sems)
        load_weight(offsets_ref, sources, refs, weight, sems)

    wait_rows(core_ref[0], rows, tokens, token_sems, sequence)

    count = rows[0].shape[0]
    width = mixed_grad.shape[1]
    mine = pl.multiple_of(core_ref[0] * count, count)
    theirs = pl.multiple_of((1 - core_ref[0]) * count, count)
    mixed_grad[...] = dot(tokens[sequence], weight[:, 3 * width :])
    for h in range(width // HEAD):
        p0, p1, p2 = [p_ref[0, :, pl.ds(j * width + h * HEAD, HEAD)] for j in range(3)]
        lanes = slice(h * HEAD, (h + 1) * HEAD)
        g0, g1, g2, floor_sum, gain_sum = head_backward(
            p0, p1, p2, mixed_grad[:, lanes], col_ref[0], row_ref[0], floor_ref[:, lanes],
            gain_ref[...], scores.at[h], key_grad.at[h], decay_grad.at[h], query_grad.at[h],
        )
        for j, g in enumerate((g0, g1, g2)):
            parts[:, pl.ds(j * width + h * HEAD, HEAD)] = g
        floor_sum_ref[0, :, lanes] = jnp.broadcast_to(floor_sum, (8, HEAD)) * 0.125
        gain_sum_ref[0, :, lanes] = jnp.broadcast_to(gain_sum, (8, HEAD)) * 0.125

    g_one_ref[0] = parts[:, : 2 * width]
    g_two_ref[0] = parts[:, 2 * width :]
    back[...] = dot(parts[...], weight[:, : 3 * width], NT)
    send_ref[0] = back[pl.ds(theirs, count), :].astype(BF)
    keep_ref[0] = back[pl.ds(mine, count), :]


def mixer_specs(count, model, width, length):
    def at(shape, index):
        return pl.BlockSpec(shape, lambda s, c, o: index(s))

    side = at((1, count, model), lambda s: (s, 0, 0))
    col = at((1, length, 1), lambda s: (s, 0, 0))
    row = at((1, 1, length), lambda s: (s, 0, 0))
    floor = at((1, width), lambda s: (0, 0))
    gain = at((1, HEAD), lambda s: (0, 0))
    wide = at((1, length, 3 * width), lambda s: (s, 0, 0))
    pairs = [at((1, length, k * width), lambda s: (s, 0, 0)) for k in (1, 2)]
    return at, side, wide, pairs, [col, row, floor, gain]


def weight_scratch(model, lanes, sources):
    return [pltpu.VMEM((model, lanes), BF), pltpu.SemaphoreType.DMA((4 * len(sources),))]


def layout_of(sources):
    return tuple((piece, low) for piece, low, _ in sources), [part for _, _, part in sources]


def mixer_forward(core, offsets, tokens, sources, segments, floor, gain):
    groups, length = segments.shape
    count, model = tokens[0].shape
    width = floor.shape[0]
    half = (groups, count, model)
    at, side, wide, pairs, small = mixer_specs(count, model, width, length)
    layout, parts = layout_of(sources)
    shape = jax.ShapeDtypeStruct
    return pl.pallas_call(
        functools.partial(mixer_forward_kernel, sources=layout),
        grid_spec=pltpu.PrefetchScalarGridSpec(
            num_scalar_prefetch=2,
            grid=(groups,),
            in_specs=[pl.BlockSpec(memory_space=pl.ANY)] * (6 + len(parts)) + small,
            out_specs=[wide, pairs[0], side, side],
            scratch_shapes=[
                pltpu.VMEM((width // HEAD, length, length), BF),
                pltpu.VMEM((length, width), BF),
                pltpu.VMEM((length, model), jnp.float32),
            ]
            + row_scratch(count, model)
            + weight_scratch(model, 4 * width, parts),
        ),
        out_shape=[
            shape((groups, length, 3 * width), jnp.float32),
            shape((groups, length, width), BF),
            shape(half, BF),
            shape(half, jnp.float32),
        ],
        compiler_params=PARAMS,
        cost_estimate=LONG,
        name="mixer_forward",
    )(
        core, offsets, *tokens, *parts, segments[:, :, None],
        segments[:, None, :], floor[None], gain[None],
    )


def mixer_backward(core, offsets, tokens, sources, projected, segments, floor, gain):
    groups, length = segments.shape
    count, model = tokens[0].shape
    width = floor.shape[0]
    half = (groups, count, model)
    at, side, wide, pairs, small = mixer_specs(count, model, width, length)
    layout, parts = layout_of(sources)
    heads = width // HEAD
    sums = at((1, 8, width), lambda s: (s, 0, 0))
    shape = jax.ShapeDtypeStruct
    return pl.pallas_call(
        functools.partial(mixer_backward_kernel, sources=layout),
        grid_spec=pltpu.PrefetchScalarGridSpec(
            num_scalar_prefetch=2,
            grid=(groups,),
            in_specs=[pl.BlockSpec(memory_space=pl.ANY)] * (6 + len(parts))
            + [wide]
            + small,
            out_specs=[pairs[1], pairs[0], side, side, sums, sums],
            scratch_shapes=[pltpu.VMEM((heads, length, length), BF)]
            + [pltpu.VMEM((heads, length, HEAD), jnp.float32)] * 3
            + [pltpu.VMEM((length, width), jnp.float32), pltpu.VMEM((length, 3 * width), BF)]
            + [pltpu.VMEM((length, model), jnp.float32)]
            + row_scratch(count, model)
            + weight_scratch(model, 4 * width, parts),
        ),
        out_shape=[
            shape((groups, length, 2 * width), BF),
            shape((groups, length, width), BF),
            shape(half, BF),
            shape(half, jnp.float32),
        ]
        + [shape((groups, 8, width), jnp.float32)] * 2,
        compiler_params=PARAMS,
        cost_estimate=LONG,
        name="mixer_backward",
    )(
        core, offsets, *tokens, *parts, projected, segments[:, :, None],
        segments[:, None, :], floor[None], gain[None],
    )


def ffn_kernel(core_ref, offsets_ref, *refs, sources, units):
    rows, tops, refs = refs[:6], refs[6:12], refs[12:]
    (*parts, send_ref, keep_ref, grads, back,
     tokens, token_sems, top_tokens, top_sems, weight, sems) = refs[len(sources) :]

    sequence = pl.program_id(0)

    @pl.when(sequence == 0)
    def _():
        start_rows(core_ref[0], rows, tokens, token_sems)
        start_rows(core_ref[0], tops, top_tokens, top_sems)
        load_weight(offsets_ref, sources, refs, weight, sems)

    wait_rows(core_ref[0], rows, tokens, token_sems, sequence)
    wait_rows(core_ref[0], tops, top_tokens, top_sems, sequence)

    width = units
    count = rows[0].shape[0]
    mine = pl.multiple_of(core_ref[0] * count, count)
    theirs = pl.multiple_of((1 - core_ref[0]) * count, count)
    both = dot(tokens[sequence], weight[:, : 2 * width])
    gate, up = both[:, :width], both[:, width:]
    active_grad = dot(top_tokens[sequence], weight[:, 2 * width : 3 * width])
    squash = jax.nn.sigmoid(gate)
    swish = gate * squash
    gate_grad = active_grad * up * squash * (1.0 + gate * (1.0 - squash))
    grads[:, : 2 * width] = jnp.concatenate([gate_grad, active_grad * swish], axis=1).astype(BF)
    spare = jnp.zeros((2 * count, grads.shape[1] - 3 * width), BF)
    grads[:, 2 * width :] = jnp.concatenate([(swish * up).astype(BF), spare], axis=1)
    low = 0
    for part_ref in parts:
        part_ref[0] = grads[:, low : low + part_ref.shape[2]]
        low += part_ref.shape[2]
    back[...] = dot(grads[:, : 2 * width], weight[:, : 2 * width], NT)
    send_ref[0] = back[pl.ds(theirs, count), :].astype(BF)
    keep_ref[0] = back[pl.ds(mine, count), :]


def ffn(core, offsets, tokens, tops, sources, width, widths):
    count, model = tokens[0].shape
    groups, length = 4, 2 * count
    total = sum(widths)
    layout, parts = layout_of(sources)

    def at(rows, lanes):
        return pl.BlockSpec((1, rows, lanes), lambda s, c, o: (s, 0, 0))

    shape = jax.ShapeDtypeStruct
    return pl.pallas_call(
        functools.partial(ffn_kernel, sources=layout, units=width),
        grid_spec=pltpu.PrefetchScalarGridSpec(
            num_scalar_prefetch=2,
            grid=(groups,),
            in_specs=[pl.BlockSpec(memory_space=pl.ANY)] * (12 + len(parts)),
            out_specs=[at(length, n) for n in widths] + [at(length // 2, model)] * 2,
            scratch_shapes=[
                pltpu.VMEM((length, total), BF),
                pltpu.VMEM((length, model), jnp.float32),
            ]
            + row_scratch(count, model) * 2
            + weight_scratch(model, total, parts),
        ),
        out_shape=[
            *[shape((groups, length, n), BF) for n in widths],
            shape((groups, length // 2, model), BF),
            shape((groups, length // 2, model), jnp.float32),
        ],
        compiler_params=PARAMS,
        cost_estimate=LONG,
        name="ffn",
    )(core, offsets, *tokens, *tops, *parts)


def rows_kernel(core_ref, offsets_ref, *refs, sources, begin, number):
    own, refs = refs[:number], refs[number:]
    out_ref, whole, sems = refs[len(sources) :]

    @pl.when(pl.program_id(0) == 0)
    def _():
        load_weight(offsets_ref, sources, refs, whole, sems, begin)

    out_ref[0] = dot(jnp.concatenate([r[0] for r in own], axis=1), whole[...], NT).astype(BF)


def rows_product(core, offsets, own, sources, begin, model, estimate=SHORT):
    groups, length, _ = own[0].shape
    width = sum(o.shape[2] for o in own)
    layout, parts = layout_of(sources)

    def at(rows, lanes):
        return pl.BlockSpec((1, rows, lanes), lambda s, c, o: (s, 0, 0))

    shape = jax.ShapeDtypeStruct
    return pl.pallas_call(
        functools.partial(rows_kernel, sources=layout, begin=begin, number=len(own)),
        grid_spec=pltpu.PrefetchScalarGridSpec(
            num_scalar_prefetch=2,
            grid=(groups,),
            in_specs=[at(length, o.shape[2]) for o in own] + [pl.BlockSpec(memory_space=pl.ANY)] * len(parts),
            out_specs=pl.BlockSpec((1, length, model), lambda s, c, o: (s ^ c[1], 0, 0)),
            scratch_shapes=weight_scratch(model, width, parts),
        ),
        out_shape=shape((groups, length, model), BF),
        compiler_params=PARAMS,
        cost_estimate=estimate,
        name="rows_product",
    )(core, offsets, *own, *parts)


def grad_kernel(core_ref, blocks_ref, *refs, number):
    rows, grads, outs, tokens = refs[:6], refs[6 : 6 + number], refs[6 + number : -1], refs[-1]
    count = rows[0].shape[0]
    for side in range(2):
        at = core_ref[0] if side == 0 else 1 - core_ref[0]
        for m in range(4):
            first = pl.multiple_of((2 * m + at) * count, count)
            part = rows[m][...] if side == 0 else rows[4][m] if m < 3 else rows[5][...]
            tokens[pl.ds(first, count), :] = part
    for grad_ref, out_ref in zip(grads, outs):
        out_ref[0] = dot(tokens[...], grad_ref[...], TN).astype(out_ref.dtype)


def grad_product(core, tokens, grads, blocks, wide, kind, estimate):
    count, model = tokens[0].shape
    side = pl.BlockSpec((count, wide), lambda i, c, b: (0, b[i]))
    three = pl.BlockSpec((3, count, wide), lambda i, c, b: (0, 0, b[i]))
    number = blocks.shape[0]
    return pl.pallas_call(
        functools.partial(grad_kernel, number=len(grads)),
        grid_spec=pltpu.PrefetchScalarGridSpec(
            num_scalar_prefetch=2,
            grid=(number,),
            in_specs=[side] * 4
            + [three, side]
            + [pl.BlockSpec(g.shape, lambda i, c, b: (0, 0)) for g in grads],
            out_specs=[pl.BlockSpec((1, wide, g.shape[1]), lambda i, c, b: (i, 0, 0)) for g in grads],
            scratch_shapes=[pltpu.VMEM((8 * count, wide), BF)],
        ),
        out_shape=[jax.ShapeDtypeStruct((number, wide, g.shape[1]), kind) for g in grads],
        compiler_params=PARAMS,
        cost_estimate=estimate,
        name="grad_product",
    )(core, blocks, *tokens, *grads)


def rms_of(values):
    return lax.rsqrt(jnp.mean(values * values, axis=-1, keepdims=True) + epsilon)


def cores_kernel(keep_ref, came_ref, own_ref, x_ref, z_ref, xz_ref):
    own_ref[...] = keep_ref[0] + came_ref[0].astype(jnp.float32)
    for m, out_ref in enumerate((x_ref, z_ref, xz_ref), 1):
        out_ref[...] = (keep_ref[m] + came_ref[m].astype(jnp.float32)).astype(BF)


def add_cores(keep, came, estimate=SHORT):
    count, model = keep.shape[1:]
    block = count // 4
    both = pl.BlockSpec((4, block, model), lambda i: (0, i, 0))
    one = pl.BlockSpec((block, model), lambda i: (i, 0))
    shape = jax.ShapeDtypeStruct
    return pl.pallas_call(
        cores_kernel,
        grid=(4,),
        in_specs=[both, both],
        out_specs=[one] * 4,
        out_shape=[shape((count, model), jnp.float32)] + [shape((count, model), BF)] * 3,
        compiler_params=PARAMS,
        cost_estimate=estimate,
        name="add_cores",
    )(keep, came)


def middle_kernel(own_ref, x_ref, z_ref, hidden_ref, gain_ref, middle_ref, normed_ref):
    branch = own_ref[...] + x_ref[...].astype(jnp.float32) + z_ref[...].astype(jnp.float32)
    middle = hidden_ref[...].astype(jnp.float32) + branch
    middle_ref[...] = middle
    normed_ref[...] = (middle * rms_of(middle) * gain_ref[...]).astype(BF)


def back_kernel(own_ref, x_ref, z_ref, values_ref, add_ref, gain_ref, out_ref, low_ref, sum_ref):
    grad = own_ref[...] + x_ref[...].astype(jnp.float32) + z_ref[...].astype(jnp.float32)
    values = values_ref[...].astype(jnp.float32)
    scale = rms_of(values)
    unit = values * scale
    wide = grad * gain_ref[...]
    inner = wide - unit * jnp.mean(wide * unit, axis=-1, keepdims=True)
    out = add_ref[...].astype(jnp.float32) + scale * inner
    out_ref[...] = out
    low_ref[...] = out.astype(BF)

    @pl.when(pl.program_id(0) == 0)
    def _():
        sum_ref[...] = jnp.zeros_like(sum_ref)

    sum_ref[...] += jnp.sum(grad * unit, axis=0, keepdims=True)


def row_call(kernel, name, kinds, *args):
    count, model = args[0].shape
    block = count // 4

    def spec(one):
        if one:
            return pl.BlockSpec((1, model), lambda i: (0, 0))
        return pl.BlockSpec((block, model), lambda i: (i, 0))

    shapes = [jax.ShapeDtypeStruct((1 if k is None else count, model), k or jnp.float32) for k in kinds]
    return pl.pallas_call(
        kernel,
        grid=(4,),
        in_specs=[spec(a.shape[0] == 1) for a in args],
        out_specs=[spec(k is None) for k in kinds],
        out_shape=shapes,
        compiler_params=PARAMS,
        cost_estimate=LONG,
        name=name,
    )(*args)


def mix_grad_kernel(parts_ref, out_ref):
    quarter = parts_ref.shape[2] // 4
    for j, at in enumerate((2, 3, 0, 1)):
        for m in range(4):
            part = parts_ref[m, :, at * quarter : (at + 1) * quarter]
            out_ref[:, j, m * quarter : (m + 1) * quarter] = part.astype(jnp.float32)


def mix_grad_of(parts):
    _, rows, wide = parts.shape
    block = min(rows, 32)
    return pl.pallas_call(
        mix_grad_kernel,
        grid=(rows // block,),
        in_specs=[pl.BlockSpec((4, block, wide), lambda i: (0, i, 0))],
        out_specs=pl.BlockSpec((block, 4, wide), lambda i: (i, 0, 0)),
        out_shape=jax.ShapeDtypeStruct((rows, 4, wide), jnp.float32),
        compiler_params=PARAMS,
        cost_estimate=SHORT,
        name="mix_grad",
    )(parts)


DOWN_FIRST = 384


def ffn_grad_kernel(first_ref, second_ref, out_ref):
    units = out_ref.shape[2] // 4
    for j in range(3):
        parts = []
        for m in range(4):
            down = first_ref.shape[2] - DOWN_FIRST
            gates = jnp.concatenate([first_ref[m, :, down:], second_ref[m]], axis=1)
            parts.append(first_ref[m, :, :units] if j == 2 else gates[:, j * units : (j + 1) * units])
        out_ref[j] = jnp.concatenate(parts, axis=1).astype(jnp.float32)


def ffn_grad_of(parts, units):
    rows = parts[0].shape[1]
    block = min(rows, 32)
    out = pl.pallas_call(
        ffn_grad_kernel,
        grid=(rows // block,),
        in_specs=[pl.BlockSpec((4, block, p.shape[2]), lambda i: (0, i, 0)) for p in parts],
        out_specs=pl.BlockSpec((3, block, 4 * units), lambda i: (0, i, 0)),
        out_shape=jax.ShapeDtypeStruct((3, rows, 4 * units), jnp.float32),
        compiler_params=PARAMS,
        cost_estimate=LONG,
        name="ffn_grad",
    )(*parts)
    return out.transpose(1, 0, 2)


def near_kernel(*refs, number, ends):
    home_ref, away_ref = refs[2 * number :]
    block = pl.program_id(0)
    last = pl.num_programs(0) // ends
    for k in range(number):
        keep_ref, came_ref = refs[2 * k], refs[2 * k + 1]
        low = sum(refs[2 * j].shape[2] for j in range(k))
        total = keep_ref[0] + came_ref[0].astype(jnp.float32)
        lanes = slice(low, low + keep_ref.shape[2])

        @pl.when(block < pl.num_programs(0) - last)
        def _():
            away_ref[0, :, lanes] = total.astype(BF)

        @pl.when(block >= pl.num_programs(0) - last)
        def _():
            home_ref[0, :, lanes] = total


def near_sums(pairs, estimate=SHORT):
    highs = lax.axis_size("h")
    blocks, rows, _ = pairs[0][0].shape
    away_count = blocks - 2
    wide = sum(keep.shape[2] for keep, _ in pairs)
    specs, args = [], []
    for pair in pairs:
        specs += [pl.BlockSpec((1,) + pair[0].shape[1:], lambda i: (i, 0, 0))] * 2
        args += list(pair)
    home, away = pl.pallas_call(
        functools.partial(near_kernel, number=len(pairs), ends=highs),
        grid=(blocks,),
        in_specs=specs,
        out_specs=[
            pl.BlockSpec((1, rows, wide), lambda i: (jnp.maximum(i - away_count, 0), 0, 0)),
            pl.BlockSpec((1, rows, wide), lambda i: (jnp.minimum(i, away_count - 1), 0, 0)),
        ],
        out_shape=[
            jax.ShapeDtypeStruct((2, rows, wide), jnp.float32),
            jax.ShapeDtypeStruct((away_count, rows, wide), BF),
        ],
        compiler_params=PARAMS,
        cost_estimate=estimate,
        name="near_sums",
    )(*args)
    return home, [away[2 * k : 2 * k + 2] for k in range(highs - 1)]


def far_kernel(*refs, counts):
    out_ref = refs[-1]
    low, at = 0, 0
    for count in counts:
        total = refs[at][0]
        for ref in refs[at + 1 : at + 1 + count]:
            total = total + ref[0].astype(jnp.float32)
        out_ref[0, :, low : low + total.shape[1]] = total.astype(BF)
        low, at = low + total.shape[1], at + 1 + count


def far_sums(pairs, estimate=SHORT):
    _, rows, _ = pairs[0][0].shape
    wide = sum(home.shape[2] for home, _ in pairs)
    args = [part for home, fars in pairs for part in (home, *fars)]
    out = pl.pallas_call(
        functools.partial(far_kernel, counts=[len(fars) for _, fars in pairs]),
        grid=(2,),
        in_specs=[pl.BlockSpec((1,) + a.shape[1:], lambda i: (i, 0, 0)) for a in args],
        out_specs=pl.BlockSpec((1, rows, wide), lambda i: (i, 0, 0)),
        out_shape=jax.ShapeDtypeStruct((2, rows, wide), BF),
        compiler_params=PARAMS,
        cost_estimate=estimate,
        name="far_sums",
    )(*args)
    return out.reshape(4, rows // 2, wide)


GROUP = ("l", "x")


def swap(values, axes):
    total = 2 ** len(axes)
    return lax.ppermute(values, axes, [(s, total - 1 - s) for s in range(total)])


def shift(values, steps):
    total = lax.axis_size("h")
    return lax.ppermute(values, "h", [(s, (s + steps) % total) for s in range(total)])


def pick(values, index):
    return lax.dynamic_index_in_dim(values, index, 0, keepdims=False)


def over_c(values):
    return swap(values, ("tensor",))


def over_x(values):
    return swap(values, ("x",))


def over_y(values):
    return swap(values, ("y",))


def over_z(values):
    return swap(values, ("l",))


def own_member():
    return lax.axis_index("l") * 2 + lax.axis_index("x")


def source_rows(rows):
    y, high = lax.axis_index("y"), lax.axis_index("h")
    highs = lax.axis_size("h")
    starts = []
    for k in range(highs):
        for side in (y, 1 - y):
            for member in range(4):
                block = ((high - k) % highs) * 8 + (member >> 1) * 4 + side * 2 + (member & 1)
                starts.append(block * rows)
    return jnp.stack(starts).astype(jnp.int32)


def trade(slices):
    return lax.all_to_all(slices, GROUP, 0, 0, tiled=True)


def after(values, *others):
    return lax.optimization_barrier((values, others))[0]


def far(block):
    return [shift(block, k) for k in range(1, lax.axis_size("h"))]


def near(parts):
    return [over_y(part) for part in parts]


def pieces(low, straight, crossed):
    out = []
    for k, (one, two) in enumerate(zip(straight, crossed), 1):
        out += [(2 * k, low, one), (2 * k + 1, low, two)]
    return out


def half_grads(core, tokens, grads, yy, kind, estimate):
    highs, high = lax.axis_size("h"), lax.axis_index("h")
    wide = tokens[0].shape[1] // (4 * highs)
    order = [(high + k) % highs for k in range(1, highs)] + [high]
    blocks = jnp.stack([(h * 2 + z) * 2 + yy for h in order for z in range(2)]).astype(jnp.int32)
    grads = [flat(g) for g in grads]
    if wide % 128 == 0:
        return grad_product(core, tokens, grads, blocks, wide, kind, estimate)
    sides = [jnp.stack(tokens[:4]), jnp.concatenate([tokens[4], tokens[5][None]])]
    ordered = [jnp.where(core[0] == 0, a, b) for a, b in (sides, sides[::-1])]
    whole = jnp.stack(ordered, axis=1)
    split = jnp.take(whole.reshape(grads[0].shape[0], -1, wide), blocks, axis=1)
    return [
        jnp.einsum("tad,tx->adx", split, g, preferred_element_type=jnp.float32).astype(kind)
        for g in grads
    ]


def grad_sends(core, tokens, grads, estimate=SHORT):
    return half_grads(core, tokens, grads, 1 - lax.axis_index("y"), BF, estimate)


def grad_keeps(core, tokens, grads, estimate=SHORT):
    return half_grads(core, tokens, grads, lax.axis_index("y"), jnp.float32, estimate)


def send_far(away):
    return [shift(part, k) for k, part in enumerate(away, 1)]


def flat(values):
    return values.reshape(-1, values.shape[-1])


def add_low(keep, came):
    return (keep.astype(jnp.float32) + came.astype(jnp.float32)).astype(BF)


def sum_highs(values):
    size, bits = lax.axis_size("h"), 1
    while bits < size:
        values = values + lax.ppermute(values, "h", [(s, s ^ bits) for s in range(size)])
        bits *= 2
    return values


def body(
    hidden_in,
    segments,
    mix_weights,
    ffn_weights,
    norm1_gain,
    norm2_gain,
    head_gain,
    lower_bound,
    out_grad,
):
    core, member = lax.axis_index("tensor"), own_member()
    core_at = jnp.stack([core, member]).astype(jnp.int32)
    rows = mix_weights.shape[0]
    offsets = source_rows(rows)
    quarter, units = lower_bound.shape[0] // 4, ffn_weights.shape[2] // 4
    model = hidden_in.shape[1]
    channels = 4 * quarter
    lanes = -(-3 * units // 128) * 128

    def slices(weights, width):
        split = weights.reshape(rows, weights.shape[1], 4, -1).transpose(2, 0, 1, 3)
        split = split.reshape(4, rows, -1)
        return jnp.pad(split, ((0, 0), (0, 0), (0, width - split.shape[2])))

    length = segments.shape[1]
    labels = jnp.pad(segments.astype(BF), ((0, 15), (0, channels - length)))
    labels = jnp.broadcast_to(labels, (4,) + labels.shape)
    hidden = hidden_in.astype(jnp.float32)
    scale_one = rms_of(hidden)
    normed = (hidden * scale_one * norm1_gain).astype(BF)
    floor = lax.dynamic_slice_in_dim(lower_bound, member * quarter, quarter)
    feed = slices(ffn_weights, lanes)
    mix = slices(mix_weights, channels)

    mix = trade(jnp.concatenate([slices(mix_weights, channels), labels], axis=1))

    gate = (mix, normed, feed)
    mix, normed, feed = lax.optimization_barrier(gate)
    labels = mix[:, rows, :length].astype(jnp.int32)
    labels = jnp.stack([pick(labels, member ^ m) for m in range(4)])
    mix = mix[:, :rows]
    cuts = [0, 384, 768, 1024, 1408, 1664, 1920, lanes]
    feed_cut = cuts[4]
    mix_far = far(mix)
    mix_near = over_y(mix)
    feed_one = trade(feed[..., :feed_cut])
    feed_rest = after(feed[..., feed_cut:], gate)
    normed_x, normed_z = over_x(normed), over_z(normed)
    top_x = over_x(after(out_grad, gate))

    gate = (mix_far, mix_near, feed_one, feed_rest, normed_x, normed_z, top_x)
    mix_cross = near(after(mix_far, gate))
    ones = [feed_one[..., low:high] for low, high in zip(cuts[:4], cuts[1:5])]
    far_a = far(after(ones[0], gate))
    normed_xz = over_x(after(normed_z, gate))
    normed_three = jnp.stack(after([normed, normed_x, normed_z], gate))
    top_z = over_z(after(out_grad, gate))

    gate = (mix_cross, far_a, normed_xz, normed_three, top_z, ones)
    normed_c, normed_cxz = over_c(after(normed_three, gate)), over_c(after(normed_xz, gate))
    top_three = jnp.stack(after([out_grad, top_x, top_z], gate))
    normed = [normed, normed_x, normed_z, normed_xz, normed_c, normed_cxz]
    mix_sources = [(0, 0, mix), (1, 0, mix_near)] + pieces(0, mix_far, mix_cross)

    gate = (normed_c, normed_cxz, top_three)
    far_b = far(after(ones[1], gate))
    near_a = over_y(after(feed_one[..., :640], gate))
    cross_a = near(after(far_a, gate))
    top_xz = over_x(after(top_z, gate))
    projected, mixed, send, keep = mixer_forward(
        core_at, offsets, after(normed, gate), mix_sources, labels, floor, head_gain
    )

    gate = (send, far_b, near_a, cross_a, top_xz)
    came = over_c(after(send, gate))
    far_c = far(after(ones[2], gate))
    near_b = over_y(after(feed_one[..., 640:1024], gate))
    feed_two = trade(after(feed_rest, gate))
    top_c = over_c(after(top_three, gate))
    own, to_x, to_z, to_xz = add_cores(keep, came)

    gate = (own, far_c, near_b, top_c)
    from_x = over_x(after(to_xz, gate))
    far_d = far(after(ones[3], gate))
    near_c = over_y(after(feed_one[..., 1024:], gate))
    cross_b = near(after(far_b, gate))
    top_cxz = over_c(after(top_xz, gate))
    tops = [out_grad, top_x, top_z, top_xz, top_c, top_cxz]

    gate = (from_x, far_d, near_c, cross_b, top_cxz, feed_two)
    to_z = add_low(to_z, after(from_x, gate))
    of_x = over_x(after(to_x, gate))
    of_z = over_z(to_z)
    far_e = far(after(feed_two[..., : cuts[5] - feed_cut], gate))
    near_d = over_y(after(feed_two, gate))

    gate = (of_x, of_z, far_e, near_d)
    far_f = far(after(feed_two[..., cuts[5] - feed_cut : cuts[6] - feed_cut], gate))
    cross_c, cross_d = near(after(far_c, gate)), near(after(far_d, gate))
    middle, normed_two = row_call(
        middle_kernel, "middle", [jnp.float32, BF], *after((own, of_x, of_z), gate), hidden_in,
        norm2_gain[None],
    )
    two_x, two_z = over_x(normed_two), over_z(normed_two)

    gate = (far_f, cross_c, cross_d, two_x, two_z)
    far_g = far(after(feed_two[..., cuts[6] - feed_cut :], gate))
    cross_e, cross_f = near(after(far_e, gate)), near(after(far_f, gate))
    two_xz = over_x(after(two_z, gate))
    two_three = jnp.stack(after([normed_two, two_x, two_z], gate))

    gate = (far_g, cross_e, cross_f, two_xz, two_three)
    cross_g = near(after(far_g, gate))
    two_c, two_cxz = over_c(after(two_three, gate)), over_c(after(two_xz, gate))
    normed_two = [normed_two, two_x, two_z, two_xz, two_c, two_cxz]
    feed_sources = [(0, 0, feed_one), (0, feed_cut, feed_two)]
    feed_sources += [(1, 0, near_a), (1, 640, near_b), (1, 1024, near_c), (1, feed_cut, near_d)]
    fars = [far_a, far_b, far_c, far_d, far_e, far_f, far_g]
    crosses = [cross_a, cross_b, cross_c, cross_d, cross_e, cross_f, cross_g]
    for low, straight, crossed in zip(cuts, fars, crosses):
        feed_sources += pieces(low, straight, crossed)

    widths = [128, 256, 384, 256, 384, 256, 256, lanes - 1920]
    *grads, send, keep = ffn(core_at, offsets, normed_two, tops, feed_sources, units, widths)
    gates, downs = grads[:5], grads[5:]
    came = over_c(send)
    down_sends = grad_sends(core_at, after(tops, send), downs, LONG)
    own, to_x, to_z, to_xz = add_cores(keep, after(came, down_sends))

    gate = (own,)
    from_x = over_x(after(to_xz, gate))
    down_one = over_y(after(down_sends[0], gate))
    gate_sends = grad_sends(core_at, after(normed_two, gate), gates, LONG)

    gate = (from_x, down_one, gate_sends)
    to_z = add_low(to_z, after(from_x, gate))
    of_x = over_x(after(to_x, gate))
    of_z = over_z(to_z)
    down_two = over_y(after(down_sends[1], gate))
    down_keeps = grad_keeps(core_at, after(tops, gate), downs, LONG)
    down_home, down_away = near_sums([(down_keeps[0], after(down_one, gate))])

    gate = (of_x, of_z, down_two, down_away)
    down_fars = send_far(after(down_away, gate))
    down_three = over_y(after(down_sends[2], gate))
    one_came = over_y(after(gate_sends[0], gate))
    middle_grad, middle_low, gain_two_grad = row_call(
        back_kernel, "middle_grad", [jnp.float32, BF, None], *after((own, of_x, of_z), gate),
        middle, out_grad, norm2_gain[None],
    )
    grad_x, grad_z = over_x(middle_low), over_z(middle_low)
    gate_keeps = grad_keeps(core_at, after(normed_two, middle_low), gates, LONG)
    down_home_two, down_away_two = near_sums(
        [(after(down_keeps[1], gate_keeps), after(down_two, gate))]
    )

    gate = (grad_x, grad_z, down_three, one_came, down_away_two, down_fars)
    down_fars_two = send_far(after(down_away_two, gate))
    two_came = over_y(after(gate_sends[1], gate))
    grad_xz = over_x(after(grad_z, gate))
    grad_three = jnp.stack(after([middle_low, grad_x, grad_z], gate))
    branch = rows_product(
        core_at, offsets, after(downs, gate), feed_sources, 2 * units, model, LONG
    )

    gate = (grad_xz, grad_three, branch, down_fars_two, two_came)
    grad_c, grad_cxz = over_c(after(grad_three, gate)), over_c(after(grad_xz, gate))
    one_home, one_away = near_sums(
        [
            (down_keeps[2], after(down_three, gate)),
            (gate_keeps[0], after(one_came, gate)),
            (gate_keeps[1], after(two_came, gate)),
        ],
        LONG,
    )
    middle_full = [middle_low, grad_x, grad_z, grad_xz, grad_c, grad_cxz]

    gate = (grad_c, grad_cxz, one_away)
    one_fars = send_far(after(one_away, gate))
    three_came, four_came = [over_y(after(part, gate)) for part in gate_sends[2:4]]
    branch = lax.psum_scatter(
        after(branch, gate).reshape(-1, model), GROUP + ("tensor",), scatter_dimension=0, tiled=True
    )
    middle_full = after(middle_full, gate)
    g_one, g_two, send, keep, floor_sums, gain_sums = mixer_backward(
        core_at, offsets, middle_full, mix_sources, projected, labels, floor, head_gain
    )

    gate = (send, one_fars, three_came, four_came)
    came = over_c(after(send, gate))
    five_came = over_y(after(gate_sends[4], gate))
    three_home, three_away = near_sums([(gate_keeps[2], after(three_came, gate))], LONG)
    own, to_x, to_z, to_xz = add_cores(keep, after(came, three_away))

    gate = (own,)
    three_fars = send_far(after(three_away, gate))
    from_x = over_x(after(to_xz, gate))
    value_send, pair_send = grad_sends(core_at, after(normed, gate), [g_two, g_one], LONG)
    (last_send,) = grad_sends(core_at, after(middle_full, value_send), [mixed])
    four_home, four_away = near_sums([(gate_keeps[3], after(four_came, last_send))])

    gate = (from_x, three_fars, four_away, five_came)
    four_fars = send_far(after(four_away, gate))
    to_z = add_low(to_z, after(from_x, gate))
    of_x = over_x(after(to_x, gate))
    of_z = over_z(to_z)
    value_came, last_came = over_y(after(value_send, gate)), over_y(after(last_send, gate))
    value_keep, pair_keep = grad_keeps(core_at, after(normed, gate), [g_two, g_one], LONG)
    five_home, five_away = near_sums([(gate_keeps[4], after(five_came, value_keep))])
    (last_keep,) = grad_keeps(core_at, after(middle_full, five_away), [mixed])

    gate = (of_x, of_z, four_fars, value_came, last_came, last_keep)
    five_fars = send_far(after(five_away, gate))
    query_came = over_y(after(pair_send[..., :quarter], gate))
    input_grad, _, gain_one_grad = row_call(
        back_kernel, "input_grad", [jnp.float32, BF, None], *after((own, of_x, of_z), gate),
        hidden_in, middle_grad, norm1_gain[None],
    )
    near_home, near_away = near_sums(
        [(value_keep, after(value_came, input_grad)), (last_keep, last_came)]
    )
    down_parts = [(down_home, down_fars), (down_home_two, down_fars_two), (one_home, one_fars)]
    down_parts = far_sums(after(down_parts, near_away))
    head_grad = jnp.sum(after(gain_sums, gate).reshape(-1, HEAD), axis=0)
    lower_grad = jnp.zeros((2, 4, quarter), jnp.float32)
    lower_grad = lax.dynamic_update_slice(
        lower_grad,
        jnp.sum(after(floor_sums, gate), axis=(0, 1)).reshape(1, 1, quarter),
        (core, member, 0),
    )
    sums = [gain_one_grad[0], gain_two_grad[0], head_grad, lower_grad.reshape(-1)]
    sums = jnp.concatenate(sums).reshape(-1, HEAD)

    gate = (five_fars, query_came, near_away, down_parts, sums)
    near_fars = send_far(after(near_away, gate))
    forget_came = over_y(after(pair_send[..., quarter:], gate))
    down_parts = trade(after(down_parts, gate))
    sums_x = over_x(after(sums, gate))
    block_out = (middle + after(branch, gate).astype(jnp.float32)).astype(BF)
    gate_parts = [(three_home, three_fars), (four_home, four_fars), (five_home, five_fars)]
    gate_parts = far_sums(after(gate_parts, gate))
    pair_came = jnp.concatenate([query_came, after(forget_came, gate_parts)], axis=-1)
    pair_home, pair_away = near_sums([(pair_keep, pair_came)])

    gate = (near_fars, down_parts, sums_x, pair_away, gate_parts, block_out)
    pair_fars = send_far(after(pair_away, gate))
    gate_parts = trade(after(gate_parts, gate))
    sums = sums + sums_x
    sums_z = over_z(after(sums, gate))

    gate = (pair_fars, gate_parts, sums_z)
    mix_parts = trade(far_sums(after([(near_home, near_fars), (pair_home, pair_fars)], gate)))
    ffn_grad = ffn_grad_of(after([down_parts, gate_parts], gate), units)
    sums = sums + sums_z
    sums = sums + over_y(after(sums, gate))
    sums = sums + swap(sums, ("tensor",))
    sums = sum_highs(sums).reshape(-1)
    gain_one, gain_two, head, lower = jnp.split(sums, [model, 2 * model, 2 * model + HEAD])
    mix_grad = mix_grad_of(mix_parts)
    return (block_out, input_grad, mix_grad, ffn_grad, gain_one, gain_two, head, lower)


def solution(mesh):
    total, cores = mesh.shape["dp"], mesh.shape["tensor"]
    fine = Mesh(mesh.devices.reshape(total // 8, 2, 2, 2, cores), ("h", "l", "y", "x", "tensor"))
    dp = ("h", "l", "y", "x")
    rows = P(dp + ("tensor",), None)
    weights = P(dp, None, "tensor")
    return jax.shard_map(
        body,
        mesh=fine,
        in_specs=(rows, P(dp, None), weights, weights, P(), P(), P(), P("tensor"), rows),
        out_specs=(rows, rows, weights, weights, P(), P(), P(), P()),
        check_vma=False,
    )
```

time: 660 us -> 590 us (0.89)
  waiting for transfers between devices: 261 us -> 206 us
  Pallas kernels: 155 us -> 209 us
  other arithmetic: 66.4 us -> 14.3 us
  local copies, waits for them, and re-layouts: 66.4 us -> 36.2 us
  starting transfers between devices: 87.2 us -> 106 us
    pallas_call x11 -> x28, Pallas kernels: 97.7 us -> 159 us  [the longest x8 54.1 us: grad_product(): pl.pallas_call(functools.partial(grad_kernel, number=len(grads)), grid_sp...]
    ppermute x13 -> x16, waiting for transfers between devices: 132 us -> 81.8 us  [shift(): lax.ppermute(values, 'h', [(s, (s + steps) % total) for s in range(total)])]
    ppermute x26 -> x61, starting transfers between devices: 23.8 us -> 58.6 us  [swap(): lax.ppermute(values, axes, [(s, total - 1 - s) for s in range(total)])]
    convert_element_type x14 -> x4, other arithmetic: 29.6 us -> 3.36 us  [the longest x1 1.94 us: body(): block_out = (middle + after(branch, gate).astype(jnp.float32)).astype(BF)]
    all_to_all x9 -> x6, starting transfers between devices: 44.8 us -> 23 us  [trade(): return lax.all_to_all(slices, GROUP, 0, 0, tiled=True)]
    add x13 -> x5, other arithmetic: 14 us -> 0.04 us  [the longest x1 0.01 us: body(): sums = sums + sums_x]
    convert_element_type x7 -> x0, local copies, waits for them, and re-layouts: 11.7 us -> none  [the longest x6 10.6 us: add_far(): return home.reshape(4, -1, home.shape[-1]).astype(BF)]
    ppermute x26 -> x61, waiting for transfers between devices: 100 us -> 111 us  [swap(): lax.ppermute(values, axes, [(s, total - 1 - s) for s in range(total)])]
  transfers between devices with their start and end apart: 53 -> 85, of which waited for: 32 -> 34; matrix products, arithmetic and copies ran while one was open for 15% -> 5% of each run, Pallas kernels for 18% -> 28%
where the time goes in v3:
time: 590 us; the launch traced here: 587 us
  Pallas kernels  209 us (35%)
  waiting for transfers between devices  206 us (35%)
  starting transfers between devices  106 us (18%)
  local copies, waits for them, and re-layouts  36.2 us (6%)
  between operations  15.2 us (3%)
  other arithmetic  14.3 us (2%)
    ppermute x61, waiting for transfers between devices, swap(): lax.ppermute(values, axes, [(s, total - 1 - s) for s in range(total)])  111 us
    ppermute x16, waiting for transfers between devices, shift(): lax.ppermute(values, 'h', [(s, (s + steps) % total) for s in range(total)])  81.8 us
    ppermute x61, starting transfers between devices, swap(): lax.ppermute(values, axes, [(s, total - 1 - s) for s in range(total)])  58.6 us
    pallas_call x8, Pallas kernels, grad_product(): pl.pallas_call(functools.partial(grad_kernel, number=len(grads)), grid_sp...  54.1 us
    pallas_call x8, Pallas kernels, near_sums(): pl.pallas_call(functools.partial(near_kernel, number=len(pairs), ends=hig...  30.9 us
    pallas_call x1, Pallas kernels, ffn(): pl.pallas_call(functools.partial(ffn_kernel, sources=layout, units=width)...  29.6 us
    pallas_call x1, Pallas kernels, mixer_backward(): pl.pallas_call(functools.partial(mixer_backward_kernel, sources=layout),...  23.5 us
    ppermute x16, starting transfers between devices, shift(): lax.ppermute(values, 'h', [(s, (s + steps) % total) for s in range(total)])  23.1 us
  transfers between devices with their start and end apart: 85, of which 34 were waited for; matrix products, arithmetic and copies ran while one was open for 5% of the time, Pallas kernels for 28%

profile of v3, /device:TPU:0, one launch (start us, length us, event | category | flops | bytes accessed | tf_op | source)
XLA Modules:
  0.0 587.1 jit_solution(13725195969651377047)
XLA Ops:
  11.3 5.4 all-to-all-start
  26.9 4.9 all-to-all-done
  46.9 41.3 %collective-permute-done.1.refs_2_ = bf16[128,2048]{1,0:T(8,128)(2,1)S(1)} collective-permute-done((bf16[128,2048]{1,0:T(8,128)(2,1)S(1)}, bf16[128,2048]{1,0:T(8,128)(2,1)S(1)}, u32[]{:S(2)}, u32[]{:S(2)}) %collective-permute-start.1) | collective-permute-done | bytes 524320 | tf_op jit(solution)/shard_map/ppermute | solution.py:700
  99.0 12.5 %collective-permute-done.7.refs_18_.refs_9_ = bf16[4,128,384]{2,1,0:T(8,128)(2,1)S(1)} collective-permute-done((bf16[4,128,384]{2,1,0:T(8,128)(2,1)S(1)}, bf16[4,128,384]{2,1,0:T(8,128)(2,1)S(1)}, u32[]{:S(2)}, u32[]{:S(2)}) %collective-permute-start.7) | collective-permute-done | bytes 393248 | tf_op jit(solution)/shard_map/ppermute | solution.py:705
  126.9 17.2 %mixer_forward.1 = (f32[4,256,768]{2,1,0:T(8,128)}, bf16[4,256,256]{2,1,0:T(8,128)(2,1)}, bf16[4,128,2048]{2,1,0:T(8,128)(2,1)}, f32[4,128,2048]{2,1,0:T(8,128)}) custom-call(s32[2]{0:T(128)} %pad_add_fusion.1.core_ref, s32[16]{0:T(128)} %stack.194.offsets_ref, bf16[128,2048]{1,0:T(8,128)(2,1)} %fusion.2.refs_0_, bf16[128,2048]{1,0:T(8,128)(2,1)} %copy-done.32, ...), custom_call_target="tpu_custom_call" | custom-call | flops 49999998976 | bytes 1 | tf_op jit(solution)/shard_map/mixer_forward/pallas_call | solution.py:275
  144.2 5.4 collective-permute-done.12.refs_14_.refs_5_
  163.3 5.8 collective-permute-done.16.refs_22_.refs_13_
  176.4 6.5 %collective-permute-done.21.refs_16_.refs_7_ = bf16[4,128,384]{2,1,0:T(8,128)(2,1)S(1)} collective-permute-done((bf16[4,128,384]{2,1,0:T(8,128)(2,1)S(1)}, bf16[4,128,384]{2,1,0:T(8,128)(2,1)S(1)}, u32[]{:S(2)}, u32[]{:S(2)}) %collective-permute-start.21) | collective-permute-done | bytes 393248 | tf_op jit(solution)/shard_map/ppermute | solution.py:700
  182.9 10.5 %collective-permute-done.20.refs_24_.refs_15_ = bf16[4,128,384]{2,1,0:T(8,128)(2,1)S(1)} collective-permute-done((bf16[4,128,384]{2,1,0:T(8,128)(2,1)S(1)}, bf16[4,128,384]{2,1,0:T(8,128)(2,1)S(1)}, u32[]{:S(2)}, u32[]{:S(2)}) %collective-permute-start.20) | collective-permute-done | bytes 393248 | tf_op jit(solution)/shard_map/ppermute | solution.py:705
  198.4 14.3 %collective-permute-done.26.refs_26_.refs_17_ = bf16[4,128,256]{2,1,0:T(8,128)(2,1)S(1)} collective-permute-done((bf16[4,128,256]{2,1,0:T(8,128)(2,1)S(1)}, bf16[4,128,256]{2,1,0:T(8,128)(2,1)S(1)}, u32[]{:S(2)}, u32[]{:S(2)}) %collective-permute-start.26) | collective-permute-done | bytes 262176 | tf_op jit(solution)/shard_map/ppermute | solution.py:705
  224.8 10.8 %collective-permute-done.30.refs_28_.refs_19_ = bf16[4,128,256]{2,1,0:T(8,128)(2,1)S(1)} collective-permute-done((bf16[4,128,256]{2,1,0:T(8,128)(2,1)S(1)}, bf16[4,128,256]{2,1,0:T(8,128)(2,1)S(1)}, u32[]{:S(2)}, u32[]{:S(2)}) %collective-permute-start.30) | collective-permute-done | bytes 262176 | tf_op jit(solution)/shard_map/ppermute | solution.py:705
  244.1 5.7 collective-permute-done.34.refs_30_.refs_21_
  253.8 5.8 collective-permute-done.39.refs_31_.refs_22_
  260.8 29.6 %ffn.1 = (bf16[4,256,128]{2,1,0:T(8,128)(2,1)}, bf16[4,256,256]{2,1,0:T(8,128)(2,1)}, bf16[4,256,384]{2,1,0:T(8,128)(2,1)}, bf16[4,256,256]{2,1,0:T(8,128)(2,1)}...) custom-call(s32[2]{0:T(128)} %pad_add_fusion.1.core_ref, ...), custom_call_target="tpu_custom_call" | custom-call | flops 49999998976 | bytes 1 | tf_op jit(solution)/shard_map/ffn/pallas_call | solution.py:395
  290.5 6.3 %grad_product.8 = (bf16[4,256,256]{2,1,0:T(8,128)(2,1)}, bf16[4,256,256]{2,1,0:T(8,128)(2,1)}, bf16[4,256,256]{2,1,0:T(8,128)(2,1)}) custom-call(s32[2]{0:T(128)} %pad_add_fusion.1.core_ref, s32[4]{0:T(128)} %get-tuple-element.560.blocks_ref, bf16[128,2048]{1,0:T(8,128)(2,1)} %add_ref.1, bf16[128,2048]{1,0:T(8,128)(2,1)} %copy-done.34, ...), custom_call_target="tpu_custom_call" | custom-call | flops 49999998976 | bytes 1 | tf_op jit(solution)/shard_map/grad_product/pallas_call | solution.py:474
  298.1 4.8 add_cores.4
  305.4 8.8 %grad_product.9 = (bf16[4,256,128]{2,1,0:T(8,128)(2,1)}, bf16[4,256,256]{2,1,0:T(8,128)(2,1)}, bf16[4,256,384]{2,1,0:T(8,128)(2,1)}, bf16[4,256,256]{2,1,0:T(8,128)(2,1)}, bf16[4,256,384]{2,1,0:T(8,128)(2,1)}) custom-call(s32[2]{0:T(128)} %pad_add_fusion.1.core_ref, s32[4]{0:T(128)} %get-tuple-element.560.blocks_ref, ...), custom_call_target="tpu_custom_call" | custom-call | flops 49999998976 | bytes 1 | tf_op jit(solution)/shard_map/grad_product/pallas_call | solution.py:474
  321.9 6.5 %grad_product.10 = (f32[4,256,256]{2,1,0:T(8,128)}, f32[4,256,256]{2,1,0:T(8,128)}, f32[4,256,256]{2,1,0:T(8,128)}) custom-call(s32[2]{0:T(128)} %pad_add_fusion.1.core_ref, s32[4]{0:T(128)} %get-tuple-element.561.blocks_ref, bf16[128,2048]{1,0:T(8,128)(2,1)} %add_ref.1, bf16[128,2048]{1,0:T(8,128)(2,1)} %copy-done.34, ...), custom_call_target="tpu_custom_call" | custom-call | flops 49999998976 | bytes 1 | tf_op jit(solution)/shard_map/grad_product/pallas_call | solution.py:474
  345.3 9.0 %grad_product.11 = (f32[4,256,128]{2,1,0:T(8,128)}, f32[4,256,256]{2,1,0:T(8,128)}, f32[4,256,384]{2,1,0:T(8,128)}, f32[4,256,256]{2,1,0:T(8,128)}, f32[4,256,384]{2,1,0:T(8,128)}) custom-call(s32[2]{0:T(128)} %pad_add_fusion.1.core_ref, s32[4]{0:T(128)} %get-tuple-element.561.blocks_ref, bf16[128,2048]{1,0:T(8,128)(2,1)} %get-tuple-element.395.refs_0_, ...), custom_call_target="tpu_custom_call" | custom-call | flops 49999998976 | bytes 1 | tf_op jit(solution)/shard_map/grad_product/pallas_call | solution.py:474
  361.5 9.7 %rows_product.1 = bf16[4,256,2048]{2,1,0:T(8,128)(2,1)} custom-call(s32[2]{0:T(128)} %pad_add_fusion.1.core_ref, s32[16]{0:T(128)} %stack.194.offsets_ref, bf16[4,256,256]{2,1,0:T(8,128)(2,1)} %get-tuple-element.410.refs_0_, bf16[4,256,256]{2,1,0:T(8,128)(2,1)} %get-tuple-element.411.refs_1_, bf16[4,256,256]{2,1,0:T(8,128)(2,1)} %get-tuple-element.412.refs_2_, ...), custom_call_target="tpu_custom_call" | custom-call | flops 49999998976 | bytes 1 | tf_op jit(solution)/shard_map/rows_product/pallas_call | solution.py:440
  381.2 23.5 %mixer_backward.1 = (bf16[4,256,512]{2,1,0:T(8,128)(2,1)}, bf16[4,256,256]{2,1,0:T(8,128)(2,1)}, bf16[4,128,2048]{2,1,0:T(8,128)(2,1)}, f32[4,128,2048]{2,1,0:T(...) custom-call(s32[2]{0:T(128)} %pad_add_fusion.1.core_ref, s32[16]{0:T(128)} %stack.194.offsets_ref, ...), custom_call_target="tpu_custom_call" | custom-call | flops 49999998976 | bytes 1 | tf_op jit(solution)/shard_map/mixer_backward/pallas_call | solution.py:315
  404.6 6.1 %collective-permute-done.56.refs_5_ = bf16[2,256,640]{2,1,0:T(8,128)(2,1)S(1)} collective-permute-done((bf16[2,256,640]{2,1,0:T(8,128)(2,1)S(1)}, bf16[2,256,640]{2,1,0:T(8,128)(2,1)S(1)}, u32[]{:S(2)}, u32[]{:S(2)}) %collective-permute-start.56) | collective-permute-done | bytes 655392 | tf_op jit(solution)/shard_map/ppermute | solution.py:705
  418.2 4.8 add_cores.5
  424.6 6.5 %grad_product.12 = (bf16[4,256,256]{2,1,0:T(8,128)(2,1)}, bf16[4,256,512]{2,1,0:T(8,128)(2,1)}) custom-call(s32[2]{0:T(128)} %pad_add_fusion.1.core_ref, s32[4]{0:T(128)} %get-tuple-element.560.blocks_ref, bf16[128,2048]{1,0:T(8,128)(2,1)} %fusion.2.refs_0_, bf16[128,2048]{1,0:T(8,128)(2,1)} %copy-done.32, bf16[128,2048]{1,0:T(8,128)(2,1)} %copy-done.30, ...), custom_call_target="tpu_custom_call" | custom-call | flops 49999998976 | bytes 1 | tf_op jit(solution)/shard_map/grad_product/pallas_call | solution.py:474
  431.0 5.2 grad_product.13
  448.3 6.6 %grad_product.14 = (f32[4,256,256]{2,1,0:T(8,128)}, f32[4,256,512]{2,1,0:T(8,128)}) custom-call(s32[2]{0:T(128)} %pad_add_fusion.1.core_ref, s32[4]{0:T(128)} %get-tuple-element.561.blocks_ref, bf16[128,2048]{1,0:T(8,128)(2,1)} %fusion.2.refs_0_, bf16[128,2048]{1,0:T(8,128)(2,1)} %copy-done.32, bf16[128,2048]{1,0:T(8,128)(2,1)} %copy-done.30, ...), custom_call_target="tpu_custom_call" | custom-call | flops 49999998976 | bytes 1 | tf_op jit(solution)/shard_map/grad_product/pallas_call | solution.py:474
  458.6 5.3 grad_product.15.refs_2_
  464.0 6.4 %collective-permute-done.67.refs_3_ = bf16[4,256,256]{2,1,0:T(8,128)(2,1)S(1)} collective-permute-done((bf16[4,256,256]{2,1,0:T(8,128)(2,1)S(1)}, bf16[4,256,256]{2,1,0:T(8,128)(2,1)S(1)}, u32[]{:S(2)}, u32[]{:S(2)}) %collective-permute-start.67) | collective-permute-done | bytes 524320 | tf_op jit(solution)/shard_map/ppermute | solution.py:700
  499.3 6.9 %collective-permute-done.71 = bf16[4,256,256]{2,1,0:T(8,128)(2,1)S(1)} collective-permute-done((bf16[4,256,256]{2,1,0:T(8,128)(2,1)S(1)}, bf16[4,256,256]{2,1,0:T(8,128)(2,1)S(1)}, u32[]{:S(2)}, u32[]{:S(2)}) %collective-permute-start.71) | collective-permute-done | bytes 524320 | tf_op jit(solution)/shard_map/ppermute | solution.py:700
  513.4 7.7 %collective-permute-done.70.refs_1_ = bf16[2,256,512]{2,1,0:T(8,128)(2,1)S(1)} collective-permute-done((bf16[2,256,512]{2,1,0:T(8,128)(2,1)}, bf16[2,256,512]{2,1,0:T(8,128)(2,1)S(1)}, u32[]{:S(2)}, u32[]{:S(2)}) %collective-permute-start.70) | collective-permute-done | bytes 524320 | tf_op jit(solution)/shard_map/ppermute | solution.py:705
  527.5 21.2 %collective-permute-done.74 = f32[49,128]{1,0:T(8,128)S(1)} collective-permute-done((f32[49,128]{1,0:T(8,128)S(1)}, f32[49,128]{1,0:T(8,128)S(1)}, u32[]{:S(2)}, u32[]{:S(2)}) %collective-permute-start.74) | collective-permute-done | bytes 25120 | tf_op jit(solution)/shard_map/ppermute | solution.py:700
  565.2 7.9 %collective-permute-done.77 = f32[49,128]{1,0:T(8,128)S(1)} collective-permute-done((f32[49,128]{1,0:T(8,128)S(1)}, f32[49,128]{1,0:T(8,128)S(1)}, u32[]{:S(2)}, u32[]{:S(2)}) %collective-permute-start.77) | collective-permute-done | bytes 25120 | tf_op jit(solution)/shard_map/ppermute | solution.py:808
  (423 shorter events, 243.0 us)
Async XLA Ops:
  11.3 20.4 %all-to-all-start = ((bf16[4,144,1024]{2,1,0:T(8,128)(2,1)}), bf16[4,144,1024]{2,1,0:T(8,128)(2,1)S(1)}, u32[]{:S(2)}, u32[]{:S(2)}) async-start(bf16[4,144,1024]{2,1,0:T(8,128)(2,1)} %pad_maximum_fusion.4), calls=%async_computation | async-start | bytes 2359296 | tf_op jit(solution)/shard_map/all_to_all | solution.py:745
  32.9 57.5 %all-to-all-start.1 = ((bf16[4,128,1408]{2,1,0:T(8,128)(2,1)}), bf16[4,128,1408]{2,1,0:T(8,128)(2,1)S(1)}, u32[]{:S(2)}, u32[]{:S(2)}) async-start(bf16[4,128,1408]{2,1,0:T(8,128)(2,1)} %slice.51), calls=%async_computation.1 | async-start | bytes 2883584 | tf_op jit(solution)/shard_map/all_to_all | solution.py:745
  36.6 51.6 %collective-permute-start.3 = (bf16[4,128,1024]{2,1,0:T(8,128)(2,1)S(1)}, bf16[4,128,1024]{2,1,0:T(8,128)(2,1)S(1)}, u32[]{:S(2)}, u32[]{:S(2)}) collective-permute-start(bf16[4,128,1024]{2,1,0:T(8,128)(2,1)S(1)} %slice.50.refs_6_), channel_id=1, source_target_pairs={{0,4},{4,0},{1,5},{5,1},{2,6},{6,2},{3,7},{7,3},{8,12},{12,8},{9,1... | collective-permute-start | bytes 3145736 | tf_op jit(solution)/shard_map/ppermute | solution.py:700
  38.2 52.2 %collective-permute-start.2 = (bf16[4,128,1024]{2,1,0:T(8,128)(2,1)S(1)}, bf16[4,128,1024]{2,1,0:T(8,128)(2,1)}, u32[]{:S(2)}, u32[]{:S(2)}) collective-permute-start(bf16[4,128,1024]{2,1,0:T(8,128)(2,1)S(1)} %slice.50.refs_6_), channel_id=1, source_target_pairs={{0,16},{16,0},{1,17},{17,1},{2,18},{18,2},{3,19},{19,3},{4,20},{20... | collective-permute-start | bytes 3145736 | tf_op jit(solution)/shard_map/ppermute | solution.py:705
  40.8 47.4 %collective-permute-start.1 = (bf16[128,2048]{1,0:T(8,128)(2,1)S(1)}, bf16[128,2048]{1,0:T(8,128)(2,1)S(1)}, u32[]{:S(2)}, u32[]{:S(2)}) collective-permute-start(bf16[128,2048]{1,0:T(8,128)(2,1)S(1)} %copy-done.13), channel_id=1, source_target_pairs={{0,8},{8,0},{1,9},{9,1},{2,10},{10,2},{3,11},{11,3},{4,12},{12,4},... | collective-permute-start | bytes 1572872 | tf_op jit(solution)/shard_map/ppermute | solution.py:700
  42.8 45.4 %collective-permute-start = (bf16[128,2048]{1,0:T(8,128)(2,1)S(1)}, bf16[128,2048]{1,0:T(8,128)(2,1)S(1)}, u32[]{:S(2)}, u32[]{:S(2)}) collective-permute-start(bf16[128,2048]{1,0:T(8,128)(2,1)S(1)} %copy-done.13), channel_id=1, source_target_pairs={{0,2},{2,0},{1,3},{3,1},{4,6},{6,4},{5,7},{7,5},{8,10},{10,8},{9,1... | collective-permute-start | bytes 1572872 | tf_op jit(solution)/shard_map/ppermute | solution.py:700
  44.2 43.9 %collective-permute-start.4 = (bf16[128,2048]{1,0:T(8,128)(2,1)S(1)}, bf16[128,2048]{1,0:T(8,128)(2,1)S(1)}, u32[]{:S(2)}, u32[]{:S(2)}) collective-permute-start(bf16[128,2048]{1,0:T(8,128)(2,1)S(1)} %copy-done.28), channel_id=1, source_target_pairs={{0,2},{2,0},{1,3},{3,1},{4,6},{6,4},{5,7},{7,5},{8,10},{10,8},{9,1... | collective-permute-start | bytes 1572872 | tf_op jit(solution)/shard_map/ppermute | solution.py:700
  90.4 24.7 %collective-permute-start.6 = (bf16[4,128,1024]{2,1,0:T(8,128)(2,1)}, bf16[4,128,1024]{2,1,0:T(8,128)(2,1)}, u32[]{:S(2)}, u32[]{:S(2)}) collective-permute-start(bf16[4,128,1024]{2,1,0:T(8,128)(2,1)} %collective-permute-done.2.refs_8_), channel_id=1, source_target_pairs={{0,4},{4,0},{1,5},{5,1},{2,6},{6,2},{3,7},{7,3},{8,12},{12,8},{9,1... | collective-permute-start | bytes 3145736 | tf_op jit(solution)/shard_map/ppermute | solution.py:700
  92.0 20.3 %collective-permute-start.5 = (bf16[128,2048]{1,0:T(8,128)(2,1)}, bf16[128,2048]{1,0:T(8,128)(2,1)}, u32[]{:S(2)}, u32[]{:S(2)}) collective-permute-start(bf16[128,2048]{1,0:T(8,128)(2,1)} %copy-done.30), channel_id=1, source_target_pairs={{0,2},{2,0},{1,3},{3,1},{4,6},{6,4},{5,7},{7,5},{8,10},{10,8},{9,1... | collective-permute-start | bytes 1572872 | tf_op jit(solution)/shard_map/ppermute | solution.py:700
  92.8 21.0 %collective-permute-start.8 = (bf16[128,2048]{1,0:T(8,128)(2,1)}, bf16[128,2048]{1,0:T(8,128)(2,1)}, u32[]{:S(2)}, u32[]{:S(2)}) collective-permute-start(bf16[128,2048]{1,0:T(8,128)(2,1)} %add_ref.1), channel_id=1, source_target_pairs={{0,8},{8,0},{1,9},{9,1},{2,10},{10,2},{3,11},{11,3},{4,12},{12,4},... | collective-permute-start | bytes 1572872 | tf_op jit(solution)/shard_map/ppermute | solution.py:700
  122.5 21.6 %collective-permute-start.11 = (bf16[4,128,384]{2,1,0:T(8,128)(2,1)S(1)}, bf16[4,128,384]{2,1,0:T(8,128)(2,1)}, u32[]{:S(2)}, u32[]{:S(2)}) collective-permute-start(bf16[4,128,384]{2,1,0:T(8,128)(2,1)S(1)} %copy-done.44), channel_id=1, source_target_pairs={{0,16},{16,0},{1,17},{17,1},{2,18},{18,2},{3,19},{19,3},{4,20},{20... | collective-permute-start | bytes 1179656 | tf_op jit(solution)/shard_map/ppermute | solution.py:705
  126.3 23.2 %collective-permute-start.12 = (bf16[4,128,640]{2,1,0:T(8,128)(2,1)S(1)}, bf16[4,128,640]{2,1,0:T(8,128)(2,1)S(1)}, u32[]{:S(2)}, u32[]{:S(2)}) collective-permute-start(bf16[4,128,640]{2,1,0:T(8,128)(2,1)S(1)} %slice.69), channel_id=1, source_target_pairs={{0,4},{4,0},{1,5},{5,1},{2,6},{6,2},{3,7},{7,3},{8,12},{12,8},{9,1... | collective-permute-start | bytes 1966088 | tf_op jit(solution)/shard_map/ppermute | solution.py:700
  150.9 25.5 %all-to-all-start.2 = ((bf16[4,128,768]{2,1,0:T(8,128)(2,1)}), bf16[4,128,768]{2,1,0:T(8,128)(2,1)S(1)}, u32[]{:S(2)}, u32[]{:S(2)}) async-start(bf16[4,128,768]{2,1,0:T(8,128)(2,1)} %slice.52), calls=%async_computation.2 | async-start | bytes 1572864 | tf_op jit(solution)/shard_map/all_to_all | solution.py:745
  154.4 357.0 %reduce-scatter.2.cloned.1.call-start = ((), (), s32[]{:S(2)}) async-start(), calls=%async_computation.7 | async-start | bytes 4718592 | tf_op jit(solution)/shard_map/reduce_scatter | solution.py:994
  169.1 24.4 %collective-permute-start.23 = (bf16[128,2048]{1,0:T(8,128)(2,1)}, bf16[128,2048]{1,0:T(8,128)(2,1)S(1)}, u32[]{:S(2)}, u32[]{:S(2)}) collective-permute-start(bf16[128,2048]{1,0:T(8,128)(2,1)} %collective-permute-done.14.refs_9_.refs_3_), channel_id=1, source_target_pairs={{0,1},{1,0},{2,3},{3,2},{4,5},{5,4},{6,7},{7,6},{8,9},{9,8},{10,11... | collective-permute-start | bytes 1572872 | tf_op jit(solution)/shard_map/ppermute | solution.py:700
  169.2 24.3 %collective-permute-start.19 = (bf16[128,2048]{1,0:T(8,128)(2,1)}, bf16[128,2048]{1,0:T(8,128)(2,1)S(1)}, u32[]{:S(2)}, u32[]{:S(2)}) collective-permute-start(bf16[128,2048]{1,0:T(8,128)(2,1)} %get-tuple-element.311), channel_id=1, source_target_pairs={{0,2},{2,0},{1,3},{3,1},{4,6},{6,4},{5,7},{7,5},{8,10},{10,8},{9,1... | collective-permute-start | bytes 1572872 | tf_op jit(solution)/shard_map/ppermute | solution.py:700
  172.5 21.0 %collective-permute-start.20 = (bf16[4,128,384]{2,1,0:T(8,128)(2,1)S(1)}, bf16[4,128,384]{2,1,0:T(8,128)(2,1)S(1)}, u32[]{:S(2)}, u32[]{:S(2)}) collective-permute-start(bf16[4,128,384]{2,1,0:T(8,128)(2,1)S(1)} %copy-done.43), channel_id=1, source_target_pairs={{0,16},{16,0},{1,17},{17,1},{2,18},{18,2},{3,19},{19,3},{4,20},{20... | collective-permute-start | bytes 1179656 | tf_op jit(solution)/shard_map/ppermute | solution.py:705
  193.9 20.0 %collective-permute-start.27 = (bf16[4,128,768]{2,1,0:T(8,128)(2,1)S(1)}, bf16[4,128,768]{2,1,0:T(8,128)(2,1)S(1)}, u32[]{:S(2)}, u32[]{:S(2)}) collective-permute-start(bf16[4,128,768]{2,1,0:T(8,128)(2,1)S(1)} %all-to-all-done.2.refs_13_.refs_4_), channel_id=1, source_target_pairs={{0,4},{4,0},{1,5},{5,1},{2,6},{6,2},{3,7},{7,3},{8,12},{12,8},{9,1... | collective-permute-start | bytes 2359304 | tf_op jit(solution)/shard_map/ppermute | solution.py:700
  378.0 26.6 %collective-permute-start.58 = (bf16[4,256,256]{2,1,0:T(8,128)(2,1)}, bf16[4,256,256]{2,1,0:T(8,128)(2,1)S(1)}, u32[]{:S(2)}, u32[]{:S(2)}) collective-permute-start(bf16[4,256,256]{2,1,0:T(8,128)(2,1)} %get-tuple-element.437), channel_id=1, source_target_pairs={{0,4},{4,0},{1,5},{5,1},{2,6},{6,2},{3,7},{7,3},{8,12},{12,8},{9,1... | collective-permute-start | bytes 1572872 | tf_op jit(solution)/shard_map/ppermute | solution.py:700
  379.5 31.2 %collective-permute-start.56 = (bf16[2,256,640]{2,1,0:T(8,128)(2,1)S(1)}, bf16[2,256,640]{2,1,0:T(8,128)(2,1)S(1)}, u32[]{:S(2)}, u32[]{:S(2)}) collective-permute-start(bf16[2,256,640]{2,1,0:T(8,128)(2,1)S(1)} %copy-done.63), channel_id=1, source_target_pairs={{0,16},{16,0},{1,17},{17,1},{2,18},{18,2},{3,19},{19,3},{4,20},{20... | collective-permute-start | bytes 1966088 | tf_op jit(solution)/shard_map/ppermute | solution.py:705
  380.6 30.2 %collective-permute-start.57 = (bf16[4,256,384]{2,1,0:T(8,128)(2,1)S(1)}, bf16[4,256,384]{2,1,0:T(8,128)(2,1)S(1)}, u32[]{:S(2)}, u32[]{:S(2)}) collective-permute-start(bf16[4,256,384]{2,1,0:T(8,128)(2,1)S(1)} %copy-done.60), channel_id=1, source_target_pairs={{0,4},{4,0},{1,5},{5,1},{2,6},{6,2},{3,7},{7,3},{8,12},{12,8},{9,1... | collective-permute-start | bytes 2359304 | tf_op jit(solution)/shard_map/ppermute | solution.py:700
  416.3 23.7 %collective-permute-start.59 = (bf16[4,256,384]{2,1,0:T(8,128)(2,1)S(1)}, bf16[4,256,384]{2,1,0:T(8,128)(2,1)S(1)}, u32[]{:S(2)}, u32[]{:S(2)}) collective-permute-start(bf16[4,256,384]{2,1,0:T(8,128)(2,1)S(1)} %copy-done.59), channel_id=1, source_target_pairs={{0,4},{4,0},{1,5},{5,1},{2,6},{6,2},{3,7},{7,3},{8,12},{12,8},{9,1... | collective-permute-start | bytes 2359304 | tf_op jit(solution)/shard_map/ppermute | solution.py:700
  423.1 19.5 %collective-permute-start.62 = (bf16[2,256,384]{2,1,0:T(8,128)(2,1)S(1)}, bf16[2,256,384]{2,1,0:T(8,128)(2,1)S(1)}, u32[]{:S(2)}, u32[]{:S(2)}) collective-permute-start(bf16[2,256,384]{2,1,0:T(8,128)(2,1)S(1)} %copy-done.88), channel_id=1, source_target_pairs={{0,16},{16,0},{1,17},{17,1},{2,18},{18,2},{3,19},{19,3},{4,20},{20... | collective-permute-start | bytes 1179656 | tf_op jit(solution)/shard_map/ppermute | solution.py:705
  442.6 21.4 %collective-permute-start.65 = (bf16[2,256,256]{2,1,0:T(8,128)(2,1)}, bf16[2,256,256]{2,1,0:T(8,128)(2,1)S(1)}, u32[]{:S(2)}, u32[]{:S(2)}) collective-permute-start(bf16[2,256,256]{2,1,0:T(8,128)(2,1)} %get-tuple-element.479), channel_id=1, source_target_pairs={{0,16},{16,0},{1,17},{17,1},{2,18},{18,2},{3,19},{19,3},{4,20},{20... | collective-permute-start | bytes 786440 | tf_op jit(solution)/shard_map/ppermute | solution.py:705
  443.0 21.0 %collective-permute-start.63 = (bf16[128,2048]{1,0:T(8,128)(2,1)S(1)}, bf16[128,2048]{1,0:T(8,128)(2,1)S(1)}, u32[]{:S(2)}, u32[]{:S(2)}) collective-permute-start(bf16[128,2048]{1,0:T(8,128)(2,1)S(1)} %copy-done.68), channel_id=1, source_target_pairs={{0,2},{2,0},{1,3},{3,1},{4,6},{6,4},{5,7},{7,5},{8,10},{10,8},{9,1... | collective-permute-start | bytes 1572872 | tf_op jit(solution)/shard_map/ppermute | solution.py:700
  447.5 23.0 %collective-permute-start.67 = (bf16[4,256,256]{2,1,0:T(8,128)(2,1)S(1)}, bf16[4,256,256]{2,1,0:T(8,128)(2,1)S(1)}, u32[]{:S(2)}, u32[]{:S(2)}) collective-permute-start(bf16[4,256,256]{2,1,0:T(8,128)(2,1)S(1)} %copy-done.41), channel_id=1, source_target_pairs={{0,4},{4,0},{1,5},{5,1},{2,6},{6,2},{3,7},{7,3},{8,12},{12,8},{9,1... | collective-permute-start | bytes 1572872 | tf_op jit(solution)/shard_map/ppermute | solution.py:700
  488.7 32.4 %all-to-all-start.3 = ((bf16[4,128,1152]{2,1,0:T(8,128)(2,1)}), bf16[4,128,1152]{2,1,0:T(8,128)(2,1)S(1)}, u32[]{:S(2)}, u32[]{:S(2)}) async-start(bf16[4,128,1152]{2,1,0:T(8,128)(2,1)} %bitcast.100), calls=%async_computation.4 | async-start | bytes 2359296 | tf_op jit(solution)/shard_map/all_to_all | solution.py:745
  493.8 19.5 %collective-permute-start.72 = (f32[49,128]{1,0:T(8,128)S(1)}, f32[49,128]{1,0:T(8,128)S(1)}, u32[]{:S(2)}, u32[]{:S(2)}) collective-permute-start(f32[49,128]{1,0:T(8,128)S(1)} %maximum_bitcast_fusion), channel_id=1, source_target_pairs={{0,2},{2,0},{1,3},{3,1},{4,6},{6,4},{5,7},{7,5},{8,10},{10,8},{9,1... | collective-permute-start | bytes 75272 | tf_op jit(solution)/shard_map/ppermute | solution.py:700
  495.8 25.3 %collective-permute-start.70 = (bf16[2,256,512]{2,1,0:T(8,128)(2,1)}, bf16[2,256,512]{2,1,0:T(8,128)(2,1)S(1)}, u32[]{:S(2)}, u32[]{:S(2)}) collective-permute-start(bf16[2,256,512]{2,1,0:T(8,128)(2,1)} %get-tuple-element.515), channel_id=1, source_target_pairs={{0,16},{16,0},{1,17},{17,1},{2,18},{18,2},{3,19},{19,3},{4,20},{20... | collective-permute-start | bytes 1572872 | tf_op jit(solution)/shard_map/ppermute | solution.py:705
  521.9 28.0 %all-to-all-start.4 = ((bf16[4,128,1024]{2,1,0:T(8,128)(2,1)}), bf16[4,128,1024]{2,1,0:T(8,128)(2,1)S(1)}, u32[]{:S(2)}, u32[]{:S(2)}) async-start(bf16[4,128,1024]{2,1,0:T(8,128)(2,1)} %bitcast.68), calls=%async_computation.5 | async-start | bytes 2097152 | tf_op jit(solution)/shard_map/all_to_all | solution.py:745
  525.4 24.5 %collective-permute-start.73 = (bf16[2,256,512]{2,1,0:T(8,128)(2,1)}, bf16[2,256,512]{2,1,0:T(8,128)(2,1)S(1)}, u32[]{:S(2)}, u32[]{:S(2)}) collective-permute-start(bf16[2,256,512]{2,1,0:T(8,128)(2,1)} %get-tuple-element.532), channel_id=1, source_target_pairs={{0,16},{16,0},{1,17},{17,1},{2,18},{18,2},{3,19},{19,3},{4,20},{20... | collective-permute-start | bytes 1572872 | tf_op jit(solution)/shard_map/ppermute | solution.py:705
  525.5 23.2 %collective-permute-start.74 = (f32[49,128]{1,0:T(8,128)S(1)}, f32[49,128]{1,0:T(8,128)S(1)}, u32[]{:S(2)}, u32[]{:S(2)}) collective-permute-start(f32[49,128]{1,0:T(8,128)S(1)} %fusion.4), channel_id=1, source_target_pairs={{0,8},{8,0},{1,9},{9,1},{2,10},{10,2},{3,11},{11,3},{4,12},{12,4},... | collective-permute-start | bytes 75272 | tf_op jit(solution)/shard_map/ppermute | solution.py:700
  (153 other events, 1435.6 us)
Sparse Core Ops, SparseCore 0:
  376.9 53.6 reduce-scatter.1

commit v4 on v3

--- a/solution.py
+++ b/solution.py
@@ -43,47 +43,53 @@
     length = seg_col.shape[0]
     row = lax.broadcasted_iota(jnp.int32, (length, length), 0)
     col = lax.broadcasted_iota(jnp.int32, (length, length), 1)
-    return seg_col == seg_row, row, col
+    same = seg_col == seg_row
+    return same & (col <= row), (col <= row).astype(BF), (same & (col >= row)).astype(BF)
 
 
 def strips(length):
     return [(s, -(-(s + STRIP) // 128) * 128) for s in range(0, length, STRIP)]
 
 
-def fill_scores(query, key, totals, allowed, scores):
+def fill_scores(query, key, totals, allowed, scores, kept=None):
     length = query.shape[0]
-    for start, wide in strips(length):
+    for k, (start, wide) in enumerate(strips(length)):
         rows = slice(start, start + STRIP)
         ref = totals[start + STRIP // 2 - 1 : start + STRIP // 2]
-        lead = (query[rows] * jnp.exp(totals[rows] - ref)).astype(BF)
-        trail = (key[:wide] * jnp.exp(jnp.minimum(ref - totals[:wide], CAP))).astype(BF)
+        lead_scale = jnp.exp(totals[rows] - ref)
+        trail_scale = jnp.exp(jnp.minimum(ref - totals[:wide], CAP))
+        lead = (query[rows] * lead_scale).astype(BF)
+        trail = (key[:wide] * trail_scale).astype(BF)
+        if kept is not None:
+            leads, lead_scales, trails, trail_scales = kept
+            leads[rows, :], lead_scales[rows, :] = lead, lead_scale
+            trails[k, :wide, :], trail_scales[k, :wide, :] = trail, trail_scale
         part = jnp.where(allowed[rows, :wide], dot(lead, trail, NT), 0.0)
         scores[rows, :wide] = part.astype(BF)
         if wide < length:
             scores[rows, wide:] = jnp.zeros((STRIP, length - wide), BF)
 
 
-def head_forward(p0, p1, p2, seg_col, seg_row, floor, gain, scores):
+def head_forward(p0, p1, p2, seen, floor, gain, scores):
     swish, gate, forget = gates(p0, p1, floor)
-    same, row, col = masks(seg_col, seg_row)
-    totals = exact_dot((col <= row).astype(BF), jnp.log(forget))
-    fill_scores(p0 * swish, 1.0 - forget, totals, same & (col <= row), scores)
+    allowed, tri, _ = seen
+    totals = exact_dot(tri, jnp.log(forget))
+    fill_scores(p0 * swish, 1.0 - forget, totals, allowed, scores)
     rec = dot(scores[...], p2.astype(BF))
     rms = lax.rsqrt(jnp.mean(rec * rec, axis=-1, keepdims=True) + epsilon)
     return (rec * rms * gain).astype(BF)
 
 
 def head_backward(
-    p0, p1, p2, mixed_grad, seg_col, seg_row, floor, gain, scores, key_grad, decay_grad, query_grad
+    p0, p1, p2, mixed_grad, seen, carry, floor, gain, scores, key_grad, decay_grad, query_grad, *kept
 ):
     length = p0.shape[0]
     swish, gate, forget = gates(p0, p1, floor)
     query = p0 * swish
     key = 1.0 - forget
-    same, row, col = masks(seg_col, seg_row)
-    allowed = same & (col <= row)
-    totals = exact_dot((col <= row).astype(BF), jnp.log(forget))
-    fill_scores(query, key, totals, allowed, scores)
+    allowed, tri, later = seen
+    totals = exact_dot(tri, jnp.log(forget))
+    fill_scores(query, key, totals, allowed, scores, kept)
     value = p2.astype(BF)
     rec = dot(scores[...], value)
     rms = lax.rsqrt(jnp.mean(rec * rec, axis=-1, keepdims=True) + epsilon)
@@ -95,13 +101,11 @@
     score_grad = jnp.where(allowed, dot(rec_low, value, NT), 0.0).astype(BF)
     key_grad[...] = jnp.zeros_like(key_grad)
     decay_grad[...] = jnp.zeros_like(decay_grad)
-    for start, wide in strips(length):
+    leads, lead_scales, trails, trail_scales = kept
+    for k, (start, wide) in enumerate(strips(length)):
         rows = slice(start, start + STRIP)
-        ref = totals[start + STRIP // 2 - 1 : start + STRIP // 2]
-        lead_scale = jnp.exp(totals[rows] - ref)
-        trail_scale = jnp.exp(jnp.minimum(ref - totals[:wide], CAP))
-        lead = (query[rows] * lead_scale).astype(BF)
-        trail = (key[:wide] * trail_scale).astype(BF)
+        lead, lead_scale = leads[rows, :], lead_scales[rows, :]
+        trail, trail_scale = trails[k, :wide, :], trail_scales[k, :wide, :]
         part = score_grad[rows, :wide]
         lead_grad = dot(part, trail)
         trail_grad = dot(part, lead, TN)
@@ -109,9 +113,6 @@
         key_grad[:wide, :] += trail_grad * trail_scale
         decay_grad[:wide, :] -= trail_grad * trail.astype(jnp.float32)
         decay_grad[rows, :] += lead_grad * lead.astype(jnp.float32)
-    before = jnp.concatenate([seg_col[:1] - 1, seg_col[:-1]], axis=0)
-    carry = (seg_col == before).astype(jnp.float32)
-    later = (same & (col >= row)).astype(BF)
     forget_grad = exact_dot(later, decay_grad[...]) * carry / forget
     joint = forget_grad - key_grad[...]
     floor_sum = jnp.sum(joint * (1.0 - gate), axis=0, keepdims=True)
@@ -172,9 +173,21 @@
     return [pltpu.VMEM((4, 2 * count, model), BF), pltpu.SemaphoreType.DMA((2, 4))]
 
 
+def store_sends(values, send_ref, last_ref):
+    sequence = pl.program_id(0)
+
+    @pl.when(sequence < 3)
+    def _():
+        send_ref[0] = values.astype(BF)
+
+    @pl.when(sequence == 3)
+    def _():
+        last_ref[...] = values.astype(BF)
+
+
 def mixer_forward_kernel(core_ref, offsets_ref, *refs, sources):
     rows, refs = refs[:6], refs[6:]
-    (col_ref, row_ref, floor_ref, gain_ref, p_ref, mixed_ref, send_ref, keep_ref, scores, whole,
+    (col_ref, row_ref, floor_ref, gain_ref, p_ref, mixed_ref, send_ref, last_ref, keep_ref, scores, whole,
      back, tokens, token_sems, weight, sems) = refs[len(sources) :]
 
     sequence = pl.program_id(0)
@@ -191,22 +204,23 @@
     mine = pl.multiple_of(core_ref[0] * count, count)
     theirs = pl.multiple_of((1 - core_ref[0]) * count, count)
     p_ref[0] = dot(tokens[sequence], weight[:, : 3 * width])
+    seen = masks(col_ref[0], row_ref[0])
     for h in range(width // HEAD):
         p0, p1, p2 = [p_ref[0, :, pl.ds(j * width + h * HEAD, HEAD)] for j in range(3)]
         lanes = slice(h * HEAD, (h + 1) * HEAD)
         whole[:, lanes] = head_forward(
-            p0, p1, p2, col_ref[0], row_ref[0], floor_ref[:, lanes], gain_ref[...], scores.at[h]
+            p0, p1, p2, seen, floor_ref[:, lanes], gain_ref[...], scores.at[h]
         )
     mixed_ref[0] = whole[...]
     back[...] = dot(whole[...], weight[:, 3 * width :], NT)
-    send_ref[0] = back[pl.ds(theirs, count), :].astype(BF)
+    store_sends(back[pl.ds(theirs, count), :], send_ref, last_ref)
     keep_ref[0] = back[pl.ds(mine, count), :]
 
 
 def mixer_backward_kernel(core_ref, offsets_ref, *refs, sources):
     rows, refs = refs[:6], refs[6:]
-    (p_ref, col_ref, row_ref, floor_ref, gain_ref, g_one_ref, g_two_ref, send_ref, keep_ref,
-     floor_sum_ref, gain_sum_ref, scores, key_grad, decay_grad, query_grad, mixed_grad, parts,
+    (p_ref, col_ref, row_ref, floor_ref, gain_ref, g0_ref, g1_ref, g2_ref, send_ref, last_ref, keep_ref,
+     floor_sum_ref, gain_sum_ref, scores, key_grad, decay_grad, query_grad, *kept, mixed_grad, parts,
      back, tokens, token_sems, weight, sems) = refs[len(sources) :]
 
     sequence = pl.program_id(0)
@@ -222,23 +236,28 @@
     width = mixed_grad.shape[1]
     mine = pl.multiple_of(core_ref[0] * count, count)
     theirs = pl.multiple_of((1 - core_ref[0]) * count, count)
+    seg_col = col_ref[0]
+    before = jnp.concatenate([seg_col[:1] - 1, seg_col[:-1]], axis=0)
+    carry = (seg_col == before).astype(jnp.float32)
     mixed_grad[...] = dot(tokens[sequence], weight[:, 3 * width :])
+    seen = masks(col_ref[0], row_ref[0])
     for h in range(width // HEAD):
         p0, p1, p2 = [p_ref[0, :, pl.ds(j * width + h * HEAD, HEAD)] for j in range(3)]
         lanes = slice(h * HEAD, (h + 1) * HEAD)
         g0, g1, g2, floor_sum, gain_sum = head_backward(
-            p0, p1, p2, mixed_grad[:, lanes], col_ref[0], row_ref[0], floor_ref[:, lanes],
+            p0, p1, p2, mixed_grad[:, lanes], seen, carry, floor_ref[:, lanes],
             gain_ref[...], scores.at[h], key_grad.at[h], decay_grad.at[h], query_grad.at[h],
+            *[ref.at[h] for ref in kept],
         )
         for j, g in enumerate((g0, g1, g2)):
             parts[:, pl.ds(j * width + h * HEAD, HEAD)] = g
         floor_sum_ref[0, :, lanes] = jnp.broadcast_to(floor_sum, (8, HEAD)) * 0.125
         gain_sum_ref[0, :, lanes] = jnp.broadcast_to(gain_sum, (8, HEAD)) * 0.125
 
-    g_one_ref[0] = parts[:, : 2 * width]
-    g_two_ref[0] = parts[:, 2 * width :]
+    for j, g_ref in enumerate((g0_ref, g1_ref, g2_ref)):
+        g_ref[0] = parts[:, j * width : (j + 1) * width]
     back[...] = dot(parts[...], weight[:, : 3 * width], NT)
-    send_ref[0] = back[pl.ds(theirs, count), :].astype(BF)
+    store_sends(back[pl.ds(theirs, count), :], send_ref, last_ref)
     keep_ref[0] = back[pl.ds(mine, count), :]
 
 
@@ -246,14 +265,18 @@
     def at(shape, index):
         return pl.BlockSpec(shape, lambda s, c, o: index(s))
 
-    side = at((1, count, model), lambda s: (s, 0, 0))
+    side = [
+        at((1, count, model), lambda s: (jnp.minimum(s, 2), 0, 0)),
+        at((count, model), lambda s: (0, 0)),
+        at((1, count, model), lambda s: (s, 0, 0)),
+    ]
     col = at((1, length, 1), lambda s: (s, 0, 0))
     row = at((1, 1, length), lambda s: (s, 0, 0))
     floor = at((1, width), lambda s: (0, 0))
     gain = at((1, HEAD), lambda s: (0, 0))
     wide = at((1, length, 3 * width), lambda s: (s, 0, 0))
-    pairs = [at((1, length, k * width), lambda s: (s, 0, 0)) for k in (1, 2)]
-    return at, side, wide, pairs, [col, row, floor, gain]
+    pair = at((1, length, width), lambda s: (s, 0, 0))
+    return at, side, wide, pair, [col, row, floor, gain]
 
 
 def weight_scratch(model, lanes, sources):
@@ -265,11 +288,10 @@
 
 
 def mixer_forward(core, offsets, tokens, sources, segments, floor, gain):
-    groups, length = segments.shape
+    groups, length, _ = segments[0].shape
     count, model = tokens[0].shape
     width = floor.shape[0]
-    half = (groups, count, model)
-    at, side, wide, pairs, small = mixer_specs(count, model, width, length)
+    at, side, wide, pair, small = mixer_specs(count, model, width, length)
     layout, parts = layout_of(sources)
     shape = jax.ShapeDtypeStruct
     return pl.pallas_call(
@@ -278,7 +300,7 @@
             num_scalar_prefetch=2,
             grid=(groups,),
             in_specs=[pl.BlockSpec(memory_space=pl.ANY)] * (6 + len(parts)) + small,
-            out_specs=[wide, pairs[0], side, side],
+            out_specs=[wide, pair] + side,
             scratch_shapes=[
                 pltpu.VMEM((width // HEAD, length, length), BF),
                 pltpu.VMEM((length, width), BF),
@@ -290,24 +312,24 @@
         out_shape=[
             shape((groups, length, 3 * width), jnp.float32),
             shape((groups, length, width), BF),
-            shape(half, BF),
-            shape(half, jnp.float32),
+            shape((groups - 1, count, model), BF),
+            shape((count, model), BF),
+            shape((groups, count, model), jnp.float32),
         ],
         compiler_params=PARAMS,
         cost_estimate=LONG,
         name="mixer_forward",
     )(
-        core, offsets, *tokens, *parts, segments[:, :, None],
-        segments[:, None, :], floor[None], gain[None],
+        core, offsets, *tokens, *parts, segments[0],
+        segments[1], floor[None], gain[None],
     )
 
 
 def mixer_backward(core, offsets, tokens, sources, projected, segments, floor, gain):
-    groups, length = segments.shape
+    groups, length, _ = segments[0].shape
     count, model = tokens[0].shape
     width = floor.shape[0]
-    half = (groups, count, model)
-    at, side, wide, pairs, small = mixer_specs(count, model, width, length)
+    at, side, wide, pair, small = mixer_specs(count, model, width, length)
     layout, parts = layout_of(sources)
     heads = width // HEAD
     sums = at((1, 8, width), lambda s: (s, 0, 0))
@@ -320,33 +342,40 @@
             in_specs=[pl.BlockSpec(memory_space=pl.ANY)] * (6 + len(parts))
             + [wide]
             + small,
-            out_specs=[pairs[1], pairs[0], side, side, sums, sums],
+            out_specs=[pair] * 3 + side + [sums, sums],
             scratch_shapes=[pltpu.VMEM((heads, length, length), BF)]
             + [pltpu.VMEM((heads, length, HEAD), jnp.float32)] * 3
+            + [pltpu.VMEM((heads, length, HEAD), kind) for kind in (BF, jnp.float32)]
+            + [
+                pltpu.VMEM((heads, length // STRIP, length, HEAD), kind)
+                for kind in (BF, jnp.float32)
+            ]
             + [pltpu.VMEM((length, width), jnp.float32), pltpu.VMEM((length, 3 * width), BF)]
             + [pltpu.VMEM((length, model), jnp.float32)]
             + row_scratch(count, model)
             + weight_scratch(model, 4 * width, parts),
         ),
         out_shape=[
-            shape((groups, length, 2 * width), BF),
             shape((groups, length, width), BF),
-            shape(half, BF),
-            shape(half, jnp.float32),
+            shape((groups, length, width), BF),
+            shape((groups, length, width), BF),
+            shape((groups - 1, count, model), BF),
+            shape((count, model), BF),
+            shape((groups, count, model), jnp.float32),
         ]
         + [shape((groups, 8, width), jnp.float32)] * 2,
         compiler_params=PARAMS,
         cost_estimate=LONG,
         name="mixer_backward",
     )(
-        core, offsets, *tokens, *parts, projected, segments[:, :, None],
-        segments[:, None, :], floor[None], gain[None],
+        core, offsets, *tokens, *parts, projected, segments[0],
+        segments[1], floor[None], gain[None],
     )
 
 
 def ffn_kernel(core_ref, offsets_ref, *refs, sources, units):
     rows, tops, refs = refs[:6], refs[6:12], refs[12:]
-    (*parts, send_ref, keep_ref, grads, back,
+    (*parts, send_ref, last_ref, keep_ref, grads, back,
      tokens, token_sems, top_tokens, top_sems, weight, sems) = refs[len(sources) :]
 
     sequence = pl.program_id(0)
@@ -378,7 +407,7 @@
         part_ref[0] = grads[:, low : low + part_ref.shape[2]]
         low += part_ref.shape[2]
     back[...] = dot(grads[:, : 2 * width], weight[:, : 2 * width], NT)
-    send_ref[0] = back[pl.ds(theirs, count), :].astype(BF)
+    store_sends(back[pl.ds(theirs, count), :], send_ref, last_ref)
     keep_ref[0] = back[pl.ds(mine, count), :]
 
 
@@ -398,7 +427,12 @@
             num_scalar_prefetch=2,
             grid=(groups,),
             in_specs=[pl.BlockSpec(memory_space=pl.ANY)] * (12 + len(parts)),
-            out_specs=[at(length, n) for n in widths] + [at(length // 2, model)] * 2,
+            out_specs=[at(length, n) for n in widths]
+            + [
+                pl.BlockSpec((1, count, model), lambda s, c, o: (jnp.minimum(s, 2), 0, 0)),
+                pl.BlockSpec((count, model), lambda s, c, o: (0, 0)),
+                at(count, model),
+            ],
             scratch_shapes=[
                 pltpu.VMEM((length, total), BF),
                 pltpu.VMEM((length, model), jnp.float32),
@@ -408,8 +442,9 @@
         ),
         out_shape=[
             *[shape((groups, length, n), BF) for n in widths],
-            shape((groups, length // 2, model), BF),
-            shape((groups, length // 2, model), jnp.float32),
+            shape((groups - 1, count, model), BF),
+            shape((count, model), BF),
+            shape((groups, count, model), jnp.float32),
         ],
         compiler_params=PARAMS,
         cost_estimate=LONG,
@@ -493,26 +528,48 @@
     return lax.rsqrt(jnp.mean(values * values, axis=-1, keepdims=True) + epsilon)
 
 
-def cores_kernel(keep_ref, came_ref, own_ref, x_ref, z_ref, xz_ref):
+def last_kernel(keep_ref, came_ref, out_ref):
+    out_ref[...] = (keep_ref[0] + came_ref[...].astype(jnp.float32)).astype(BF)
+
+
+def add_last(keep, came):
+    count, model = came.shape
+    block = count // 2
+    return pl.pallas_call(
+        last_kernel,
+        grid=(2,),
+        in_specs=[
+            pl.BlockSpec((1, block, model), lambda i: (3, i, 0)),
+            pl.BlockSpec((block, model), lambda i: (i, 0)),
+        ],
+        out_specs=pl.BlockSpec((block, model), lambda i: (i, 0)),
+        out_shape=jax.ShapeDtypeStruct(came.shape, BF),
+        compiler_params=PARAMS,
+        cost_estimate=SHORT,
+        name="add_last",
+    )(keep, came)
+
+
+def cores_kernel(keep_ref, came_ref, own_ref, x_ref, z_ref):
     own_ref[...] = keep_ref[0] + came_ref[0].astype(jnp.float32)
-    for m, out_ref in enumerate((x_ref, z_ref, xz_ref), 1):
+    for m, out_ref in enumerate((x_ref, z_ref), 1):
         out_ref[...] = (keep_ref[m] + came_ref[m].astype(jnp.float32)).astype(BF)
 
 
-def add_cores(keep, came, estimate=SHORT):
+def add_cores(keep, came):
     count, model = keep.shape[1:]
-    block = count // 4
-    both = pl.BlockSpec((4, block, model), lambda i: (0, i, 0))
+    block = count // 2
+    three = pl.BlockSpec((3, block, model), lambda i: (0, i, 0))
     one = pl.BlockSpec((block, model), lambda i: (i, 0))
     shape = jax.ShapeDtypeStruct
     return pl.pallas_call(
         cores_kernel,
-        grid=(4,),
-        in_specs=[both, both],
-        out_specs=[one] * 4,
-        out_shape=[shape((count, model), jnp.float32)] + [shape((count, model), BF)] * 3,
+        grid=(2,),
+        in_specs=[three, three],
+        out_specs=[one] * 3,
+        out_shape=[shape((count, model), jnp.float32)] + [shape((count, model), BF)] * 2,
         compiler_params=PARAMS,
-        cost_estimate=estimate,
+        cost_estimate=SHORT,
         name="add_cores",
     )(keep, came)
 
@@ -566,7 +623,7 @@
 
 def mix_grad_kernel(parts_ref, out_ref):
     quarter = parts_ref.shape[2] // 4
-    for j, at in enumerate((2, 3, 0, 1)):
+    for j, at in enumerate((1, 3, 0, 2)):
         for m in range(4):
             part = parts_ref[m, :, at * quarter : (at + 1) * quarter]
             out_ref[:, j, m * quarter : (m + 1) * quarter] = part.astype(jnp.float32)
@@ -574,7 +631,7 @@
 
 def mix_grad_of(parts):
     _, rows, wide = parts.shape
-    block = min(rows, 32)
+    block = min(rows, 64)
     return pl.pallas_call(
         mix_grad_kernel,
         grid=(rows // block,),
@@ -802,6 +859,15 @@
     return (keep.astype(jnp.float32) + came.astype(jnp.float32)).astype(BF)
 
 
+def sum_pair(values, first, second):
+    parts = [values, swap(values, (second,)), swap(values, (first,)), swap(values, (first, second))]
+    return jnp.stack(parts), lax.axis_index(first) * 2 + lax.axis_index(second)
+
+
+def add_pair(parts, place):
+    return sum(pick(parts, place ^ m) for m in range(4))
+
+
 def sum_highs(values):
     size, bits = lax.axis_size("h"), 1
     while bits < size:
@@ -852,7 +918,7 @@
     labels = mix[:, rows, :length].astype(jnp.int32)
     labels = jnp.stack([pick(labels, member ^ m) for m in range(4)])
     mix = mix[:, :rows]
-    cuts = [0, 384, 768, 1024, 1408, 1664, 1920, lanes]
+    cuts = [0, 512, 1024, 1152, 1408, 1664, 1920, lanes]
     feed_cut = cuts[4]
     mix_far = far(mix)
     mix_near = over_y(mix)
@@ -861,62 +927,69 @@
     normed_x, normed_z = over_x(normed), over_z(normed)
     top_x = over_x(after(out_grad, gate))
 
-    gate = (mix_far, mix_near, feed_one, feed_rest, normed_x, normed_z, top_x)
+    columns = jnp.broadcast_to(labels[:, :, None], labels.shape + (1,))
+    gate = (mix_far, mix_near, feed_one, feed_rest, normed_x, normed_z, top_x, floor, columns)
+    floor = after(floor, gate)
+    labels = (after(columns, gate), labels[:, None, :])
     mix_cross = near(after(mix_far, gate))
     ones = [feed_one[..., low:high] for low, high in zip(cuts[:4], cuts[1:5])]
     far_a = far(after(ones[0], gate))
     normed_xz = over_x(after(normed_z, gate))
     normed_three = jnp.stack(after([normed, normed_x, normed_z], gate))
     top_z = over_z(after(out_grad, gate))
-
-    gate = (mix_cross, far_a, normed_xz, normed_three, top_z, ones)
+    near_a = over_y(after(feed_one[..., :256], gate))
+
+    gate = (mix_cross, far_a, normed_xz, normed_three, top_z, ones, near_a)
     normed_c, normed_cxz = over_c(after(normed_three, gate)), over_c(after(normed_xz, gate))
-    top_three = jnp.stack(after([out_grad, top_x, top_z], gate))
     normed = [normed, normed_x, normed_z, normed_xz, normed_c, normed_cxz]
     mix_sources = [(0, 0, mix), (1, 0, mix_near)] + pieces(0, mix_far, mix_cross)
 
-    gate = (normed_c, normed_cxz, top_three)
+    gate = (normed_c, normed_cxz)
     far_b = far(after(ones[1], gate))
-    near_a = over_y(after(feed_one[..., :640], gate))
+    near_b = over_y(after(feed_one[..., 256:768], gate))
     cross_a = near(after(far_a, gate))
     top_xz = over_x(after(top_z, gate))
-    projected, mixed, send, keep = mixer_forward(
+    feed_two = trade(after(feed_rest, gate))
+    projected, mixed, send, send_xz, keep = mixer_forward(
         core_at, offsets, after(normed, gate), mix_sources, labels, floor, head_gain
     )
 
-    gate = (send, far_b, near_a, cross_a, top_xz)
+    gate = (send, far_b, near_b, cross_a, top_xz, feed_two)
+    came_xz = over_c(after(send_xz, gate))
     came = over_c(after(send, gate))
+    near_c = over_y(after(feed_one[..., 768:1024], gate))
     far_c = far(after(ones[2], gate))
-    near_b = over_y(after(feed_one[..., 640:1024], gate))
-    feed_two = trade(after(feed_rest, gate))
-    top_c = over_c(after(top_three, gate))
-    own, to_x, to_z, to_xz = add_cores(keep, came)
-
-    gate = (own, far_c, near_b, top_c)
+    to_xz = add_last(keep, came_xz)
+
+    gate = (to_xz, near_c, far_c)
     from_x = over_x(after(to_xz, gate))
     far_d = far(after(ones[3], gate))
-    near_c = over_y(after(feed_one[..., 1024:], gate))
     cross_b = near(after(far_b, gate))
-    top_cxz = over_c(after(top_xz, gate))
-    tops = [out_grad, top_x, top_z, top_xz, top_c, top_cxz]
-
-    gate = (from_x, far_d, near_c, cross_b, top_cxz, feed_two)
+    own, to_x, to_z = add_cores(keep, after(came, gate))
+    top_three = jnp.stack(after([out_grad, top_x, top_z], gate))
+
+    gate = (from_x, far_d, cross_b, own, top_three)
     to_z = add_low(to_z, after(from_x, gate))
     of_x = over_x(after(to_x, gate))
     of_z = over_z(to_z)
     far_e = far(after(feed_two[..., : cuts[5] - feed_cut], gate))
-    near_d = over_y(after(feed_two, gate))
-
-    gate = (of_x, of_z, far_e, near_d)
+    near_d = over_y(after(feed_one[..., 1024:], gate))
+    near_e = over_y(after(feed_two[..., :384], gate))
+
+    gate = (of_x, of_z, far_e, near_d, near_e)
     far_f = far(after(feed_two[..., cuts[5] - feed_cut : cuts[6] - feed_cut], gate))
-    cross_c, cross_d = near(after(far_c, gate)), near(after(far_d, gate))
+    near_f = over_y(after(feed_two[..., 384:], gate))
+    cross_cd = [
+        over_y(jnp.concatenate([one, two], axis=-1))
+        for one, two in zip(after(far_c, gate), after(far_d, gate))
+    ]
     middle, normed_two = row_call(
         middle_kernel, "middle", [jnp.float32, BF], *after((own, of_x, of_z), gate), hidden_in,
         norm2_gain[None],
     )
     two_x, two_z = over_x(normed_two), over_z(normed_two)
 
-    gate = (far_f, cross_c, cross_d, two_x, two_z)
+    gate = (far_f, near_f, cross_cd, two_x, two_z)
     far_g = far(after(feed_two[..., cuts[6] - feed_cut :], gate))
     cross_e, cross_f = near(after(far_e, gate)), near(after(far_f, gate))
     two_xz = over_x(after(two_z, gate))
@@ -925,27 +998,33 @@
     gate = (far_g, cross_e, cross_f, two_xz, two_three)
     cross_g = near(after(far_g, gate))
     two_c, two_cxz = over_c(after(two_three, gate)), over_c(after(two_xz, gate))
+    top_c, top_cxz = over_c(after(top_three, gate)), over_c(after(top_xz, gate))
+    tops = [out_grad, top_x, top_z, top_xz, top_c, top_cxz]
     normed_two = [normed_two, two_x, two_z, two_xz, two_c, two_cxz]
     feed_sources = [(0, 0, feed_one), (0, feed_cut, feed_two)]
-    feed_sources += [(1, 0, near_a), (1, 640, near_b), (1, 1024, near_c), (1, feed_cut, near_d)]
+    feed_sources += [(1, 0, near_a), (1, 256, near_b), (1, 768, near_c), (1, 1024, near_d)]
+    feed_sources += [(1, feed_cut, near_e), (1, feed_cut + 384, near_f)]
     fars = [far_a, far_b, far_c, far_d, far_e, far_f, far_g]
-    crosses = [cross_a, cross_b, cross_c, cross_d, cross_e, cross_f, cross_g]
-    for low, straight, crossed in zip(cuts, fars, crosses):
-        feed_sources += pieces(low, straight, crossed)
-
-    widths = [128, 256, 384, 256, 384, 256, 256, lanes - 1920]
-    *grads, send, keep = ffn(core_at, offsets, normed_two, tops, feed_sources, units, widths)
-    gates, downs = grads[:5], grads[5:]
-    came = over_c(send)
+    for low, part in zip(cuts, fars):
+        feed_sources += [(2 * k, low, one) for k, one in enumerate(part, 1)]
+    crosses = [cross_a, cross_b, cross_cd, cross_e, cross_f, cross_g]
+    for low, part in zip(cuts[:3] + cuts[4:], crosses):
+        feed_sources += [(2 * k + 1, low, one) for k, one in enumerate(part, 1)]
+
+    widths = [128, 256, 384, 256, 256, 128, 256, 256, lanes - 1920]
+    *grads, send, send_xz, keep = ffn(core_at, offsets, normed_two, tops, feed_sources, units, widths)
+    gates, downs = grads[:6], grads[6:]
+    came_xz, came = over_c(send_xz), over_c(send)
     down_sends = grad_sends(core_at, after(tops, send), downs, LONG)
-    own, to_x, to_z, to_xz = add_cores(keep, after(came, down_sends))
-
-    gate = (own,)
+    to_xz = add_last(keep, after(came_xz, down_sends))
+
+    gate = (to_xz,)
     from_x = over_x(after(to_xz, gate))
     down_one = over_y(after(down_sends[0], gate))
     gate_sends = grad_sends(core_at, after(normed_two, gate), gates, LONG)
-
-    gate = (from_x, down_one, gate_sends)
+    own, to_x, to_z = add_cores(keep, after(came, gate_sends))
+
+    gate = (from_x, down_one, own)
     to_z = add_low(to_z, after(from_x, gate))
     of_x = over_x(after(to_x, gate))
     of_z = over_z(to_z)
@@ -995,45 +1074,53 @@
         after(branch, gate).reshape(-1, model), GROUP + ("tensor",), scatter_dimension=0, tiled=True
     )
     middle_full = after(middle_full, gate)
-    g_one, g_two, send, keep, floor_sums, gain_sums = mixer_backward(
+    *mix_grads, send, send_xz, keep, floor_sums, gain_sums = mixer_backward(
         core_at, offsets, middle_full, mix_sources, projected, labels, floor, head_gain
     )
 
     gate = (send, one_fars, three_came, four_came)
-    came = over_c(after(send, gate))
+    came_xz, came = over_c(after(send_xz, gate)), over_c(after(send, gate))
     five_came = over_y(after(gate_sends[4], gate))
     three_home, three_away = near_sums([(gate_keeps[2], after(three_came, gate))], LONG)
-    own, to_x, to_z, to_xz = add_cores(keep, after(came, three_away))
-
-    gate = (own,)
+    to_xz = add_last(keep, after(came_xz, three_away))
+
+    gate = (to_xz,)
     three_fars = send_far(after(three_away, gate))
     from_x = over_x(after(to_xz, gate))
-    value_send, pair_send = grad_sends(core_at, after(normed, gate), [g_two, g_one], LONG)
-    (last_send,) = grad_sends(core_at, after(middle_full, value_send), [mixed])
-    four_home, four_away = near_sums([(gate_keeps[3], after(four_came, last_send))])
-
-    gate = (from_x, three_fars, four_away, five_came)
+    six_came = over_y(after(gate_sends[5], gate))
+    query_send, forget_send, value_send = grad_sends(core_at, after(normed, gate), mix_grads, LONG)
+    own, to_x, to_z = add_cores(keep, after(came, value_send))
+    four_home, four_away = near_sums(
+        [
+            (gate_keeps[3], after(four_came, own)),
+            (gate_keeps[4], five_came),
+            (gate_keeps[5], six_came),
+        ]
+    )
+
+    gate = (from_x, three_fars, four_away)
     four_fars = send_far(after(four_away, gate))
     to_z = add_low(to_z, after(from_x, gate))
     of_x = over_x(after(to_x, gate))
     of_z = over_z(to_z)
-    value_came, last_came = over_y(after(value_send, gate)), over_y(after(last_send, gate))
-    value_keep, pair_keep = grad_keeps(core_at, after(normed, gate), [g_two, g_one], LONG)
-    five_home, five_away = near_sums([(gate_keeps[4], after(five_came, value_keep))])
-    (last_keep,) = grad_keeps(core_at, after(middle_full, five_away), [mixed])
-
-    gate = (of_x, of_z, four_fars, value_came, last_came, last_keep)
-    five_fars = send_far(after(five_away, gate))
-    query_came = over_y(after(pair_send[..., :quarter], gate))
+    value_came, query_came = over_y(after(value_send, gate)), over_y(after(query_send, gate))
+    query_keep, forget_keep, value_keep = grad_keeps(core_at, after(normed, gate), mix_grads, LONG)
+    (last_send,) = grad_sends(core_at, after(middle_full, value_keep), [mixed])
+    down_parts = [(down_home, down_fars), (down_home_two, down_fars_two), (one_home, one_fars)]
+    down_parts = far_sums(after(down_parts, last_send))
+    near_home, near_away = near_sums(
+        [(value_keep, after(value_came, down_parts)), (query_keep, query_came)]
+    )
+
+    gate = (of_x, of_z, four_fars, near_away)
+    near_fars = send_far(after(near_away, gate))
+    last_came, forget_came = over_y(after(last_send, gate)), over_y(after(forget_send, gate))
+    down_parts = trade(after(down_parts, gate))
     input_grad, _, gain_one_grad = row_call(
         back_kernel, "input_grad", [jnp.float32, BF, None], *after((own, of_x, of_z), gate),
         hidden_in, middle_grad, norm1_gain[None],
     )
-    near_home, near_away = near_sums(
-        [(value_keep, after(value_came, input_grad)), (last_keep, last_came)]
-    )
-    down_parts = [(down_home, down_fars), (down_home_two, down_fars_two), (one_home, one_fars)]
-    down_parts = far_sums(after(down_parts, near_away))
+    (last_keep,) = grad_keeps(core_at, after(middle_full, input_grad), [mixed])
     head_grad = jnp.sum(after(gain_sums, gate).reshape(-1, HEAD), axis=0)
     lower_grad = jnp.zeros((2, 4, quarter), jnp.float32)
     lower_grad = lax.dynamic_update_slice(
@@ -1043,32 +1130,25 @@
     )
     sums = [gain_one_grad[0], gain_two_grad[0], head_grad, lower_grad.reshape(-1)]
     sums = jnp.concatenate(sums).reshape(-1, HEAD)
-
-    gate = (five_fars, query_came, near_away, down_parts, sums)
-    near_fars = send_far(after(near_away, gate))
-    forget_came = over_y(after(pair_send[..., quarter:], gate))
-    down_parts = trade(after(down_parts, gate))
-    sums_x = over_x(after(sums, gate))
-    block_out = (middle + after(branch, gate).astype(jnp.float32)).astype(BF)
-    gate_parts = [(three_home, three_fars), (four_home, four_fars), (five_home, five_fars)]
-    gate_parts = far_sums(after(gate_parts, gate))
-    pair_came = jnp.concatenate([query_came, after(forget_came, gate_parts)], axis=-1)
-    pair_home, pair_away = near_sums([(pair_keep, pair_came)])
-
-    gate = (near_fars, down_parts, sums_x, pair_away, gate_parts, block_out)
+    block_out = (middle + after(branch, last_keep).astype(jnp.float32)).astype(BF)
+    gate_parts = [(three_home, three_fars), (four_home, four_fars)]
+    gate_parts = far_sums(after(gate_parts, block_out))
+    pair_home, pair_away = near_sums(
+        [(last_keep, after(last_came, gate_parts)), (forget_keep, forget_came)]
+    )
+
+    gate = (near_fars, down_parts, sums, pair_away, gate_parts, block_out)
     pair_fars = send_far(after(pair_away, gate))
     gate_parts = trade(after(gate_parts, gate))
-    sums = sums + sums_x
-    sums_z = over_z(after(sums, gate))
-
-    gate = (pair_fars, gate_parts, sums_z)
-    mix_parts = trade(far_sums(after([(near_home, near_fars), (pair_home, pair_fars)], gate)))
+    sums, place = sum_pair(after(sums, gate), "l", "x")
+
+    gate = (pair_fars, gate_parts, sums)
+    mix_parts = far_sums(after([(near_home, near_fars), (pair_home, pair_fars)], gate))
+    sums, place = sum_pair(add_pair(after(sums, mix_parts), place), "y", "tensor")
+    sums = sum_highs(add_pair(sums, place)).reshape(-1)
+    mix_parts = trade(mix_parts)
+    gain_one, gain_two, head, lower = jnp.split(sums, [model, 2 * model, 2 * model + HEAD])
     ffn_grad = ffn_grad_of(after([down_parts, gate_parts], gate), units)
-    sums = sums + sums_z
-    sums = sums + over_y(after(sums, gate))
-    sums = sums + swap(sums, ("tensor",))
-    sums = sum_highs(sums).reshape(-1)
-    gain_one, gain_two, head, lower = jnp.split(sums, [model, 2 * model, 2 * model + HEAD])
     mix_grad = mix_grad_of(mix_parts)
     return (block_out, input_grad, mix_grad, ffn_grad, gain_one, gain_two, head, lower)
 

time: 590 us -> 552 us (0.936)
  waiting for transfers between devices: 206 us -> 166 us
    ppermute x16 -> x15, waiting for transfers between devices: 81.8 us -> 39.8 us  [shift(): lax.ppermute(values, 'h', [(s, (s + steps) % total) for s in range(total)])]
    ppermute x1, waiting for transfers between devices: 7.91 us -> 1.36 us  [sum_highs(): lax.ppermute(values, 'h', [(s, s ^ bits) for s in range(size)])]
    unnamed x202 -> x188, local copies, waits for them, and re-layouts: 17.6 us -> 21.5 us
    ppermute x61 -> x68, waiting for transfers between devices: 111 us -> 115 us  [swap(): lax.ppermute(values, axes, [(s, total - 1 - s) for s in range(total)])]
    ppermute x16 -> x15, starting transfers between devices: 23.1 us -> 19.5 us  [shift(): lax.ppermute(values, 'h', [(s, (s + steps) % total) for s in range(total)])]
    pallas_call x8 -> x7, Pallas kernels: 30.9 us -> 27.7 us  [near_sums(): pl.pallas_call(functools.partial(near_kernel, number=len(pairs), ends=hig...]
    pallas_call x3 -> x6, Pallas kernels: 14.4 us -> 16.9 us  [the longest x3 10.3 us: add_cores(): pl.pallas_call(cores_kernel, grid=(2,), in_specs=[three, three], out_spec...]
    ppermute x61 -> x68, starting transfers between devices: 58.6 us -> 57.2 us  [swap(): lax.ppermute(values, axes, [(s, total - 1 - s) for s in range(total)])]
  transfers between devices with their start and end apart: 85 -> 91, of which waited for: 34 -> 31; matrix products, arithmetic and copies ran while one was open for 5% -> 6% of each run, Pallas kernels for 28% -> 30%
where the time goes in v4:
time: 552 us; the launch traced here: 549 us
  Pallas kernels  210 us (38%)
  waiting for transfers between devices  166 us (30%)
  starting transfers between devices  101 us (18%)
  local copies, waits for them, and re-layouts  42.1 us (8%)
  between operations  15.2 us (3%)
  other arithmetic  15.1 us (3%)
    ppermute x68, waiting for transfers between devices, swap(): lax.ppermute(values, axes, [(s, total - 1 - s) for s in range(total)])  115 us
    ppermute x68, starting transfers between devices, swap(): lax.ppermute(values, axes, [(s, total - 1 - s) for s in range(total)])  57.2 us
    pallas_call x8, Pallas kernels, grad_product(): pl.pallas_call(functools.partial(grad_kernel, number=len(grads)), grid_sp...  54.2 us
    ppermute x15, waiting for transfers between devices, shift(): lax.ppermute(values, 'h', [(s, (s + steps) % total) for s in range(total)])  39.8 us
    pallas_call x1, Pallas kernels, ffn(): pl.pallas_call(functools.partial(ffn_kernel, sources=layout, units=width)...  30.5 us
    pallas_call x7, Pallas kernels, near_sums(): pl.pallas_call(functools.partial(near_kernel, number=len(pairs), ends=hig...  27.7 us
    pallas_call x1, Pallas kernels, mixer_backward(): pl.pallas_call(functools.partial(mixer_backward_kernel, sources=layout),...  23.9 us
    all_to_all x6, starting transfers between devices, trade(): return lax.all_to_all(slices, GROUP, 0, 0, tiled=True)  23 us
  transfers between devices with their start and end apart: 91, of which 31 were waited for; matrix products, arithmetic and copies ran while one was open for 6% of the time, Pallas kernels for 30%

profile of v4, /device:TPU:0, one launch (start us, length us, event | category | flops | bytes accessed | tf_op | source)
XLA Modules:
  0.0 549.2 jit_solution(9933221168919587417)
XLA Ops:
  11.3 5.4 all-to-all-start
  26.9 4.9 all-to-all-done
  49.1 17.0 %collective-permute-done.refs_1_ = bf16[128,2048]{1,0:T(8,128)(2,1)} collective-permute-done((bf16[128,2048]{1,0:T(8,128)(2,1)S(1)}, bf16[128,2048]{1,0:T(8,128)(2,1)}, u32[]{:S(2)}, u32[]{:S(2)}) %collective-permute-start) | collective-permute-done | bytes 524320 | tf_op jit(solution)/shard_map/ppermute | solution.py:757
  66.1 22.1 %collective-permute-done.1.refs_2_ = bf16[128,2048]{1,0:T(8,128)(2,1)} collective-permute-done((bf16[128,2048]{1,0:T(8,128)(2,1)S(1)}, bf16[128,2048]{1,0:T(8,128)(2,1)}, u32[]{:S(2)}, u32[]{:S(2)}) %collective-permute-start.1) | collective-permute-done | bytes 524320 | tf_op jit(solution)/shard_map/ppermute | solution.py:757
  98.3 19.8 %collective-permute-done.9.refs_14_.refs_5_ = bf16[4,128,256]{2,1,0:T(8,128)(2,1)S(1)} collective-permute-done((bf16[4,128,256]{2,1,0:T(8,128)(2,1)S(1)}, bf16[4,128,256]{2,1,0:T(8,128)(2,1)S(1)}, u32[]{:S(2)}, u32[]{:S(2)}) %collective-permute-start.9) | collective-permute-done | bytes 262176 | tf_op jit(solution)/shard_map/ppermute | solution.py:757
  131.1 18.0 %mixer_forward.1 = (f32[4,256,768]{2,1,0:T(8,128)}, bf16[4,256,256]{2,1,0:T(8,128)(2,1)}, bf16[3,128,2048]{2,1,0:T(8,128)(2,1)}, bf16[128,2048]{1,0:T(8,128)(2,1)}, f32[4,128,2048]{2,1,0:T(8,128)}) custom-call(s32[2]{0:T(128)} %pad_add_fusion.1.core_ref, s32[16]{0:T(128)} %stack.222.offsets_ref, bf16[128,2048]{1,0:T(8,128)(2,1)} %fusion.2.refs_0_, ...), custom_call_target="tpu_custom_call" | custom-call | flops 49999998976 | bytes 1 | tf_op jit(solution)/shard_map/mixer_forward/pallas_call | solution.py:297
  172.1 4.9 collective-permute-done.21.refs_23_.refs_14_
  182.7 13.6 %collective-permute-done.25.refs_24_.refs_15_ = bf16[4,128,256]{2,1,0:T(8,128)(2,1)S(1)} collective-permute-done((bf16[4,128,256]{2,1,0:T(8,128)(2,1)S(1)}, bf16[4,128,256]{2,1,0:T(8,128)(2,1)S(1)}, u32[]{:S(2)}, u32[]{:S(2)}) %collective-permute-start.25) | collective-permute-done | bytes 262176 | tf_op jit(solution)/shard_map/ppermute | solution.py:762
  208.6 12.5 %collective-permute-done.30.refs_25_.refs_16_ = bf16[4,128,256]{2,1,0:T(8,128)(2,1)S(1)} collective-permute-done((bf16[4,128,256]{2,1,0:T(8,128)(2,1)S(1)}, bf16[4,128,256]{2,1,0:T(8,128)(2,1)S(1)}, u32[]{:S(2)}, u32[]{:S(2)}) %collective-permute-start.30) | collective-permute-done | bytes 262176 | tf_op jit(solution)/shard_map/ppermute | solution.py:762
  228.9 6.2 %collective-permute-done.34.refs_26_.refs_17_ = bf16[4,128,256]{2,1,0:T(8,128)(2,1)} collective-permute-done((bf16[4,128,256]{2,1,0:T(8,128)(2,1)S(1)}, bf16[4,128,256]{2,1,0:T(8,128)(2,1)}, u32[]{:S(2)}, u32[]{:S(2)}) %collective-permute-start.34) | collective-permute-done | bytes 262176 | tf_op jit(solution)/shard_map/ppermute | solution.py:762
  237.6 7.6 %collective-permute-done.41.refs_32_.refs_23_ = bf16[4,128,256]{2,1,0:T(8,128)(2,1)S(1)} collective-permute-done((bf16[4,128,256]{2,1,0:T(8,128)(2,1)}, bf16[4,128,256]{2,1,0:T(8,128)(2,1)S(1)}, u32[]{:S(2)}, u32[]{:S(2)}) %collective-permute-start.41) | collective-permute-done | bytes 262176 | tf_op jit(solution)/shard_map/ppermute | solution.py:757
  246.5 30.5 %ffn.1 = (bf16[4,256,128]{2,1,0:T(8,128)(2,1)}, bf16[4,256,256]{2,1,0:T(8,128)(2,1)}, bf16[4,256,384]{2,1,0:T(8,128)(2,1)}, bf16[4,256,256]{2,1,0:T(8,128)(2,1)}...) custom-call(s32[2]{0:T(128)} %pad_add_fusion.1.core_ref, ...), custom_call_target="tpu_custom_call" | custom-call | flops 49999998976 | bytes 1 | tf_op jit(solution)/shard_map/ffn/pallas_call | solution.py:424
  277.6 6.3 %grad_product.8 = (bf16[4,256,256]{2,1,0:T(8,128)(2,1)}, bf16[4,256,256]{2,1,0:T(8,128)(2,1)}, bf16[4,256,256]{2,1,0:T(8,128)(2,1)}) custom-call(s32[2]{0:T(128)} %pad_add_fusion.1.core_ref, s32[4]{0:T(128)} %get-tuple-element.582.blocks_ref, bf16[128,2048]{1,0:T(8,128)(2,1)} %add_ref.1, bf16[128,2048]{1,0:T(8,128)(2,1)} %collective-permute-done.4.refs_7_.refs_1_, ...), custom_call_target="tpu_custom_call" | custom-call | flops 49999998976 | bytes 1 | tf_op jit(solution)/shard_map/grad_product/pallas_call | solution.py:509
  288.5 8.9 %grad_product.9 = (bf16[4,256,128]{2,1,0:T(8,128)(2,1)}, bf16[4,256,256]{2,1,0:T(8,128)(2,1)}, bf16[4,256,384]{2,1,0:T(8,128)(2,1)}, bf16[4,256,256]{2,1,0:T(8,1...) custom-call(s32[2]{0:T(128)} %pad_add_fusion.1.core_ref, s32[4]{0:T(128)} %get-tuple-element.582.blocks_ref, ...), custom_call_target="tpu_custom_call" | custom-call | flops 49999998976 | bytes 1 | tf_op jit(solution)/shard_map/grad_product/pallas_call | solution.py:509
  306.3 6.5 %grad_product.10 = (f32[4,256,256]{2,1,0:T(8,128)}, f32[4,256,256]{2,1,0:T(8,128)}, f32[4,256,256]{2,1,0:T(8,128)}) custom-call(s32[2]{0:T(128)} %pad_add_fusion.1.core_ref, s32[4]{0:T(128)} %get-tuple-element.583.blocks_ref, bf16[128,2048]{1,0:T(8,128)(2,1)} %add_ref.1, bf16[128,2048]{1,0:T(8,128)(2,1)} %collective-permute-done.4.refs_7_.refs_1_, ...), custom_call_target="tpu_custom_call" | custom-call | flops 49999998976 | bytes 1 | tf_op jit(solution)/shard_map/grad_product/pallas_call | solution.py:509
  318.1 4.5 middle_grad.1
  328.2 8.8 %grad_product.11 = (f32[4,256,128]{2,1,0:T(8,128)}, f32[4,256,256]{2,1,0:T(8,128)}, f32[4,256,384]{2,1,0:T(8,128)}, f32[4,256,256]{2,1,0:T(8,128)}, f32[4,256,256]{2,1,0:T(8,128)}, /*index=5*/f32[4,256,128]{2,1,0:T(8,128)}) custom-call(s32[2]{0:T(128)} %pad_add_fusion.1.core_ref, s32[4]{0:T(128)} %get-tuple-element.583.blocks_ref, ...), custom_call_target="tpu_custom_call" | custom-call | flops 49999998976 | bytes 1 | tf_op jit(solution)/shard_map/grad_product/pallas_call | solution.py:509
  346.6 9.8 %rows_product.1 = bf16[4,256,2048]{2,1,0:T(8,128)(2,1)} custom-call(s32[2]{0:T(128)} %pad_add_fusion.1.core_ref, s32[16]{0:T(128)} %stack.222.offsets_ref, bf16[4,256,256]{2,1,0:T(8,128)(2,1)} %get-tuple-element.431.refs_0_, bf16[4,256,256]{2,1,0:T(8,128)(2,1)} %get-tuple-element.432.refs_1_, bf16[4,256,256]{2,1,0:T(8,128)(2,1)} %get-tuple-element.433.refs_2_, ...), custom_call_target="tpu_custom_call" | custom-call | flops 49999998976 | bytes 1 | tf_op jit(solution)/shard_map/rows_product/pallas_call | solution.py:475
  357.5 4.4 near_sums.9
  366.9 23.9 %mixer_backward.1 = (bf16[4,256,256]{2,1,0:T(8,128)(2,1)}, bf16[4,256,256]{2,1,0:T(8,128)(2,1)}, bf16[4,256,256]{2,1,0:T(8,128)(2,1)}, bf16[3,128,2048]{2,1,0:T(...) custom-call(s32[2]{0:T(128)} %pad_add_fusion.1.core_ref, ...), custom_call_target="tpu_custom_call" | custom-call | flops 49999998976 | bytes 1 | tf_op jit(solution)/shard_map/mixer_backward/pallas_call | solution.py:337
  390.8 4.3 collective-permute-done.61.refs_1_
  408.4 6.6 %grad_product.12 = (bf16[4,256,256]{2,1,0:T(8,128)(2,1)}, bf16[4,256,256]{2,1,0:T(8,128)(2,1)}, bf16[4,256,256]{2,1,0:T(8,128)(2,1)}) custom-call(s32[2]{0:T(128)} %pad_add_fusion.1.core_ref, s32[4]{0:T(128)} %get-tuple-element.582.blocks_ref, bf16[128,2048]{1,0:T(8,128)(2,1)} %fusion.2.refs_0_, bf16[128,2048]{1,0:T(8,128)(2,1)} %collective-permute-done.refs_1_, ...), custom_call_target="tpu_custom_call" | custom-call | flops 49999998976 | bytes 1 | tf_op jit(solution)/shard_map/grad_product/pallas_call | solution.py:509
  421.3 4.3 near_sums.11
  432.0 6.5 %grad_product.13 = (f32[4,256,256]{2,1,0:T(8,128)}, f32[4,256,256]{2,1,0:T(8,128)}, f32[4,256,256]{2,1,0:T(8,128)}) custom-call(s32[2]{0:T(128)} %pad_add_fusion.1.core_ref, s32[4]{0:T(128)} %get-tuple-element.583.blocks_ref, bf16[128,2048]{1,0:T(8,128)(2,1)} %fusion.2.refs_0_, bf16[128,2048]{1,0:T(8,128)(2,1)} %collective-permute-done.refs_1_, ...), custom_call_target="tpu_custom_call" | custom-call | flops 49999998976 | bytes 1 | tf_op jit(solution)/shard_map/grad_product/pallas_call | solution.py:509
  438.5 5.2 grad_product.14
  446.8 7.6 %collective-permute-done.72.refs_3_ = bf16[4,256,256]{2,1,0:T(8,128)(2,1)S(1)} collective-permute-done((bf16[4,256,256]{2,1,0:T(8,128)(2,1)S(1)}, bf16[4,256,256]{2,1,0:T(8,128)(2,1)S(1)}, u32[]{:S(2)}, u32[]{:S(2)}) %collective-permute-start.72) | collective-permute-done | bytes 524320 | tf_op jit(solution)/shard_map/ppermute | solution.py:757
  455.2 4.1 near_sums.12
  466.6 4.5 input_grad.1
  471.9 5.5 grad_product.15.refs_0_
  484.6 4.0 near_sums.13
  498.7 19.2 %collective-permute-done.79 = f32[49,128]{1,0:T(8,128)S(1)} collective-permute-done((f32[49,128]{1,0:T(8,128)S(1)}, f32[49,128]{1,0:T(8,128)S(1)}, u32[]{:S(2)}, u32[]{:S(2)}) %collective-permute-start.79) | collective-permute-done | bytes 25120 | tf_op jit(solution)/shard_map/ppermute | solution.py:757
  530.3 4.4 ffn_grad.1
  (425 shorter events, 222.3 us)
Async XLA Ops:
  32.9 55.3 %all-to-all-start.1 = ((bf16[4,128,1408]{2,1,0:T(8,128)(2,1)}), bf16[4,128,1408]{2,1,0:T(8,128)(2,1)S(1)}, u32[]{:S(2)}, u32[]{:S(2)}) async-start(bf16[4,128,1408]{2,1,0:T(8,128)(2,1)} %slice.56), calls=%async_computation.1 | async-start | bytes 2883584 | tf_op jit(solution)/shard_map/all_to_all | solution.py:802
  37.6 50.7 %collective-permute-start.2 = (bf16[4,128,1024]{2,1,0:T(8,128)(2,1)}, bf16[4,128,1024]{2,1,0:T(8,128)(2,1)}, u32[]{:S(2)}, u32[]{:S(2)}) collective-permute-start(bf16[4,128,1024]{2,1,0:T(8,128)(2,1)} %slice.55.refs_6_), channel_id=1, source_target_pairs={{0,16},{16,0},{1,17},{17,1},{2,18},{18,2},{3,19},{19,3},{4,20},{20... | collective-permute-start | bytes 3145736 | tf_op jit(solution)/shard_map/ppermute | solution.py:762
  40.2 48.1 %collective-permute-start.3 = (bf16[4,128,1024]{2,1,0:T(8,128)(2,1)}, bf16[4,128,1024]{2,1,0:T(8,128)(2,1)}, u32[]{:S(2)}, u32[]{:S(2)}) collective-permute-start(bf16[4,128,1024]{2,1,0:T(8,128)(2,1)} %slice.55.refs_6_), channel_id=1, source_target_pairs={{0,4},{4,0},{1,5},{5,1},{2,6},{6,2},{3,7},{7,3},{8,12},{12,8},{9,1... | collective-permute-start | bytes 3145736 | tf_op jit(solution)/shard_map/ppermute | solution.py:757
  41.7 24.5 %collective-permute-start = (bf16[128,2048]{1,0:T(8,128)(2,1)S(1)}, bf16[128,2048]{1,0:T(8,128)(2,1)}, u32[]{:S(2)}, u32[]{:S(2)}) collective-permute-start(bf16[128,2048]{1,0:T(8,128)(2,1)S(1)} %copy-done.10), channel_id=1, source_target_pairs={{0,2},{2,0},{1,3},{3,1},{4,6},{6,4},{5,7},{7,5},{8,10},{10,8},{9,1... | collective-permute-start | bytes 1572872 | tf_op jit(solution)/shard_map/ppermute | solution.py:757
  43.7 44.6 %collective-permute-start.1 = (bf16[128,2048]{1,0:T(8,128)(2,1)S(1)}, bf16[128,2048]{1,0:T(8,128)(2,1)}, u32[]{:S(2)}, u32[]{:S(2)}) collective-permute-start(bf16[128,2048]{1,0:T(8,128)(2,1)S(1)} %copy-done.10), channel_id=1, source_target_pairs={{0,8},{8,0},{1,9},{9,1},{2,10},{10,2},{3,11},{11,3},{4,12},{12,4},... | collective-permute-start | bytes 1572872 | tf_op jit(solution)/shard_map/ppermute | solution.py:757
  45.1 43.2 %collective-permute-start.4 = (bf16[128,2048]{1,0:T(8,128)(2,1)}, bf16[128,2048]{1,0:T(8,128)(2,1)}, u32[]{:S(2)}, u32[]{:S(2)}) collective-permute-start(bf16[128,2048]{1,0:T(8,128)(2,1)} %add_ref.1), channel_id=1, source_target_pairs={{0,2},{2,0},{1,3},{3,1},{4,6},{6,4},{5,7},{7,5},{8,10},{10,8},{9,1... | collective-permute-start | bytes 1572872 | tf_op jit(solution)/shard_map/ppermute | solution.py:757
  88.3 29.9 %collective-permute-start.6 = (bf16[4,128,1024]{2,1,0:T(8,128)(2,1)}, bf16[4,128,1024]{2,1,0:T(8,128)(2,1)S(1)}, u32[]{:S(2)}, u32[]{:S(2)}) collective-permute-start(bf16[4,128,1024]{2,1,0:T(8,128)(2,1)} %collective-permute-done.2.refs_8_), channel_id=1, source_target_pairs={{0,4},{4,0},{1,5},{5,1},{2,6},{6,2},{3,7},{7,3},{8,12},{12,8},{9,1... | collective-permute-start | bytes 3145736 | tf_op jit(solution)/shard_map/ppermute | solution.py:757
  89.9 28.2 %collective-permute-start.5 = (bf16[128,2048]{1,0:T(8,128)(2,1)}, bf16[128,2048]{1,0:T(8,128)(2,1)}, u32[]{:S(2)}, u32[]{:S(2)}) collective-permute-start(bf16[128,2048]{1,0:T(8,128)(2,1)} %collective-permute-done.1.refs_2_), channel_id=1, source_target_pairs={{0,2},{2,0},{1,3},{3,1},{4,6},{6,4},{5,7},{7,5},{8,10},{10,8},{9,1... | collective-permute-start | bytes 1572872 | tf_op jit(solution)/shard_map/ppermute | solution.py:757
  91.8 26.4 %collective-permute-start.7 = (bf16[4,128,512]{2,1,0:T(8,128)(2,1)S(1)}, bf16[4,128,512]{2,1,0:T(8,128)(2,1)S(1)}, u32[]{:S(2)}, u32[]{:S(2)}) collective-permute-start(bf16[4,128,512]{2,1,0:T(8,128)(2,1)S(1)} %get-tuple-element.295), channel_id=1, source_target_pairs={{0,16},{16,0},{1,17},{17,1},{2,18},{18,2},{3,19},{19,3},{4,20},{20... | collective-permute-start | bytes 1572872 | tf_op jit(solution)/shard_map/ppermute | solution.py:762
  94.4 23.7 %collective-permute-start.8 = (bf16[128,2048]{1,0:T(8,128)(2,1)}, bf16[128,2048]{1,0:T(8,128)(2,1)S(1)}, u32[]{:S(2)}, u32[]{:S(2)}) collective-permute-start(bf16[128,2048]{1,0:T(8,128)(2,1)} %add_ref.1), channel_id=1, source_target_pairs={{0,8},{8,0},{1,9},{9,1},{2,10},{10,2},{3,11},{11,3},{4,12},{12,4},... | collective-permute-start | bytes 1572872 | tf_op jit(solution)/shard_map/ppermute | solution.py:757
  95.8 22.3 %collective-permute-start.9 = (bf16[4,128,256]{2,1,0:T(8,128)(2,1)S(1)}, bf16[4,128,256]{2,1,0:T(8,128)(2,1)S(1)}, u32[]{:S(2)}, u32[]{:S(2)}) collective-permute-start(bf16[4,128,256]{2,1,0:T(8,128)(2,1)S(1)} %get-tuple-element.297), channel_id=1, source_target_pairs={{0,4},{4,0},{1,5},{5,1},{2,6},{6,2},{3,7},{7,3},{8,12},{12,8},{9,1... | collective-permute-start | bytes 786440 | tf_op jit(solution)/shard_map/ppermute | solution.py:757
  122.6 26.5 %collective-permute-start.12 = (bf16[4,128,512]{2,1,0:T(8,128)(2,1)}, bf16[4,128,512]{2,1,0:T(8,128)(2,1)S(1)}, u32[]{:S(2)}, u32[]{:S(2)}) collective-permute-start(bf16[4,128,512]{2,1,0:T(8,128)(2,1)} %get-tuple-element.310), channel_id=1, source_target_pairs={{0,16},{16,0},{1,17},{17,1},{2,18},{18,2},{3,19},{19,3},{4,20},{20... | collective-permute-start | bytes 1572872 | tf_op jit(solution)/shard_map/ppermute | solution.py:762
  125.3 23.9 %collective-permute-start.13 = (bf16[4,128,512]{2,1,0:T(8,128)(2,1)}, bf16[4,128,512]{2,1,0:T(8,128)(2,1)}, u32[]{:S(2)}, u32[]{:S(2)}) collective-permute-start(bf16[4,128,512]{2,1,0:T(8,128)(2,1)} %get-tuple-element.311), channel_id=1, source_target_pairs={{0,4},{4,0},{1,5},{5,1},{2,6},{6,2},{3,7},{7,3},{8,12},{12,8},{9,1... | collective-permute-start | bytes 1572872 | tf_op jit(solution)/shard_map/ppermute | solution.py:757
  126.8 24.0 %collective-permute-start.14 = (bf16[4,128,512]{2,1,0:T(8,128)(2,1)}, bf16[4,128,512]{2,1,0:T(8,128)(2,1)}, u32[]{:S(2)}, u32[]{:S(2)}) collective-permute-start(bf16[4,128,512]{2,1,0:T(8,128)(2,1)} %copy-done.57), channel_id=1, source_target_pairs={{0,4},{4,0},{1,5},{5,1},{2,6},{6,2},{3,7},{7,3},{8,12},{12,8},{9,1... | collective-permute-start | bytes 1572872 | tf_op jit(solution)/shard_map/ppermute | solution.py:757
  127.3 23.5 %collective-permute-start.15 = (bf16[128,2048]{1,0:T(8,128)(2,1)}, bf16[128,2048]{1,0:T(8,128)(2,1)}, u32[]{:S(2)}, u32[]{:S(2)}) collective-permute-start(bf16[128,2048]{1,0:T(8,128)(2,1)} %copy-done.29), channel_id=1, source_target_pairs={{0,2},{2,0},{1,3},{3,1},{4,6},{6,4},{5,7},{7,5},{8,10},{10,8},{9,1... | collective-permute-start | bytes 1572872 | tf_op jit(solution)/shard_map/ppermute | solution.py:757
  127.3 25.5 %all-to-all-start.2 = ((bf16[4,128,768]{2,1,0:T(8,128)(2,1)}), bf16[4,128,768]{2,1,0:T(8,128)(2,1)S(1)}, u32[]{:S(2)}, u32[]{:S(2)}) async-start(bf16[4,128,768]{2,1,0:T(8,128)(2,1)} %slice.57), calls=%async_computation.2 | async-start | bytes 1572864 | tf_op jit(solution)/shard_map/all_to_all | solution.py:802
  130.9 346.5 %reduce-scatter.2.cloned.1.call-start = ((), (), s32[]{:S(2)}) async-start(), calls=%async_computation.7 | async-start | bytes 4718592 | tf_op jit(solution)/shard_map/reduce_scatter | solution.py:1073
  363.5 31.6 %collective-permute-start.59 = (bf16[2,256,640]{2,1,0:T(8,128)(2,1)S(1)}, bf16[2,256,640]{2,1,0:T(8,128)(2,1)S(1)}, u32[]{:S(2)}, u32[]{:S(2)}) collective-permute-start(bf16[2,256,640]{2,1,0:T(8,128)(2,1)S(1)} %copy-done.55), channel_id=1, source_target_pairs={{0,16},{16,0},{1,17},{17,1},{2,18},{18,2},{3,19},{19,3},{4,20},{20... | collective-permute-start | bytes 1966088 | tf_op jit(solution)/shard_map/ppermute | solution.py:762
  364.9 30.2 %collective-permute-start.60 = (bf16[4,256,384]{2,1,0:T(8,128)(2,1)S(1)}, bf16[4,256,384]{2,1,0:T(8,128)(2,1)S(1)}, u32[]{:S(2)}, u32[]{:S(2)}) collective-permute-start(bf16[4,256,384]{2,1,0:T(8,128)(2,1)S(1)} %copy-done.52), channel_id=1, source_target_pairs={{0,4},{4,0},{1,5},{5,1},{2,6},{6,2},{3,7},{7,3},{8,12},{12,8},{9,1... | collective-permute-start | bytes 2359304 | tf_op jit(solution)/shard_map/ppermute | solution.py:757
  365.5 29.6 %collective-permute-start.61 = (bf16[4,256,256]{2,1,0:T(8,128)(2,1)}, bf16[4,256,256]{2,1,0:T(8,128)(2,1)S(1)}, u32[]{:S(2)}, u32[]{:S(2)}) collective-permute-start(bf16[4,256,256]{2,1,0:T(8,128)(2,1)} %get-tuple-element.459), channel_id=1, source_target_pairs={{0,4},{4,0},{1,5},{5,1},{2,6},{6,2},{3,7},{7,3},{8,12},{12,8},{9,1... | collective-permute-start | bytes 1572872 | tf_op jit(solution)/shard_map/ppermute | solution.py:757
  404.4 21.2 %collective-permute-start.64 = (bf16[128,2048]{1,0:T(8,128)(2,1)}, bf16[128,2048]{1,0:T(8,128)(2,1)S(1)}, u32[]{:S(2)}, u32[]{:S(2)}) collective-permute-start(bf16[128,2048]{1,0:T(8,128)(2,1)} %add_last.5), channel_id=1, source_target_pairs={{0,2},{2,0},{1,3},{3,1},{4,6},{6,4},{5,7},{7,5},{8,10},{10,8},{9,1... | collective-permute-start | bytes 1572872 | tf_op jit(solution)/shard_map/ppermute | solution.py:757
  425.6 33.6 %collective-permute-start.68 = (bf16[128,2048]{1,0:T(8,128)(2,1)S(1)}, bf16[128,2048]{1,0:T(8,128)(2,1)S(1)}, u32[]{:S(2)}, u32[]{:S(2)}) collective-permute-start(bf16[128,2048]{1,0:T(8,128)(2,1)S(1)} %copy-done.66), channel_id=1, source_target_pairs={{0,2},{2,0},{1,3},{3,1},{4,6},{6,4},{5,7},{7,5},{8,10},{10,8},{9,1... | collective-permute-start | bytes 1572872 | tf_op jit(solution)/shard_map/ppermute | solution.py:757
  427.5 31.7 %collective-permute-start.69 = (bf16[128,2048]{1,0:T(8,128)(2,1)S(1)}, bf16[128,2048]{1,0:T(8,128)(2,1)S(1)}, u32[]{:S(2)}, u32[]{:S(2)}) collective-permute-start(bf16[128,2048]{1,0:T(8,128)(2,1)S(1)} %add_convert_fusion.1), channel_id=1, source_target_pairs={{0,8},{8,0},{1,9},{9,1},{2,10},{10,2},{3,11},{11,3},{4,12},{12,4},... | collective-permute-start | bytes 1572872 | tf_op jit(solution)/shard_map/ppermute | solution.py:757
  427.8 31.5 %collective-permute-start.70 = (bf16[2,256,640]{2,1,0:T(8,128)(2,1)S(1)}, bf16[2,256,640]{2,1,0:T(8,128)(2,1)S(1)}, u32[]{:S(2)}, u32[]{:S(2)}) collective-permute-start(bf16[2,256,640]{2,1,0:T(8,128)(2,1)S(1)} %copy-done.54), channel_id=1, source_target_pairs={{0,16},{16,0},{1,17},{17,1},{2,18},{18,2},{3,19},{19,3},{4,20},{20... | collective-permute-start | bytes 1966088 | tf_op jit(solution)/shard_map/ppermute | solution.py:762
  431.7 22.6 %collective-permute-start.72 = (bf16[4,256,256]{2,1,0:T(8,128)(2,1)S(1)}, bf16[4,256,256]{2,1,0:T(8,128)(2,1)S(1)}, u32[]{:S(2)}, u32[]{:S(2)}) collective-permute-start(bf16[4,256,256]{2,1,0:T(8,128)(2,1)S(1)} %copy-done.67), channel_id=1, source_target_pairs={{0,4},{4,0},{1,5},{5,1},{2,6},{6,2},{3,7},{7,3},{8,12},{12,8},{9,1... | collective-permute-start | bytes 1572872 | tf_op jit(solution)/shard_map/ppermute | solution.py:757
  460.1 28.5 %collective-permute-start.73 = (bf16[2,256,512]{2,1,0:T(8,128)(2,1)}, bf16[2,256,512]{2,1,0:T(8,128)(2,1)}, u32[]{:S(2)}, u32[]{:S(2)}) collective-permute-start(bf16[2,256,512]{2,1,0:T(8,128)(2,1)} %get-tuple-element.531), channel_id=1, source_target_pairs={{0,16},{16,0},{1,17},{17,1},{2,18},{18,2},{3,19},{19,3},{4,20},{20... | collective-permute-start | bytes 1572872 | tf_op jit(solution)/shard_map/ppermute | solution.py:762
  461.0 21.1 %collective-permute-start.74 = (bf16[4,256,256]{2,1,0:T(8,128)(2,1)}, bf16[4,256,256]{2,1,0:T(8,128)(2,1)S(1)}, u32[]{:S(2)}, u32[]{:S(2)}) collective-permute-start(bf16[4,256,256]{2,1,0:T(8,128)(2,1)} %grad_product.14), channel_id=1, source_target_pairs={{0,4},{4,0},{1,5},{5,1},{2,6},{6,2},{3,7},{7,3},{8,12},{12,8},{9,1... | collective-permute-start | bytes 1572872 | tf_op jit(solution)/shard_map/ppermute | solution.py:757
  461.7 22.9 %collective-permute-start.75 = (bf16[4,256,256]{2,1,0:T(8,128)(2,1)}, bf16[4,256,256]{2,1,0:T(8,128)(2,1)}, u32[]{:S(2)}, u32[]{:S(2)}) collective-permute-start(bf16[4,256,256]{2,1,0:T(8,128)(2,1)} %get-tuple-element.542), channel_id=1, source_target_pairs={{0,4},{4,0},{1,5},{5,1},{2,6},{6,2},{3,7},{7,3},{8,12},{12,8},{9,1... | collective-permute-start | bytes 1572872 | tf_op jit(solution)/shard_map/ppermute | solution.py:757
  463.0 27.8 %all-to-all-start.3 = ((bf16[4,128,1152]{2,1,0:T(8,128)(2,1)}), bf16[4,128,1152]{2,1,0:T(8,128)(2,1)S(1)}, u32[]{:S(2)}, u32[]{:S(2)}) async-start(bf16[4,128,1152]{2,1,0:T(8,128)(2,1)} %bitcast.64), calls=%async_computation.4 | async-start | bytes 2359296 | tf_op jit(solution)/shard_map/all_to_all | solution.py:802
  490.8 27.1 %all-to-all-start.4 = ((bf16[4,128,1024]{2,1,0:T(8,128)(2,1)}), bf16[4,128,1024]{2,1,0:T(8,128)(2,1)S(1)}, u32[]{:S(2)}, u32[]{:S(2)}) async-start(bf16[4,128,1024]{2,1,0:T(8,128)(2,1)} %bitcast.66), calls=%async_computation.5 | async-start | bytes 2097152 | tf_op jit(solution)/shard_map/all_to_all | solution.py:802
  494.4 23.6 %collective-permute-start.76 = (bf16[2,256,512]{2,1,0:T(8,128)(2,1)}, bf16[2,256,512]{2,1,0:T(8,128)(2,1)S(1)}, u32[]{:S(2)}, u32[]{:S(2)}) collective-permute-start(bf16[2,256,512]{2,1,0:T(8,128)(2,1)} %get-tuple-element.552), channel_id=1, source_target_pairs={{0,16},{16,0},{1,17},{17,1},{2,18},{18,2},{3,19},{19,3},{4,20},{20... | collective-permute-start | bytes 1572872 | tf_op jit(solution)/shard_map/ppermute | solution.py:762
  495.3 22.6 %collective-permute-start.79 = (f32[49,128]{1,0:T(8,128)S(1)}, f32[49,128]{1,0:T(8,128)S(1)}, u32[]{:S(2)}, u32[]{:S(2)}) collective-permute-start(f32[49,128]{1,0:T(8,128)S(1)} %maximum_bitcast_fusion), channel_id=1, source_target_pairs={{0,10},{2,8},{8,2},{10,0},{1,11},{3,9},{9,3},{11,1},{4,14},{6,12},... | collective-permute-start | bytes 75272 | tf_op jit(solution)/shard_map/ppermute | solution.py:757
  (152 other events, 1429.9 us)
Sparse Core Ops, SparseCore 0:
  362.1 56.6 reduce-scatter.1

commit v5 on v4

--- a/solution.py
+++ b/solution.py
@@ -373,29 +373,58 @@
     )
 
 
-def ffn_kernel(core_ref, offsets_ref, *refs, sources, units):
-    rows, tops, refs = refs[:6], refs[6:12], refs[12:]
-    (*parts, send_ref, last_ref, keep_ref, grads, back,
-     tokens, token_sems, top_tokens, top_sems, weight, sems) = refs[len(sources) :]
-
+def tops_kernel(core_ref, offsets_ref, *refs, sources):
+    rows, refs = refs[:6], refs[6:]
+    out_ref, tokens, token_sems, weight, sems = refs[len(sources) :]
     sequence = pl.program_id(0)
 
     @pl.when(sequence == 0)
     def _():
         start_rows(core_ref[0], rows, tokens, token_sems)
-        start_rows(core_ref[0], tops, top_tokens, top_sems)
         load_weight(offsets_ref, sources, refs, weight, sems)
 
     wait_rows(core_ref[0], rows, tokens, token_sems, sequence)
-    wait_rows(core_ref[0], tops, top_tokens, top_sems, sequence)
-
+    out_ref[0] = dot(tokens[sequence], weight[...])
+
+
+def tops_product(core, offsets, tokens, sources, width):
+    count, model = tokens[0].shape
+    layout, parts = layout_of(sources)
+    return pl.pallas_call(
+        functools.partial(tops_kernel, sources=layout),
+        grid_spec=pltpu.PrefetchScalarGridSpec(
+            num_scalar_prefetch=2,
+            grid=(4,),
+            in_specs=[pl.BlockSpec(memory_space=pl.ANY)] * (6 + len(parts)),
+            out_specs=pl.BlockSpec((1, 2 * count, width), lambda s, c, o: (s, 0, 0)),
+            scratch_shapes=row_scratch(count, model) + weight_scratch(model, width, parts),
+        ),
+        out_shape=jax.ShapeDtypeStruct((4, 2 * count, width), jnp.float32),
+        compiler_params=PARAMS,
+        cost_estimate=LONG,
+        name="tops_product",
+    )(core, offsets, *tokens, *parts)
+
+
+def ffn_kernel(core_ref, offsets_ref, *refs, sources, units):
+    rows, active_grad_ref, refs = refs[:6], refs[6], refs[7:]
+    (*parts, send_ref, last_ref, keep_ref, grads, back,
+     tokens, token_sems, weight, sems) = refs[len(sources) :]
+    sequence = pl.program_id(0)
+
+    @pl.when(sequence == 0)
+    def _():
+        start_rows(core_ref[0], rows, tokens, token_sems)
+        load_weight(offsets_ref, sources, refs, weight, sems, grads.shape[1] - 2 * units)
+
+    wait_rows(core_ref[0], rows, tokens, token_sems, sequence)
     width = units
     count = rows[0].shape[0]
     mine = pl.multiple_of(core_ref[0] * count, count)
     theirs = pl.multiple_of((1 - core_ref[0]) * count, count)
-    both = dot(tokens[sequence], weight[:, : 2 * width])
+    both = dot(tokens[sequence], weight[...])
     gate, up = both[:, :width], both[:, width:]
-    active_grad = dot(top_tokens[sequence], weight[:, 2 * width : 3 * width])
+    active_grad = active_grad_ref[0, :, :width]
     squash = jax.nn.sigmoid(gate)
     swish = gate * squash
     gate_grad = active_grad * up * squash * (1.0 + gate * (1.0 - squash))
@@ -406,12 +435,12 @@
     for part_ref in parts:
         part_ref[0] = grads[:, low : low + part_ref.shape[2]]
         low += part_ref.shape[2]
-    back[...] = dot(grads[:, : 2 * width], weight[:, : 2 * width], NT)
+    back[...] = dot(grads[:, : 2 * width], weight[...], NT)
     store_sends(back[pl.ds(theirs, count), :], send_ref, last_ref)
     keep_ref[0] = back[pl.ds(mine, count), :]
 
 
-def ffn(core, offsets, tokens, tops, sources, width, widths):
+def ffn(core, offsets, tokens, active_grad, sources, width, widths):
     count, model = tokens[0].shape
     groups, length = 4, 2 * count
     total = sum(widths)
@@ -426,7 +455,9 @@
         grid_spec=pltpu.PrefetchScalarGridSpec(
             num_scalar_prefetch=2,
             grid=(groups,),
-            in_specs=[pl.BlockSpec(memory_space=pl.ANY)] * (12 + len(parts)),
+            in_specs=[pl.BlockSpec(memory_space=pl.ANY)] * 6
+            + [at(length, active_grad.shape[2])]
+            + [pl.BlockSpec(memory_space=pl.ANY)] * len(parts),
             out_specs=[at(length, n) for n in widths]
             + [
                 pl.BlockSpec((1, count, model), lambda s, c, o: (jnp.minimum(s, 2), 0, 0)),
@@ -437,8 +468,8 @@
                 pltpu.VMEM((length, total), BF),
                 pltpu.VMEM((length, model), jnp.float32),
             ]
-            + row_scratch(count, model) * 2
-            + weight_scratch(model, total, parts),
+            + row_scratch(count, model)
+            + weight_scratch(model, 2 * width, parts),
         ),
         out_shape=[
             *[shape((groups, length, n), BF) for n in widths],
@@ -449,7 +480,7 @@
         compiler_params=PARAMS,
         cost_estimate=LONG,
         name="ffn",
-    )(core, offsets, *tokens, *tops, *parts)
+    )(core, offsets, *tokens, active_grad, *parts)
 
 
 def rows_kernel(core_ref, offsets_ref, *refs, sources, begin, number):
@@ -644,7 +675,7 @@
     )(parts)
 
 
-DOWN_FIRST = 384
+DOWN_FIRST = 256
 
 
 def ffn_grad_kernel(first_ref, second_ref, out_ref):
@@ -908,7 +939,10 @@
     scale_one = rms_of(hidden)
     normed = (hidden * scale_one * norm1_gain).astype(BF)
     floor = lax.dynamic_slice_in_dim(lower_bound, member * quarter, quarter)
-    feed = slices(ffn_weights, lanes)
+    feed = slices(ffn_weights, 3 * units)
+    spare = lanes - 3 * units
+    down = jnp.pad(feed[..., 2 * units :], ((0, 0), (0, 0), (0, spare)))
+    feed = jnp.concatenate([down, feed[..., : 2 * units]], axis=-1)
     mix = slices(mix_weights, channels)
 
     mix = trade(jnp.concatenate([slices(mix_weights, channels), labels], axis=1))
@@ -958,17 +992,20 @@
     came_xz = over_c(after(send_xz, gate))
     came = over_c(after(send, gate))
     near_c = over_y(after(feed_one[..., 768:1024], gate))
+    top_cxz = over_c(after(top_xz, gate))
+    top_three = jnp.stack(after([out_grad, top_x, top_z], gate))
     far_c = far(after(ones[2], gate))
     to_xz = add_last(keep, came_xz)
 
-    gate = (to_xz, near_c, far_c)
+    gate = (to_xz, near_c, far_c, top_cxz, top_three)
     from_x = over_x(after(to_xz, gate))
     far_d = far(after(ones[3], gate))
     cross_b = near(after(far_b, gate))
     own, to_x, to_z = add_cores(keep, after(came, gate))
-    top_three = jnp.stack(after([out_grad, top_x, top_z], gate))
-
-    gate = (from_x, far_d, cross_b, own, top_three)
+    top_c = over_c(after(top_three, gate))
+    tops = [out_grad, top_x, top_z, top_xz, top_c, top_cxz]
+
+    gate = (from_x, far_d, cross_b, own, top_c)
     to_z = add_low(to_z, after(from_x, gate))
     of_x = over_x(after(to_x, gate))
     of_z = over_z(to_z)
@@ -988,8 +1025,14 @@
         norm2_gain[None],
     )
     two_x, two_z = over_x(normed_two), over_z(normed_two)
-
-    gate = (far_f, near_f, cross_cd, two_x, two_z)
+    down_sources = [(0, 0, feed_one), (1, 0, near_a), (1, 256, near_b)]
+    for low, straight, crossed in zip(cuts, [far_a, far_b], [cross_a, cross_b]):
+        down_sources += pieces(low, straight, crossed)
+    active_grad = tops_product(
+        core_at, offsets, after(tops, normed_two), down_sources, lanes - 2 * units
+    )
+
+    gate = (far_f, near_f, cross_cd, two_x, two_z, active_grad)
     far_g = far(after(feed_two[..., cuts[6] - feed_cut :], gate))
     cross_e, cross_f = near(after(far_e, gate)), near(after(far_f, gate))
     two_xz = over_x(after(two_z, gate))
@@ -998,8 +1041,6 @@
     gate = (far_g, cross_e, cross_f, two_xz, two_three)
     cross_g = near(after(far_g, gate))
     two_c, two_cxz = over_c(after(two_three, gate)), over_c(after(two_xz, gate))
-    top_c, top_cxz = over_c(after(top_three, gate)), over_c(after(top_xz, gate))
-    tops = [out_grad, top_x, top_z, top_xz, top_c, top_cxz]
     normed_two = [normed_two, two_x, two_z, two_xz, two_c, two_cxz]
     feed_sources = [(0, 0, feed_one), (0, feed_cut, feed_two)]
     feed_sources += [(1, 0, near_a), (1, 256, near_b), (1, 768, near_c), (1, 1024, near_d)]
@@ -1011,8 +1052,10 @@
     for low, part in zip(cuts[:3] + cuts[4:], crosses):
         feed_sources += [(2 * k + 1, low, one) for k, one in enumerate(part, 1)]
 
-    widths = [128, 256, 384, 256, 256, 128, 256, 256, lanes - 1920]
-    *grads, send, send_xz, keep = ffn(core_at, offsets, normed_two, tops, feed_sources, units, widths)
+    widths = [256, 128, 384, 256, 256, 128, 256, 256, lanes - 1920]
+    *grads, send, send_xz, keep = ffn(
+        core_at, offsets, normed_two, active_grad, feed_sources, units, widths
+    )
     gates, downs = grads[:6], grads[6:]
     came_xz, came = over_c(send_xz), over_c(send)
     down_sends = grad_sends(core_at, after(tops, send), downs, LONG)
@@ -1035,7 +1078,7 @@
     gate = (of_x, of_z, down_two, down_away)
     down_fars = send_far(after(down_away, gate))
     down_three = over_y(after(down_sends[2], gate))
-    one_came = over_y(after(gate_sends[0], gate))
+    two_came = over_y(after(gate_sends[1], gate))
     middle_grad, middle_low, gain_two_grad = row_call(
         back_kernel, "middle_grad", [jnp.float32, BF, None], *after((own, of_x, of_z), gate),
         middle, out_grad, norm2_gain[None],
@@ -1046,22 +1089,21 @@
         [(after(down_keeps[1], gate_keeps), after(down_two, gate))]
     )
 
-    gate = (grad_x, grad_z, down_three, one_came, down_away_two, down_fars)
+    gate = (grad_x, grad_z, down_three, two_came, down_away_two, down_fars)
     down_fars_two = send_far(after(down_away_two, gate))
-    two_came = over_y(after(gate_sends[1], gate))
+    one_came = over_y(after(gate_sends[0], gate))
     grad_xz = over_x(after(grad_z, gate))
     grad_three = jnp.stack(after([middle_low, grad_x, grad_z], gate))
     branch = rows_product(
-        core_at, offsets, after(downs, gate), feed_sources, 2 * units, model, LONG
-    )
-
-    gate = (grad_xz, grad_three, branch, down_fars_two, two_came)
+        core_at, offsets, after(downs, gate), down_sources, 0, model, LONG
+    )
+
+    gate = early = (grad_xz, grad_three, branch, down_fars_two, one_came)
     grad_c, grad_cxz = over_c(after(grad_three, gate)), over_c(after(grad_xz, gate))
     one_home, one_away = near_sums(
         [
             (down_keeps[2], after(down_three, gate)),
             (gate_keeps[0], after(one_came, gate)),
-            (gate_keeps[1], after(two_came, gate)),
         ],
         LONG,
     )
@@ -1069,7 +1111,7 @@
 
     gate = (grad_c, grad_cxz, one_away)
     one_fars = send_far(after(one_away, gate))
-    three_came, four_came = [over_y(after(part, gate)) for part in gate_sends[2:4]]
+    three_came, four_came = [over_y(after(part, early)) for part in gate_sends[2:4]]
     branch = lax.psum_scatter(
         after(branch, gate).reshape(-1, model), GROUP + ("tensor",), scatter_dimension=0, tiled=True
     )
@@ -1081,7 +1123,9 @@
     gate = (send, one_fars, three_came, four_came)
     came_xz, came = over_c(after(send_xz, gate)), over_c(after(send, gate))
     five_came = over_y(after(gate_sends[4], gate))
-    three_home, three_away = near_sums([(gate_keeps[2], after(three_came, gate))], LONG)
+    three_home, three_away = near_sums(
+        [(gate_keeps[1], after(two_came, gate)), (gate_keeps[2], three_came)], LONG
+    )
     to_xz = add_last(keep, after(came_xz, three_away))
 
     gate = (to_xz,)

time: 552 us -> 545 us (0.987)
  waiting for transfers between devices: 166 us -> 158 us
    pallas_call x0 -> x1, Pallas kernels: none -> 8.87 us  [tops_product(): pl.pallas_call(functools.partial(tops_kernel, sources=layout), grid_spec=...]
    pallas_call x1, Pallas kernels: 30.5 us -> 23.8 us  [ffn(): pl.pallas_call(functools.partial(ffn_kernel, sources=layout, units=width)...]
    ppermute x68, waiting for transfers between devices: 115 us -> 108 us  [swap(): lax.ppermute(values, axes, [(s, total - 1 - s) for s in range(total)])]
    unnamed x188 -> x184, local copies, waits for them, and re-layouts: 21.5 us -> 24 us
  transfers between devices with their start and end apart: 91 -> 91, of which waited for: 31 -> 31; matrix products, arithmetic and copies ran while one was open for 6% -> 5% of each run, Pallas kernels for 30% -> 32%
where the time goes in v5:
time: 545 us; the launch traced here: 542 us
  Pallas kernels  212 us (39%)
  waiting for transfers between devices  158 us (29%)
  starting transfers between devices  104 us (19%)
  local copies, waits for them, and re-layouts  38.5 us (7%)
  between operations  15.2 us (3%)
  other arithmetic  14.6 us (3%)
    ppermute x68, waiting for transfers between devices, swap(): lax.ppermute(values, axes, [(s, total - 1 - s) for s in range(total)])  108 us
    ppermute x68, starting transfers between devices, swap(): lax.ppermute(values, axes, [(s, total - 1 - s) for s in range(total)])  56.4 us
    pallas_call x8, Pallas kernels, grad_product(): pl.pallas_call(functools.partial(grad_kernel, number=len(grads)), grid_sp...  54.2 us
    ppermute x15, waiting for transfers between devices, shift(): lax.ppermute(values, 'h', [(s, (s + steps) % total) for s in range(total)])  40 us
    pallas_call x7, Pallas kernels, near_sums(): pl.pallas_call(functools.partial(near_kernel, number=len(pairs), ends=hig...  27.8 us
    pallas_call x1, Pallas kernels, mixer_backward(): pl.pallas_call(functools.partial(mixer_backward_kernel, sources=layout),...  24 us
    unnamed x184, local copies, waits for them, and re-layouts  24 us
    pallas_call x1, Pallas kernels, ffn(): pl.pallas_call(functools.partial(ffn_kernel, sources=layout, units=width)...  23.8 us
  transfers between devices with their start and end apart: 91, of which 31 were waited for; matrix products, arithmetic and copies ran while one was open for 5% of the time, Pallas kernels for 32%

profile of v5, /device:TPU:0, one launch (start us, length us, event | category | flops | bytes accessed | tf_op | source)
XLA Modules:
  0.0 542.0 jit_solution(18352852411856809155)
XLA Ops:
  11.3 5.2 all-to-all-start
  25.8 5.8 %all-to-all-done = bf16[4,144,1024]{2,1,0:T(8,128)(2,1)S(1)} async-done(((bf16[4,144,1024]{2,1,0:T(8,128)(2,1)}), bf16[4,144,1024]{2,1,0:T(8,128)(2,1)S(1)}, u32[]{:S(2)}, u32[]{:S(2)}) %all-to-all-start) | async-done | bytes 1179680 | tf_op jit(solution)/shard_map/all_to_all | solution.py:833
  49.0 17.0 %collective-permute-done.refs_1_ = bf16[128,2048]{1,0:T(8,128)(2,1)} collective-permute-done((bf16[128,2048]{1,0:T(8,128)(2,1)S(1)}, bf16[128,2048]{1,0:T(8,128)(2,1)}, u32[]{:S(2)}, u32[]{:S(2)}) %collective-permute-start) | collective-permute-done | bytes 524320 | tf_op jit(solution)/shard_map/ppermute | solution.py:788
  66.0 22.1 %collective-permute-done.1.refs_2_ = bf16[128,2048]{1,0:T(8,128)(2,1)} collective-permute-done((bf16[128,2048]{1,0:T(8,128)(2,1)S(1)}, bf16[128,2048]{1,0:T(8,128)(2,1)}, u32[]{:S(2)}, u32[]{:S(2)}) %collective-permute-start.1) | collective-permute-done | bytes 524320 | tf_op jit(solution)/shard_map/ppermute | solution.py:788
  98.2 19.8 %collective-permute-done.9.refs_7_.refs_9_.refs_4_ = bf16[4,128,256]{2,1,0:T(8,128)(2,1)S(1)} collective-permute-done((bf16[4,128,256]{2,1,0:T(8,128)(2,1)S(1)}, bf16[4,128,256]{2,1,0:T(8,128)(2,1)S(1)}, u32[]{:S(2)}, u32[]{:S(2)}) %collective-permute-start.9) | collective-permute-done | bytes 262176 | tf_op jit(solution)/shard_map/ppermute | solution.py:788
  131.0 17.9 %mixer_forward.1 = (f32[4,256,768]{2,1,0:T(8,128)}, bf16[4,256,256]{2,1,0:T(8,128)(2,1)}, bf16[3,128,2048]{2,1,0:T(8,128)(2,1)}, bf16[128,2048]{1,0:T(8,128)(2,1)}, f32[4,128,2048]{2,1,0:T(8,128)}) custom-call(s32[2]{0:T(128)} %pad_add_fusion.1.core_ref, s32[16]{0:T(128)} %stack.222.offsets_ref, bf16[128,2048]{1,0:T(8,128)(2,1)} %fusion.4.refs_0_, ...), custom_call_target="tpu_custom_call" | custom-call | flops 49999998976 | bytes 1 | tf_op jit(solution)/shard_map/mixer_forward/pallas_call | solution.py:297
  159.0 4.1 collective-permute-done.19.refs_17_
  169.9 8.6 %collective-permute-done.22.refs_18_ = bf16[4,128,256]{2,1,0:T(8,128)(2,1)S(1)} collective-permute-done((bf16[4,128,256]{2,1,0:T(8,128)(2,1)S(1)}, bf16[4,128,256]{2,1,0:T(8,128)(2,1)S(1)}, u32[]{:S(2)}, u32[]{:S(2)}) %collective-permute-start.22) | collective-permute-done | bytes 262176 | tf_op jit(solution)/shard_map/ppermute | solution.py:793
  184.9 12.6 %collective-permute-done.27.refs_19_ = bf16[4,128,256]{2,1,0:T(8,128)(2,1)S(1)} collective-permute-done((bf16[4,128,256]{2,1,0:T(8,128)(2,1)S(1)}, bf16[4,128,256]{2,1,0:T(8,128)(2,1)S(1)}, u32[]{:S(2)}, u32[]{:S(2)}) %collective-permute-start.27) | collective-permute-done | bytes 262176 | tf_op jit(solution)/shard_map/ppermute | solution.py:793
  210.2 8.9 %tops_product.1.refs_6_ = f32[4,256,768]{2,1,0:T(8,128)} custom-call(s32[2]{0:T(128)} %pad_add_fusion.1.core_ref, s32[16]{0:T(128)} %stack.222.offsets_ref, bf16[128,2048]{1,0:T(8,128)(2,1)} %add_ref.1, bf16[128,2048]{1,0:T(8,128)(2,1)} %collective-permute-done.4.refs_1_, bf16[128,2048]{1,0:T(8,128)(2,1)} %copy-done.29, ...), custom_call_target="tpu_custom_call" | custom-call | flops 49999998976 | bytes 1 | tf_op jit(solution)/shard_map/tops_product/pallas_call | solution.py:393
  219.1 4.2 collective-permute-done.32.refs_20_
  230.9 6.7 %collective-permute-done.36.refs_21_ = bf16[4,128,256]{2,1,0:T(8,128)(2,1)} collective-permute-done((bf16[4,128,256]{2,1,0:T(8,128)(2,1)S(1)}, bf16[4,128,256]{2,1,0:T(8,128)(2,1)}, u32[]{:S(2)}, u32[]{:S(2)}) %collective-permute-start.36) | collective-permute-done | bytes 262176 | tf_op jit(solution)/shard_map/ppermute | solution.py:793
  240.3 7.2 %collective-permute-done.41.refs_27_ = bf16[4,128,256]{2,1,0:T(8,128)(2,1)S(1)} collective-permute-done((bf16[4,128,256]{2,1,0:T(8,128)(2,1)}, bf16[4,128,256]{2,1,0:T(8,128)(2,1)S(1)}, u32[]{:S(2)}, u32[]{:S(2)}) %collective-permute-start.41) | collective-permute-done | bytes 262176 | tf_op jit(solution)/shard_map/ppermute | solution.py:788
  249.3 23.8 %ffn.1 = (bf16[4,256,256]{2,1,0:T(8,128)(2,1)}, bf16[4,256,128]{2,1,0:T(8,128)(2,1)}, bf16[4,256,384]{2,1,0:T(8,128)(2,1)}, bf16[4,256,256]{2,1,0:T(8,128)(2,1)}...) custom-call(s32[2]{0:T(128)} %pad_add_fusion.1.core_ref, ...), custom_call_target="tpu_custom_call" | custom-call | flops 49999998976 | bytes 1 | tf_op jit(solution)/shard_map/ffn/pallas_call | solution.py:453
  273.7 6.3 %grad_product.8 = (bf16[4,256,256]{2,1,0:T(8,128)(2,1)}, bf16[4,256,256]{2,1,0:T(8,128)(2,1)}, bf16[4,256,256]{2,1,0:T(8,128)(2,1)}) custom-call(s32[2]{0:T(128)} %pad_add_fusion.1.core_ref, s32[4]{0:T(128)} %get-tuple-element.592.blocks_ref, bf16[128,2048]{1,0:T(8,128)(2,1)} %add_ref.1, bf16[128,2048]{1,0:T(8,128)(2,1)} %collective-permute-done.4.refs_1_, ...), custom_call_target="tpu_custom_call" | custom-call | flops 49999998976 | bytes 1 | tf_op jit(solution)/shard_map/grad_product/pallas_call | solution.py:540
  284.9 8.9 %grad_product.9 = (bf16[4,256,256]{2,1,0:T(8,128)(2,1)}, bf16[4,256,128]{2,1,0:T(8,128)(2,1)}, bf16[4,256,384]{2,1,0:T(8,128)(2,1)}, bf16[4,256,256]{2,1,0:T(8,1...) custom-call(s32[2]{0:T(128)} %pad_add_fusion.1.core_ref, s32[4]{0:T(128)} %get-tuple-element.592.blocks_ref, ...), custom_call_target="tpu_custom_call" | custom-call | flops 49999998976 | bytes 1 | tf_op jit(solution)/shard_map/grad_product/pallas_call | solution.py:540
  302.6 6.5 %grad_product.10 = (f32[4,256,256]{2,1,0:T(8,128)}, f32[4,256,256]{2,1,0:T(8,128)}, f32[4,256,256]{2,1,0:T(8,128)}) custom-call(s32[2]{0:T(128)} %pad_add_fusion.1.core_ref, s32[4]{0:T(128)} %get-tuple-element.593.blocks_ref, bf16[128,2048]{1,0:T(8,128)(2,1)} %add_ref.1, bf16[128,2048]{1,0:T(8,128)(2,1)} %collective-permute-done.4.refs_1_, ...), custom_call_target="tpu_custom_call" | custom-call | flops 49999998976 | bytes 1 | tf_op jit(solution)/shard_map/grad_product/pallas_call | solution.py:540
  314.1 4.6 middle_grad.1
  324.5 8.8 %grad_product.11 = (f32[4,256,256]{2,1,0:T(8,128)}, f32[4,256,128]{2,1,0:T(8,128)}, f32[4,256,384]{2,1,0:T(8,128)}, f32[4,256,256]{2,1,0:T(8,128)}, f32[4,256,256]{2,1,0:T(8,128)}, /*index=5*/f32[4,256,128]{2,1,0:T(8,128)}) custom-call(s32[2]{0:T(128)} %pad_add_fusion.1.core_ref, s32[4]{0:T(128)} %get-tuple-element.593.blocks_ref, ...), custom_call_target="tpu_custom_call" | custom-call | flops 49999998976 | bytes 1 | tf_op jit(solution)/shard_map/grad_product/pallas_call | solution.py:540
  342.9 9.3 %rows_product.1 = bf16[4,256,2048]{2,1,0:T(8,128)(2,1)} custom-call(s32[2]{0:T(128)} %pad_add_fusion.1.core_ref, s32[16]{0:T(128)} %stack.222.offsets_ref, bf16[4,256,256]{2,1,0:T(8,128)(2,1)} %get-tuple-element.442.refs_0_, bf16[4,256,256]{2,1,0:T(8,128)(2,1)} %get-tuple-element.443.refs_1_, bf16[4,256,256]{2,1,0:T(8,128)(2,1)} %get-tuple-element.444.refs_2_, ...), custom_call_target="tpu_custom_call" | custom-call | flops 49999998976 | bytes 1 | tf_op jit(solution)/shard_map/rows_product/pallas_call | solution.py:506
  361.7 24.0 %mixer_backward.1 = (bf16[4,256,256]{2,1,0:T(8,128)(2,1)}, bf16[4,256,256]{2,1,0:T(8,128)(2,1)}, bf16[4,256,256]{2,1,0:T(8,128)(2,1)}, bf16[3,128,2048]{2,1,0:T(...) custom-call(s32[2]{0:T(128)} %pad_add_fusion.1.core_ref, ...), custom_call_target="tpu_custom_call" | custom-call | flops 49999998976 | bytes 1 | tf_op jit(solution)/shard_map/mixer_backward/pallas_call | solution.py:337
  388.2 4.2 near_sums.10
  399.8 6.6 %grad_product.12 = (bf16[4,256,256]{2,1,0:T(8,128)(2,1)}, bf16[4,256,256]{2,1,0:T(8,128)(2,1)}, bf16[4,256,256]{2,1,0:T(8,128)(2,1)}) custom-call(s32[2]{0:T(128)} %pad_add_fusion.1.core_ref, s32[4]{0:T(128)} %get-tuple-element.592.blocks_ref, bf16[128,2048]{1,0:T(8,128)(2,1)} %fusion.4.refs_0_, bf16[128,2048]{1,0:T(8,128)(2,1)} %collective-permute-done.refs_1_, ...), custom_call_target="tpu_custom_call" | custom-call | flops 49999998976 | bytes 1 | tf_op jit(solution)/shard_map/grad_product/pallas_call | solution.py:540
  412.5 4.3 near_sums.11
  427.5 6.5 %grad_product.13 = (f32[4,256,256]{2,1,0:T(8,128)}, f32[4,256,256]{2,1,0:T(8,128)}, f32[4,256,256]{2,1,0:T(8,128)}) custom-call(s32[2]{0:T(128)} %pad_add_fusion.1.core_ref, s32[4]{0:T(128)} %get-tuple-element.593.blocks_ref, bf16[128,2048]{1,0:T(8,128)(2,1)} %fusion.4.refs_0_, bf16[128,2048]{1,0:T(8,128)(2,1)} %collective-permute-done.refs_1_, ...), custom_call_target="tpu_custom_call" | custom-call | flops 49999998976 | bytes 1 | tf_op jit(solution)/shard_map/grad_product/pallas_call | solution.py:540
  434.0 5.3 grad_product.14
  442.1 6.7 %collective-permute-done.72.refs_3_ = bf16[4,256,256]{2,1,0:T(8,128)(2,1)S(1)} collective-permute-done((bf16[4,256,256]{2,1,0:T(8,128)(2,1)S(1)}, bf16[4,256,256]{2,1,0:T(8,128)(2,1)S(1)}, u32[]{:S(2)}, u32[]{:S(2)}) %collective-permute-start.72) | collective-permute-done | bytes 524320 | tf_op jit(solution)/shard_map/ppermute | solution.py:788
  449.6 4.1 near_sums.12
  461.2 4.5 input_grad.1
  466.6 5.5 %grad_product.15.refs_0_ = f32[4,256,256]{2,1,0:T(8,128)} custom-call(s32[2]{0:T(128)} %pad_add_fusion.1.core_ref, s32[4]{0:T(128)} %get-tuple-element.593.blocks_ref, bf16[128,2048]{1,0:T(8,128)(2,1)} %get-tuple-element.533.refs_0_, bf16[128,2048]{1,0:T(8,128)(2,1)} %copy-done.5, bf16[128,2048]{1,0:T(8,128)(2,1)} %copy-done.6, ...), custom_call_target="tpu_custom_call" | custom-call | flops 1 | bytes 1 | tf_op jit(solution)/shard_map/grad_product/pallas_call | solution.py:540
  491.3 19.6 %collective-permute-done.79 = f32[49,128]{1,0:T(8,128)S(1)} collective-permute-done((f32[49,128]{1,0:T(8,128)S(1)}, f32[49,128]{1,0:T(8,128)S(1)}, u32[]{:S(2)}, u32[]{:S(2)}) %collective-permute-start.79) | collective-permute-done | bytes 25120 | tf_op jit(solution)/shard_map/ppermute | solution.py:788
  523.9 4.4 ffn_grad.1
  (423 shorter events, 222.9 us)
Async XLA Ops:
  32.8 55.3 %all-to-all-start.1 = ((bf16[4,128,1408]{2,1,0:T(8,128)(2,1)}), bf16[4,128,1408]{2,1,0:T(8,128)(2,1)S(1)}, u32[]{:S(2)}, u32[]{:S(2)}) async-start(bf16[4,128,1408]{2,1,0:T(8,128)(2,1)} %slice.64), calls=%async_computation.1 | async-start | bytes 2883584 | tf_op jit(solution)/shard_map/all_to_all | solution.py:833
  37.4 50.7 %collective-permute-start.2 = (bf16[4,128,1024]{2,1,0:T(8,128)(2,1)}, bf16[4,128,1024]{2,1,0:T(8,128)(2,1)}, u32[]{:S(2)}, u32[]{:S(2)}) collective-permute-start(bf16[4,128,1024]{2,1,0:T(8,128)(2,1)} %slice.63.refs_6_), channel_id=1, source_target_pairs={{0,16},{16,0},{1,17},{17,1},{2,18},{18,2},{3,19},{19,3},{4,20},{20... | collective-permute-start | bytes 3145736 | tf_op jit(solution)/shard_map/ppermute | solution.py:793
  40.0 48.1 %collective-permute-start.3 = (bf16[4,128,1024]{2,1,0:T(8,128)(2,1)}, bf16[4,128,1024]{2,1,0:T(8,128)(2,1)}, u32[]{:S(2)}, u32[]{:S(2)}) collective-permute-start(bf16[4,128,1024]{2,1,0:T(8,128)(2,1)} %slice.63.refs_6_), channel_id=1, source_target_pairs={{0,4},{4,0},{1,5},{5,1},{2,6},{6,2},{3,7},{7,3},{8,12},{12,8},{9,1... | collective-permute-start | bytes 3145736 | tf_op jit(solution)/shard_map/ppermute | solution.py:788
  41.5 24.5 %collective-permute-start = (bf16[128,2048]{1,0:T(8,128)(2,1)S(1)}, bf16[128,2048]{1,0:T(8,128)(2,1)}, u32[]{:S(2)}, u32[]{:S(2)}) collective-permute-start(bf16[128,2048]{1,0:T(8,128)(2,1)S(1)} %copy-done.10), channel_id=1, source_target_pairs={{0,2},{2,0},{1,3},{3,1},{4,6},{6,4},{5,7},{7,5},{8,10},{10,8},{9,1... | collective-permute-start | bytes 1572872 | tf_op jit(solution)/shard_map/ppermute | solution.py:788
  43.6 44.6 %collective-permute-start.1 = (bf16[128,2048]{1,0:T(8,128)(2,1)S(1)}, bf16[128,2048]{1,0:T(8,128)(2,1)}, u32[]{:S(2)}, u32[]{:S(2)}) collective-permute-start(bf16[128,2048]{1,0:T(8,128)(2,1)S(1)} %copy-done.10), channel_id=1, source_target_pairs={{0,8},{8,0},{1,9},{9,1},{2,10},{10,2},{3,11},{11,3},{4,12},{12,4},... | collective-permute-start | bytes 1572872 | tf_op jit(solution)/shard_map/ppermute | solution.py:788
  45.0 43.2 %collective-permute-start.4 = (bf16[128,2048]{1,0:T(8,128)(2,1)}, bf16[128,2048]{1,0:T(8,128)(2,1)}, u32[]{:S(2)}, u32[]{:S(2)}) collective-permute-start(bf16[128,2048]{1,0:T(8,128)(2,1)} %add_ref.1), channel_id=1, source_target_pairs={{0,2},{2,0},{1,3},{3,1},{4,6},{6,4},{5,7},{7,5},{8,10},{10,8},{9,1... | collective-permute-start | bytes 1572872 | tf_op jit(solution)/shard_map/ppermute | solution.py:788
  88.2 29.9 %collective-permute-start.6 = (bf16[4,128,1024]{2,1,0:T(8,128)(2,1)}, bf16[4,128,1024]{2,1,0:T(8,128)(2,1)S(1)}, u32[]{:S(2)}, u32[]{:S(2)}) collective-permute-start(bf16[4,128,1024]{2,1,0:T(8,128)(2,1)} %collective-permute-done.2.refs_8_), channel_id=1, source_target_pairs={{0,4},{4,0},{1,5},{5,1},{2,6},{6,2},{3,7},{7,3},{8,12},{12,8},{9,1... | collective-permute-start | bytes 3145736 | tf_op jit(solution)/shard_map/ppermute | solution.py:788
  89.8 28.2 %collective-permute-start.5 = (bf16[128,2048]{1,0:T(8,128)(2,1)}, bf16[128,2048]{1,0:T(8,128)(2,1)}, u32[]{:S(2)}, u32[]{:S(2)}) collective-permute-start(bf16[128,2048]{1,0:T(8,128)(2,1)} %collective-permute-done.1.refs_2_), channel_id=1, source_target_pairs={{0,2},{2,0},{1,3},{3,1},{4,6},{6,4},{5,7},{7,5},{8,10},{10,8},{9,1... | collective-permute-start | bytes 1572872 | tf_op jit(solution)/shard_map/ppermute | solution.py:788
  91.6 26.4 %collective-permute-start.7 = (bf16[4,128,512]{2,1,0:T(8,128)(2,1)S(1)}, bf16[4,128,512]{2,1,0:T(8,128)(2,1)S(1)}, u32[]{:S(2)}, u32[]{:S(2)}) collective-permute-start(bf16[4,128,512]{2,1,0:T(8,128)(2,1)S(1)} %get-tuple-element.300), channel_id=1, source_target_pairs={{0,16},{16,0},{1,17},{17,1},{2,18},{18,2},{3,19},{19,3},{4,20},{20... | collective-permute-start | bytes 1572872 | tf_op jit(solution)/shard_map/ppermute | solution.py:793
  94.3 23.7 %collective-permute-start.8 = (bf16[128,2048]{1,0:T(8,128)(2,1)}, bf16[128,2048]{1,0:T(8,128)(2,1)S(1)}, u32[]{:S(2)}, u32[]{:S(2)}) collective-permute-start(bf16[128,2048]{1,0:T(8,128)(2,1)} %add_ref.1), channel_id=1, source_target_pairs={{0,8},{8,0},{1,9},{9,1},{2,10},{10,2},{3,11},{11,3},{4,12},{12,4},... | collective-permute-start | bytes 1572872 | tf_op jit(solution)/shard_map/ppermute | solution.py:788
  95.6 22.3 %collective-permute-start.9 = (bf16[4,128,256]{2,1,0:T(8,128)(2,1)S(1)}, bf16[4,128,256]{2,1,0:T(8,128)(2,1)S(1)}, u32[]{:S(2)}, u32[]{:S(2)}) collective-permute-start(bf16[4,128,256]{2,1,0:T(8,128)(2,1)S(1)} %get-tuple-element.302), channel_id=1, source_target_pairs={{0,4},{4,0},{1,5},{5,1},{2,6},{6,2},{3,7},{7,3},{8,12},{12,8},{9,1... | collective-permute-start | bytes 786440 | tf_op jit(solution)/shard_map/ppermute | solution.py:788
  122.5 26.4 %collective-permute-start.12 = (bf16[4,128,512]{2,1,0:T(8,128)(2,1)}, bf16[4,128,512]{2,1,0:T(8,128)(2,1)}, u32[]{:S(2)}, u32[]{:S(2)}) collective-permute-start(bf16[4,128,512]{2,1,0:T(8,128)(2,1)} %get-tuple-element.315), channel_id=1, source_target_pairs={{0,16},{16,0},{1,17},{17,1},{2,18},{18,2},{3,19},{19,3},{4,20},{20... | collective-permute-start | bytes 1572872 | tf_op jit(solution)/shard_map/ppermute | solution.py:793
  125.1 23.8 %collective-permute-start.13 = (bf16[4,128,512]{2,1,0:T(8,128)(2,1)}, bf16[4,128,512]{2,1,0:T(8,128)(2,1)}, u32[]{:S(2)}, u32[]{:S(2)}) collective-permute-start(bf16[4,128,512]{2,1,0:T(8,128)(2,1)} %get-tuple-element.316), channel_id=1, source_target_pairs={{0,4},{4,0},{1,5},{5,1},{2,6},{6,2},{3,7},{7,3},{8,12},{12,8},{9,1... | collective-permute-start | bytes 1572872 | tf_op jit(solution)/shard_map/ppermute | solution.py:788
  126.7 24.0 %collective-permute-start.14 = (bf16[4,128,512]{2,1,0:T(8,128)(2,1)}, bf16[4,128,512]{2,1,0:T(8,128)(2,1)}, u32[]{:S(2)}, u32[]{:S(2)}) collective-permute-start(bf16[4,128,512]{2,1,0:T(8,128)(2,1)} %copy-done.56), channel_id=1, source_target_pairs={{0,4},{4,0},{1,5},{5,1},{2,6},{6,2},{3,7},{7,3},{8,12},{12,8},{9,1... | collective-permute-start | bytes 1572872 | tf_op jit(solution)/shard_map/ppermute | solution.py:788
  127.2 23.5 %collective-permute-start.15 = (bf16[128,2048]{1,0:T(8,128)(2,1)}, bf16[128,2048]{1,0:T(8,128)(2,1)}, u32[]{:S(2)}, u32[]{:S(2)}) collective-permute-start(bf16[128,2048]{1,0:T(8,128)(2,1)} %copy-done.29), channel_id=1, source_target_pairs={{0,2},{2,0},{1,3},{3,1},{4,6},{6,4},{5,7},{7,5},{8,10},{10,8},{9,1... | collective-permute-start | bytes 1572872 | tf_op jit(solution)/shard_map/ppermute | solution.py:788
  127.2 25.4 %all-to-all-start.2 = ((bf16[4,128,768]{2,1,0:T(8,128)(2,1)}), bf16[4,128,768]{2,1,0:T(8,128)(2,1)S(1)}, u32[]{:S(2)}, u32[]{:S(2)}) async-start(bf16[4,128,768]{2,1,0:T(8,128)(2,1)} %slice.65), calls=%async_computation.2 | async-start | bytes 1572864 | tf_op jit(solution)/shard_map/all_to_all | solution.py:833
  130.7 341.4 %reduce-scatter.2.cloned.1.call-start = ((), (), s32[]{:S(2)}) async-start(), calls=%async_computation.7 | async-start | bytes 4718592 | tf_op jit(solution)/shard_map/reduce_scatter | solution.py:1115
  353.0 32.7 %collective-permute-start.60 = (bf16[4,256,384]{2,1,0:T(8,128)(2,1)}, bf16[4,256,384]{2,1,0:T(8,128)(2,1)S(1)}, u32[]{:S(2)}, u32[]{:S(2)}) collective-permute-start(bf16[4,256,384]{2,1,0:T(8,128)(2,1)} %get-tuple-element.468), channel_id=1, source_target_pairs={{0,4},{4,0},{1,5},{5,1},{2,6},{6,2},{3,7},{7,3},{8,12},{12,8},{9,1... | collective-permute-start | bytes 2359304 | tf_op jit(solution)/shard_map/ppermute | solution.py:788
  353.5 32.2 %collective-permute-start.61 = (bf16[4,256,256]{2,1,0:T(8,128)(2,1)}, bf16[4,256,256]{2,1,0:T(8,128)(2,1)S(1)}, u32[]{:S(2)}, u32[]{:S(2)}) collective-permute-start(bf16[4,256,256]{2,1,0:T(8,128)(2,1)} %get-tuple-element.469), channel_id=1, source_target_pairs={{0,4},{4,0},{1,5},{5,1},{2,6},{6,2},{3,7},{7,3},{8,12},{12,8},{9,1... | collective-permute-start | bytes 1572872 | tf_op jit(solution)/shard_map/ppermute | solution.py:788
  360.5 25.8 %collective-permute-start.59 = (bf16[2,256,512]{2,1,0:T(8,128)(2,1)}, bf16[2,256,512]{2,1,0:T(8,128)(2,1)S(1)}, u32[]{:S(2)}, u32[]{:S(2)}) collective-permute-start(bf16[2,256,512]{2,1,0:T(8,128)(2,1)} %get-tuple-element.467), channel_id=1, source_target_pairs={{0,16},{16,0},{1,17},{17,1},{2,18},{18,2},{3,19},{19,3},{4,20},{20... | collective-permute-start | bytes 1572872 | tf_op jit(solution)/shard_map/ppermute | solution.py:793
  387.6 23.4 %collective-permute-start.66 = (bf16[4,256,256]{2,1,0:T(8,128)(2,1)S(1)}, bf16[4,256,256]{2,1,0:T(8,128)(2,1)S(1)}, u32[]{:S(2)}, u32[]{:S(2)}) collective-permute-start(bf16[4,256,256]{2,1,0:T(8,128)(2,1)S(1)} %copy-done.58), channel_id=1, source_target_pairs={{0,4},{4,0},{1,5},{5,1},{2,6},{6,2},{3,7},{7,3},{8,12},{12,8},{9,1... | collective-permute-start | bytes 1572872 | tf_op jit(solution)/shard_map/ppermute | solution.py:788
  395.4 23.5 %collective-permute-start.64 = (bf16[128,2048]{1,0:T(8,128)(2,1)}, bf16[128,2048]{1,0:T(8,128)(2,1)S(1)}, u32[]{:S(2)}, u32[]{:S(2)}) collective-permute-start(bf16[128,2048]{1,0:T(8,128)(2,1)} %add_last.5), channel_id=1, source_target_pairs={{0,2},{2,0},{1,3},{3,1},{4,6},{6,4},{5,7},{7,5},{8,10},{10,8},{9,1... | collective-permute-start | bytes 1572872 | tf_op jit(solution)/shard_map/ppermute | solution.py:788
  396.8 25.4 %collective-permute-start.65 = (bf16[2,256,512]{2,1,0:T(8,128)(2,1)S(1)}, bf16[2,256,512]{2,1,0:T(8,128)(2,1)S(1)}, u32[]{:S(2)}, u32[]{:S(2)}) collective-permute-start(bf16[2,256,512]{2,1,0:T(8,128)(2,1)S(1)} %copy-done.68), channel_id=1, source_target_pairs={{0,16},{16,0},{1,17},{17,1},{2,18},{18,2},{3,19},{19,3},{4,20},{20... | collective-permute-start | bytes 1572872 | tf_op jit(solution)/shard_map/ppermute | solution.py:793
  422.2 31.5 %collective-permute-start.68 = (bf16[128,2048]{1,0:T(8,128)(2,1)S(1)}, bf16[128,2048]{1,0:T(8,128)(2,1)S(1)}, u32[]{:S(2)}, u32[]{:S(2)}) collective-permute-start(bf16[128,2048]{1,0:T(8,128)(2,1)S(1)} %copy-done.63), channel_id=1, source_target_pairs={{0,2},{2,0},{1,3},{3,1},{4,6},{6,4},{5,7},{7,5},{8,10},{10,8},{9,1... | collective-permute-start | bytes 1572872 | tf_op jit(solution)/shard_map/ppermute | solution.py:788
  422.9 30.8 %collective-permute-start.69 = (bf16[128,2048]{1,0:T(8,128)(2,1)S(1)}, bf16[128,2048]{1,0:T(8,128)(2,1)S(1)}, u32[]{:S(2)}, u32[]{:S(2)}) collective-permute-start(bf16[128,2048]{1,0:T(8,128)(2,1)S(1)} %add_convert_fusion.1), channel_id=1, source_target_pairs={{0,8},{8,0},{1,9},{9,1},{2,10},{10,2},{3,11},{11,3},{4,12},{12,4},... | collective-permute-start | bytes 1572872 | tf_op jit(solution)/shard_map/ppermute | solution.py:788
  423.0 30.7 %collective-permute-start.70 = (bf16[2,256,640]{2,1,0:T(8,128)(2,1)S(1)}, bf16[2,256,640]{2,1,0:T(8,128)(2,1)S(1)}, u32[]{:S(2)}, u32[]{:S(2)}) collective-permute-start(bf16[2,256,640]{2,1,0:T(8,128)(2,1)S(1)} %copy-done.54), channel_id=1, source_target_pairs={{0,16},{16,0},{1,17},{17,1},{2,18},{18,2},{3,19},{19,3},{4,20},{20... | collective-permute-start | bytes 1966088 | tf_op jit(solution)/shard_map/ppermute | solution.py:793
  426.9 21.9 %collective-permute-start.72 = (bf16[4,256,256]{2,1,0:T(8,128)(2,1)S(1)}, bf16[4,256,256]{2,1,0:T(8,128)(2,1)S(1)}, u32[]{:S(2)}, u32[]{:S(2)}) collective-permute-start(bf16[4,256,256]{2,1,0:T(8,128)(2,1)S(1)} %copy-done.64), channel_id=1, source_target_pairs={{0,4},{4,0},{1,5},{5,1},{2,6},{6,2},{3,7},{7,3},{8,12},{12,8},{9,1... | collective-permute-start | bytes 1572872 | tf_op jit(solution)/shard_map/ppermute | solution.py:788
  454.5 27.5 %collective-permute-start.73 = (bf16[2,256,512]{2,1,0:T(8,128)(2,1)}, bf16[2,256,512]{2,1,0:T(8,128)(2,1)}, u32[]{:S(2)}, u32[]{:S(2)}) collective-permute-start(bf16[2,256,512]{2,1,0:T(8,128)(2,1)} %get-tuple-element.541), channel_id=1, source_target_pairs={{0,16},{16,0},{1,17},{17,1},{2,18},{18,2},{3,19},{19,3},{4,20},{20... | collective-permute-start | bytes 1572872 | tf_op jit(solution)/shard_map/ppermute | solution.py:793
  457.3 25.4 %all-to-all-start.3 = ((bf16[4,128,1024]{2,1,0:T(8,128)(2,1)}), bf16[4,128,1024]{2,1,0:T(8,128)(2,1)S(1)}, u32[]{:S(2)}, u32[]{:S(2)}) async-start(bf16[4,128,1024]{2,1,0:T(8,128)(2,1)} %bitcast.64), calls=%async_computation.4 | async-start | bytes 2097152 | tf_op jit(solution)/shard_map/all_to_all | solution.py:833
  482.7 28.3 %all-to-all-start.4 = ((bf16[4,128,1152]{2,1,0:T(8,128)(2,1)}), bf16[4,128,1152]{2,1,0:T(8,128)(2,1)S(1)}, u32[]{:S(2)}, u32[]{:S(2)}) async-start(bf16[4,128,1152]{2,1,0:T(8,128)(2,1)} %bitcast.66), calls=%async_computation.5 | async-start | bytes 2359296 | tf_op jit(solution)/shard_map/all_to_all | solution.py:833
  486.2 24.7 %collective-permute-start.76 = (bf16[2,256,512]{2,1,0:T(8,128)(2,1)}, bf16[2,256,512]{2,1,0:T(8,128)(2,1)S(1)}, u32[]{:S(2)}, u32[]{:S(2)}) collective-permute-start(bf16[2,256,512]{2,1,0:T(8,128)(2,1)} %get-tuple-element.562), channel_id=1, source_target_pairs={{0,16},{16,0},{1,17},{17,1},{2,18},{18,2},{3,19},{19,3},{4,20},{20... | collective-permute-start | bytes 1572872 | tf_op jit(solution)/shard_map/ppermute | solution.py:793
  487.8 23.1 %collective-permute-start.79 = (f32[49,128]{1,0:T(8,128)S(1)}, f32[49,128]{1,0:T(8,128)S(1)}, u32[]{:S(2)}, u32[]{:S(2)}) collective-permute-start(f32[49,128]{1,0:T(8,128)S(1)} %maximum_bitcast_fusion), channel_id=1, source_target_pairs={{0,10},{2,8},{8,2},{10,0},{1,11},{3,9},{9,3},{11,1},{4,14},{6,12},... | collective-permute-start | bytes 75272 | tf_op jit(solution)/shard_map/ppermute | solution.py:788
  (149 other events, 1513.0 us)
Sparse Core Ops, SparseCore 0:
  359.3 56.5 reduce-scatter.1

commit v6 on v5

--- a/solution.py
+++ b/solution.py
@@ -632,7 +632,7 @@
 
 def row_call(kernel, name, kinds, *args):
     count, model = args[0].shape
-    block = count // 4
+    block = count // 2
 
     def spec(one):
         if one:
@@ -642,7 +642,7 @@
     shapes = [jax.ShapeDtypeStruct((1 if k is None else count, model), k or jnp.float32) for k in kinds]
     return pl.pallas_call(
         kernel,
-        grid=(4,),
+        grid=(2,),
         in_specs=[spec(a.shape[0] == 1) for a in args],
         out_specs=[spec(k is None) for k in kinds],
         out_shape=shapes,
@@ -705,45 +705,43 @@
     return out.transpose(1, 0, 2)
 
 
-def near_kernel(*refs, number, ends):
+def near_kernel(*refs, number):
     home_ref, away_ref = refs[2 * number :]
-    block = pl.program_id(0)
-    last = pl.num_programs(0) // ends
-    for k in range(number):
-        keep_ref, came_ref = refs[2 * k], refs[2 * k + 1]
-        low = sum(refs[2 * j].shape[2] for j in range(k))
-        total = keep_ref[0] + came_ref[0].astype(jnp.float32)
+    at_home = pl.program_id(0) == pl.num_programs(0) - 1
+    low = 0
+    for keep_ref, came_ref in zip(refs[: 2 * number : 2], refs[1 : 2 * number : 2]):
         lanes = slice(low, low + keep_ref.shape[2])
-
-        @pl.when(block < pl.num_programs(0) - last)
+        low += keep_ref.shape[2]
+
+        @pl.when(jnp.logical_not(at_home))
         def _():
-            away_ref[0, :, lanes] = total.astype(BF)
-
-        @pl.when(block >= pl.num_programs(0) - last)
+            total = keep_ref[...] + came_ref[...].astype(jnp.float32)
+            away_ref[:, :, lanes] = total.astype(BF)
+
+        @pl.when(at_home)
         def _():
-            home_ref[0, :, lanes] = total
+            home_ref[:, :, lanes] = keep_ref[...] + came_ref[...].astype(jnp.float32)
 
 
 def near_sums(pairs, estimate=SHORT):
     highs = lax.axis_size("h")
     blocks, rows, _ = pairs[0][0].shape
-    away_count = blocks - 2
     wide = sum(keep.shape[2] for keep, _ in pairs)
     specs, args = [], []
     for pair in pairs:
-        specs += [pl.BlockSpec((1,) + pair[0].shape[1:], lambda i: (i, 0, 0))] * 2
+        specs += [pl.BlockSpec((2,) + pair[0].shape[1:], lambda i: (i, 0, 0))] * 2
         args += list(pair)
     home, away = pl.pallas_call(
-        functools.partial(near_kernel, number=len(pairs), ends=highs),
-        grid=(blocks,),
+        functools.partial(near_kernel, number=len(pairs)),
+        grid=(highs,),
         in_specs=specs,
         out_specs=[
-            pl.BlockSpec((1, rows, wide), lambda i: (jnp.maximum(i - away_count, 0), 0, 0)),
-            pl.BlockSpec((1, rows, wide), lambda i: (jnp.minimum(i, away_count - 1), 0, 0)),
+            pl.BlockSpec((2, rows, wide), lambda i: (0, 0, 0)),
+            pl.BlockSpec((2, rows, wide), lambda i: (jnp.minimum(i, highs - 2), 0, 0)),
         ],
         out_shape=[
             jax.ShapeDtypeStruct((2, rows, wide), jnp.float32),
-            jax.ShapeDtypeStruct((away_count, rows, wide), BF),
+            jax.ShapeDtypeStruct((blocks - 2, rows, wide), BF),
         ],
         compiler_params=PARAMS,
         cost_estimate=estimate,

time: 545 us -> 546 us (level)
  Pallas kernels: 212 us -> 201 us
  waiting for transfers between devices: 158 us -> 167 us
    pallas_call x10, Pallas kernels: 40.7 us -> 30.4 us  [the longest x7 20.8 us: near_sums(): pl.pallas_call(functools.partial(near_kernel, number=len(pairs)), grid=(h...]
    ppermute x68, waiting for transfers between devices: 108 us -> 115 us  [swap(): lax.ppermute(values, axes, [(s, total - 1 - s) for s in range(total)])]
  transfers between devices with their start and end apart: 91 -> 91, of which waited for: 31 -> 34; matrix products, arithmetic and copies ran while one was open for 5% -> 5% of each run, Pallas kernels for 32% -> 31%
where the time goes in v6:
time: 546 us; the launch traced here: 540 us
  Pallas kernels  201 us (37%)
  waiting for transfers between devices  167 us (31%)
  starting transfers between devices  103 us (19%)
  local copies, waits for them, and re-layouts  37.7 us (7%)
  between operations  15.6 us (3%)
  other arithmetic  14.6 us (3%)
    ppermute x68, waiting for transfers between devices, swap(): lax.ppermute(values, axes, [(s, total - 1 - s) for s in range(total)])  115 us
    ppermute x68, starting transfers between devices, swap(): lax.ppermute(values, axes, [(s, total - 1 - s) for s in range(total)])  56.4 us
    pallas_call x8, Pallas kernels, grad_product(): pl.pallas_call(functools.partial(grad_kernel, number=len(grads)), grid_sp...  54.2 us
    ppermute x15, waiting for transfers between devices, shift(): lax.ppermute(values, 'h', [(s, (s + steps) % total) for s in range(total)])  40.8 us
    pallas_call x1, Pallas kernels, mixer_backward(): pl.pallas_call(functools.partial(mixer_backward_kernel, sources=layout),...  24 us
    pallas_call x1, Pallas kernels, ffn(): pl.pallas_call(functools.partial(ffn_kernel, sources=layout, units=width)...  23.8 us
    all_to_all x6, starting transfers between devices, trade(): return lax.all_to_all(slices, GROUP, 0, 0, tiled=True)  23.4 us
    unnamed x184, local copies, waits for them, and re-layouts  23.2 us
  transfers between devices with their start and end apart: 91, of which 34 were waited for; matrix products, arithmetic and copies ran while one was open for 5% of the time, Pallas kernels for 31%

profile of v6, /device:TPU:0, one launch (start us, length us, event | category | flops | bytes accessed | tf_op | source)
XLA Modules:
  0.0 539.8 jit_solution(7393645849990457766)
XLA Ops:
  11.3 5.2 all-to-all-start
  25.8 5.8 %all-to-all-done = bf16[4,144,1024]{2,1,0:T(8,128)(2,1)S(1)} async-done(((bf16[4,144,1024]{2,1,0:T(8,128)(2,1)}), bf16[4,144,1024]{2,1,0:T(8,128)(2,1)S(1)}, u32[]{:S(2)}, u32[]{:S(2)}) %all-to-all-start) | async-done | bytes 1179680 | tf_op jit(solution)/shard_map/all_to_all | solution.py:831
  32.8 3.6 all-to-all-start.1
  49.0 17.0 %collective-permute-done.refs_1_ = bf16[128,2048]{1,0:T(8,128)(2,1)} collective-permute-done((bf16[128,2048]{1,0:T(8,128)(2,1)S(1)}, bf16[128,2048]{1,0:T(8,128)(2,1)}, u32[]{:S(2)}, u32[]{:S(2)}) %collective-permute-start) | collective-permute-done | bytes 524320 | tf_op jit(solution)/shard_map/ppermute | solution.py:786
  66.0 22.1 %collective-permute-done.1.refs_2_ = bf16[128,2048]{1,0:T(8,128)(2,1)} collective-permute-done((bf16[128,2048]{1,0:T(8,128)(2,1)S(1)}, bf16[128,2048]{1,0:T(8,128)(2,1)}, u32[]{:S(2)}, u32[]{:S(2)}) %collective-permute-start.1) | collective-permute-done | bytes 524320 | tf_op jit(solution)/shard_map/ppermute | solution.py:786
  98.2 19.8 %collective-permute-done.9.refs_7_.refs_9_.refs_4_ = bf16[4,128,256]{2,1,0:T(8,128)(2,1)S(1)} collective-permute-done((bf16[4,128,256]{2,1,0:T(8,128)(2,1)S(1)}, bf16[4,128,256]{2,1,0:T(8,128)(2,1)S(1)}, u32[]{:S(2)}, u32[]{:S(2)}) %collective-permute-start.9) | collective-permute-done | bytes 262176 | tf_op jit(solution)/shard_map/ppermute | solution.py:786
  131.0 17.9 %mixer_forward.1 = (f32[4,256,768]{2,1,0:T(8,128)}, bf16[4,256,256]{2,1,0:T(8,128)(2,1)}, bf16[3,128,2048]{2,1,0:T(8,128)(2,1)}, bf16[128,2048]{1,0:T(8,128)(2,1)}, f32[4,128,2048]{2,1,0:T(8,128)}) custom-call(s32[2]{0:T(128)} %pad_add_fusion.1.core_ref, s32[16]{0:T(128)} %stack.222.offsets_ref, bf16[128,2048]{1,0:T(8,128)(2,1)} %fusion.4.refs_0_, ...), custom_call_target="tpu_custom_call" | custom-call | flops 49999998976 | bytes 1 | tf_op jit(solution)/shard_map/mixer_forward/pallas_call | solution.py:297
  159.0 4.1 collective-permute-done.19.refs_17_
  169.9 8.6 %collective-permute-done.22.refs_18_ = bf16[4,128,256]{2,1,0:T(8,128)(2,1)S(1)} collective-permute-done((bf16[4,128,256]{2,1,0:T(8,128)(2,1)S(1)}, bf16[4,128,256]{2,1,0:T(8,128)(2,1)S(1)}, u32[]{:S(2)}, u32[]{:S(2)}) %collective-permute-start.22) | collective-permute-done | bytes 262176 | tf_op jit(solution)/shard_map/ppermute | solution.py:791
  184.9 12.6 %collective-permute-done.27.refs_19_ = bf16[4,128,256]{2,1,0:T(8,128)(2,1)S(1)} collective-permute-done((bf16[4,128,256]{2,1,0:T(8,128)(2,1)S(1)}, bf16[4,128,256]{2,1,0:T(8,128)(2,1)S(1)}, u32[]{:S(2)}, u32[]{:S(2)}) %collective-permute-start.27) | collective-permute-done | bytes 262176 | tf_op jit(solution)/shard_map/ppermute | solution.py:791
  209.0 8.9 %tops_product.1.refs_6_ = f32[4,256,768]{2,1,0:T(8,128)} custom-call(s32[2]{0:T(128)} %pad_add_fusion.1.core_ref, s32[16]{0:T(128)} %stack.222.offsets_ref, bf16[128,2048]{1,0:T(8,128)(2,1)} %add_ref.1, bf16[128,2048]{1,0:T(8,128)(2,1)} %collective-permute-done.4.refs_1_, bf16[128,2048]{1,0:T(8,128)(2,1)} %copy-done.29, ...), custom_call_target="tpu_custom_call" | custom-call | flops 49999998976 | bytes 1 | tf_op jit(solution)/shard_map/tops_product/pallas_call | solution.py:393
  217.9 4.2 collective-permute-done.32.refs_20_
  229.7 6.7 %collective-permute-done.36.refs_21_ = bf16[4,128,256]{2,1,0:T(8,128)(2,1)} collective-permute-done((bf16[4,128,256]{2,1,0:T(8,128)(2,1)S(1)}, bf16[4,128,256]{2,1,0:T(8,128)(2,1)}, u32[]{:S(2)}, u32[]{:S(2)}) %collective-permute-start.36) | collective-permute-done | bytes 262176 | tf_op jit(solution)/shard_map/ppermute | solution.py:791
  239.1 7.2 %collective-permute-done.41.refs_27_ = bf16[4,128,256]{2,1,0:T(8,128)(2,1)S(1)} collective-permute-done((bf16[4,128,256]{2,1,0:T(8,128)(2,1)}, bf16[4,128,256]{2,1,0:T(8,128)(2,1)S(1)}, u32[]{:S(2)}, u32[]{:S(2)}) %collective-permute-start.41) | collective-permute-done | bytes 262176 | tf_op jit(solution)/shard_map/ppermute | solution.py:786
  248.1 23.8 %ffn.1 = (bf16[4,256,256]{2,1,0:T(8,128)(2,1)}, bf16[4,256,128]{2,1,0:T(8,128)(2,1)}, bf16[4,256,384]{2,1,0:T(8,128)(2,1)}, bf16[4,256,256]{2,1,0:T(8,128)(2,1)}...) custom-call(s32[2]{0:T(128)} %pad_add_fusion.1.core_ref, ...), custom_call_target="tpu_custom_call" | custom-call | flops 49999998976 | bytes 1 | tf_op jit(solution)/shard_map/ffn/pallas_call | solution.py:453
  272.5 6.3 %grad_product.8 = (bf16[4,256,256]{2,1,0:T(8,128)(2,1)}, bf16[4,256,256]{2,1,0:T(8,128)(2,1)}, bf16[4,256,256]{2,1,0:T(8,128)(2,1)}) custom-call(s32[2]{0:T(128)} %pad_add_fusion.1.core_ref, s32[4]{0:T(128)} %get-tuple-element.592.blocks_ref, bf16[128,2048]{1,0:T(8,128)(2,1)} %add_ref.1, bf16[128,2048]{1,0:T(8,128)(2,1)} %collective-permute-done.4.refs_1_, ...), custom_call_target="tpu_custom_call" | custom-call | flops 49999998976 | bytes 1 | tf_op jit(solution)/shard_map/grad_product/pallas_call | solution.py:540
  283.7 8.8 %grad_product.9 = (bf16[4,256,256]{2,1,0:T(8,128)(2,1)}, bf16[4,256,128]{2,1,0:T(8,128)(2,1)}, bf16[4,256,384]{2,1,0:T(8,128)(2,1)}, bf16[4,256,256]{2,1,0:T(8,1...) custom-call(s32[2]{0:T(128)} %pad_add_fusion.1.core_ref, s32[4]{0:T(128)} %get-tuple-element.592.blocks_ref, ...), custom_call_target="tpu_custom_call" | custom-call | flops 49999998976 | bytes 1 | tf_op jit(solution)/shard_map/grad_product/pallas_call | solution.py:540
  301.4 6.5 %grad_product.10 = (f32[4,256,256]{2,1,0:T(8,128)}, f32[4,256,256]{2,1,0:T(8,128)}, f32[4,256,256]{2,1,0:T(8,128)}) custom-call(s32[2]{0:T(128)} %pad_add_fusion.1.core_ref, s32[4]{0:T(128)} %get-tuple-element.593.blocks_ref, bf16[128,2048]{1,0:T(8,128)(2,1)} %add_ref.1, bf16[128,2048]{1,0:T(8,128)(2,1)} %collective-permute-done.4.refs_1_, ...), custom_call_target="tpu_custom_call" | custom-call | flops 49999998976 | bytes 1 | tf_op jit(solution)/shard_map/grad_product/pallas_call | solution.py:540
  312.9 3.5 middle_grad.1
  322.3 8.8 %grad_product.11 = (f32[4,256,256]{2,1,0:T(8,128)}, f32[4,256,128]{2,1,0:T(8,128)}, f32[4,256,384]{2,1,0:T(8,128)}, f32[4,256,256]{2,1,0:T(8,128)}, f32[4,256,256]{2,1,0:T(8,128)}, /*index=5*/f32[4,256,128]{2,1,0:T(8,128)}) custom-call(s32[2]{0:T(128)} %pad_add_fusion.1.core_ref, s32[4]{0:T(128)} %get-tuple-element.593.blocks_ref, ...), custom_call_target="tpu_custom_call" | custom-call | flops 49999998976 | bytes 1 | tf_op jit(solution)/shard_map/grad_product/pallas_call | solution.py:540
  340.7 9.3 %rows_product.1 = bf16[4,256,2048]{2,1,0:T(8,128)(2,1)} custom-call(s32[2]{0:T(128)} %pad_add_fusion.1.core_ref, s32[16]{0:T(128)} %stack.222.offsets_ref, bf16[4,256,256]{2,1,0:T(8,128)(2,1)} %get-tuple-element.442.refs_0_, bf16[4,256,256]{2,1,0:T(8,128)(2,1)} %get-tuple-element.443.refs_1_, bf16[4,256,256]{2,1,0:T(8,128)(2,1)} %get-tuple-element.444.refs_2_, ...), custom_call_target="tpu_custom_call" | custom-call | flops 49999998976 | bytes 1 | tf_op jit(solution)/shard_map/rows_product/pallas_call | solution.py:506
  358.5 24.0 %mixer_backward.1 = (bf16[4,256,256]{2,1,0:T(8,128)(2,1)}, bf16[4,256,256]{2,1,0:T(8,128)(2,1)}, bf16[4,256,256]{2,1,0:T(8,128)(2,1)}, bf16[3,128,2048]{2,1,0:T(...) custom-call(s32[2]{0:T(128)} %pad_add_fusion.1.core_ref, ...), custom_call_target="tpu_custom_call" | custom-call | flops 49999998976 | bytes 1 | tf_op jit(solution)/shard_map/mixer_backward/pallas_call | solution.py:337
  395.6 6.6 %grad_product.12 = (bf16[4,256,256]{2,1,0:T(8,128)(2,1)}, bf16[4,256,256]{2,1,0:T(8,128)(2,1)}, bf16[4,256,256]{2,1,0:T(8,128)(2,1)}) custom-call(s32[2]{0:T(128)} %pad_add_fusion.1.core_ref, s32[4]{0:T(128)} %get-tuple-element.592.blocks_ref, bf16[128,2048]{1,0:T(8,128)(2,1)} %fusion.4.refs_0_, bf16[128,2048]{1,0:T(8,128)(2,1)} %collective-permute-done.refs_1_, ...), custom_call_target="tpu_custom_call" | custom-call | flops 49999998976 | bytes 1 | tf_op jit(solution)/shard_map/grad_product/pallas_call | solution.py:540
  411.9 3.8 collective-permute-done.64
  424.0 6.5 %grad_product.13 = (f32[4,256,256]{2,1,0:T(8,128)}, f32[4,256,256]{2,1,0:T(8,128)}, f32[4,256,256]{2,1,0:T(8,128)}) custom-call(s32[2]{0:T(128)} %pad_add_fusion.1.core_ref, s32[4]{0:T(128)} %get-tuple-element.593.blocks_ref, bf16[128,2048]{1,0:T(8,128)(2,1)} %fusion.4.refs_0_, bf16[128,2048]{1,0:T(8,128)(2,1)} %collective-permute-done.refs_1_, ...), custom_call_target="tpu_custom_call" | custom-call | flops 49999998976 | bytes 1 | tf_op jit(solution)/shard_map/grad_product/pallas_call | solution.py:540
  430.5 5.3 grad_product.14
  438.6 7.1 %collective-permute-done.72.refs_3_ = bf16[4,256,256]{2,1,0:T(8,128)(2,1)S(1)} collective-permute-done((bf16[4,256,256]{2,1,0:T(8,128)(2,1)S(1)}, bf16[4,256,256]{2,1,0:T(8,128)(2,1)S(1)}, u32[]{:S(2)}, u32[]{:S(2)}) %collective-permute-start.72) | collective-permute-done | bytes 524320 | tf_op jit(solution)/shard_map/ppermute | solution.py:786
  453.5 4.1 all-to-all-start.3
  461.7 5.5 %grad_product.15.refs_0_ = f32[4,256,256]{2,1,0:T(8,128)} custom-call(s32[2]{0:T(128)} %pad_add_fusion.1.core_ref, s32[4]{0:T(128)} %get-tuple-element.593.blocks_ref, bf16[128,2048]{1,0:T(8,128)(2,1)} %get-tuple-element.533.refs_0_, bf16[128,2048]{1,0:T(8,128)(2,1)} %copy-done.5, bf16[128,2048]{1,0:T(8,128)(2,1)} %copy-done.6, ...), custom_call_target="tpu_custom_call" | custom-call | flops 1 | bytes 1 | tf_op jit(solution)/shard_map/grad_product/pallas_call | solution.py:540
  479.7 3.5 all-to-all-start.4
  487.9 20.3 %collective-permute-done.79 = f32[49,128]{1,0:T(8,128)S(1)} collective-permute-done((f32[49,128]{1,0:T(8,128)S(1)}, f32[49,128]{1,0:T(8,128)S(1)}, u32[]{:S(2)}, u32[]{:S(2)}) %collective-permute-start.79) | collective-permute-done | bytes 25120 | tf_op jit(solution)/shard_map/ppermute | solution.py:786
  520.8 4.4 ffn_grad.1
  (423 shorter events, 222.4 us)
Async XLA Ops:
  32.8 55.3 %all-to-all-start.1 = ((bf16[4,128,1408]{2,1,0:T(8,128)(2,1)}), bf16[4,128,1408]{2,1,0:T(8,128)(2,1)S(1)}, u32[]{:S(2)}, u32[]{:S(2)}) async-start(bf16[4,128,1408]{2,1,0:T(8,128)(2,1)} %slice.64), calls=%async_computation.1 | async-start | bytes 2883584 | tf_op jit(solution)/shard_map/all_to_all | solution.py:831
  37.4 50.7 %collective-permute-start.2 = (bf16[4,128,1024]{2,1,0:T(8,128)(2,1)}, bf16[4,128,1024]{2,1,0:T(8,128)(2,1)}, u32[]{:S(2)}, u32[]{:S(2)}) collective-permute-start(bf16[4,128,1024]{2,1,0:T(8,128)(2,1)} %slice.63.refs_6_), channel_id=1, source_target_pairs={{0,16},{16,0},{1,17},{17,1},{2,18},{18,2},{3,19},{19,3},{4,20},{20... | collective-permute-start | bytes 3145736 | tf_op jit(solution)/shard_map/ppermute | solution.py:791
  40.0 48.1 %collective-permute-start.3 = (bf16[4,128,1024]{2,1,0:T(8,128)(2,1)}, bf16[4,128,1024]{2,1,0:T(8,128)(2,1)}, u32[]{:S(2)}, u32[]{:S(2)}) collective-permute-start(bf16[4,128,1024]{2,1,0:T(8,128)(2,1)} %slice.63.refs_6_), channel_id=1, source_target_pairs={{0,4},{4,0},{1,5},{5,1},{2,6},{6,2},{3,7},{7,3},{8,12},{12,8},{9,1... | collective-permute-start | bytes 3145736 | tf_op jit(solution)/shard_map/ppermute | solution.py:786
  41.5 24.5 %collective-permute-start = (bf16[128,2048]{1,0:T(8,128)(2,1)S(1)}, bf16[128,2048]{1,0:T(8,128)(2,1)}, u32[]{:S(2)}, u32[]{:S(2)}) collective-permute-start(bf16[128,2048]{1,0:T(8,128)(2,1)S(1)} %copy-done.10), channel_id=1, source_target_pairs={{0,2},{2,0},{1,3},{3,1},{4,6},{6,4},{5,7},{7,5},{8,10},{10,8},{9,1... | collective-permute-start | bytes 1572872 | tf_op jit(solution)/shard_map/ppermute | solution.py:786
  43.6 44.6 %collective-permute-start.1 = (bf16[128,2048]{1,0:T(8,128)(2,1)S(1)}, bf16[128,2048]{1,0:T(8,128)(2,1)}, u32[]{:S(2)}, u32[]{:S(2)}) collective-permute-start(bf16[128,2048]{1,0:T(8,128)(2,1)S(1)} %copy-done.10), channel_id=1, source_target_pairs={{0,8},{8,0},{1,9},{9,1},{2,10},{10,2},{3,11},{11,3},{4,12},{12,4},... | collective-permute-start | bytes 1572872 | tf_op jit(solution)/shard_map/ppermute | solution.py:786
  45.0 43.2 %collective-permute-start.4 = (bf16[128,2048]{1,0:T(8,128)(2,1)}, bf16[128,2048]{1,0:T(8,128)(2,1)}, u32[]{:S(2)}, u32[]{:S(2)}) collective-permute-start(bf16[128,2048]{1,0:T(8,128)(2,1)} %add_ref.1), channel_id=1, source_target_pairs={{0,2},{2,0},{1,3},{3,1},{4,6},{6,4},{5,7},{7,5},{8,10},{10,8},{9,1... | collective-permute-start | bytes 1572872 | tf_op jit(solution)/shard_map/ppermute | solution.py:786
  88.2 29.9 %collective-permute-start.6 = (bf16[4,128,1024]{2,1,0:T(8,128)(2,1)}, bf16[4,128,1024]{2,1,0:T(8,128)(2,1)S(1)}, u32[]{:S(2)}, u32[]{:S(2)}) collective-permute-start(bf16[4,128,1024]{2,1,0:T(8,128)(2,1)} %collective-permute-done.2.refs_8_), channel_id=1, source_target_pairs={{0,4},{4,0},{1,5},{5,1},{2,6},{6,2},{3,7},{7,3},{8,12},{12,8},{9,1... | collective-permute-start | bytes 3145736 | tf_op jit(solution)/shard_map/ppermute | solution.py:786
  89.8 28.2 %collective-permute-start.5 = (bf16[128,2048]{1,0:T(8,128)(2,1)}, bf16[128,2048]{1,0:T(8,128)(2,1)}, u32[]{:S(2)}, u32[]{:S(2)}) collective-permute-start(bf16[128,2048]{1,0:T(8,128)(2,1)} %collective-permute-done.1.refs_2_), channel_id=1, source_target_pairs={{0,2},{2,0},{1,3},{3,1},{4,6},{6,4},{5,7},{7,5},{8,10},{10,8},{9,1... | collective-permute-start | bytes 1572872 | tf_op jit(solution)/shard_map/ppermute | solution.py:786
  91.6 26.4 %collective-permute-start.7 = (bf16[4,128,512]{2,1,0:T(8,128)(2,1)S(1)}, bf16[4,128,512]{2,1,0:T(8,128)(2,1)S(1)}, u32[]{:S(2)}, u32[]{:S(2)}) collective-permute-start(bf16[4,128,512]{2,1,0:T(8,128)(2,1)S(1)} %get-tuple-element.300), channel_id=1, source_target_pairs={{0,16},{16,0},{1,17},{17,1},{2,18},{18,2},{3,19},{19,3},{4,20},{20... | collective-permute-start | bytes 1572872 | tf_op jit(solution)/shard_map/ppermute | solution.py:791
  94.3 23.7 %collective-permute-start.8 = (bf16[128,2048]{1,0:T(8,128)(2,1)}, bf16[128,2048]{1,0:T(8,128)(2,1)S(1)}, u32[]{:S(2)}, u32[]{:S(2)}) collective-permute-start(bf16[128,2048]{1,0:T(8,128)(2,1)} %add_ref.1), channel_id=1, source_target_pairs={{0,8},{8,0},{1,9},{9,1},{2,10},{10,2},{3,11},{11,3},{4,12},{12,4},... | collective-permute-start | bytes 1572872 | tf_op jit(solution)/shard_map/ppermute | solution.py:786
  122.5 26.4 %collective-permute-start.12 = (bf16[4,128,512]{2,1,0:T(8,128)(2,1)}, bf16[4,128,512]{2,1,0:T(8,128)(2,1)}, u32[]{:S(2)}, u32[]{:S(2)}) collective-permute-start(bf16[4,128,512]{2,1,0:T(8,128)(2,1)} %get-tuple-element.315), channel_id=1, source_target_pairs={{0,16},{16,0},{1,17},{17,1},{2,18},{18,2},{3,19},{19,3},{4,20},{20... | collective-permute-start | bytes 1572872 | tf_op jit(solution)/shard_map/ppermute | solution.py:791
  125.1 23.8 %collective-permute-start.13 = (bf16[4,128,512]{2,1,0:T(8,128)(2,1)}, bf16[4,128,512]{2,1,0:T(8,128)(2,1)}, u32[]{:S(2)}, u32[]{:S(2)}) collective-permute-start(bf16[4,128,512]{2,1,0:T(8,128)(2,1)} %get-tuple-element.316), channel_id=1, source_target_pairs={{0,4},{4,0},{1,5},{5,1},{2,6},{6,2},{3,7},{7,3},{8,12},{12,8},{9,1... | collective-permute-start | bytes 1572872 | tf_op jit(solution)/shard_map/ppermute | solution.py:786
  126.7 24.0 %collective-permute-start.14 = (bf16[4,128,512]{2,1,0:T(8,128)(2,1)}, bf16[4,128,512]{2,1,0:T(8,128)(2,1)}, u32[]{:S(2)}, u32[]{:S(2)}) collective-permute-start(bf16[4,128,512]{2,1,0:T(8,128)(2,1)} %copy-done.56), channel_id=1, source_target_pairs={{0,4},{4,0},{1,5},{5,1},{2,6},{6,2},{3,7},{7,3},{8,12},{12,8},{9,1... | collective-permute-start | bytes 1572872 | tf_op jit(solution)/shard_map/ppermute | solution.py:786
  127.2 23.5 %collective-permute-start.15 = (bf16[128,2048]{1,0:T(8,128)(2,1)}, bf16[128,2048]{1,0:T(8,128)(2,1)}, u32[]{:S(2)}, u32[]{:S(2)}) collective-permute-start(bf16[128,2048]{1,0:T(8,128)(2,1)} %copy-done.29), channel_id=1, source_target_pairs={{0,2},{2,0},{1,3},{3,1},{4,6},{6,4},{5,7},{7,5},{8,10},{10,8},{9,1... | collective-permute-start | bytes 1572872 | tf_op jit(solution)/shard_map/ppermute | solution.py:786
  127.2 25.4 %all-to-all-start.2 = ((bf16[4,128,768]{2,1,0:T(8,128)(2,1)}), bf16[4,128,768]{2,1,0:T(8,128)(2,1)S(1)}, u32[]{:S(2)}, u32[]{:S(2)}) async-start(bf16[4,128,768]{2,1,0:T(8,128)(2,1)} %slice.65), calls=%async_computation.2 | async-start | bytes 1572864 | tf_op jit(solution)/shard_map/all_to_all | solution.py:831
  130.7 336.5 %reduce-scatter.2.cloned.1.call-start = ((), (), s32[]{:S(2)}) async-start(), calls=%async_computation.7 | async-start | bytes 4718592 | tf_op jit(solution)/shard_map/reduce_scatter | solution.py:1113
  350.8 31.8 %collective-permute-start.60 = (bf16[4,256,384]{2,1,0:T(8,128)(2,1)}, bf16[4,256,384]{2,1,0:T(8,128)(2,1)S(1)}, u32[]{:S(2)}, u32[]{:S(2)}) collective-permute-start(bf16[4,256,384]{2,1,0:T(8,128)(2,1)} %get-tuple-element.468), channel_id=1, source_target_pairs={{0,4},{4,0},{1,5},{5,1},{2,6},{6,2},{3,7},{7,3},{8,12},{12,8},{9,1... | collective-permute-start | bytes 2359304 | tf_op jit(solution)/shard_map/ppermute | solution.py:786
  351.3 31.3 %collective-permute-start.61 = (bf16[4,256,256]{2,1,0:T(8,128)(2,1)}, bf16[4,256,256]{2,1,0:T(8,128)(2,1)S(1)}, u32[]{:S(2)}, u32[]{:S(2)}) collective-permute-start(bf16[4,256,256]{2,1,0:T(8,128)(2,1)} %get-tuple-element.469), channel_id=1, source_target_pairs={{0,4},{4,0},{1,5},{5,1},{2,6},{6,2},{3,7},{7,3},{8,12},{12,8},{9,1... | collective-permute-start | bytes 1572872 | tf_op jit(solution)/shard_map/ppermute | solution.py:786
  357.3 25.8 %collective-permute-start.59 = (bf16[2,256,512]{2,1,0:T(8,128)(2,1)}, bf16[2,256,512]{2,1,0:T(8,128)(2,1)S(1)}, u32[]{:S(2)}, u32[]{:S(2)}) collective-permute-start(bf16[2,256,512]{2,1,0:T(8,128)(2,1)} %get-tuple-element.467), channel_id=1, source_target_pairs={{0,16},{16,0},{1,17},{17,1},{2,18},{18,2},{3,19},{19,3},{4,20},{20... | collective-permute-start | bytes 1572872 | tf_op jit(solution)/shard_map/ppermute | solution.py:791
  384.4 22.4 %collective-permute-start.66 = (bf16[4,256,256]{2,1,0:T(8,128)(2,1)S(1)}, bf16[4,256,256]{2,1,0:T(8,128)(2,1)S(1)}, u32[]{:S(2)}, u32[]{:S(2)}) collective-permute-start(bf16[4,256,256]{2,1,0:T(8,128)(2,1)S(1)} %copy-done.58), channel_id=1, source_target_pairs={{0,4},{4,0},{1,5},{5,1},{2,6},{6,2},{3,7},{7,3},{8,12},{12,8},{9,1... | collective-permute-start | bytes 1572872 | tf_op jit(solution)/shard_map/ppermute | solution.py:786
  391.3 24.4 %collective-permute-start.64 = (bf16[128,2048]{1,0:T(8,128)(2,1)}, bf16[128,2048]{1,0:T(8,128)(2,1)S(1)}, u32[]{:S(2)}, u32[]{:S(2)}) collective-permute-start(bf16[128,2048]{1,0:T(8,128)(2,1)} %add_last.5), channel_id=1, source_target_pairs={{0,2},{2,0},{1,3},{3,1},{4,6},{6,4},{5,7},{7,5},{8,10},{10,8},{9,1... | collective-permute-start | bytes 1572872 | tf_op jit(solution)/shard_map/ppermute | solution.py:786
  393.2 25.8 %collective-permute-start.65 = (bf16[2,256,512]{2,1,0:T(8,128)(2,1)S(1)}, bf16[2,256,512]{2,1,0:T(8,128)(2,1)S(1)}, u32[]{:S(2)}, u32[]{:S(2)}) collective-permute-start(bf16[2,256,512]{2,1,0:T(8,128)(2,1)S(1)} %copy-done.68), channel_id=1, source_target_pairs={{0,16},{16,0},{1,17},{17,1},{2,18},{18,2},{3,19},{19,3},{4,20},{20... | collective-permute-start | bytes 1572872 | tf_op jit(solution)/shard_map/ppermute | solution.py:791
  419.0 30.7 %collective-permute-start.68 = (bf16[128,2048]{1,0:T(8,128)(2,1)S(1)}, bf16[128,2048]{1,0:T(8,128)(2,1)S(1)}, u32[]{:S(2)}, u32[]{:S(2)}) collective-permute-start(bf16[128,2048]{1,0:T(8,128)(2,1)S(1)} %copy-done.63), channel_id=1, source_target_pairs={{0,2},{2,0},{1,3},{3,1},{4,6},{6,4},{5,7},{7,5},{8,10},{10,8},{9,1... | collective-permute-start | bytes 1572872 | tf_op jit(solution)/shard_map/ppermute | solution.py:786
  419.5 30.2 %collective-permute-start.69 = (bf16[128,2048]{1,0:T(8,128)(2,1)S(1)}, bf16[128,2048]{1,0:T(8,128)(2,1)S(1)}, u32[]{:S(2)}, u32[]{:S(2)}) collective-permute-start(bf16[128,2048]{1,0:T(8,128)(2,1)S(1)} %add_convert_fusion.1), channel_id=1, source_target_pairs={{0,8},{8,0},{1,9},{9,1},{2,10},{10,2},{3,11},{11,3},{4,12},{12,4},... | collective-permute-start | bytes 1572872 | tf_op jit(solution)/shard_map/ppermute | solution.py:786
  419.6 31.0 %collective-permute-start.70 = (bf16[2,256,640]{2,1,0:T(8,128)(2,1)S(1)}, bf16[2,256,640]{2,1,0:T(8,128)(2,1)S(1)}, u32[]{:S(2)}, u32[]{:S(2)}) collective-permute-start(bf16[2,256,640]{2,1,0:T(8,128)(2,1)S(1)} %copy-done.54), channel_id=1, source_target_pairs={{0,16},{16,0},{1,17},{17,1},{2,18},{18,2},{3,19},{19,3},{4,20},{20... | collective-permute-start | bytes 1966088 | tf_op jit(solution)/shard_map/ppermute | solution.py:791
  422.7 23.0 %collective-permute-start.72 = (bf16[4,256,256]{2,1,0:T(8,128)(2,1)S(1)}, bf16[4,256,256]{2,1,0:T(8,128)(2,1)S(1)}, u32[]{:S(2)}, u32[]{:S(2)}) collective-permute-start(bf16[4,256,256]{2,1,0:T(8,128)(2,1)S(1)} %copy-done.64), channel_id=1, source_target_pairs={{0,4},{4,0},{1,5},{5,1},{2,6},{6,2},{3,7},{7,3},{8,12},{12,8},{9,1... | collective-permute-start | bytes 1572872 | tf_op jit(solution)/shard_map/ppermute | solution.py:786
  450.5 27.1 %collective-permute-start.73 = (bf16[2,256,512]{2,1,0:T(8,128)(2,1)}, bf16[2,256,512]{2,1,0:T(8,128)(2,1)}, u32[]{:S(2)}, u32[]{:S(2)}) collective-permute-start(bf16[2,256,512]{2,1,0:T(8,128)(2,1)} %get-tuple-element.541), channel_id=1, source_target_pairs={{0,16},{16,0},{1,17},{17,1},{2,18},{18,2},{3,19},{19,3},{4,20},{20... | collective-permute-start | bytes 1572872 | tf_op jit(solution)/shard_map/ppermute | solution.py:791
  452.1 22.5 %collective-permute-start.75 = (bf16[4,256,256]{2,1,0:T(8,128)(2,1)}, bf16[4,256,256]{2,1,0:T(8,128)(2,1)}, u32[]{:S(2)}, u32[]{:S(2)}) collective-permute-start(bf16[4,256,256]{2,1,0:T(8,128)(2,1)} %get-tuple-element.552), channel_id=1, source_target_pairs={{0,4},{4,0},{1,5},{5,1},{2,6},{6,2},{3,7},{7,3},{8,12},{12,8},{9,1... | collective-permute-start | bytes 1572872 | tf_op jit(solution)/shard_map/ppermute | solution.py:786
  453.5 26.2 %all-to-all-start.3 = ((bf16[4,128,1024]{2,1,0:T(8,128)(2,1)}), bf16[4,128,1024]{2,1,0:T(8,128)(2,1)S(1)}, u32[]{:S(2)}, u32[]{:S(2)}) async-start(bf16[4,128,1024]{2,1,0:T(8,128)(2,1)} %bitcast.64), calls=%async_computation.4 | async-start | bytes 2097152 | tf_op jit(solution)/shard_map/all_to_all | solution.py:831
  479.7 28.6 %all-to-all-start.4 = ((bf16[4,128,1152]{2,1,0:T(8,128)(2,1)}), bf16[4,128,1152]{2,1,0:T(8,128)(2,1)S(1)}, u32[]{:S(2)}, u32[]{:S(2)}) async-start(bf16[4,128,1152]{2,1,0:T(8,128)(2,1)} %bitcast.66), calls=%async_computation.5 | async-start | bytes 2359296 | tf_op jit(solution)/shard_map/all_to_all | solution.py:831
  483.2 25.1 %collective-permute-start.76 = (bf16[2,256,512]{2,1,0:T(8,128)(2,1)}, bf16[2,256,512]{2,1,0:T(8,128)(2,1)S(1)}, u32[]{:S(2)}, u32[]{:S(2)}) collective-permute-start(bf16[2,256,512]{2,1,0:T(8,128)(2,1)} %get-tuple-element.562), channel_id=1, source_target_pairs={{0,16},{16,0},{1,17},{17,1},{2,18},{18,2},{3,19},{19,3},{4,20},{20... | collective-permute-start | bytes 1572872 | tf_op jit(solution)/shard_map/ppermute | solution.py:791
  484.4 23.8 %collective-permute-start.79 = (f32[49,128]{1,0:T(8,128)S(1)}, f32[49,128]{1,0:T(8,128)S(1)}, u32[]{:S(2)}, u32[]{:S(2)}) collective-permute-start(f32[49,128]{1,0:T(8,128)S(1)} %maximum_bitcast_fusion), channel_id=1, source_target_pairs={{0,10},{2,8},{8,2},{10,0},{1,11},{3,9},{9,3},{11,1},{4,14},{6,12},... | collective-permute-start | bytes 75272 | tf_op jit(solution)/shard_map/ppermute | solution.py:786
  (149 other events, 1500.7 us)
Sparse Core Ops, SparseCore 0:
  356.1 56.6 reduce-scatter.1

commit v7 on v6

--- a/solution.py
+++ b/solution.py
@@ -565,10 +565,10 @@
 
 def add_last(keep, came):
     count, model = came.shape
-    block = count // 2
+    block = count
     return pl.pallas_call(
         last_kernel,
-        grid=(2,),
+        grid=(1,),
         in_specs=[
             pl.BlockSpec((1, block, model), lambda i: (3, i, 0)),
             pl.BlockSpec((block, model), lambda i: (i, 0)),
@@ -632,7 +632,7 @@
 
 def row_call(kernel, name, kinds, *args):
     count, model = args[0].shape
-    block = count // 2
+    block = count // 4
 
     def spec(one):
         if one:
@@ -642,7 +642,7 @@
     shapes = [jax.ShapeDtypeStruct((1 if k is None else count, model), k or jnp.float32) for k in kinds]
     return pl.pallas_call(
         kernel,
-        grid=(2,),
+        grid=(4,),
         in_specs=[spec(a.shape[0] == 1) for a in args],
         out_specs=[spec(k is None) for k in kinds],
         out_shape=shapes,

time: 546 us -> 549 us (level)
  no operation moved by 1% of the time
where the time goes in v7:
time: 549 us; the launch traced here: 542 us
  Pallas kernels  205 us (37%)
  waiting for transfers between devices  166 us (30%)
  starting transfers between devices  103 us (19%)
  local copies, waits for them, and re-layouts  37.7 us (7%)
  between operations  15.4 us (3%)
  other arithmetic  14.6 us (3%)
    ppermute x68, waiting for transfers between devices, swap(): lax.ppermute(values, axes, [(s, total - 1 - s) for s in range(total)])  113 us
    ppermute x68, starting transfers between devices, swap(): lax.ppermute(values, axes, [(s, total - 1 - s) for s in range(total)])  56.3 us
    pallas_call x8, Pallas kernels, grad_product(): pl.pallas_call(functools.partial(grad_kernel, number=len(grads)), grid_sp...  54.1 us
    ppermute x15, waiting for transfers between devices, shift(): lax.ppermute(values, 'h', [(s, (s + steps) % total) for s in range(total)])  40.9 us
    pallas_call x1, Pallas kernels, mixer_backward(): pl.pallas_call(functools.partial(mixer_backward_kernel, sources=layout),...  24 us
    pallas_call x1, Pallas kernels, ffn(): pl.pallas_call(functools.partial(ffn_kernel, sources=layout, units=width)...  23.8 us
    all_to_all x6, starting transfers between devices, trade(): return lax.all_to_all(slices, GROUP, 0, 0, tiled=True)  23.4 us
    unnamed x184, local copies, waits for them, and re-layouts  23.2 us
  transfers between devices with their start and end apart: 91, of which 34 were waited for; matrix products, arithmetic and copies ran while one was open for 5% of the time, Pallas kernels for 31%

profile of v7, /device:TPU:0, one launch (start us, length us, event | category | flops | bytes accessed | tf_op | source)
XLA Modules:
  0.0 542.3 jit_solution(8836808979612706535)
XLA Ops:
  11.3 5.2 all-to-all-start
  25.8 5.8 %all-to-all-done = bf16[4,144,1024]{2,1,0:T(8,128)(2,1)S(1)} async-done(((bf16[4,144,1024]{2,1,0:T(8,128)(2,1)}), bf16[4,144,1024]{2,1,0:T(8,128)(2,1)S(1)}, u32[]{:S(2)}, u32[]{:S(2)}) %all-to-all-start) | async-done | bytes 1179680 | tf_op jit(solution)/shard_map/all_to_all | solution.py:831
  49.0 17.0 %collective-permute-done.refs_1_ = bf16[128,2048]{1,0:T(8,128)(2,1)} collective-permute-done((bf16[128,2048]{1,0:T(8,128)(2,1)S(1)}, bf16[128,2048]{1,0:T(8,128)(2,1)}, u32[]{:S(2)}, u32[]{:S(2)}) %collective-permute-start) | collective-permute-done | bytes 524320 | tf_op jit(solution)/shard_map/ppermute | solution.py:786
  66.0 22.1 %collective-permute-done.1.refs_2_ = bf16[128,2048]{1,0:T(8,128)(2,1)} collective-permute-done((bf16[128,2048]{1,0:T(8,128)(2,1)S(1)}, bf16[128,2048]{1,0:T(8,128)(2,1)}, u32[]{:S(2)}, u32[]{:S(2)}) %collective-permute-start.1) | collective-permute-done | bytes 524320 | tf_op jit(solution)/shard_map/ppermute | solution.py:786
  98.2 19.8 %collective-permute-done.9.refs_7_.refs_9_.refs_4_ = bf16[4,128,256]{2,1,0:T(8,128)(2,1)S(1)} collective-permute-done((bf16[4,128,256]{2,1,0:T(8,128)(2,1)S(1)}, bf16[4,128,256]{2,1,0:T(8,128)(2,1)S(1)}, u32[]{:S(2)}, u32[]{:S(2)}) %collective-permute-start.9) | collective-permute-done | bytes 262176 | tf_op jit(solution)/shard_map/ppermute | solution.py:786
  131.3 17.9 %mixer_forward.1 = (f32[4,256,768]{2,1,0:T(8,128)}, bf16[4,256,256]{2,1,0:T(8,128)(2,1)}, bf16[3,128,2048]{2,1,0:T(8,128)(2,1)}, bf16[128,2048]{1,0:T(8,128)(2,1)}, f32[4,128,2048]{2,1,0:T(8,128)}) custom-call(s32[2]{0:T(128)} %pad_add_fusion.1.core_ref, s32[16]{0:T(128)} %stack.222.offsets_ref, bf16[128,2048]{1,0:T(8,128)(2,1)} %fusion.4.refs_0_, ...), custom_call_target="tpu_custom_call" | custom-call | flops 49999998976 | bytes 1 | tf_op jit(solution)/shard_map/mixer_forward/pallas_call | solution.py:297
  159.1 4.0 collective-permute-done.19.refs_17_
  169.9 8.6 %collective-permute-done.22.refs_18_ = bf16[4,128,256]{2,1,0:T(8,128)(2,1)S(1)} collective-permute-done((bf16[4,128,256]{2,1,0:T(8,128)(2,1)S(1)}, bf16[4,128,256]{2,1,0:T(8,128)(2,1)S(1)}, u32[]{:S(2)}, u32[]{:S(2)}) %collective-permute-start.22) | collective-permute-done | bytes 262176 | tf_op jit(solution)/shard_map/ppermute | solution.py:791
  184.9 12.6 %collective-permute-done.27.refs_19_ = bf16[4,128,256]{2,1,0:T(8,128)(2,1)S(1)} collective-permute-done((bf16[4,128,256]{2,1,0:T(8,128)(2,1)S(1)}, bf16[4,128,256]{2,1,0:T(8,128)(2,1)S(1)}, u32[]{:S(2)}, u32[]{:S(2)}) %collective-permute-start.27) | collective-permute-done | bytes 262176 | tf_op jit(solution)/shard_map/ppermute | solution.py:791
  200.9 3.9 middle.1
  210.2 8.9 %tops_product.1.refs_6_ = f32[4,256,768]{2,1,0:T(8,128)} custom-call(s32[2]{0:T(128)} %pad_add_fusion.1.core_ref, s32[16]{0:T(128)} %stack.222.offsets_ref, bf16[128,2048]{1,0:T(8,128)(2,1)} %add_ref.1, bf16[128,2048]{1,0:T(8,128)(2,1)} %collective-permute-done.4.refs_1_, bf16[128,2048]{1,0:T(8,128)(2,1)} %copy-done.29, ...), custom_call_target="tpu_custom_call" | custom-call | flops 49999998976 | bytes 1 | tf_op jit(solution)/shard_map/tops_product/pallas_call | solution.py:393
  219.1 4.2 collective-permute-done.32.refs_20_
  230.9 6.7 %collective-permute-done.36.refs_21_ = bf16[4,128,256]{2,1,0:T(8,128)(2,1)} collective-permute-done((bf16[4,128,256]{2,1,0:T(8,128)(2,1)S(1)}, bf16[4,128,256]{2,1,0:T(8,128)(2,1)}, u32[]{:S(2)}, u32[]{:S(2)}) %collective-permute-start.36) | collective-permute-done | bytes 262176 | tf_op jit(solution)/shard_map/ppermute | solution.py:791
  240.3 7.2 %collective-permute-done.41.refs_27_ = bf16[4,128,256]{2,1,0:T(8,128)(2,1)S(1)} collective-permute-done((bf16[4,128,256]{2,1,0:T(8,128)(2,1)}, bf16[4,128,256]{2,1,0:T(8,128)(2,1)S(1)}, u32[]{:S(2)}, u32[]{:S(2)}) %collective-permute-start.41) | collective-permute-done | bytes 262176 | tf_op jit(solution)/shard_map/ppermute | solution.py:786
  249.3 23.8 %ffn.1 = (bf16[4,256,256]{2,1,0:T(8,128)(2,1)}, bf16[4,256,128]{2,1,0:T(8,128)(2,1)}, bf16[4,256,384]{2,1,0:T(8,128)(2,1)}, bf16[4,256,256]{2,1,0:T(8,128)(2,1)}...) custom-call(s32[2]{0:T(128)} %pad_add_fusion.1.core_ref, ...), custom_call_target="tpu_custom_call" | custom-call | flops 49999998976 | bytes 1 | tf_op jit(solution)/shard_map/ffn/pallas_call | solution.py:453
  273.7 6.3 %grad_product.8 = (bf16[4,256,256]{2,1,0:T(8,128)(2,1)}, bf16[4,256,256]{2,1,0:T(8,128)(2,1)}, bf16[4,256,256]{2,1,0:T(8,128)(2,1)}) custom-call(s32[2]{0:T(128)} %pad_add_fusion.1.core_ref, s32[4]{0:T(128)} %get-tuple-element.592.blocks_ref, bf16[128,2048]{1,0:T(8,128)(2,1)} %add_ref.1, bf16[128,2048]{1,0:T(8,128)(2,1)} %collective-permute-done.4.refs_1_, ...), custom_call_target="tpu_custom_call" | custom-call | flops 49999998976 | bytes 1 | tf_op jit(solution)/shard_map/grad_product/pallas_call | solution.py:540
  285.1 8.8 %grad_product.9 = (bf16[4,256,256]{2,1,0:T(8,128)(2,1)}, bf16[4,256,128]{2,1,0:T(8,128)(2,1)}, bf16[4,256,384]{2,1,0:T(8,128)(2,1)}, bf16[4,256,256]{2,1,0:T(8,1...) custom-call(s32[2]{0:T(128)} %pad_add_fusion.1.core_ref, s32[4]{0:T(128)} %get-tuple-element.592.blocks_ref, ...), custom_call_target="tpu_custom_call" | custom-call | flops 49999998976 | bytes 1 | tf_op jit(solution)/shard_map/grad_product/pallas_call | solution.py:540
  302.8 6.5 %grad_product.10 = (f32[4,256,256]{2,1,0:T(8,128)}, f32[4,256,256]{2,1,0:T(8,128)}, f32[4,256,256]{2,1,0:T(8,128)}) custom-call(s32[2]{0:T(128)} %pad_add_fusion.1.core_ref, s32[4]{0:T(128)} %get-tuple-element.593.blocks_ref, bf16[128,2048]{1,0:T(8,128)(2,1)} %add_ref.1, bf16[128,2048]{1,0:T(8,128)(2,1)} %collective-permute-done.4.refs_1_, ...), custom_call_target="tpu_custom_call" | custom-call | flops 49999998976 | bytes 1 | tf_op jit(solution)/shard_map/grad_product/pallas_call | solution.py:540
  314.3 4.6 middle_grad.1
  324.7 8.8 %grad_product.11 = (f32[4,256,256]{2,1,0:T(8,128)}, f32[4,256,128]{2,1,0:T(8,128)}, f32[4,256,384]{2,1,0:T(8,128)}, f32[4,256,256]{2,1,0:T(8,128)}, f32[4,256,256]{2,1,0:T(8,128)}, /*index=5*/f32[4,256,128]{2,1,0:T(8,128)}) custom-call(s32[2]{0:T(128)} %pad_add_fusion.1.core_ref, s32[4]{0:T(128)} %get-tuple-element.593.blocks_ref, ...), custom_call_target="tpu_custom_call" | custom-call | flops 49999998976 | bytes 1 | tf_op jit(solution)/shard_map/grad_product/pallas_call | solution.py:540
  343.1 9.3 %rows_product.1 = bf16[4,256,2048]{2,1,0:T(8,128)(2,1)} custom-call(s32[2]{0:T(128)} %pad_add_fusion.1.core_ref, s32[16]{0:T(128)} %stack.222.offsets_ref, bf16[4,256,256]{2,1,0:T(8,128)(2,1)} %get-tuple-element.442.refs_0_, bf16[4,256,256]{2,1,0:T(8,128)(2,1)} %get-tuple-element.443.refs_1_, bf16[4,256,256]{2,1,0:T(8,128)(2,1)} %get-tuple-element.444.refs_2_, ...), custom_call_target="tpu_custom_call" | custom-call | flops 49999998976 | bytes 1 | tf_op jit(solution)/shard_map/rows_product/pallas_call | solution.py:506
  360.9 24.0 %mixer_backward.1 = (bf16[4,256,256]{2,1,0:T(8,128)(2,1)}, bf16[4,256,256]{2,1,0:T(8,128)(2,1)}, bf16[4,256,256]{2,1,0:T(8,128)(2,1)}, bf16[3,128,2048]{2,1,0:T(...) custom-call(s32[2]{0:T(128)} %pad_add_fusion.1.core_ref, ...), custom_call_target="tpu_custom_call" | custom-call | flops 49999998976 | bytes 1 | tf_op jit(solution)/shard_map/mixer_backward/pallas_call | solution.py:337
  398.2 6.5 %grad_product.12 = (bf16[4,256,256]{2,1,0:T(8,128)(2,1)}, bf16[4,256,256]{2,1,0:T(8,128)(2,1)}, bf16[4,256,256]{2,1,0:T(8,128)(2,1)}) custom-call(s32[2]{0:T(128)} %pad_add_fusion.1.core_ref, s32[4]{0:T(128)} %get-tuple-element.592.blocks_ref, bf16[128,2048]{1,0:T(8,128)(2,1)} %fusion.4.refs_0_, bf16[128,2048]{1,0:T(8,128)(2,1)} %collective-permute-done.refs_1_, ...), custom_call_target="tpu_custom_call" | custom-call | flops 49999998976 | bytes 1 | tf_op jit(solution)/shard_map/grad_product/pallas_call | solution.py:540
  414.4 3.6 collective-permute-done.64
  426.6 6.5 %grad_product.13 = (f32[4,256,256]{2,1,0:T(8,128)}, f32[4,256,256]{2,1,0:T(8,128)}, f32[4,256,256]{2,1,0:T(8,128)}) custom-call(s32[2]{0:T(128)} %pad_add_fusion.1.core_ref, s32[4]{0:T(128)} %get-tuple-element.593.blocks_ref, bf16[128,2048]{1,0:T(8,128)(2,1)} %fusion.4.refs_0_, bf16[128,2048]{1,0:T(8,128)(2,1)} %collective-permute-done.refs_1_, ...), custom_call_target="tpu_custom_call" | custom-call | flops 49999998976 | bytes 1 | tf_op jit(solution)/shard_map/grad_product/pallas_call | solution.py:540
  433.1 5.3 grad_product.14
  441.1 7.0 %collective-permute-done.72.refs_3_ = bf16[4,256,256]{2,1,0:T(8,128)(2,1)S(1)} collective-permute-done((bf16[4,256,256]{2,1,0:T(8,128)(2,1)S(1)}, bf16[4,256,256]{2,1,0:T(8,128)(2,1)S(1)}, u32[]{:S(2)}, u32[]{:S(2)}) %collective-permute-start.72) | collective-permute-done | bytes 524320 | tf_op jit(solution)/shard_map/ppermute | solution.py:786
  456.0 4.1 all-to-all-start.3
  460.1 4.5 input_grad.1
  465.4 5.5 %grad_product.15.refs_0_ = f32[4,256,256]{2,1,0:T(8,128)} custom-call(s32[2]{0:T(128)} %pad_add_fusion.1.core_ref, s32[4]{0:T(128)} %get-tuple-element.593.blocks_ref, bf16[128,2048]{1,0:T(8,128)(2,1)} %get-tuple-element.533.refs_0_, bf16[128,2048]{1,0:T(8,128)(2,1)} %copy-done.5, bf16[128,2048]{1,0:T(8,128)(2,1)} %copy-done.6, ...), custom_call_target="tpu_custom_call" | custom-call | flops 1 | bytes 1 | tf_op jit(solution)/shard_map/grad_product/pallas_call | solution.py:540
  490.5 20.5 %collective-permute-done.79 = f32[49,128]{1,0:T(8,128)S(1)} collective-permute-done((f32[49,128]{1,0:T(8,128)S(1)}, f32[49,128]{1,0:T(8,128)S(1)}, u32[]{:S(2)}, u32[]{:S(2)}) %collective-permute-start.79) | collective-permute-done | bytes 25120 | tf_op jit(solution)/shard_map/ppermute | solution.py:786
  523.1 4.4 ffn_grad.1
  (423 shorter events, 222.9 us)
Async XLA Ops:
  32.8 55.3 %all-to-all-start.1 = ((bf16[4,128,1408]{2,1,0:T(8,128)(2,1)}), bf16[4,128,1408]{2,1,0:T(8,128)(2,1)S(1)}, u32[]{:S(2)}, u32[]{:S(2)}) async-start(bf16[4,128,1408]{2,1,0:T(8,128)(2,1)} %slice.64), calls=%async_computation.1 | async-start | bytes 2883584 | tf_op jit(solution)/shard_map/all_to_all | solution.py:831
  37.4 50.7 %collective-permute-start.2 = (bf16[4,128,1024]{2,1,0:T(8,128)(2,1)}, bf16[4,128,1024]{2,1,0:T(8,128)(2,1)}, u32[]{:S(2)}, u32[]{:S(2)}) collective-permute-start(bf16[4,128,1024]{2,1,0:T(8,128)(2,1)} %slice.63.refs_6_), channel_id=1, source_target_pairs={{0,16},{16,0},{1,17},{17,1},{2,18},{18,2},{3,19},{19,3},{4,20},{20... | collective-permute-start | bytes 3145736 | tf_op jit(solution)/shard_map/ppermute | solution.py:791
  40.0 48.1 %collective-permute-start.3 = (bf16[4,128,1024]{2,1,0:T(8,128)(2,1)}, bf16[4,128,1024]{2,1,0:T(8,128)(2,1)}, u32[]{:S(2)}, u32[]{:S(2)}) collective-permute-start(bf16[4,128,1024]{2,1,0:T(8,128)(2,1)} %slice.63.refs_6_), channel_id=1, source_target_pairs={{0,4},{4,0},{1,5},{5,1},{2,6},{6,2},{3,7},{7,3},{8,12},{12,8},{9,1... | collective-permute-start | bytes 3145736 | tf_op jit(solution)/shard_map/ppermute | solution.py:786
  41.5 24.5 %collective-permute-start = (bf16[128,2048]{1,0:T(8,128)(2,1)S(1)}, bf16[128,2048]{1,0:T(8,128)(2,1)}, u32[]{:S(2)}, u32[]{:S(2)}) collective-permute-start(bf16[128,2048]{1,0:T(8,128)(2,1)S(1)} %copy-done.10), channel_id=1, source_target_pairs={{0,2},{2,0},{1,3},{3,1},{4,6},{6,4},{5,7},{7,5},{8,10},{10,8},{9,1... | collective-permute-start | bytes 1572872 | tf_op jit(solution)/shard_map/ppermute | solution.py:786
  43.6 44.6 %collective-permute-start.1 = (bf16[128,2048]{1,0:T(8,128)(2,1)S(1)}, bf16[128,2048]{1,0:T(8,128)(2,1)}, u32[]{:S(2)}, u32[]{:S(2)}) collective-permute-start(bf16[128,2048]{1,0:T(8,128)(2,1)S(1)} %copy-done.10), channel_id=1, source_target_pairs={{0,8},{8,0},{1,9},{9,1},{2,10},{10,2},{3,11},{11,3},{4,12},{12,4},... | collective-permute-start | bytes 1572872 | tf_op jit(solution)/shard_map/ppermute | solution.py:786
  45.0 43.2 %collective-permute-start.4 = (bf16[128,2048]{1,0:T(8,128)(2,1)}, bf16[128,2048]{1,0:T(8,128)(2,1)}, u32[]{:S(2)}, u32[]{:S(2)}) collective-permute-start(bf16[128,2048]{1,0:T(8,128)(2,1)} %add_ref.1), channel_id=1, source_target_pairs={{0,2},{2,0},{1,3},{3,1},{4,6},{6,4},{5,7},{7,5},{8,10},{10,8},{9,1... | collective-permute-start | bytes 1572872 | tf_op jit(solution)/shard_map/ppermute | solution.py:786
  88.2 29.9 %collective-permute-start.6 = (bf16[4,128,1024]{2,1,0:T(8,128)(2,1)}, bf16[4,128,1024]{2,1,0:T(8,128)(2,1)S(1)}, u32[]{:S(2)}, u32[]{:S(2)}) collective-permute-start(bf16[4,128,1024]{2,1,0:T(8,128)(2,1)} %collective-permute-done.2.refs_8_), channel_id=1, source_target_pairs={{0,4},{4,0},{1,5},{5,1},{2,6},{6,2},{3,7},{7,3},{8,12},{12,8},{9,1... | collective-permute-start | bytes 3145736 | tf_op jit(solution)/shard_map/ppermute | solution.py:786
  89.8 28.2 %collective-permute-start.5 = (bf16[128,2048]{1,0:T(8,128)(2,1)}, bf16[128,2048]{1,0:T(8,128)(2,1)}, u32[]{:S(2)}, u32[]{:S(2)}) collective-permute-start(bf16[128,2048]{1,0:T(8,128)(2,1)} %collective-permute-done.1.refs_2_), channel_id=1, source_target_pairs={{0,2},{2,0},{1,3},{3,1},{4,6},{6,4},{5,7},{7,5},{8,10},{10,8},{9,1... | collective-permute-start | bytes 1572872 | tf_op jit(solution)/shard_map/ppermute | solution.py:786
  91.6 26.4 %collective-permute-start.7 = (bf16[4,128,512]{2,1,0:T(8,128)(2,1)S(1)}, bf16[4,128,512]{2,1,0:T(8,128)(2,1)S(1)}, u32[]{:S(2)}, u32[]{:S(2)}) collective-permute-start(bf16[4,128,512]{2,1,0:T(8,128)(2,1)S(1)} %get-tuple-element.300), channel_id=1, source_target_pairs={{0,16},{16,0},{1,17},{17,1},{2,18},{18,2},{3,19},{19,3},{4,20},{20... | collective-permute-start | bytes 1572872 | tf_op jit(solution)/shard_map/ppermute | solution.py:791
  94.3 23.7 %collective-permute-start.8 = (bf16[128,2048]{1,0:T(8,128)(2,1)}, bf16[128,2048]{1,0:T(8,128)(2,1)S(1)}, u32[]{:S(2)}, u32[]{:S(2)}) collective-permute-start(bf16[128,2048]{1,0:T(8,128)(2,1)} %add_ref.1), channel_id=1, source_target_pairs={{0,8},{8,0},{1,9},{9,1},{2,10},{10,2},{3,11},{11,3},{4,12},{12,4},... | collective-permute-start | bytes 1572872 | tf_op jit(solution)/shard_map/ppermute | solution.py:786
  122.5 26.7 %collective-permute-start.12 = (bf16[4,128,512]{2,1,0:T(8,128)(2,1)}, bf16[4,128,512]{2,1,0:T(8,128)(2,1)}, u32[]{:S(2)}, u32[]{:S(2)}) collective-permute-start(bf16[4,128,512]{2,1,0:T(8,128)(2,1)} %get-tuple-element.315), channel_id=1, source_target_pairs={{0,16},{16,0},{1,17},{17,1},{2,18},{18,2},{3,19},{19,3},{4,20},{20... | collective-permute-start | bytes 1572872 | tf_op jit(solution)/shard_map/ppermute | solution.py:791
  125.1 24.0 %collective-permute-start.13 = (bf16[4,128,512]{2,1,0:T(8,128)(2,1)}, bf16[4,128,512]{2,1,0:T(8,128)(2,1)}, u32[]{:S(2)}, u32[]{:S(2)}) collective-permute-start(bf16[4,128,512]{2,1,0:T(8,128)(2,1)} %get-tuple-element.316), channel_id=1, source_target_pairs={{0,4},{4,0},{1,5},{5,1},{2,6},{6,2},{3,7},{7,3},{8,12},{12,8},{9,1... | collective-permute-start | bytes 1572872 | tf_op jit(solution)/shard_map/ppermute | solution.py:786
  126.7 24.0 %collective-permute-start.14 = (bf16[4,128,512]{2,1,0:T(8,128)(2,1)}, bf16[4,128,512]{2,1,0:T(8,128)(2,1)}, u32[]{:S(2)}, u32[]{:S(2)}) collective-permute-start(bf16[4,128,512]{2,1,0:T(8,128)(2,1)} %copy-done.56), channel_id=1, source_target_pairs={{0,4},{4,0},{1,5},{5,1},{2,6},{6,2},{3,7},{7,3},{8,12},{12,8},{9,1... | collective-permute-start | bytes 1572872 | tf_op jit(solution)/shard_map/ppermute | solution.py:786
  127.2 23.5 %collective-permute-start.15 = (bf16[128,2048]{1,0:T(8,128)(2,1)}, bf16[128,2048]{1,0:T(8,128)(2,1)}, u32[]{:S(2)}, u32[]{:S(2)}) collective-permute-start(bf16[128,2048]{1,0:T(8,128)(2,1)} %copy-done.29), channel_id=1, source_target_pairs={{0,2},{2,0},{1,3},{3,1},{4,6},{6,4},{5,7},{7,5},{8,10},{10,8},{9,1... | collective-permute-start | bytes 1572872 | tf_op jit(solution)/shard_map/ppermute | solution.py:786
  127.2 25.4 %all-to-all-start.2 = ((bf16[4,128,768]{2,1,0:T(8,128)(2,1)}), bf16[4,128,768]{2,1,0:T(8,128)(2,1)S(1)}, u32[]{:S(2)}, u32[]{:S(2)}) async-start(bf16[4,128,768]{2,1,0:T(8,128)(2,1)} %slice.65), calls=%async_computation.2 | async-start | bytes 1572864 | tf_op jit(solution)/shard_map/all_to_all | solution.py:831
  130.7 340.2 %reduce-scatter.2.cloned.1.call-start = ((), (), s32[]{:S(2)}) async-start(), calls=%async_computation.7 | async-start | bytes 4718592 | tf_op jit(solution)/shard_map/reduce_scatter | solution.py:1113
  353.2 31.8 %collective-permute-start.60 = (bf16[4,256,384]{2,1,0:T(8,128)(2,1)}, bf16[4,256,384]{2,1,0:T(8,128)(2,1)S(1)}, u32[]{:S(2)}, u32[]{:S(2)}) collective-permute-start(bf16[4,256,384]{2,1,0:T(8,128)(2,1)} %get-tuple-element.468), channel_id=1, source_target_pairs={{0,4},{4,0},{1,5},{5,1},{2,6},{6,2},{3,7},{7,3},{8,12},{12,8},{9,1... | collective-permute-start | bytes 2359304 | tf_op jit(solution)/shard_map/ppermute | solution.py:786
  353.7 31.3 %collective-permute-start.61 = (bf16[4,256,256]{2,1,0:T(8,128)(2,1)}, bf16[4,256,256]{2,1,0:T(8,128)(2,1)S(1)}, u32[]{:S(2)}, u32[]{:S(2)}) collective-permute-start(bf16[4,256,256]{2,1,0:T(8,128)(2,1)} %get-tuple-element.469), channel_id=1, source_target_pairs={{0,4},{4,0},{1,5},{5,1},{2,6},{6,2},{3,7},{7,3},{8,12},{12,8},{9,1... | collective-permute-start | bytes 1572872 | tf_op jit(solution)/shard_map/ppermute | solution.py:786
  359.6 25.8 %collective-permute-start.59 = (bf16[2,256,512]{2,1,0:T(8,128)(2,1)}, bf16[2,256,512]{2,1,0:T(8,128)(2,1)S(1)}, u32[]{:S(2)}, u32[]{:S(2)}) collective-permute-start(bf16[2,256,512]{2,1,0:T(8,128)(2,1)} %get-tuple-element.467), channel_id=1, source_target_pairs={{0,16},{16,0},{1,17},{17,1},{2,18},{18,2},{3,19},{19,3},{4,20},{20... | collective-permute-start | bytes 1572872 | tf_op jit(solution)/shard_map/ppermute | solution.py:791
  386.8 22.6 %collective-permute-start.66 = (bf16[4,256,256]{2,1,0:T(8,128)(2,1)S(1)}, bf16[4,256,256]{2,1,0:T(8,128)(2,1)S(1)}, u32[]{:S(2)}, u32[]{:S(2)}) collective-permute-start(bf16[4,256,256]{2,1,0:T(8,128)(2,1)S(1)} %copy-done.58), channel_id=1, source_target_pairs={{0,4},{4,0},{1,5},{5,1},{2,6},{6,2},{3,7},{7,3},{8,12},{12,8},{9,1... | collective-permute-start | bytes 1572872 | tf_op jit(solution)/shard_map/ppermute | solution.py:786
  393.8 24.2 %collective-permute-start.64 = (bf16[128,2048]{1,0:T(8,128)(2,1)}, bf16[128,2048]{1,0:T(8,128)(2,1)S(1)}, u32[]{:S(2)}, u32[]{:S(2)}) collective-permute-start(bf16[128,2048]{1,0:T(8,128)(2,1)} %add_last.5), channel_id=1, source_target_pairs={{0,2},{2,0},{1,3},{3,1},{4,6},{6,4},{5,7},{7,5},{8,10},{10,8},{9,1... | collective-permute-start | bytes 1572872 | tf_op jit(solution)/shard_map/ppermute | solution.py:786
  395.7 25.8 %collective-permute-start.65 = (bf16[2,256,512]{2,1,0:T(8,128)(2,1)S(1)}, bf16[2,256,512]{2,1,0:T(8,128)(2,1)S(1)}, u32[]{:S(2)}, u32[]{:S(2)}) collective-permute-start(bf16[2,256,512]{2,1,0:T(8,128)(2,1)S(1)} %copy-done.68), channel_id=1, source_target_pairs={{0,16},{16,0},{1,17},{17,1},{2,18},{18,2},{3,19},{19,3},{4,20},{20... | collective-permute-start | bytes 1572872 | tf_op jit(solution)/shard_map/ppermute | solution.py:791
  421.5 30.6 %collective-permute-start.68 = (bf16[128,2048]{1,0:T(8,128)(2,1)S(1)}, bf16[128,2048]{1,0:T(8,128)(2,1)S(1)}, u32[]{:S(2)}, u32[]{:S(2)}) collective-permute-start(bf16[128,2048]{1,0:T(8,128)(2,1)S(1)} %copy-done.63), channel_id=1, source_target_pairs={{0,2},{2,0},{1,3},{3,1},{4,6},{6,4},{5,7},{7,5},{8,10},{10,8},{9,1... | collective-permute-start | bytes 1572872 | tf_op jit(solution)/shard_map/ppermute | solution.py:786
  422.0 30.2 %collective-permute-start.69 = (bf16[128,2048]{1,0:T(8,128)(2,1)S(1)}, bf16[128,2048]{1,0:T(8,128)(2,1)S(1)}, u32[]{:S(2)}, u32[]{:S(2)}) collective-permute-start(bf16[128,2048]{1,0:T(8,128)(2,1)S(1)} %add_convert_fusion.1), channel_id=1, source_target_pairs={{0,8},{8,0},{1,9},{9,1},{2,10},{10,2},{3,11},{11,3},{4,12},{12,4},... | collective-permute-start | bytes 1572872 | tf_op jit(solution)/shard_map/ppermute | solution.py:786
  422.0 31.0 %collective-permute-start.70 = (bf16[2,256,640]{2,1,0:T(8,128)(2,1)S(1)}, bf16[2,256,640]{2,1,0:T(8,128)(2,1)S(1)}, u32[]{:S(2)}, u32[]{:S(2)}) collective-permute-start(bf16[2,256,640]{2,1,0:T(8,128)(2,1)S(1)} %copy-done.54), channel_id=1, source_target_pairs={{0,16},{16,0},{1,17},{17,1},{2,18},{18,2},{3,19},{19,3},{4,20},{20... | collective-permute-start | bytes 1966088 | tf_op jit(solution)/shard_map/ppermute | solution.py:791
  425.3 22.9 %collective-permute-start.72 = (bf16[4,256,256]{2,1,0:T(8,128)(2,1)S(1)}, bf16[4,256,256]{2,1,0:T(8,128)(2,1)S(1)}, u32[]{:S(2)}, u32[]{:S(2)}) collective-permute-start(bf16[4,256,256]{2,1,0:T(8,128)(2,1)S(1)} %copy-done.64), channel_id=1, source_target_pairs={{0,4},{4,0},{1,5},{5,1},{2,6},{6,2},{3,7},{7,3},{8,12},{12,8},{9,1... | collective-permute-start | bytes 1572872 | tf_op jit(solution)/shard_map/ppermute | solution.py:786
  453.0 27.2 %collective-permute-start.73 = (bf16[2,256,512]{2,1,0:T(8,128)(2,1)}, bf16[2,256,512]{2,1,0:T(8,128)(2,1)}, u32[]{:S(2)}, u32[]{:S(2)}) collective-permute-start(bf16[2,256,512]{2,1,0:T(8,128)(2,1)} %get-tuple-element.541), channel_id=1, source_target_pairs={{0,16},{16,0},{1,17},{17,1},{2,18},{18,2},{3,19},{19,3},{4,20},{20... | collective-permute-start | bytes 1572872 | tf_op jit(solution)/shard_map/ppermute | solution.py:791
  454.5 22.6 %collective-permute-start.75 = (bf16[4,256,256]{2,1,0:T(8,128)(2,1)}, bf16[4,256,256]{2,1,0:T(8,128)(2,1)}, u32[]{:S(2)}, u32[]{:S(2)}) collective-permute-start(bf16[4,256,256]{2,1,0:T(8,128)(2,1)} %get-tuple-element.552), channel_id=1, source_target_pairs={{0,4},{4,0},{1,5},{5,1},{2,6},{6,2},{3,7},{7,3},{8,12},{12,8},{9,1... | collective-permute-start | bytes 1572872 | tf_op jit(solution)/shard_map/ppermute | solution.py:786
  456.0 26.3 %all-to-all-start.3 = ((bf16[4,128,1024]{2,1,0:T(8,128)(2,1)}), bf16[4,128,1024]{2,1,0:T(8,128)(2,1)S(1)}, u32[]{:S(2)}, u32[]{:S(2)}) async-start(bf16[4,128,1024]{2,1,0:T(8,128)(2,1)} %bitcast.64), calls=%async_computation.4 | async-start | bytes 2097152 | tf_op jit(solution)/shard_map/all_to_all | solution.py:831
  482.2 28.7 %all-to-all-start.4 = ((bf16[4,128,1152]{2,1,0:T(8,128)(2,1)}), bf16[4,128,1152]{2,1,0:T(8,128)(2,1)S(1)}, u32[]{:S(2)}, u32[]{:S(2)}) async-start(bf16[4,128,1152]{2,1,0:T(8,128)(2,1)} %bitcast.66), calls=%async_computation.5 | async-start | bytes 2359296 | tf_op jit(solution)/shard_map/all_to_all | solution.py:831
  485.8 25.2 %collective-permute-start.76 = (bf16[2,256,512]{2,1,0:T(8,128)(2,1)}, bf16[2,256,512]{2,1,0:T(8,128)(2,1)S(1)}, u32[]{:S(2)}, u32[]{:S(2)}) collective-permute-start(bf16[2,256,512]{2,1,0:T(8,128)(2,1)} %get-tuple-element.562), channel_id=1, source_target_pairs={{0,16},{16,0},{1,17},{17,1},{2,18},{18,2},{3,19},{19,3},{4,20},{20... | collective-permute-start | bytes 1572872 | tf_op jit(solution)/shard_map/ppermute | solution.py:791
  487.0 24.0 %collective-permute-start.79 = (f32[49,128]{1,0:T(8,128)S(1)}, f32[49,128]{1,0:T(8,128)S(1)}, u32[]{:S(2)}, u32[]{:S(2)}) collective-permute-start(f32[49,128]{1,0:T(8,128)S(1)} %maximum_bitcast_fusion), channel_id=1, source_target_pairs={{0,10},{2,8},{8,2},{10,0},{1,11},{3,9},{9,3},{11,1},{4,14},{6,12},... | collective-permute-start | bytes 75272 | tf_op jit(solution)/shard_map/ppermute | solution.py:786
  (149 other events, 1516.3 us)
Sparse Core Ops, SparseCore 0:
  358.5 56.6 reduce-scatter.1
